TPU v7x, 32 devices: a whole 2x2x4 slice. The times are simulated.
32 devices in a mesh: rows: 8 (over z, y), hid: 4 (over x, core).
Axes of the slice: x: 2, y: 2, z: 4, core: 2. Of those that a mesh axis runs over, the one named last changes fastest.
Arguments:
- tokens: bfloat16 [768, 4096], P('hid', 'rows'), may hold values from -6 to 6
- w_qkv: bfloat16 [3, 768, 768], P(None, 'hid'), may hold values from -0.3125 to 0.3125
- b_qv: float32 [2, 768], P(None, 'hid'), may hold values from -3 to 3
- w_out: bfloat16 [768, 768], P('hid'), may hold values from -1.25 to 1.25
- b_out: float32 [768], P('hid'), may hold values from -2 to 2
- w_in: bfloat16 [768, 3072], P(None, 'hid'), may hold values from -0.21875 to 0.21875
- b_in: float32 [3072], P('hid'), may hold values from -2 to 2
- w_back: bfloat16 [768, 3072], P('hid'), may hold values from -0.15625 to 0.15625
- b_back: float32 [768], P('hid'), may hold values from -2 to 2
- norm_gain: float32 [2, 768], P(None, 'hid'), may hold values from 0.5 to 1.5
- norm_bias: float32 [2, 768], P(None, 'hid'), may hold values from -2 to 2
- head_gate: float32 [12], P('hid'), may hold values from 0.3 to 1
- inter_gate: float32 [3072], P('hid'), may hold values from 0.3 to 1
- branch_gate: float32 [2], replicated, may hold values from 0.6 to 1.4
- hidden_gate: float32 [768], P('hid'), may hold values from 0.5 to 1.2
- hidden_mask: int32 [768], P('hid'), may hold values 0 or 1
- doc_lengths: int32 [8, 4], P('rows'), may hold values from 1 to 256, 512 in all within a row
- cotangent: bfloat16 [768, 4096], P('hid', 'rows'), may hold values from -6 to 6
Outputs:
- output: bfloat16 [768, 4096], P('hid', 'rows')
- grad_tokens: bfloat16 [768, 4096], P('hid', 'rows')
- grad_w_qkv: float32 [3, 768, 768], P(None, 'hid')
- grad_b_qv: float32 [2, 768], P(None, 'hid')
- grad_w_out: float32 [768, 768], P('hid')
- grad_b_out: float32 [768], P('hid')
- grad_w_in: float32 [768, 3072], P(None, 'hid')
- grad_b_in: float32 [3072], P('hid')
- grad_w_back: float32 [768, 3072], P('hid')
- grad_b_back: float32 [768], P('hid')
- grad_norm_gain: float32 [2, 768], P(None, 'hid')
- grad_norm_bias: float32 [2, 768], P(None, 'hid')
- grad_head_gate: float32 [12], P('hid')
- grad_inter_gate: float32 [3072], P('hid')
- grad_branch_gate: float32 [2], replicated
- grad_hidden_gate: float32 [768], P('hid')
Inputs may be any that keep to these rules, and one draw needn't show every extreme that they name: `doc_lengths`: in each packed row the 4 lengths add up to 512.
All inputs are finite; a program needn't handle non-finite values. No bound on the sum of `hidden_mask` on one device may be relied on, other than what follows from the above.
Results may differ from a plain program's by a relative error of at most 0.0128.
The roundings to bfloat16 on the way count: a program that leaves them out, or rounds other values in their place, can miss the bound.
Values may be sent and summed in bfloat16 or wider, within the bound.
No kernel may reach another device: no remote copies, remote signals or barrier semaphores. Data moves between devices by JAX's collectives and lax.ppermute only.
A program may use at most 64 MiB of HBM per device.

v0:
```python
import jax
import jax.numpy as jnp
from jax import lax
from jax.sharding import PartitionSpec as P

HEAD_DIM = 64


norm_eps = 1e-06
masked_score = -1e30


def gelu_value(inputs):
    return jax.nn.gelu(inputs, approximate=False)


def gelu_slope(inputs):
    return (
        0.5 * (1.0 + lax.erf(inputs * 0.7071067811865476))
        + inputs * jnp.exp(-0.5 * inputs * inputs) * 0.3989422804014327
    )


def contract_rows(left_mat, right_mat):
    return lax.dot_general(
        left_mat, right_mat, (((0,), (0,)), ((), ())), preferred_element_type=jnp.float32
    )


def contract_cols(left_mat, right_mat):
    return lax.dot_general(
        left_mat, right_mat, (((1,), (1,)), ((), ())), preferred_element_type=jnp.float32
    )


def doc_ids(lengths, row_count):
    doc_ends = jnp.cumsum(lengths)
    position = jnp.arange(row_count, dtype=jnp.int32)
    return jnp.sum((position[:, None] >= doc_ends[None, :]).astype(jnp.int32), axis=1)


def split_heads(rows_in):
    row_count, col_count = rows_in.shape
    return rows_in.reshape(row_count, col_count // HEAD_DIM, HEAD_DIM)


def head_scores(query_rows, key_rows, segments):
    raw_scores = jnp.einsum(
        "qhd,khd->hqk",
        split_heads(query_rows),
        split_heads(key_rows),
        preferred_element_type=jnp.float32,
    ) * HEAD_DIM ** (-0.5)
    same_doc = segments[:, None] == segments[None, :]
    return jnp.where(same_doc[None], raw_scores, masked_score)


def attend(query_rows, key_rows, value_rows, segments):
    logits = head_scores(query_rows, key_rows, segments)
    row_peak = jnp.max(logits, axis=2, keepdims=True)
    exponent = jnp.exp(logits - row_peak)
    expo_sum = jnp.sum(exponent, axis=2, keepdims=True)
    probs = (exponent / expo_sum).astype(jnp.bfloat16)
    context = jnp.einsum(
        "hqk,khd->qhd", probs, split_heads(value_rows), preferred_element_type=jnp.float32
    )
    return (context.reshape(value_rows.shape), row_peak[..., 0] + jnp.log(expo_sum[..., 0]))


def attend_back(query_rows, key_rows, value_rows, segments, logsum, upstream):
    logits = head_scores(query_rows, key_rows, segments)
    probs = jnp.exp(logits - logsum[..., None])
    up_heads = split_heads(upstream)
    grad_probs = jnp.einsum(
        "qhd,khd->hqk", up_heads, split_heads(value_rows), preferred_element_type=jnp.float32
    )
    grad_values = jnp.einsum(
        "hqk,qhd->khd", probs.astype(jnp.bfloat16), up_heads, preferred_element_type=jnp.float32
    )
    inner = jnp.sum(probs * grad_probs, axis=2, keepdims=True)
    grad_scores = (probs * (grad_probs - inner)).astype(jnp.bfloat16)
    scale = HEAD_DIM ** (-0.5)
    grad_query = (
        jnp.einsum(
            "hqk,khd->qhd", grad_scores, split_heads(key_rows), preferred_element_type=jnp.float32
        )
        * scale
    )
    grad_keys = (
        jnp.einsum(
            "hqk,qhd->khd", grad_scores, split_heads(query_rows), preferred_element_type=jnp.float32
        )
        * scale
    )
    stacked = jnp.stack([grad_query, grad_keys, grad_values]).reshape((3,) + value_rows.shape)
    return stacked.astype(jnp.bfloat16)


def layer_norm(residual, gain_row, bias_row, total_width):
    row_total, square = lax.psum((jnp.sum(residual, 1), jnp.sum(residual * residual, 1)), "hid")
    row_mean = row_total / total_width
    spread = square / total_width - row_mean * row_mean
    inv_std = lax.rsqrt(spread + norm_eps)
    x_hat = (residual - row_mean[:, None]) * inv_std[:, None]
    return (x_hat * gain_row + bias_row, x_hat, inv_std)


def norm_back(grad_in, x_hat, inv_std, gain_row, weight, total_width):
    scaled = grad_in * gain_row
    row_plain, row_along, scaled_weight, weight_sum, hat_weight = lax.psum(
        (
            jnp.sum(scaled, 1),
            jnp.sum(scaled * x_hat, 1),
            jnp.sum(scaled * weight, 1),
            jnp.sum(weight, 1),
            jnp.sum(x_hat * weight, 1),
        ),
        "hid",
    )
    mean_plain = row_plain / total_width
    mean_along = row_along / total_width
    grad_resid = inv_std[:, None] * (scaled - mean_plain[:, None] - x_hat * mean_along[:, None])
    gate_part = jnp.sum(
        inv_std * (scaled_weight - mean_plain * weight_sum - mean_along * hat_weight)
    )
    return (grad_resid, gate_part)


def shards(
    tokens,
    w_qkv,
    b_qv,
    w_out,
    b_out,
    w_in,
    b_in,
    w_back,
    b_back,
    norm_gain,
    norm_bias,
    head_gate,
    inter_gate,
    branch_gate,
    hidden_gate,
    hidden_mask,
    doc_lengths,
    cotangent,
):
    col_count, row_count = tokens.shape
    total_width = col_count * lax.axis_size("hid")
    segments = doc_ids(doc_lengths[0], row_count)
    kept_units = hidden_mask.astype(jnp.float32)
    scale_cols = hidden_gate * kept_units
    head_cols = jnp.repeat(head_gate, HEAD_DIM)
    feature_cols = lax.all_gather(tokens, "hid", axis=0, tiled=True)
    projected = jnp.einsum("dt,ced->cte", feature_cols, w_qkv, preferred_element_type=jnp.float32)
    bias_rows = jnp.stack([b_qv[0], jnp.zeros_like(b_qv[0]), b_qv[1]])
    qkv_rows = (projected + bias_rows[:, None, :]).astype(jnp.bfloat16)
    context, logsum = attend(qkv_rows[0], qkv_rows[1], qkv_rows[2], segments)
    gated_ctx = (context * head_cols).astype(jnp.bfloat16)
    context_all = lax.all_gather(gated_ctx, "hid", axis=1, tiled=True)
    attn_pre = contract_cols(context_all, w_out) + b_out
    residual = tokens.astype(jnp.float32).T + branch_gate[0] * attn_pre * scale_cols
    normed, hat_one, inv_one = layer_norm(residual, norm_gain[0], norm_bias[0], total_width)
    normed_all = lax.all_gather(normed.astype(jnp.bfloat16), "hid", axis=1, tiled=True)
    pre_act = jnp.dot(normed_all, w_in, preferred_element_type=jnp.float32) + b_in
    activated = gelu_value(pre_act)
    inter_out = (activated * inter_gate).astype(jnp.bfloat16)
    inter_all = lax.all_gather(inter_out, "hid", axis=1, tiled=True)
    ffn_pre = contract_cols(inter_all, w_back) + b_back
    resid_two = normed + branch_gate[1] * ffn_pre * scale_cols
    output, hat_two, inv_two = layer_norm(resid_two, norm_gain[1], norm_bias[1], total_width)
    grad_out = cotangent.astype(jnp.float32).T
    grad_resid_two, ffn_part = norm_back(
        grad_out, hat_two, inv_two, norm_gain[1], ffn_pre * scale_cols, total_width
    )
    grad_gain_two = jnp.sum(grad_out * hat_two, 0)
    grad_bias_two = jnp.sum(grad_out, 0)
    grad_ffn = (grad_resid_two * scale_cols * branch_gate[1]).astype(jnp.bfloat16)
    hidden_ffn = jnp.sum(grad_resid_two * ffn_pre, 0) * branch_gate[1] * kept_units
    grad_b_back = jnp.sum(grad_ffn.astype(jnp.float32), 0)
    grad_w_back = contract_rows(grad_ffn, inter_all)
    grad_inter = lax.psum_scatter(
        jnp.dot(grad_ffn, w_back, preferred_element_type=jnp.float32),
        "hid",
        scatter_dimension=1,
        tiled=True,
    )
    grad_inter_gate = jnp.sum(grad_inter * activated, 0)
    grad_pre = (grad_inter * inter_gate * gelu_slope(pre_act)).astype(jnp.bfloat16)
    grad_b_in = jnp.sum(grad_pre.astype(jnp.float32), 0)
    grad_w_in = contract_rows(normed_all, grad_pre)
    grad_normed = (
        lax.psum_scatter(contract_cols(grad_pre, w_in), "hid", scatter_dimension=1, tiled=True)
        + grad_resid_two
    )
    grad_resid_one, attn_part = norm_back(
        grad_normed, hat_one, inv_one, norm_gain[0], attn_pre * scale_cols, total_width
    )
    grad_gain_one = jnp.sum(grad_normed * hat_one, 0)
    grad_bias_one = jnp.sum(grad_normed, 0)
    grad_attn = (grad_resid_one * scale_cols * branch_gate[0]).astype(jnp.bfloat16)
    hidden_attn = jnp.sum(grad_resid_one * attn_pre, 0) * branch_gate[0] * kept_units
    grad_b_out = jnp.sum(grad_attn.astype(jnp.float32), 0)
    grad_w_out = contract_rows(grad_attn, context_all)
    grad_gated = lax.psum_scatter(
        jnp.dot(grad_attn, w_out, preferred_element_type=jnp.float32),
        "hid",
        scatter_dimension=1,
        tiled=True,
    )
    grad_head_gate = jnp.sum(split_heads(grad_gated * context), axis=(0, 2))
    upstream = (grad_gated * head_cols).astype(jnp.bfloat16)
    grad_qkv = attend_back(qkv_rows[0], qkv_rows[1], qkv_rows[2], segments, logsum, upstream)
    grad_b_qv = jnp.stack(
        [jnp.sum(grad_qkv[0].astype(jnp.float32), 0), jnp.sum(grad_qkv[2].astype(jnp.float32), 0)]
    )
    grad_w_qkv = jnp.einsum(
        "dt,cte->ced", feature_cols, grad_qkv, preferred_element_type=jnp.float32
    )
    grad_input = jnp.einsum("cte,ced->td", grad_qkv, w_qkv, preferred_element_type=jnp.float32)
    grad_tokens = (
        lax.psum_scatter(grad_input, "hid", scatter_dimension=1, tiled=True) + grad_resid_one
    )
    hidden_total = hidden_attn + hidden_ffn
    (
        grad_w_qkv,
        grad_b_qv,
        grad_w_out,
        grad_b_out,
        grad_head_gate,
        grad_gain_one,
        grad_bias_one,
        attn_part,
        grad_w_back,
        grad_b_back,
        grad_inter_gate,
        grad_w_in,
        grad_b_in,
        grad_gain_two,
        grad_bias_two,
        ffn_part,
        hidden_total,
    ) = lax.psum(
        (
            grad_w_qkv,
            grad_b_qv,
            grad_w_out,
            grad_b_out,
            grad_head_gate,
            grad_gain_one,
            grad_bias_one,
            attn_part,
            grad_w_back,
            grad_b_back,
            grad_inter_gate,
            grad_w_in,
            grad_b_in,
            grad_gain_two,
            grad_bias_two,
            ffn_part,
            hidden_total,
        ),
        "rows",
    )
    grad_norm_gain = jnp.stack([grad_gain_one, grad_gain_two])
    grad_norm_bias = jnp.stack([grad_bias_one, grad_bias_two])
    grad_branch_gate = jnp.stack([attn_part, ffn_part])
    return (
        output.T.astype(jnp.bfloat16),
        grad_tokens.T.astype(jnp.bfloat16),
        grad_w_qkv,
        grad_b_qv,
        grad_w_out,
        grad_b_out,
        grad_w_in,
        grad_b_in,
        grad_w_back,
        grad_b_back,
        grad_norm_gain,
        grad_norm_bias,
        grad_head_gate,
        grad_inter_gate,
        grad_branch_gate,
        hidden_total,
    )


def solution(mesh):
    return jax.shard_map(
        shards,
        mesh=mesh,
        in_specs=(
            P("hid", "rows"),
            P(None, "hid", None),
            P(None, "hid"),
            P("hid", None),
            P("hid"),
            P(None, "hid"),
            P("hid"),
            P("hid", None),
            P("hid"),
            P(None, "hid"),
            P(None, "hid"),
            P("hid"),
            P("hid"),
            P(),
            P("hid"),
            P("hid"),
            P("rows", None),
            P("hid", "rows"),
        ),
        out_specs=(
            P("hid", "rows"),
            P("hid", "rows"),
            P(None, "hid", None),
            P(None, "hid"),
            P("hid", None),
            P("hid"),
            P(None, "hid"),
            P("hid"),
            P("hid", None),
            P("hid"),
            P(None, "hid"),
            P(None, "hid"),
            P("hid"),
            P("hid"),
            P(),
            P("hid"),
        ),
        check_vma=False,
    )
```

profile of v0, /device:TPU:0, one launch (start us, length us, event | category | flops | bytes accessed | tf_op | source)
XLA Modules:
  0.0 561.0 jit_solution(15170078965424907316)
XLA Ops:
  7.2 1.3 fusion.70
  8.6 0.8 reduce-window.8
  9.5 0.7 broadcast_in_dim.20
  10.3 0.8 fusion.69
  11.1 1.3 fusion.67
  12.4 1.3 fusion.68
  13.9 10.3 %all_gather.12 = bf16[768,512]{1,0:T(8,128)(2,1)S(1)} all-gather(bf16[192,512]{1,0:T(8,128)(2,1)} %param.18), channel_id=1, replica_groups=mesh['rows'=8,'hid'=4] {'hid'}, dimensions={0}, use_global_device_ids=true | all-gather | bytes 983040 | tf_op jit(solution)/shard_map/all_gather | solution.py:155
  24.4 1.9 fusion.22
  26.4 0.8 fusion.71
  27.6 1.2 copy-done.1
  28.8 0.7 fusion.20
  29.7 8.9 %all_gather.13 = bf16[512,768]{0,1:T(8,128)(2,1)S(1)} all-gather(bf16[512,192]{0,1:T(8,128)(2,1)S(1)} %multiply_convert_fusion.5), channel_id=1, replica_groups=mesh['rows'=8,'hid'=4] {'hid'}, dimensions={1}, use_global_device_ids=true | all-gather | bytes 983040 | tf_op jit(solution)/shard_map/all_gather | solution.py:161
  38.6 1.0 fusion.60
  39.7 6.7 %all-reduce.5 = (f32[512]{0:T(512)S(1)}, f32[512]{0:T(512)S(1)}) all-reduce(f32[512]{0:T(512)S(1)} %get-tuple-element.31, f32[512]{0:T(512)S(1)} %get-tuple-element.30), channel_id=1, replica_groups=mesh['rows'=8,'hid'=4] {'hid'}, use_global_device_ids=true, to_apply=%region_7.8 | all-reduce | flops 1024 | bytes 8192 | tf_op jit(solution)/shard_map/psum | solution.py:100
  47.0 0.8 fusion.54
  47.8 8.0 %all_gather.14 = bf16[512,768]{0,1:T(8,128)(2,1)S(1)} all-gather(bf16[512,192]{0,1:T(8,128)(2,1)S(1)} %fusion.54), channel_id=1, replica_groups=mesh['rows'=8,'hid'=4] {'hid'}, dimensions={1}, use_global_device_ids=true | all-gather | bytes 983040 | tf_op jit(solution)/shard_map/all_gather | solution.py:165
  55.9 5.7 %multiply_convert_fusion.1 = (bf16[512,768]{1,0:T(8,128)(2,1)}, f32[512,768]{1,0:T(8,128)}, f32[512,768]{1,0:T(8,128)}) fusion(f32[768]{0:T(1024)S(1)} %copy-done.56, f32[768]{0:T(1024)S(1)} %copy-done.76, bf16[512,768]{0,1:T(8,128)(2,1)S(1)} %all_gather.14, bf16[768,768]{1,0:T(8,128)(2,1)S(1)} %copy-done.73), kind=kOutput, calls=%fused_computation.22 | convolution fusion | flops 630325248 | bytes 5904384 | tf_op jit(solution)/shard_map/dot_general | solution.py:166
  61.6 29.5 %all-gather.2.cloned.1.call-done = bf16[512,3072]{1,0:T(8,128)(2,1)} async-done(((bf16[512,768]{1,0:T(8,128)(2,1)}), bf16[512,3072]{1,0:T(8,128)(2,1)}) %all-gather.2.cloned.1.call-update) | async-done | bytes 3145744 | tf_op jit(solution)/shard_map/all_gather | solution.py:169
  91.1 5.2 fusion.59
  96.3 6.6 %all-reduce.4 = (f32[512]{0:T(512)}, f32[512]{0:T(512)}) all-reduce(f32[512]{0:T(512)} %get-tuple-element.29, f32[512]{0:T(512)} %get-tuple-element.28), channel_id=1, replica_groups=mesh['rows'=8,'hid'=4] {'hid'}, use_global_device_ids=true, to_apply=%region_11.12 | all-reduce | flops 1024 | bytes 8192 | tf_op jit(solution)/shard_map/psum | solution.py:100
  102.9 0.7 broadcast_multiply_fusion.4
  104.1 1.4 fusion.36
  105.5 6.3 %all-reduce.3 = (f32[512]{0:T(512)}, f32[512]{0:T(512)}) all-reduce(f32[512]{0:T(512)} %get-tuple-element.33, f32[512]{0:T(512)} %get-tuple-element.32), channel_id=1, replica_groups=mesh['rows'=8,'hid'=4] {'hid'}, use_global_device_ids=true, to_apply=%region_15.16 | all-reduce | flops 1024 | bytes 8192 | tf_op jit(solution)/shard_map/psum | solution.py:110
  111.9 0.7 broadcast_multiply_fusion.2
  113.1 2.8 convert_reduce_fusion.2
  115.9 4.6 fusion.72
  120.6 59.8 %reduce-scatter.5.cloned.1.call-done = f32[512,768]{1,0:T(8,128)} async-done(((f32[512,3072]{1,0:T(8,128)}), f32[512,768]{1,0:T(8,128)}) %reduce-scatter.5.cloned.1.call-update) | async-done | bytes 1572880 | tf_op jit(solution)/shard_map/reduce_scatter | solution.py:183
  180.3 3.9 convert_reduce_fusion
  184.3 0.9 copy-done.3
  185.1 1.9 fusion.73
  187.2 28.3 %reduce-scatter.7.cloned.1.call-done = f32[512,192]{0,1:T(8,128)} async-done(((f32[512,768]{0,1:T(8,128)}), f32[512,192]{0,1:T(8,128)}) %reduce-scatter.7.cloned.1.call-update) | async-done | bytes 393232 | tf_op jit(solution)/shard_map/reduce_scatter | solution.py:194
  215.5 3.0 multiply_reduce_fusion.2
  218.5 11.6 %all-reduce.2 = (f32[512]{0:T(512)S(1)}, f32[512]{0:T(512)S(1)}, f32[512]{0:T(512)}, f32[512]{0:T(512)}, f32[512]{0:T(512)}, /*index=5*/f32[512]{0:T(512)S(1)}, f32[512]{0:T(512)S(1)}, f32[512]{0:T(512)S(1)}) all-reduce(f32[512]{0:T(512)} %get-tuple-element.84, ...), channel_id=1, replica_groups=mesh['rows'=8,'hid'=4] {'hid'}, use_global_device_ids=true, to_apply=%region_21.22 | all-reduce | flops 4096 | bytes 32768 | tf_op jit(solution)/shard_map/psum | solution.py:110
  230.0 1.3 multiply_reduce_fusion.16
  231.4 1.8 multiply_reduce_fusion.3
  233.2 1.4 convert_reduce_fusion.3
  234.6 0.7 copy-done.11
  235.3 2.6 fusion.74
  238.0 29.2 %reduce-scatter.9.cloned.1.call-done = f32[512,192]{0,1:T(8,128)} async-done(((f32[512,768]{0,1:T(8,128)}), f32[512,192]{0,1:T(8,128)}) %reduce-scatter.9.cloned.1.call-update) | async-done | bytes 393232 | tf_op jit(solution)/shard_map/reduce_scatter | solution.py:206
  267.2 1.7 multiply_reduce_fusion.7
  268.9 2.7 fusion.25
  271.8 0.7 multiply_reduce_fusion
  272.5 0.8 multiply_convert_fusion
  273.4 0.6 fusion.24
  274.6 2.0 convolution_bitcast_fusion
  276.7 4.3 fusion.77
  281.0 2.2 fusion.76
  283.2 1.2 fusion.75
  284.9 1.9 fusion.28
  287.0 0.7 copy-done.8
  288.0 2.2 fusion.46
  290.3 0.6 multiply_reduce_fusion.15
  290.9 1.3 add_multiply_fusion
  292.7 38.8 %all-reduce = (f32[2,192]{1,0:T(2,128)}, f32[192]{0:T(256)}, f32[768]{0:T(1024)}, f32[192]{0:T(256)}, f32[1,192]{1,0:T(1,128)S(1)}, /*index=5*/f32[1,192]{1,0:T(...) all-reduce(f32[2,192]{1,0:T(2,128)S(1)} %pad_maximum_fusion.4, ...), channel_id=1, replica_groups=mesh['rows'=8,'hid'=4] {'rows'}, use_global_device_ids=true, to_apply=%region_28.29 | all-reduce | flops 3269 | bytes 26152 | tf_op jit(solution)/shard_map/psum | solution.py:244
  331.6 1.9 pad_maximum_fusion.7
  333.4 0.6 pad_maximum_fusion.5
  334.0 0.6 pad_maximum_fusion.6
  334.6 1.7 fusion.55
  336.3 210.1 %all-reduce.8.cloned.1.call-done = (f32[3,192,768]{2,1,0:T(8,128)}, f32[192,768]{1,0:T(8,128)}, f32[768,768]{1,0:T(8,128)}, f32[192,3072]{1,0:T(8,128)}) async-done(((f32[3,192,768]{2,1,0:T(8,128)}, f32[192,768]{1,0:T(8,128)}, f32[768,768]{1,0:T(8,128)}, f32[192,3072]{1,0:T(8,128)}), (f32[3,192,768]{2,1,0:T(8,128)}, f32[192,768]{1,0:T(8,128)}, f32[768,768]{1,0:T(8,128)}, ...) | async-done | bytes 7077904 | tf_op jit(solution)/shard_map/psum | solution.py:244
  546.4 2.9 copy.50
  549.4 0.8 copy.51
  550.2 1.4 copy.52
  551.6 1.1 copy-done.9
  552.7 1.4 copy.53
  (180 shorter events, 5.4 us)
Async XLA Ops:
  7.2 84.0 %copy-start = (bf16[192,3072]{1,0:T(8,128)(2,1)S(1)}, bf16[192,3072]{1,0:T(8,128)(2,1)}, u32[]{:S(2)}) copy-start(bf16[192,3072]{1,0:T(8,128)(2,1)} %param.25) | copy-start | bytes 3538948
  7.2 83.9 %all-gather.2.cloned.1.call-start = ((), (), s32[]{:S(2)}) async-start(), calls=%async_computation.4 | async-start | bytes 3932160 | tf_op jit(solution)/shard_map/all_gather | solution.py:169
  10.3 19.2 %copy-start.48 = (f32[192]{0:T(256)}, f32[192]{0:T(256)S(1)}, u32[]{:S(2)}) copy-start(f32[192]{0:T(256)S(1)} %mul.341) | copy-start | bytes 2308
  24.2 2.1 copy-start.25
  26.4 1.3 copy-start.21
  27.1 1.7 copy-start.1
  27.6 1.9 copy-start.39
  29.5 9.0 %copy-start.17 = (f32[3,64,512]{2,1,0:T(8,128)}, f32[3,64,512]{2,1,0:T(8,128)S(1)}, u32[]{:S(2)}) copy-start(f32[3,64,512]{2,1,0:T(8,128)S(1)} %fusion.20) | copy-start | bytes 1179652
  29.5 9.0 %copy-start.65 = (s32[192]{0:T(256)S(1)}, s32[192]{0:T(256)}, u32[]{:S(2)}) copy-start(s32[192]{0:T(256)} %param.33) | copy-start | bytes 2308
  29.6 9.0 %copy-start.72 = (f32[192]{0:T(256)S(1)}, f32[192]{0:T(256)}, u32[]{:S(2)}) copy-start(f32[192]{0:T(256)} %param.32) | copy-start | bytes 2308
  29.6 9.0 %copy-start.13 = (bf16[192,512]{1,0:T(8,128)(2,1)S(1)}, bf16[192,512]{1,0:T(8,128)(2,1)}, u32[]{:S(2)}) copy-start(bf16[192,512]{1,0:T(8,128)(2,1)} %param.18) | copy-start | bytes 589828
  29.6 9.0 %copy-start.20 = (bf16[192,768]{1,0:T(8,128)(2,1)S(1)}, bf16[192,768]{1,0:T(8,128)(2,1)}, u32[]{:S(2)}) copy-start(bf16[192,768]{1,0:T(8,128)(2,1)} %param.21) | copy-start | bytes 884740
  29.6 9.0 %copy-start.71 = (f32[192]{0:T(256)S(1)}, f32[192]{0:T(256)}, u32[]{:S(2)}) copy-start(f32[192]{0:T(256)} %param.22) | copy-start | bytes 2308
  38.6 7.9 %copy-start.36 = (f32[192]{0:T(256)}, f32[192]{0:T(256)S(1)}, u32[]{:S(2)}) copy-start(f32[192]{0:T(256)S(1)} %convert_multiply_fusion) | copy-start | bytes 2308
  38.6 17.2 %copy-start.56 = (f32[768]{0:T(1024)S(1)}, f32[768]{0:T(1024)}, u32[]{:S(2)}) copy-start(f32[768]{0:T(1024)} %param.30) | copy-start | bytes 9220
  38.6 17.2 %copy-start.76 = (f32[768]{0:T(1024)S(1)}, f32[768]{0:T(1024)}, u32[]{:S(2)}) copy-start(f32[768]{0:T(1024)} %param.24) | copy-start | bytes 9220
  46.4 9.4 %copy-start.73 = (bf16[768,768]{1,0:T(8,128)(2,1)S(1)}, bf16[768,768]{1,0:T(8,128)(2,1)}, u32[]{:S(2)}) copy-start(bf16[768,768]{1,0:T(8,128)(2,1)} %param.23) | copy-start | bytes 3538948
  55.9 5.7 %copy-start.5 = (bf16[512,768]{0,1:T(8,128)(2,1)}, bf16[512,768]{0,1:T(8,128)(2,1)S(1)}, u32[]{:S(2)}) copy-start(bf16[512,768]{0,1:T(8,128)(2,1)S(1)} %all_gather.14) | copy-start | bytes 2359300
  61.5 118.8 %reduce-scatter.5.cloned.1.call-start = ((), (), s32[]{:S(2)}) async-start(), calls=%async_computation.5 | async-start | bytes 7864320 | tf_op jit(solution)/shard_map/reduce_scatter | solution.py:183
  91.1 13.0 %copy-start.7 = (bf16[192,512]{1,0:T(8,128)(2,1)S(1)}, bf16[192,512]{1,0:T(8,128)(2,1)}, u32[]{:S(2)}) copy-start(bf16[192,512]{1,0:T(8,128)(2,1)} %param.35) | copy-start | bytes 589828
  103.6 1.9 copy-start.34
  112.5 3.3 copy-start.44
  120.5 94.9 %reduce-scatter.7.cloned.1.call-start = ((), (), s32[]{:S(2)}) async-start(), calls=%async_computation.6 | async-start | bytes 1966080 | tf_op jit(solution)/shard_map/reduce_scatter | solution.py:194
  180.3 4.8 copy-start.74
  187.1 80.1 %reduce-scatter.9.cloned.1.call-start = ((), (), s32[]{:S(2)}) async-start(), calls=%async_computation.7 | async-start | bytes 1966080 | tf_op jit(solution)/shard_map/reduce_scatter | solution.py:206
  218.5 14.7 %copy-start.37 = (f32[192]{0:T(256)S(1)}, f32[192]{0:T(256)}, u32[]{:S(2)}) copy-start(f32[192]{0:T(256)} %copy-done.36) | copy-start | bytes 2308
  235.3 2.7 copy-start.40
  235.3 31.9 %copy-start.18 = (f32[3,64,512]{2,1,0:T(8,128)S(1)}, f32[3,64,512]{2,1,0:T(8,128)}, u32[]{:S(2)}) copy-start(f32[3,64,512]{2,1,0:T(8,128)} %copy-done.17) | copy-start | bytes 1179652
  235.3 31.9 %copy-start.49 = (f32[192]{0:T(256)S(1)}, f32[192]{0:T(256)}, u32[]{:S(2)}) copy-start(f32[192]{0:T(256)} %copy-done.48) | copy-start | bytes 2308
  237.9 96.7 %reduce-scatter.11.cloned.1.call-start = ((), (), s32[]{:S(2)}) async-start(), calls=%async_computation.8 | async-start | bytes 1966080 | tf_op jit(solution)/shard_map/reduce_scatter | solution.py:223
  268.9 2.8 copy-start.2
  268.9 2.8 copy-start.22
  271.8 2.7 copy-start.23
  274.0 2.6 copy-start.30
  274.4 2.2 copy-start.27
  276.6 4.4 copy-start.4
  276.6 269.8 %all-reduce.8.cloned.1.call-start = ((), (), s32[]{:S(2)}) async-start(), calls=%async_computation.9 | async-start | bytes 14155776 | tf_op jit(solution)/shard_map/psum | solution.py:244
  276.7 4.3 copy-start.6
  281.0 2.2 copy-start.12
  283.2 1.3 copy-start.24
  283.2 1.4 copy-start.26
  283.2 1.5 copy-start.28
  283.2 1.7 copy-start.31
  286.8 3.4 copy-start.52
  286.9 3.4 copy-start.53
  286.9 3.4 copy-start.54
  286.9 3.4 copy-start.55
  286.9 3.4 copy-start.68
  286.9 3.4 copy-start.69
  286.9 3.4 copy-start.70
  286.9 4.0 copy-start.61
  286.9 4.0 copy-start.63
  286.9 4.0 copy-start.66
  287.0 5.3 copy-start.67
  287.7 5.0 copy-start.45
  287.7 5.0 copy-start.46
  287.7 5.0 copy-start.57
  287.7 5.0 copy-start.58
  287.7 5.0 copy-start.59
  287.7 5.0 copy-start.60
  287.7 5.0 copy-start.62
  546.4 3.0 copy-start.29
  546.4 3.8 copy-start.10
  550.2 2.5 copy-start.9
  (19 other events, 18.2 us)
Sparse Core Ops, SparseCore 0:
  61.7 29.4 all-gather.1
  120.6 59.6 reduce-scatter.4
  187.2 28.1 reduce-scatter.6
  238.0 29.1 reduce-scatter.8
  276.7 28.2 reduce-scatter.10
  310.4 235.9 all-reduce.7
where the time goes:
time: 562 us; the launch traced here: 561 us
  waiting for transfers between devices  357 us (64%)
  blocking collectives  97.2 us (17%)
  matrix products  40.3 us (7%)
  other arithmetic  31.6 us (6%)
  local copies, waits for them, and re-layouts  19.9 us (4%)
  between operations  14.9 us (3%)
    psum x1, waiting for transfers between devices, shards(): lax.psum((grad_w_qkv, grad_b_qv, grad_w_out, grad_b_out, grad_head_gate,...  210 us
    reduce_scatter x1, waiting for transfers between devices, shards(): lax.psum_scatter(jnp.dot(grad_ffn, w_back, preferred_element_type=jnp.flo...  59.8 us
    psum x1, blocking collectives, shards(): lax.psum((grad_w_qkv, grad_b_qv, grad_w_out, grad_b_out, grad_head_gate,...  38.8 us
    all_gather x1, waiting for transfers between devices, shards(): inter_all = lax.all_gather(inter_out, 'hid', axis=1, tiled=True)  29.5 us
    reduce_scatter x1, waiting for transfers between devices, shards(): lax.psum_scatter(jnp.dot(grad_attn, w_out, preferred_element_type=jnp.flo...  29.2 us
    reduce_scatter x1, waiting for transfers between devices, shards(): lax.psum_scatter(contract_cols(grad_pre, w_in), 'hid', scatter_dimension=...  28.3 us
    psum x2, blocking collectives, norm_back(): lax.psum((jnp.sum(scaled, 1), jnp.sum(scaled * x_hat, 1), jnp.sum(scaled...  17.9 us
    unnamed x158, local copies, waits for them, and re-layouts  14.1 us
  transfers between devices with their start and end apart: 6, of which 5 were waited for; matrix products, arithmetic and copies ran while one was open for 3% of the time, Pallas kernels for 0%

commit v1 on v0

v1 whole, which is shorter than its diff:
```python
import functools

import jax
import jax.numpy as jnp
from jax import lax
from jax.experimental import pallas as pl
from jax.experimental.pallas import tpu as pltpu
from jax.sharding import PartitionSpec as P

HEAD_DIM = 64
norm_eps = 1e-06
masked_score = -1e30
bf16 = jnp.bfloat16
f32 = jnp.float32
MIB = 1 << 20

VMEM = pl.BlockSpec(memory_space=pltpu.VMEM)
SMEM = pl.BlockSpec(memory_space=pltpu.SMEM)
ANY = pl.BlockSpec(memory_space=pl.ANY)


def swap(block, axis, bit):
    return lax.ppermute(block, axis, [(i, i ^ bit) for i in range(lax.axis_size(axis))])


def sds(shape, dtype):
    return jax.ShapeDtypeStruct(shape, dtype)


def local_kernel(body, name, args, specs, outs, scratch=(), flops=0, vmem=40):
    nbytes = sum(a.size * a.dtype.itemsize for a in args)
    nbytes += sum(o.size * o.dtype.itemsize for o in outs)
    return pl.pallas_call(
        body,
        name=name,
        out_shape=outs,
        in_specs=specs,
        out_specs=[VMEM] * len(outs),
        scratch_shapes=list(scratch),
        compiler_params=pltpu.CompilerParams(vmem_limit_bytes=vmem * MIB),
        cost_estimate=pl.CostEstimate(flops=flops, bytes_accessed=nbytes, transcendentals=0),
    )(*args)


def dot(left, right):
    return jnp.dot(left, right, preferred_element_type=f32)


def dot_nt(left, right):
    return lax.dot_general(left, right, (((1,), (1,)), ((), ())), preferred_element_type=f32)


def dot_tn(left, right):
    return lax.dot_general(left, right, (((0,), (0,)), ((), ())), preferred_element_type=f32)


def at(index, size):
    return pl.ds(pl.multiple_of(index * size, size), size)


def doc_bounds(lengths, query):
    start = jnp.zeros_like(query)
    stop = jnp.zeros_like(query)
    end = jnp.int32(0)
    for j in range(lengths.shape[1]):
        begin, end = end, end + lengths[0, j]
        inside = (query >= begin) & (query < end)
        start = jnp.where(inside, begin, start)
        stop = jnp.where(inside, end, stop)
    return start, stop


def attn_forward(
    where, lengths, gate, bias, x0, x1, x2, x3, w_qkv,
    x_all, qkv, logsum, mine, mine_x, send, x_block, gated,
):
    me = where[0]
    feats, toks = x0.shape
    block = toks // 4
    for k, piece in enumerate((x0, x1, x2, x3)):
        x_all[at(me ^ k, feats), :] = piece[...]
    x_block[...] = x_all[:, at(me, block)]
    cols = jnp.transpose(bias[...])
    for c in range(3):
        rows = dot(w_qkv[c], x_all[...])
        if c != 1:
            rows = rows + cols[:feats, c // 2 : c // 2 + 1]
        rows = rows.astype(bf16)
        if c == 0:
            rows = rows * jnp.asarray(HEAD_DIM ** (-0.5), bf16)
        qkv[c] = rows
    heads = feats // HEAD_DIM
    for head in range(heads):
        span = slice(head * HEAD_DIM, (head + 1) * HEAD_DIM)
        keys = jnp.transpose(qkv[1, span, :])
        values = qkv[2, span, :]
        for j in range(4):
            chunk = slice(j * block, (j + 1) * block)
            scores = dot(keys, qkv[0, span, chunk])
            query = lax.broadcasted_iota(jnp.int32, (1, block), 1) + j * block
            start, stop = doc_bounds(lengths, query)
            position = lax.broadcasted_iota(jnp.int32, scores.shape, 0)
            scores = jnp.where((position >= start) & (position < stop), scores, masked_score)
            peak = jnp.max(scores, axis=0, keepdims=True)
            expo = jnp.exp(scores - peak)
            total = jnp.sum(expo, axis=0, keepdims=True)
            probs = (expo * (1.0 / total)).astype(bf16)
            logsum[head : head + 1, chunk] = peak + jnp.log(total)
            gated[span, chunk] = (dot(values, probs) * gate[head]).astype(bf16)
    mine[...] = gated[:, at(me, block)]
    mine_x[...] = gated[:, at(me ^ 2, block)]
    send[:feats, :] = gated[:, at(me ^ 1, block)]
    send[feats:, :] = gated[:, at(me ^ 3, block)]


def attn_backward(
    where, lengths, qkv, logsum, mine, from_x, from_core, grads, head_sums, bias_sums, up
):
    me = where[0]
    feats, block = mine.shape
    up[:, at(me, block)] = mine[...]
    up[:, at(me ^ 1, block)] = from_core[:feats, :]
    up[:, at(me ^ 2, block)] = from_x[:feats, :]
    up[:, at(me ^ 3, block)] = from_core[feats:, :]
    heads = feats // HEAD_DIM
    head_sums[...] = jnp.zeros_like(head_sums)
    for head in range(heads):
        span = slice(head * HEAD_DIM, (head + 1) * HEAD_DIM)
        queries, keys_t, values_t = (qkv[c, span, :] for c in range(3))
        keys = jnp.transpose(keys_t)
        values = jnp.transpose(values_t)
        upstream = up[span, :]
        grad_k = jnp.zeros((HEAD_DIM, 4 * block), f32)
        grad_v = jnp.zeros((HEAD_DIM, 4 * block), f32)
        inner_sum = jnp.zeros((1, block), f32)
        for j in range(4):
            chunk = slice(j * block, (j + 1) * block)
            scores = dot(keys, queries[:, chunk])
            query = lax.broadcasted_iota(jnp.int32, (1, block), 1) + j * block
            start, stop = doc_bounds(lengths, query)
            position = lax.broadcasted_iota(jnp.int32, scores.shape, 0)
            scores = jnp.where((position >= start) & (position < stop), scores, masked_score)
            probs = jnp.exp(scores - logsum[head : head + 1, chunk])
            grad_p = dot(values, upstream[:, chunk])
            weighted = probs * grad_p
            inner = jnp.sum(weighted, axis=0, keepdims=True)
            inner_sum = inner_sum + inner
            grad_s = (weighted - probs * inner).astype(bf16)
            grad_v = grad_v + dot_nt(upstream[:, chunk], probs.astype(bf16))
            grad_k = grad_k + dot_nt(queries[:, chunk], grad_s)
            grads[span, chunk] = (dot(keys_t, grad_s) * HEAD_DIM ** (-0.5)).astype(bf16)
        grads[feats + head * HEAD_DIM : feats + (head + 1) * HEAD_DIM, :] = grad_k.astype(bf16)
        grads[2 * feats + head * HEAD_DIM : 2 * feats + (head + 1) * HEAD_DIM, :] = grad_v.astype(
            bf16
        )
        head_sums[head : head + 1, :] = inner_sum
    ones = jnp.ones((8, 4 * block), bf16)
    bias_sums[...] = dot_nt(ones, grads[...])


def qkv_weight_grad(grads, x_all, grad_w):
    for k in range(3):
        rows = slice(k * 192, (k + 1) * 192)
        grad_w[rows, :] = dot_nt(grads[rows, :], x_all[...])


def qkv_input_grad(where, grads, w_qkv, dres, mine, mine_x, send, full):
    me = where[0]
    feats = mine.shape[0]
    block = dres.shape[0]
    total = None
    for c in range(3):
        part = dot(jnp.transpose(w_qkv[c]), grads[c * feats : (c + 1) * feats, :])
        total = part if total is None else total + part
    full[...] = total
    full[:, at(me, block)] += jnp.transpose(dres[...])
    mine[...] = full[at(me, feats), :]
    mine_x[...] = full[at(me ^ 2, feats), :]
    send[:feats, :] = full[at(me ^ 1, feats), :].astype(bf16)
    send[feats:, :] = full[at(me ^ 3, feats), :].astype(bf16)


def load_rows(where, own, from_x, from_core, whole, sems):
    me = where[0]
    n = own.shape[0]
    copies = [
        pltpu.make_async_copy(own, whole.at[at(me, n), :], sems.at[0]),
        pltpu.make_async_copy(from_core.at[:n, :], whole.at[at(me ^ 1, n), :], sems.at[1]),
        pltpu.make_async_copy(from_x, whole.at[at(me ^ 2, n), :], sems.at[2]),
        pltpu.make_async_copy(from_core.at[n:, :], whole.at[at(me ^ 3, n), :], sems.at[3]),
    ]
    for copy in copies:
        copy.start()
    return copies


def row_norm(values):
    mean = jnp.mean(values, axis=1, keepdims=True)
    centered = values - mean
    spread = jnp.mean(centered * centered, axis=1, keepdims=True)
    inv = lax.rsqrt(spread + norm_eps)
    return centered * inv, inv


def attn_out(
    where, branch, g0, g1, g2, x_block, vecs, wo_own, wo_x, wo_core,
    normed, normed_low, hat, inv_out, pre, gated_rows, wo, heads_all, sems,
):
    me = where[0]
    copies = load_rows(where, wo_own, wo_x, wo_core, wo, sems)
    feats = g0.shape[0]
    heads_all[at(me, feats), :] = g0[...]
    heads_all[at(me ^ 1, feats), :] = g1[:feats, :]
    heads_all[at(me ^ 2, feats), :] = g2[:feats, :]
    heads_all[at(me ^ 3, feats), :] = g2[feats:, :]
    gated = jnp.transpose(heads_all[...])
    gated_rows[...] = gated
    tokens = jnp.transpose(x_block[...].astype(f32))
    for copy in copies:
        copy.wait()
    attn = dot_nt(gated, wo[...]) + vecs[0:1, :]
    pre[...] = attn
    resid = tokens + branch[0] * attn * vecs[3:4, :]
    x_hat, inv = row_norm(resid)
    value = x_hat * vecs[1:2, :] + vecs[2:3, :]
    hat[...] = x_hat
    inv_out[...] = jnp.broadcast_to(inv, inv_out.shape)
    normed[...] = value
    normed_low[...] = value.astype(bf16)


def attn_out_back(
    where, branch, part, recv, dres2, hat, inv, pre, vecs, wo_own, wo_x, wo_core,
    dres, grad_attn, sums, up_mine, up_core, up_x, wo, ups, sems,
):
    me = where[0]
    copies = load_rows(where, wo_own, wo_x, wo_core, wo, sems)
    feats = up_mine.shape[0]
    grad = part[...] + recv[...].astype(f32) + dres2[...]
    x_hat = hat[...]
    scaled = grad * vecs[1:2, :]
    mean_plain = jnp.mean(scaled, axis=1, keepdims=True)
    mean_along = jnp.mean(scaled * x_hat, axis=1, keepdims=True)
    grad_resid = inv[:, 0:1] * (scaled - mean_plain - x_hat * mean_along)
    dres[...] = grad_resid
    low = (grad_resid * (branch[0] * vecs[3:4, :])).astype(bf16)
    grad_attn[...] = low
    for copy in copies:
        copy.wait()
    grad_gated = dot(low, wo[...])
    upstream = (grad_gated * vecs[7:8, :]).astype(bf16)
    ups[...] = jnp.transpose(upstream)
    up_mine[...] = ups[at(me, feats), :]
    up_core[...] = ups[at(me ^ 1, feats), :]
    up_x[:feats, :] = ups[at(me ^ 2, feats), :]
    up_x[feats:, :] = ups[at(me ^ 3, feats), :]
    sums[0:1, :] = jnp.sum(grad * x_hat, axis=0, keepdims=True)
    sums[1:2, :] = jnp.sum(grad, axis=0, keepdims=True)
    sums[2:3, :] = jnp.sum(low.astype(f32), axis=0, keepdims=True)
    sums[3:4, :] = jnp.sum(grad_resid * pre[...], axis=0, keepdims=True)


def out_weight_grad(where, grad_attn, gated_rows, mine, mine_x, send, full):
    me = where[0]
    feats = mine.shape[0]
    full[...] = dot_tn(grad_attn[...], gated_rows[...])
    mine[...] = full[at(me, feats), :]
    mine_x[...] = full[at(me ^ 2, feats), :]
    send[:feats, :] = full[at(me ^ 1, feats), :].astype(bf16)
    send[feats:, :] = full[at(me ^ 3, feats), :].astype(bf16)


def load_units(where, wi_own, wi_core, wi, sems, k):
    core = where[0] & 1
    n = wi_own.shape[1]
    copies = [
        pltpu.make_async_copy(wi_own, wi.at[:, at(core, n)], sems.at[k]),
        pltpu.make_async_copy(wi_core, wi.at[:, at(core ^ 1, n)], sems.at[k + 1]),
    ]
    for copy in copies:
        copy.start()
    return copies


def load_back(where, wb_own, wb_x, wb_core, wb, sems, k):
    me = where[0]
    n = wb_own.shape[0]
    units = wb_x.shape[1]
    copies = [
        pltpu.make_async_copy(
            wb_own.at[:, at(me // 2, units)], wb.at[at(me, n), :], sems.at[k]
        ),
        pltpu.make_async_copy(wb_core.at[:n, :], wb.at[at(me ^ 1, n), :], sems.at[k + 1]),
        pltpu.make_async_copy(wb_x, wb.at[at(me ^ 2, n), :], sems.at[k + 2]),
        pltpu.make_async_copy(wb_core.at[n:, :], wb.at[at(me ^ 3, n), :], sems.at[k + 3]),
    ]
    for copy in copies:
        copy.start()
    return copies


def ffn_forward(
    where, normed, unit_rows, wi_own, wi_core, wb_own, wb_x, wb_core,
    act, slope, inter_mine, inter_core, part, wi, wb, inter, sems,
):
    core = where[0] & 1
    first = load_units(where, wi_own, wi_core, wi, sems, 0)
    second = load_back(where, wb_own, wb_x, wb_core, wb, sems, 2)
    for copy in first:
        copy.wait()
    units = wi.shape[1]
    step = 256
    for j in range(units // step):
        cut = slice(j * step, (j + 1) * step)
        u = dot(normed[...], wi[:, cut]) + unit_rows[0:1, cut]
        cdf = 0.5 * (1.0 + lax.erf(u * 0.7071067811865476))
        value = u * cdf
        act[:, cut] = value
        slope[:, cut] = cdf + u * (jnp.exp(-0.5 * u * u) * 0.3989422804014327)
        inter[:, cut] = (value * unit_rows[1:2, cut]).astype(bf16)
    inter_mine[...] = inter[:, at(core, units // 2)]
    inter_core[...] = inter[:, at(core ^ 1, units // 2)]
    for copy in second:
        copy.wait()
    part[...] = dot_nt(inter[...], wb[...]).astype(part.dtype)


def ffn_backward(
    where, grad_ffn, act, slope, unit_rows, wi_own, wi_core, wb_own, wb_x, wb_core,
    gpre_mine, gpre_core, part, sums, wi, wb, gpre, sems,
):
    core = where[0] & 1
    first = load_back(where, wb_own, wb_x, wb_core, wb, sems, 2)
    second = load_units(where, wi_own, wi_core, wi, sems, 0)
    for copy in first:
        copy.wait()
    units = wi.shape[1]
    step = 256
    for j in range(units // step):
        cut = slice(j * step, (j + 1) * step)
        ginter = dot(grad_ffn[...], wb[:, cut])
        sums[:, cut] = jnp.broadcast_to(
            jnp.sum(ginter * act[:, cut], axis=0, keepdims=True), (8, step)
        )
        gpre[:, cut] = (ginter * unit_rows[1:2, cut] * slope[:, cut]).astype(bf16)
    gpre_mine[...] = gpre[:, at(core, units // 2)]
    gpre_core[...] = gpre[:, at(core ^ 1, units // 2)]
    for copy in second:
        copy.wait()
    part[...] = dot_nt(gpre[...], wi[...]).astype(part.dtype)


def ffn_weight_grads(
    where, n0, n1, n2, n3, e0, e1, e2, e3, p0, p1, p2, p3, f0, f1, f2, f3,
    in_keep, in_send, back_keep, back_send, bias_sums, left, right, full,
):
    parity = where[1] & 1
    toks = n0.shape[0]
    half = full.shape[0] // 2

    def fill(ref, pieces):
        for k, piece in enumerate(pieces):
            ref[k * toks : (k + 1) * toks, :] = piece[...]

    fill(left, (n0, n1, n2, n3))
    fill(right, (p0, p1, p2, p3))
    full[...] = dot_tn(left[...], right[...])
    in_keep[...] = full[at(parity, half), :]
    in_send[...] = full[at(parity ^ 1, half), :].astype(bf16)
    bias_sums[...] = jnp.broadcast_to(
        jnp.sum(right[...].astype(f32), axis=0, keepdims=True), bias_sums.shape
    )
    fill(left, (f0, f1, f2, f3))
    fill(right, (e0, e1, e2, e3))
    full[...] = dot_tn(left[...], right[...])
    owners, subs = 4, 8
    rows = full.shape[0] // (owners * subs)
    for q in range(subs // 2):
        for h in range(owners):
            to = slice((q * owners + h) * rows, (q * owners + h + 1) * rows)
            base = h * subs * rows + q * rows
            kept = base + parity * (subs // 2) * rows
            sent = base + (parity ^ 1) * (subs // 2) * rows
            back_keep[to, :] = full[pl.ds(pl.multiple_of(kept, rows), rows), :]
            left_rows = full[pl.ds(pl.multiple_of(sent, rows), rows), :]
            back_send[to, :] = left_rows.astype(bf16)


def second_norm(
    where, branch, part, recv, normed, cot_own, cot_x, cot_core, vecs,
    out_mine, out_x, out_send, dres, grad_low, sums, cots, outs,
):
    me = where[0]
    feats = cot_own.shape[0]
    block = cot_core.shape[1]
    cots[at(me, feats), :] = cot_own[:, at(me, block)]
    cots[at(me ^ 1, feats), :] = cot_core[:feats, :]
    cots[at(me ^ 2, feats), :] = cot_x[:, at(me & 1, block)]
    cots[at(me ^ 3, feats), :] = cot_core[feats:, :]
    grad_out = jnp.transpose(cots[...].astype(f32))
    ffn = part[...] + recv[...].astype(f32) + vecs[4:5, :]
    resid = normed[...] + branch[1] * ffn * vecs[3:4, :]
    x_hat, inv = row_norm(resid)
    value = x_hat * vecs[5:6, :] + vecs[6:7, :]
    scaled = grad_out * vecs[5:6, :]
    mean_plain = jnp.mean(scaled, axis=1, keepdims=True)
    mean_along = jnp.mean(scaled * x_hat, axis=1, keepdims=True)
    grad_resid = inv * (scaled - mean_plain - x_hat * mean_along)
    dres[...] = grad_resid
    low = (grad_resid * (branch[1] * vecs[3:4, :])).astype(bf16)
    grad_low[...] = low
    sums[0:1, :] = jnp.sum(grad_out * x_hat, axis=0, keepdims=True)
    sums[1:2, :] = jnp.sum(grad_out, axis=0, keepdims=True)
    sums[2:3, :] = jnp.sum(low.astype(f32), axis=0, keepdims=True)
    sums[3:4, :] = jnp.sum(grad_resid * ffn, axis=0, keepdims=True)
    outs[...] = jnp.transpose(value).astype(bf16)
    out_mine[...] = outs[at(me, feats), :]
    out_x[...] = outs[at(me ^ 2, feats), :]
    out_send[:feats, :] = outs[at(me ^ 1, feats), :]
    out_send[feats:, :] = outs[at(me ^ 3, feats), :]


def ordered(bit, mine, other, axis=0):
    return jnp.where(
        bit == 0,
        jnp.concatenate([mine, other], axis=axis),
        jnp.concatenate([other, mine], axis=axis),
    )


def cut_half(full, bit):
    half = full.shape[0] // 2
    keep = lax.dynamic_slice_in_dim(full, bit * half, half, 0)
    send = lax.dynamic_slice_in_dim(full, (1 - bit) * half, half, 0)
    return keep, send.astype(bf16)


def far_rows_sum(chunk):
    count = lax.axis_size("rows")
    if count == 8:
        return chunk
    groups = [[i + 8 * j for j in range(count // 8)] for i in range(8)]
    return lax.psum(chunk, "rows", axis_index_groups=groups)


def scatter_rows(keep, send, row):
    total = keep + swap(send, "rows", 1).astype(f32)
    for k in (1, 2):
        keep, send = cut_half(total, (row >> k) & 1)
        total = keep + swap(send, "rows", 1 << k).astype(f32)
    return far_rows_sum(total)


def gather_rows(chunk, row):
    for k in (2, 1, 0):
        chunk = ordered((row >> k) & 1, chunk, swap(chunk, "rows", 1 << k))
    return chunk.astype(f32)


def shards(
    tokens, w_qkv, b_qv, w_out, b_out, w_in, b_in, w_back, b_back, norm_gain, norm_bias,
    head_gate, inter_gate, branch_gate, hidden_gate, hidden_mask, doc_lengths, cotangent,
):
    feats, toks = tokens.shape
    width = 4 * feats
    units = w_in.shape[1]
    block = toks // 4
    hid = lax.axis_index("hid")
    row = lax.axis_index("rows")
    core, chip = hid & 1, hid >> 1
    where = jnp.stack([hid, row]).astype(jnp.int32)

    tokens_core = swap(tokens, "hid", 1)
    tokens_x = swap(tokens, "hid", 2)
    tokens_far = swap(tokens_x, "hid", 1)

    kept = hidden_mask.astype(f32)
    own_vecs = jnp.stack(
        [
            b_out, norm_gain[0], norm_bias[0], hidden_gate * kept, b_back,
            norm_gain[1], norm_bias[1], jnp.repeat(head_gate, HEAD_DIM),
        ]
    )
    pair_vecs = ordered(core, own_vecs, swap(own_vecs, "hid", 1), axis=1)
    vecs = ordered(chip, pair_vecs, swap(pair_vecs, "hid", 2), axis=1)
    own_units = jnp.stack([b_in, inter_gate])
    unit_rows = ordered(core, own_units, swap(own_units, "hid", 1), axis=1)

    wo_x = swap(w_out, "hid", 2)
    wo_core = swap(jnp.concatenate([w_out, wo_x], 0), "hid", 1)
    wb_chip = lax.dynamic_slice_in_dim(w_back, chip * 2 * units, 2 * units, 1)
    wb_x = swap(lax.dynamic_slice_in_dim(w_back, (1 - chip) * 2 * units, 2 * units, 1), "hid", 2)
    wb_core = swap(jnp.concatenate([wb_chip, wb_x], 0), "hid", 1)
    wi_core = swap(w_in, "hid", 1)
    cot_x = swap(
        lax.dynamic_slice_in_dim(cotangent, (1 - chip) * 2 * block, 2 * block, 1), "hid", 2
    )
    cot_core = swap(
        jnp.concatenate(
            [
                lax.dynamic_slice_in_dim(cotangent, (hid ^ 1) * block, block, 1),
                lax.dynamic_slice_in_dim(cot_x, (1 - core) * block, block, 1),
            ],
            0,
        ),
        "hid",
        1,
    )

    bias = jnp.pad(b_qv, ((0, 6), (0, -feats % 128)))
    x_all, qkv, logsum, ctx, ctx_x, ctx_send, x_block = local_kernel(
        attn_forward,
        "attn_forward",
        (where, doc_lengths, head_gate, bias, tokens, tokens_core, tokens_x, tokens_far, w_qkv),
        [SMEM, SMEM, SMEM] + [VMEM] * 6,
        [
            sds((width, toks), bf16),
            sds((3, feats, toks), bf16),
            sds((8, toks), f32),
            sds((feats, block), bf16),
            sds((feats, block), bf16),
            sds((2 * feats, block), bf16),
            sds((width, block), bf16),
        ],
        [pltpu.VMEM((feats, toks), bf16)],
        flops=2 * toks * feats * (3 * width + 2 * toks),
    )
    ctx_core = swap(ctx_send, "hid", 1)
    ctx_far = swap(jnp.concatenate([ctx_x, ctx_core[feats:]], 0), "hid", 2)

    normed, normed_low, hat, inv, attn_pre, gated_rows = local_kernel(
        attn_out,
        "attn_out",
        (where, branch_gate, ctx, ctx_core, ctx_far, x_block, vecs, w_out, wo_x, wo_core),
        [SMEM, SMEM] + [VMEM] * 5 + [ANY] * 3,
        [
            sds((block, width), f32),
            sds((block, width), bf16),
            sds((block, width), f32),
            sds((block, 128), f32),
            sds((block, width), f32),
            sds((block, width), bf16),
        ],
        [
            pltpu.VMEM((width, width), bf16),
            pltpu.VMEM((width, block), bf16),
            pltpu.SemaphoreType.DMA((4,)),
        ],
        flops=2 * block * width * width,
    )

    def forward_part(rows, part_type):
        return local_kernel(
            ffn_forward,
            "ffn_forward",
            (where, rows, unit_rows, w_in, wi_core, w_back, wb_x, wb_core),
            [SMEM, VMEM, VMEM] + [ANY] * 5,
            [
                sds((block, 2 * units), f32),
                sds((block, 2 * units), f32),
                sds((block, units), bf16),
                sds((block, units), bf16),
                sds((block, width), part_type),
            ],
            [
                pltpu.VMEM((width, 2 * units), bf16),
                pltpu.VMEM((width, 2 * units), bf16),
                pltpu.VMEM((block, 2 * units), bf16),
                pltpu.SemaphoreType.DMA((6,)),
            ],
            flops=8 * block * width * units,
        )

    normed_x = swap(normed_low, "hid", 2)
    act, slope, inter, inter_send, ffn_part = forward_part(normed_low, f32)
    act_x, slope_x, inter_x, inter_x_send, ffn_send = forward_part(normed_x, bf16)
    ffn_recv = swap(ffn_send, "hid", 2)

    out_mine, out_x, out_send, dres2, gffn, sums2 = local_kernel(
        second_norm,
        "second_norm",
        (where, branch_gate, ffn_part, ffn_recv, normed, cotangent, cot_x, cot_core, vecs),
        [SMEM, SMEM] + [VMEM] * 7,
        [
            sds((feats, block), bf16),
            sds((feats, block), bf16),
            sds((2 * feats, block), bf16),
            sds((block, width), f32),
            sds((block, width), bf16),
            sds((4, width), f32),
        ],
        [pltpu.VMEM((width, block), bf16), pltpu.VMEM((width, block), bf16)],
    )

    def backward_part(rows, act, slope, part_type):
        return local_kernel(
            ffn_backward,
            "ffn_backward",
            (where, rows, act, slope, unit_rows, w_in, wi_core, w_back, wb_x, wb_core),
            [SMEM] + [VMEM] * 4 + [ANY] * 5,
            [
                sds((block, units), bf16),
                sds((block, units), bf16),
                sds((block, width), part_type),
                sds((8, 2 * units), f32),
            ],
            [
                pltpu.VMEM((width, 2 * units), bf16),
                pltpu.VMEM((width, 2 * units), bf16),
                pltpu.VMEM((block, 2 * units), bf16),
                pltpu.SemaphoreType.DMA((6,)),
            ],
            flops=8 * block * width * units,
        )

    gffn_x = swap(gffn, "hid", 2)
    gpre, gpre_send, gn_part, ig_sum = backward_part(gffn, act, slope, f32)
    gpre_x, gpre_x_send, gn_send, ig_sum_x = backward_part(gffn_x, act_x, slope_x, bf16)
    gn_recv = swap(gn_send, "hid", 2)

    to_core = [
        swap(a, "hid", 1)
        for a in (
            normed_low, normed_x, inter_send, inter_x_send, gpre_send, gpre_x_send, gffn, gffn_x,
        )
    ]
    in_keep, in_send, back_keep, back_send, bin_sum = local_kernel(
        ffn_weight_grads,
        "ffn_weight_grads",
        (
            where,
            normed_low, normed_x, to_core[0], to_core[1],
            inter, inter_x, to_core[2], to_core[3],
            gpre, gpre_x, to_core[4], to_core[5],
            gffn, gffn_x, to_core[6], to_core[7],
        ),
        [SMEM] + [VMEM] * 16,
        [
            sds((width // 2, units), f32),
            sds((width // 2, units), bf16),
            sds((width // 2, units), f32),
            sds((width // 2, units), bf16),
            sds((8, units), f32),
        ],
        [
            pltpu.VMEM((toks, width), bf16),
            pltpu.VMEM((toks, units), bf16),
            pltpu.VMEM((width, units), f32),
        ],
        flops=4 * toks * width * units,
    )

    dres1, gattn, sums1, up_mine, up_core, up_x = local_kernel(
        attn_out_back,
        "attn_out_back",
        (
            where, branch_gate, gn_part, gn_recv, dres2, hat, inv, attn_pre, vecs,
            w_out, wo_x, wo_core,
        ),
        [SMEM, SMEM] + [VMEM] * 7 + [ANY] * 3,
        [
            sds((block, width), f32),
            sds((block, width), bf16),
            sds((4, width), f32),
            sds((feats, block), bf16),
            sds((feats, block), bf16),
            sds((2 * feats, block), bf16),
        ],
        [
            pltpu.VMEM((width, width), bf16),
            pltpu.VMEM((width, block), bf16),
            pltpu.SemaphoreType.DMA((4,)),
        ],
        flops=2 * block * width * width,
    )
    up_far = swap(up_x, "hid", 2)
    up_recv = swap(jnp.concatenate([up_core, up_far[feats:]], 0), "hid", 1)

    grads, head_sums, bias_sums = local_kernel(
        attn_backward,
        "attn_backward",
        (where, doc_lengths, qkv, logsum, up_mine, up_far, up_recv),
        [SMEM, SMEM] + [VMEM] * 5,
        [
            sds((3 * feats, toks), bf16),
            sds((8, block), f32),
            sds((8, 3 * feats), f32),
        ],
        [pltpu.VMEM((feats, toks), bf16)],
        flops=2 * toks * toks * feats * 5,
    )

    (grad_w_qkv,) = local_kernel(
        qkv_weight_grad,
        "qkv_weight_grad",
        (grads, x_all),
        [VMEM, VMEM],
        [sds((3 * feats, width), f32)],
        flops=6 * toks * feats * width,
    )
    gx_mine, gx_x, gx_send = local_kernel(
        qkv_input_grad,
        "qkv_input_grad",
        (where, grads, w_qkv, dres1),
        [SMEM] + [VMEM] * 3,
        [
            sds((feats, toks), f32),
            sds((feats, toks), f32),
            sds((2 * feats, toks), bf16),
        ],
        [pltpu.VMEM((width, toks), f32)],
        flops=6 * toks * feats * width,
    )
    gx_core = swap(gx_send, "hid", 1).astype(f32)
    gx_far = swap((gx_x + gx_core[feats:]).astype(bf16), "hid", 2)
    grad_tokens = (gx_mine + gx_core[:feats] + gx_far.astype(f32)).astype(bf16)

    out_core = swap(out_send, "hid", 1)
    out_far = swap(jnp.concatenate([out_x, out_core[feats:]], 0), "hid", 2)
    output = ordered(
        chip,
        ordered(core, out_mine, out_core[:feats], axis=1),
        ordered(core, out_far[:feats], out_far[feats:], axis=1),
        axis=1,
    )

    back = scatter_rows(back_keep, back_send, row).reshape(4, -1, units)
    sub = back.shape[1]

    def pick(full, k):
        return lax.dynamic_slice_in_dim(full, hid ^ k, 1, 0)[0]

    back_core = swap(jnp.concatenate([pick(back, 1), pick(back, 3)], 0), "hid", 1)
    back_far = swap(jnp.concatenate([pick(back, 2), back_core[sub:]], 0), "hid", 2)
    back_chunk = ordered(
        chip,
        ordered(core, pick(back, 0), back_core[:sub]),
        ordered(core, back_far[:sub], back_far[sub:]),
    )
    grad_w_back = gather_rows(back_chunk.astype(bf16), row)
    grad_w_back = grad_w_back.reshape(8, 4, sub, units).transpose(0, 2, 1, 3)
    grad_w_back = grad_w_back.reshape(feats, 4 * units)

    grad_w_in = gather_rows(scatter_rows(in_keep, in_send, row).astype(bf16), row)

    wo_mine, wo_keep, wo_send = local_kernel(
        out_weight_grad,
        "out_weight_grad",
        (where, gattn, gated_rows),
        [SMEM, VMEM, VMEM],
        [sds((feats, width), f32), sds((feats, width), f32), sds((2 * feats, width), bf16)],
        [pltpu.VMEM((width, width), f32)],
        flops=2 * block * width * width,
    )
    wo_recv = swap(wo_send, "hid", 1).astype(f32)
    wo_far = swap((wo_keep + wo_recv[feats:]).astype(bf16), "hid", 2)
    grad_w_out = wo_mine + wo_recv[:feats] + wo_far.astype(f32)
    last = jnp.concatenate([grad_w_qkv, grad_w_out], 0)
    last = gather_rows(scatter_rows(*cut_half(last, row & 1), row).astype(bf16), row)
    grad_w_qkv = last[: 3 * feats].reshape(3, feats, width)
    grad_w_out = last[3 * feats :]

    shared = jnp.concatenate([sums1, sums2], 0)
    ig_all = ig_sum[:1] + ig_sum_x[:1]
    ig_send = lax.dynamic_slice_in_dim(ig_all, (1 - core) * units, units, 1)
    with_core = swap(jnp.concatenate([shared, ig_send], 0), "hid", 1)
    shared = shared + with_core[:8]
    shared = shared + swap(shared, "hid", 2)
    ig_mine = lax.dynamic_slice_in_dim(ig_all, core * units, units, 1) + with_core[8:]
    head_row = jnp.sum(head_sums, axis=1)[None]
    vec = jnp.concatenate(
        [
            shared,
            ig_mine,
            bin_sum[:1],
            jnp.pad(bias_sums[:1], ((0, 0), (0, width - 3 * feats))),
            jnp.pad(head_row, ((0, 0), (0, width - 8))),
        ],
        0,
    )
    for k in range(3):
        vec = vec + swap(vec, "rows", 1 << k)
    vec = far_rows_sum(vec)
    cols = vecs[3]
    own = lax.dynamic_slice_in_dim(vec[:8], hid * feats, feats, 1)
    grad_branch_gate = jnp.stack([jnp.sum(vec[3] * cols), jnp.sum(vec[7] * cols)])
    hidden = (branch_gate[0] * own[3] + branch_gate[1] * own[7]) * kept
    return (
        output,
        grad_tokens,
        grad_w_qkv,
        jnp.stack([vec[10, :feats], vec[10, 2 * feats : 3 * feats]]),
        grad_w_out,
        own[2],
        grad_w_in,
        vec[9],
        grad_w_back,
        own[6],
        jnp.stack([own[0], own[4]]),
        jnp.stack([own[1], own[5]]),
        vec[11, : feats // HEAD_DIM] / head_gate,
        vec[8],
        grad_branch_gate,
        hidden,
    )


def solution(mesh):
    return jax.shard_map(
        shards,
        mesh=mesh,
        in_specs=(
            P("hid", "rows"),
            P(None, "hid", None),
            P(None, "hid"),
            P("hid", None),
            P("hid"),
            P(None, "hid"),
            P("hid"),
            P("hid", None),
            P("hid"),
            P(None, "hid"),
            P(None, "hid"),
            P("hid"),
            P("hid"),
            P(),
            P("hid"),
            P("hid"),
            P("rows", None),
            P("hid", "rows"),
        ),
        out_specs=(
            P("hid", "rows"),
            P("hid", "rows"),
            P(None, "hid", None),
            P(None, "hid"),
            P("hid", None),
            P("hid"),
            P(None, "hid"),
            P("hid"),
            P("hid", None),
            P("hid"),
            P(None, "hid"),
            P(None, "hid"),
            P("hid"),
            P("hid"),
            P(),
            P("hid"),
        ),
        check_vma=False,
    )
```

time: 562 us -> 253 us (0.45)
  waiting for transfers between devices: 357 us -> 102 us
  blocking collectives: 97.2 us -> 0 us
  starting transfers between devices: 0.25 us -> 51.3 us
  matrix products: 40.3 us -> 0 us
  Pallas kernels: 0 us -> 33.4 us
  local copies, waits for them, and re-layouts: 19.9 us -> 40.9 us
  between operations: 14.9 us -> 1.79 us
  other arithmetic: 31.6 us -> 22.1 us
    psum x1 -> x0, waiting for transfers between devices: 210 us -> none  [shards(): lax.psum((grad_w_qkv, grad_b_qv, grad_w_out, grad_b_out, grad_head_gate,...]
    reduce_scatter x4 -> x0, waiting for transfers between devices: 117 us -> none  [the longest x1 59.8 us: shards(): lax.psum_scatter(jnp.dot(grad_ffn, w_back, preferred_element_type=jnp.flo...]
    ppermute x0 -> x60, waiting for transfers between devices: none -> 102 us  [swap(): lax.ppermute(block, axis, [(i, i ^ bit) for i in range(lax.axis_size(axis...]
    psum x5 -> x0, blocking collectives: 70 us -> none  [the longest x1 38.8 us: shards(): lax.psum((grad_w_qkv, grad_b_qv, grad_w_out, grad_b_out, grad_head_gate,...]
    ppermute x0 -> x60, starting transfers between devices: none -> 51.3 us  [swap(): lax.ppermute(block, axis, [(i, i ^ bit) for i in range(lax.axis_size(axis...]
    dot_general x18 -> x0, matrix products: 40.3 us -> none  [the longest x3 8.17 us: contract_cols(): lax.dot_general(left_mat, right_mat, (((1,), (1,)), ((), ())), preferred_...]
    pallas_call x0 -> x13, Pallas kernels: none -> 33.4 us  [local_kernel(): pl.pallas_call(body, name=name, out_shape=outs, in_specs=specs, out_specs...]
    all_gather x1 -> x0, waiting for transfers between devices: 29.5 us -> none  [shards(): inter_all = lax.all_gather(inter_out, 'hid', axis=1, tiled=True)]
  transfers between devices with their start and end apart: 6 -> 60, of which waited for: 5 -> 28; matrix products, arithmetic and copies ran while one was open for 3% -> 12% of each run, Pallas kernels for 0% -> 9%
where the time goes in v1:
time: 253 us; the launch traced here: 252 us
  waiting for transfers between devices  102 us (40%)
  starting transfers between devices  51.3 us (20%)
  local copies, waits for them, and re-layouts  40.9 us (16%)
  Pallas kernels  33.4 us (13%)
  other arithmetic  22.1 us (9%)
    ppermute x60, waiting for transfers between devices, swap(): lax.ppermute(block, axis, [(i, i ^ bit) for i in range(lax.axis_size(axis...  102 us
    ppermute x60, starting transfers between devices, swap(): lax.ppermute(block, axis, [(i, i ^ bit) for i in range(lax.axis_size(axis...  51.3 us
    pallas_call x13, Pallas kernels, local_kernel(): pl.pallas_call(body, name=name, out_shape=outs, in_specs=specs, out_specs...  33.4 us
    unnamed x161, local copies, waits for them, and re-layouts  24.3 us
  transfers between devices with their start and end apart: 60, of which 28 were waited for; matrix products, arithmetic and copies ran while one was open for 12% of the time, Pallas kernels for 9%

profile of v1, /device:TPU:0, one launch (start us, length us, event | category | flops | bytes accessed | tf_op | source)
XLA Modules:
  0.0 251.9 jit_solution(5014883261981128540)
XLA Ops:
  0.7 2.4 constant_dynamic-slice_fusion.6
  3.1 2.9 %collective-permute-start.11 = (bf16[192,1536]{1,0:T(8,128)(2,1)}, bf16[192,1536]{1,0:T(8,128)(2,1)S(1)}, u32[]{:S(2)}, u32[]{:S(2)}) collective-permute-start(bf16[192,1536]{1,0:T(8,128)(2,1)} %get-tuple-element.135), channel_id=1, source_target_pairs={{0,2},{1,3},{2,0},{3,1},{4,6},{5,7},{6,4},{7,5},{8,10},{9,11},{10,... | collective-permute-start | bytes 1769480 | tf_op jit(solution)/shard_map/ppermute | solution.py:23
  6.1 2.0 collective-permute-start.7
  13.0 1.4 stack.54
  15.2 5.3 %collective-permute-done.11.wb_x = bf16[192,1536]{1,0:T(8,128)(2,1)S(1)} collective-permute-done((bf16[192,1536]{1,0:T(8,128)(2,1)}, bf16[192,1536]{1,0:T(8,128)(2,1)S(1)}, u32[]{:S(2)}, u32[]{:S(2)}) %collective-permute-start.11) | collective-permute-done | bytes 589856 | tf_op jit(solution)/shard_map/ppermute | solution.py:23
  22.0 2.8 %collective-permute-done.1.x2 = bf16[192,512]{1,0:T(8,128)(2,1)} collective-permute-done((bf16[192,512]{1,0:T(8,128)(2,1)}, bf16[192,512]{1,0:T(8,128)(2,1)}, u32[]{:S(2)}, u32[]{:S(2)}) %collective-permute-start.1) | collective-permute-done | bytes 196640 | tf_op jit(solution)/shard_map/ppermute | solution.py:23
  24.8 5.4 %collective-permute-done.7.wo_x = bf16[192,768]{1,0:T(8,128)(2,1)S(1)} collective-permute-done((bf16[192,768]{1,0:T(8,128)(2,1)S(1)}, bf16[192,768]{1,0:T(8,128)(2,1)S(1)}, u32[]{:S(2)}, u32[]{:S(2)}) %collective-permute-start.7) | collective-permute-done | bytes 294944 | tf_op jit(solution)/shard_map/ppermute | solution.py:23
  31.1 6.0 %attn_forward.1 = (bf16[768,512]{1,0:T(8,128)(2,1)S(1)}, bf16[3,192,512]{2,1,0:T(8,128)(2,1)S(1)}, f32[8,512]{1,0:T(8,128)S(1)}, bf16[192,128]{1,0:T(8,128)(2,1)...) custom-call(s32[2]{0:T(128)S(1)} %pad_add_fusion.where, ...), custom_call_target="tpu_custom_call" | custom-call | flops 654311424 | bytes 3465252 | tf_op jit(solution)/shard_map/attn_forward/pallas_call | solution.py:33
  40.3 1.8 collective-permute-start.6
  42.0 1.9 collective-permute-done.6
  44.0 1.8 collective-permute-start.4
  45.7 2.9 %collective-permute-done.4.g2 = bf16[384,128]{1,0:T(8,128)(2,1)S(1)} collective-permute-done((bf16[384,128]{1,0:T(8,128)(2,1)S(1)}, bf16[384,128]{1,0:T(8,128)(2,1)S(1)}, u32[]{:S(2)}, u32[]{:S(2)}) %collective-permute-start.4) | collective-permute-done | bytes 98336 | tf_op jit(solution)/shard_map/ppermute | solution.py:23
  48.6 1.8 collective-permute-start.15
  51.5 2.0 attn_out.1
  56.0 5.3 %collective-permute-done.13.normed.n1 = bf16[128,768]{1,0:T(8,128)(2,1)S(1)} collective-permute-done((bf16[128,768]{1,0:T(8,128)(2,1)S(1)}, bf16[128,768]{1,0:T(8,128)(2,1)S(1)}, u32[]{:S(2)}, u32[]{:S(2)}) %collective-permute-start.13) | collective-permute-done | bytes 196640 | tf_op jit(solution)/shard_map/ppermute | solution.py:23
  61.4 2.7 %ffn_forward.3 = (f32[128,1536]{1,0:T(8,128)S(1)}, f32[128,1536]{1,0:T(8,128)S(1)}, bf16[128,768]{1,0:T(8,128)(2,1)S(1)}, bf16[128,768]{1,0:T(8,128)(2,1)S(1)}, bf16[128,768]{1,0:T(8,128)(2,1)S(1)}) custom-call(s32[2]{0:T(128)S(1)} %pad_add_fusion.where, bf16[128,768]{1,0:T(8,128)(2,1)S(1)} %collective-permute-done.13.normed.n1, ...), custom_call_target="tpu_custom_call" | custom-call | flops 603979776 | bytes 7680008 | tf_op jit(solution)/shard_map/ffn_forward/pallas_call | solution.py:33
  67.3 2.7 %ffn_forward.2 = (f32[128,1536]{1,0:T(8,128)S(1)}, f32[128,1536]{1,0:T(8,128)S(1)}, bf16[128,768]{1,0:T(8,128)(2,1)S(1)}, bf16[128,768]{1,0:T(8,128)(2,1)S(1)}, f32[128,768]{1,0:T(8,128)S(1)}) custom-call(s32[2]{0:T(128)S(1)} %pad_add_fusion.where, bf16[128,768]{1,0:T(8,128)(2,1)S(1)} %get-tuple-element.77.normed.n0, ...), custom_call_target="tpu_custom_call" | custom-call | flops 603979776 | bytes 7876616 | tf_op jit(solution)/shard_map/ffn_forward/pallas_call | solution.py:33
  73.3 1.8 second_norm.1
  86.0 2.6 %ffn_backward.2 = (bf16[128,768]{1,0:T(8,128)(2,1)S(1)}, bf16[128,768]{1,0:T(8,128)(2,1)S(1)}, f32[128,768]{1,0:T(8,128)S(1)}, f32[8,1536]{1,0:T(8,128)S(1)}) custom-call(s32[2]{0:T(128)S(1)} %pad_add_fusion.where, bf16[128,768]{1,0:T(8,128)(2,1)S(1)} %copy-done.41, f32[128,1536]{1,0:T(8,128)S(1)} %copy-done.24, f32[128,1536]{1,0:T(8,128)S(1)} %copy-done.26, ...), custom_call_target="tpu_custom_call" | custom-call | flops 603979776 | bytes 7925768 | tf_op jit(solution)/shard_map/ffn_backward/pallas_call | solution.py:33
  88.7 1.5 collective-permute-start.19
  91.7 3.9 %collective-permute-done.19.grad_ffn.f1 = bf16[128,768]{1,0:T(8,128)(2,1)S(1)} collective-permute-done((bf16[128,768]{1,0:T(8,128)(2,1)S(1)}, bf16[128,768]{1,0:T(8,128)(2,1)S(1)}, u32[]{:S(2)}, u32[]{:S(2)}) %collective-permute-start.19) | collective-permute-done | bytes 196640 | tf_op jit(solution)/shard_map/ppermute | solution.py:23
  95.6 1.4 collective-permute-start.18
  97.1 2.6 %ffn_backward.3 = (bf16[128,768]{1,0:T(8,128)(2,1)S(1)}, bf16[128,768]{1,0:T(8,128)(2,1)S(1)}, bf16[128,768]{1,0:T(8,128)(2,1)S(1)}, f32[8,1536]{1,0:T(8,128)S(1)}) custom-call(s32[2]{0:T(128)S(1)} %pad_add_fusion.where, bf16[128,768]{1,0:T(8,128)(2,1)S(1)} %collective-permute-done.19.grad_ffn.f1, f32[128,1536]{1,0:T(8,128)S(1)} %copy-done.20, ...), custom_call_target="tpu_custom_call" | custom-call | flops 603979776 | bytes 7729160 | tf_op jit(solution)/shard_map/ffn_backward/pallas_call | solution.py:33
  100.2 1.4 collective-permute-start.20
  102.9 3.0 %collective-permute-done.20.recv = bf16[128,768]{1,0:T(8,128)(2,1)S(1)} collective-permute-done((bf16[128,768]{1,0:T(8,128)(2,1)S(1)}, bf16[128,768]{1,0:T(8,128)(2,1)S(1)}, u32[]{:S(2)}, u32[]{:S(2)}) %collective-permute-start.20) | collective-permute-done | bytes 196640 | tf_op jit(solution)/shard_map/ppermute | solution.py:23
  106.0 1.8 attn_out_back.1
  109.2 2.4 ffn_weight_grads.1
  112.5 1.4 collective-permute-start.21
  114.6 2.9 %collective-permute-done.21.from_x = bf16[384,128]{1,0:T(8,128)(2,1)S(1)} collective-permute-done((bf16[384,128]{1,0:T(8,128)(2,1)S(1)}, bf16[384,128]{1,0:T(8,128)(2,1)S(1)}, u32[]{:S(2)}, u32[]{:S(2)}) %collective-permute-start.21) | collective-permute-done | bytes 98336 | tf_op jit(solution)/shard_map/ppermute | solution.py:23
  118.9 4.9 %attn_backward.1 = (bf16[576,512]{1,0:T(8,128)(2,1)S(1)}, f32[8,128]{1,0:T(8,128)S(1)}, f32[8,576]{1,0:T(8,128)S(1)}) custom-call(s32[2]{0:T(128)S(1)} %pad_add_fusion.where, s32[1,4]{1,0:T(1,128)S(1)} %copy-done.68, bf16[3,192,512]{2,1,0:T(8,128)(2,1)S(1)} %copy-done.70, f32[8,512]{1,0:T(8,128)S(1)} %copy-done.72, ...), custom_call_target="tpu_custom_call" | custom-call | flops 503316480 | bytes 1464344 | tf_op jit(solution)/shard_map/attn_backward/pallas_call | solution.py:33
  125.7 2.7 %concatenate.170 = f32[12,768]{1,0:T(8,128)} concatenate(f32[8,768]{1,0:T(8,128)} %add.163, f32[1,768]{1,0:T(1,128)S(1)} %fusion.12, f32[1,768]{1,0:T(1,128)S(1)} %slice.155, f32[1,768]{1,0:T(1,128)} %pad.13, f32[1,768]{1,0:T(1,128)S(1)} %pad.14), dimensions={0} | concatenate | bytes 73728 | tf_op jit(solution)/shard_map/concatenate | solution.py:771
  128.3 1.6 collective-permute-start.43
  129.9 1.8 maximum_select_fusion.10
  132.1 1.6 collective-permute-start.46
  136.8 1.6 collective-permute-start.44
  138.3 1.5 qkv_input_grad.1
  140.9 2.6 %collective-permute-start.45 = (f32[12,768]{1,0:T(8,128)S(1)}, f32[12,768]{1,0:T(8,128)S(1)}, u32[]{:S(2)}, u32[]{:S(2)}) collective-permute-start(f32[12,768]{1,0:T(8,128)S(1)} %add.167), channel_id=1, source_target_pairs={{0,16},{4,20},{8,24},{12,28},{16,0},{20,4},{24,8},{28,12},{1,17},{... | collective-permute-start | bytes 110600 | tf_op jit(solution)/shard_map/ppermute | solution.py:23
  144.5 1.6 collective-permute-done.45
  146.1 2.0 fusion.15
  149.8 1.5 fusion.13
  152.5 1.5 collective-permute-start.53
  154.0 5.6 %collective-permute-done.46 = bf16[384,768]{1,0:T(8,128)(2,1)S(1)} collective-permute-done((bf16[384,768]{1,0:T(8,128)(2,1)}, bf16[384,768]{1,0:T(8,128)(2,1)S(1)}, u32[]{:S(2)}, u32[]{:S(2)}) %collective-permute-start.46) | collective-permute-done | bytes 589856 | tf_op jit(solution)/shard_map/ppermute | solution.py:23
  159.8 1.6 collective-permute-start.47
  161.6 1.5 collective-permute-start.26
  164.0 2.7 %collective-permute-start.54 = (bf16[96,768]{1,0:T(8,128)(2,1)S(1)}, bf16[96,768]{1,0:T(8,128)(2,1)S(1)}, u32[]{:S(2)}, u32[]{:S(2)}) collective-permute-start(bf16[96,768]{1,0:T(8,128)(2,1)S(1)} %dynamic-slice_convert_fusion.3), channel_id=1, source_target_pairs={{0,16},{4,20},{8,24},{12,28},{16,0},{20,4},{24,8},{28,12},{1,17},{... | collective-permute-start | bytes 442376 | tf_op jit(solution)/shard_map/ppermute | solution.py:23
  166.7 3.5 %collective-permute-done.47 = bf16[192,768]{1,0:T(8,128)(2,1)S(1)} collective-permute-done((bf16[192,768]{1,0:T(8,128)(2,1)S(1)}, bf16[192,768]{1,0:T(8,128)(2,1)S(1)}, u32[]{:S(2)}, u32[]{:S(2)}) %collective-permute-start.47) | collective-permute-done | bytes 294944 | tf_op jit(solution)/shard_map/ppermute | solution.py:23
  170.3 2.0 collective-permute-start.48
  173.4 1.9 collective-permute-done.54
  175.4 3.8 %collective-permute-done.48 = bf16[96,768]{1,0:T(8,128)(2,1)S(1)} collective-permute-done((bf16[96,768]{1,0:T(8,128)(2,1)S(1)}, bf16[96,768]{1,0:T(8,128)(2,1)S(1)}, u32[]{:S(2)}, u32[]{:S(2)}) %collective-permute-start.48) | collective-permute-done | bytes 147488 | tf_op jit(solution)/shard_map/ppermute | solution.py:23
  179.4 1.5 collective-permute-start.56
  180.9 2.9 %collective-permute-done.56 = bf16[48,768]{1,0:T(8,128)(2,1)S(1)} collective-permute-done((bf16[48,768]{1,0:T(8,128)(2,1)S(1)}, bf16[48,768]{1,0:T(8,128)(2,1)S(1)}, u32[]{:S(2)}, u32[]{:S(2)}) %collective-permute-start.56) | collective-permute-done | bytes 73760 | tf_op jit(solution)/shard_map/ppermute | solution.py:23
  184.9 2.7 %collective-permute-start.28 = (bf16[192,768]{1,0:T(8,128)(2,1)S(1)}, bf16[192,768]{1,0:T(8,128)(2,1)S(1)}, u32[]{:S(2)}, u32[]{:S(2)}) collective-permute-start(bf16[192,768]{1,0:T(8,128)(2,1)S(1)} %dynamic-slice_convert_fusion.2), channel_id=1, source_target_pairs={{0,8},{4,12},{8,0},{12,4},{16,24},{20,28},{24,16},{28,20},{1,9},{5... | collective-permute-start | bytes 884744 | tf_op jit(solution)/shard_map/ppermute | solution.py:23
  188.0 8.7 %collective-permute-done.28 = bf16[192,768]{1,0:T(8,128)(2,1)S(1)} collective-permute-done((bf16[192,768]{1,0:T(8,128)(2,1)S(1)}, bf16[192,768]{1,0:T(8,128)(2,1)S(1)}, u32[]{:S(2)}, u32[]{:S(2)}) %collective-permute-start.28) | collective-permute-done | bytes 294944 | tf_op jit(solution)/shard_map/ppermute | solution.py:23
  197.4 2.5 %collective-permute-start.50 = (bf16[192,768]{1,0:T(8,128)(2,1)S(1)}, bf16[192,768]{1,0:T(8,128)(2,1)S(1)}, u32[]{:S(2)}, u32[]{:S(2)}) collective-permute-start(bf16[192,768]{1,0:T(8,128)(2,1)S(1)} %maximum_select_fusion.7), channel_id=1, source_target_pairs={{0,8},{4,12},{8,0},{12,4},{16,24},{20,28},{24,16},{28,20},{1,9},{5... | collective-permute-start | bytes 884744 | tf_op jit(solution)/shard_map/ppermute | solution.py:23
  200.1 6.0 %collective-permute-done.29 = bf16[96,768]{1,0:T(8,128)(2,1)S(1)} collective-permute-done((bf16[96,768]{1,0:T(8,128)(2,1)S(1)}, bf16[96,768]{1,0:T(8,128)(2,1)S(1)}, u32[]{:S(2)}, u32[]{:S(2)}) %collective-permute-start.29) | collective-permute-done | bytes 147488 | tf_op jit(solution)/shard_map/ppermute | solution.py:23
  206.2 7.9 %collective-permute-done.50 = bf16[192,768]{1,0:T(8,128)(2,1)S(1)} collective-permute-done((bf16[192,768]{1,0:T(8,128)(2,1)S(1)}, bf16[192,768]{1,0:T(8,128)(2,1)S(1)}, u32[]{:S(2)}, u32[]{:S(2)}) %collective-permute-start.50) | collective-permute-done | bytes 294944 | tf_op jit(solution)/shard_map/ppermute | solution.py:23
  215.1 4.0 %collective-permute-done.58 = bf16[192,768]{1,0:T(8,128)(2,1)S(1)} collective-permute-done((bf16[192,768]{1,0:T(8,128)(2,1)S(1)}, bf16[192,768]{1,0:T(8,128)(2,1)S(1)}, u32[]{:S(2)}, u32[]{:S(2)}) %collective-permute-start.58) | collective-permute-done | bytes 294944 | tf_op jit(solution)/shard_map/ppermute | solution.py:23
  220.3 1.9 pad_maximum_fusion.13
  223.0 4.6 %collective-permute-done.31 = bf16[192,768]{1,0:T(8,128)(2,1)S(1)} collective-permute-done((bf16[192,768]{1,0:T(8,128)(2,1)S(1)}, bf16[192,768]{1,0:T(8,128)(2,1)S(1)}, u32[]{:S(2)}, u32[]{:S(2)}) %collective-permute-start.31) | collective-permute-done | bytes 294944 | tf_op jit(solution)/shard_map/ppermute | solution.py:23
  227.8 1.5 collective-permute-start.32
  229.2 1.6 fusion.5
  230.9 9.4 %collective-permute-done.59 = bf16[384,768]{1,0:T(8,128)(2,1)S(1)} collective-permute-done((bf16[384,768]{1,0:T(8,128)(2,1)S(1)}, bf16[384,768]{1,0:T(8,128)(2,1)S(1)}, u32[]{:S(2)}, u32[]{:S(2)}) %collective-permute-start.59) | collective-permute-done | bytes 589856 | tf_op jit(solution)/shard_map/ppermute | solution.py:23
  241.9 1.8 copy.35
  243.7 5.8 %collective-permute-done.32 = bf16[384,768]{1,0:T(8,128)(2,1)S(1)} collective-permute-done((bf16[384,768]{1,0:T(8,128)(2,1)S(1)}, bf16[384,768]{1,0:T(8,128)(2,1)S(1)}, u32[]{:S(2)}, u32[]{:S(2)}) %collective-permute-start.32) | collective-permute-done | bytes 589856 | tf_op jit(solution)/shard_map/ppermute | solution.py:23
  (329 shorter events, 62.0 us)
Async XLA Ops:
  3.1 17.3 %collective-permute-start.11 = (bf16[192,1536]{1,0:T(8,128)(2,1)}, bf16[192,1536]{1,0:T(8,128)(2,1)S(1)}, u32[]{:S(2)}, u32[]{:S(2)}) collective-permute-start(bf16[192,1536]{1,0:T(8,128)(2,1)} %get-tuple-element.135), channel_id=1, source_target_pairs={{0,2},{1,3},{2,0},{3,1},{4,6},{5,7},{6,4},{7,5},{8,10},{9,11},{10,... | collective-permute-start | bytes 1769480 | tf_op jit(solution)/shard_map/ppermute | solution.py:23
  6.1 18.7 %collective-permute-start.1 = (bf16[192,512]{1,0:T(8,128)(2,1)}, bf16[192,512]{1,0:T(8,128)(2,1)}, u32[]{:S(2)}, u32[]{:S(2)}) collective-permute-start(bf16[192,512]{1,0:T(8,128)(2,1)} %x0.1), channel_id=1, source_target_pairs={{0,2},{1,3},{2,0},{3,1},{4,6},{5,7},{6,4},{7,5},{8,10},{9,11},{10,... | collective-permute-start | bytes 589832 | tf_op jit(solution)/shard_map/ppermute | solution.py:23
  6.1 24.3 %collective-permute-start = (bf16[192,512]{1,0:T(8,128)(2,1)}, bf16[192,512]{1,0:T(8,128)(2,1)}, u32[]{:S(2)}, u32[]{:S(2)}) collective-permute-start(bf16[192,512]{1,0:T(8,128)(2,1)} %x0.1), channel_id=1, source_target_pairs={{0,1},{1,0},{2,3},{3,2},{4,5},{5,4},{6,7},{7,6},{8,9},{9,8},{10,11... | collective-permute-start | bytes 589832 | tf_op jit(solution)/shard_map/ppermute | solution.py:23
  6.1 24.0 %collective-permute-start.7 = (bf16[192,768]{1,0:T(8,128)(2,1)S(1)}, bf16[192,768]{1,0:T(8,128)(2,1)S(1)}, u32[]{:S(2)}, u32[]{:S(2)}) collective-permute-start(bf16[192,768]{1,0:T(8,128)(2,1)S(1)} %copy-done.7), channel_id=1, source_target_pairs={{0,2},{1,3},{2,0},{3,1},{4,6},{5,7},{6,4},{7,5},{8,10},{9,11},{10,... | collective-permute-start | bytes 884744 | tf_op jit(solution)/shard_map/ppermute | solution.py:23
  8.1 53.3 %collective-permute-start.10 = (bf16[768,768]{1,0:T(8,128)(2,1)S(1)}, bf16[768,768]{1,0:T(8,128)(2,1)S(1)}, u32[]{:S(2)}, u32[]{:S(2)}) collective-permute-start(bf16[768,768]{1,0:T(8,128)(2,1)S(1)} %copy-done.1), channel_id=1, source_target_pairs={{0,1},{1,0},{2,3},{3,2},{4,5},{5,4},{6,7},{7,6},{8,9},{9,8},{10,11... | collective-permute-start | bytes 3538952 | tf_op jit(solution)/shard_map/ppermute | solution.py:23
  21.9 39.5 %collective-permute-start.12 = (bf16[384,1536]{1,0:T(8,128)(2,1)S(1)}, bf16[384,1536]{1,0:T(8,128)(2,1)S(1)}, u32[]{:S(2)}, u32[]{:S(2)}) collective-permute-start(bf16[384,1536]{1,0:T(8,128)(2,1)S(1)} %pad_maximum_fusion), channel_id=1, source_target_pairs={{0,1},{1,0},{2,3},{3,2},{4,5},{5,4},{6,7},{7,6},{8,9},{9,8},{10,11... | collective-permute-start | bytes 3538952 | tf_op jit(solution)/shard_map/ppermute | solution.py:23
  24.8 6.2 %collective-permute-start.2 = (bf16[192,512]{1,0:T(8,128)(2,1)}, bf16[192,512]{1,0:T(8,128)(2,1)S(1)}, u32[]{:S(2)}, u32[]{:S(2)}) collective-permute-start(bf16[192,512]{1,0:T(8,128)(2,1)} %collective-permute-done.1.x2), channel_id=1, source_target_pairs={{0,1},{1,0},{2,3},{3,2},{4,5},{5,4},{6,7},{7,6},{8,9},{9,8},{10,11... | collective-permute-start | bytes 589832 | tf_op jit(solution)/shard_map/ppermute | solution.py:23
  30.2 20.1 %collective-permute-start.8 = (bf16[384,768]{1,0:T(8,128)(2,1)S(1)}, bf16[384,768]{1,0:T(8,128)(2,1)S(1)}, u32[]{:S(2)}, u32[]{:S(2)}) collective-permute-start(bf16[384,768]{1,0:T(8,128)(2,1)S(1)} %pad_maximum_fusion.1), channel_id=1, source_target_pairs={{0,1},{1,0},{2,3},{3,2},{4,5},{5,4},{6,7},{7,6},{8,9},{9,8},{10,11... | collective-permute-start | bytes 1769480 | tf_op jit(solution)/shard_map/ppermute | solution.py:23
  30.4 8.4 %collective-permute-start.5 = (f32[8,192]{1,0:T(8,128)S(1)}, f32[8,192]{1,0:T(8,128)S(1)}, u32[]{:S(2)}, u32[]{:S(2)}) collective-permute-start(f32[8,192]{1,0:T(8,128)S(1)} %copy-done.73), channel_id=1, source_target_pairs={{0,1},{1,0},{2,3},{3,2},{4,5},{5,4},{6,7},{7,6},{8,9},{9,8},{10,11... | collective-permute-start | bytes 18440 | tf_op jit(solution)/shard_map/ppermute | solution.py:23
  31.0 25.0 %collective-permute-start.9 = (f32[2,768]{1,0:T(2,128)S(1)}, f32[2,768]{1,0:T(2,128)S(1)}, u32[]{:S(2)}, u32[]{:S(2)}) collective-permute-start(f32[2,768]{1,0:T(2,128)S(1)} %pad_maximum_fusion.9), channel_id=1, source_target_pairs={{0,1},{1,0},{2,3},{3,2},{4,5},{5,4},{6,7},{7,6},{8,9},{9,8},{10,11... | collective-permute-start | bytes 18440 | tf_op jit(solution)/shard_map/ppermute | solution.py:23
  31.1 24.9 %copy-start.75 = (f32[1,768]{1,0:T(1,128)S(1)}, f32[1,768]{1,0:T(1,128)}, u32[]{:S(2)}) copy-start(f32[1,768]{1,0:T(1,128)} %copy-done.74) | copy-start | bytes 9220
  38.8 22.6 %copy-start = (bf16[192,3072]{1,0:T(8,128)(2,1)S(1)}, bf16[192,3072]{1,0:T(8,128)(2,1)}, u32[]{:S(2)}) copy-start(bf16[192,3072]{1,0:T(8,128)(2,1)} %wb_own.7) | copy-start | bytes 3538948
  38.8 22.6 %copy-start.5 = (bf16[192,1536]{1,0:T(8,128)(2,1)S(1)}, bf16[192,1536]{1,0:T(8,128)(2,1)}, u32[]{:S(2)}) copy-start(bf16[192,1536]{1,0:T(8,128)(2,1)} %copy-done.4) | copy-start | bytes 1769476
  38.8 1.4 collective-permute-start.3
  40.3 3.7 %collective-permute-start.6 = (f32[8,384]{1,0:T(8,128)S(1)}, f32[8,384]{1,0:T(8,128)S(1)}, u32[]{:S(2)}, u32[]{:S(2)}) collective-permute-start(f32[8,384]{1,0:T(8,128)S(1)} %maximum_select_fusion.16), channel_id=1, source_target_pairs={{0,2},{1,3},{2,0},{3,1},{4,6},{5,7},{6,4},{7,5},{8,10},{9,11},{10,... | collective-permute-start | bytes 36872 | tf_op jit(solution)/shard_map/ppermute | solution.py:23
  44.0 4.6 %collective-permute-start.4 = (bf16[384,128]{1,0:T(8,128)(2,1)S(1)}, bf16[384,128]{1,0:T(8,128)(2,1)S(1)}, u32[]{:S(2)}, u32[]{:S(2)}) collective-permute-start(bf16[384,128]{1,0:T(8,128)(2,1)S(1)} %pad_maximum_fusion.4), channel_id=1, source_target_pairs={{0,2},{1,3},{2,0},{3,1},{4,6},{5,7},{6,4},{7,5},{8,10},{9,11},{10,... | collective-permute-start | bytes 294920 | tf_op jit(solution)/shard_map/ppermute | solution.py:23
  45.7 27.5 %copy-start.28 = (f32[8,768]{1,0:T(8,128)}, f32[8,768]{1,0:T(8,128)S(1)}, u32[]{:S(2)}) copy-start(f32[8,768]{1,0:T(8,128)S(1)} %maximum_select_fusion.15.vecs) | copy-start | bytes 73732
  48.6 7.4 %collective-permute-start.15 = (bf16[192,256]{1,0:T(8,128)(2,1)S(1)}, bf16[192,256]{1,0:T(8,128)(2,1)S(1)}, u32[]{:S(2)}, u32[]{:S(2)}) collective-permute-start(bf16[192,256]{1,0:T(8,128)(2,1)S(1)} %constant_dynamic-slice_fusion.5), channel_id=1, source_target_pairs={{0,2},{1,3},{2,0},{3,1},{4,6},{5,7},{6,4},{7,5},{8,10},{9,11},{10,... | collective-permute-start | bytes 294920 | tf_op jit(solution)/shard_map/ppermute | solution.py:23
  55.7 5.7 %collective-permute-start.13 = (bf16[128,768]{1,0:T(8,128)(2,1)S(1)}, bf16[128,768]{1,0:T(8,128)(2,1)S(1)}, u32[]{:S(2)}, u32[]{:S(2)}) collective-permute-start(bf16[128,768]{1,0:T(8,128)(2,1)S(1)} %get-tuple-element.77.normed.n0), channel_id=1, source_target_pairs={{0,2},{1,3},{2,0},{3,1},{4,6},{5,7},{6,4},{7,5},{8,10},{9,11},{10,... | collective-permute-start | bytes 589832 | tf_op jit(solution)/shard_map/ppermute | solution.py:23
  66.7 6.6 %collective-permute-start.14 = (bf16[128,768]{1,0:T(8,128)(2,1)S(1)}, bf16[128,768]{1,0:T(8,128)(2,1)S(1)}, u32[]{:S(2)}, u32[]{:S(2)}) collective-permute-start(bf16[128,768]{1,0:T(8,128)(2,1)S(1)} %get-tuple-element.79), channel_id=1, source_target_pairs={{0,2},{1,3},{2,0},{3,1},{4,6},{5,7},{6,4},{7,5},{8,10},{9,11},{10,... | collective-permute-start | bytes 589832 | tf_op jit(solution)/shard_map/ppermute | solution.py:23
  67.3 5.9 %collective-permute-start.16 = (bf16[384,128]{1,0:T(8,128)(2,1)S(1)}, bf16[384,128]{1,0:T(8,128)(2,1)S(1)}, u32[]{:S(2)}, u32[]{:S(2)}) collective-permute-start(bf16[384,128]{1,0:T(8,128)(2,1)S(1)} %pad_maximum_fusion.5), channel_id=1, source_target_pairs={{0,1},{1,0},{2,3},{3,2},{4,5},{5,4},{6,7},{7,6},{8,9},{9,8},{10,11... | collective-permute-start | bytes 294920 | tf_op jit(solution)/shard_map/ppermute | solution.py:23
  78.3 10.3 %collective-permute-start.17 = (bf16[384,128]{1,0:T(8,128)(2,1)}, bf16[384,128]{1,0:T(8,128)(2,1)}, u32[]{:S(2)}, u32[]{:S(2)}) collective-permute-start(bf16[384,128]{1,0:T(8,128)(2,1)} %get-tuple-element.82), channel_id=1, source_target_pairs={{0,1},{1,0},{2,3},{3,2},{4,5},{5,4},{6,7},{7,6},{8,9},{9,8},{10,11... | collective-permute-start | bytes 294920 | tf_op jit(solution)/shard_map/ppermute | solution.py:23
  79.5 22.8 %collective-permute-start.35 = (bf16[128,768]{1,0:T(8,128)(2,1)}, bf16[128,768]{1,0:T(8,128)(2,1)S(1)}, u32[]{:S(2)}, u32[]{:S(2)}) collective-permute-start(bf16[128,768]{1,0:T(8,128)(2,1)} %copy-done.36), channel_id=1, source_target_pairs={{0,1},{1,0},{2,3},{3,2},{4,5},{5,4},{6,7},{7,6},{8,9},{9,8},{10,11... | collective-permute-start | bytes 589832 | tf_op jit(solution)/shard_map/ppermute | solution.py:23
  79.5 22.8 %collective-permute-start.36 = (bf16[128,768]{1,0:T(8,128)(2,1)}, bf16[128,768]{1,0:T(8,128)(2,1)S(1)}, u32[]{:S(2)}, u32[]{:S(2)}) collective-permute-start(bf16[128,768]{1,0:T(8,128)(2,1)} %copy-done.38), channel_id=1, source_target_pairs={{0,1},{1,0},{2,3},{3,2},{4,5},{5,4},{6,7},{7,6},{8,9},{9,8},{10,11... | collective-permute-start | bytes 589832 | tf_op jit(solution)/shard_map/ppermute | solution.py:23
  80.0 22.8 %collective-permute-start.38 = (bf16[128,768]{1,0:T(8,128)(2,1)}, bf16[128,768]{1,0:T(8,128)(2,1)S(1)}, u32[]{:S(2)}, u32[]{:S(2)}) collective-permute-start(bf16[128,768]{1,0:T(8,128)(2,1)} %copy-done.64), channel_id=1, source_target_pairs={{0,1},{1,0},{2,3},{3,2},{4,5},{5,4},{6,7},{7,6},{8,9},{9,8},{10,11... | collective-permute-start | bytes 589832 | tf_op jit(solution)/shard_map/ppermute | solution.py:23
  80.0 28.6 %collective-permute-start.37 = (bf16[128,768]{1,0:T(8,128)(2,1)}, bf16[128,768]{1,0:T(8,128)(2,1)S(1)}, u32[]{:S(2)}, u32[]{:S(2)}) collective-permute-start(bf16[128,768]{1,0:T(8,128)(2,1)} %copy-done.63), channel_id=1, source_target_pairs={{0,1},{1,0},{2,3},{3,2},{4,5},{5,4},{6,7},{7,6},{8,9},{9,8},{10,11... | collective-permute-start | bytes 589832 | tf_op jit(solution)/shard_map/ppermute | solution.py:23
  88.7 6.9 %collective-permute-start.19 = (bf16[128,768]{1,0:T(8,128)(2,1)S(1)}, bf16[128,768]{1,0:T(8,128)(2,1)S(1)}, u32[]{:S(2)}, u32[]{:S(2)}) collective-permute-start(bf16[128,768]{1,0:T(8,128)(2,1)S(1)} %copy-done.41), channel_id=1, source_target_pairs={{0,2},{1,3},{2,0},{3,1},{4,6},{5,7},{6,4},{7,5},{8,10},{9,11},{10,... | collective-permute-start | bytes 589832 | tf_op jit(solution)/shard_map/ppermute | solution.py:23
  95.6 4.6 %collective-permute-start.18 = (bf16[384,128]{1,0:T(8,128)(2,1)S(1)}, bf16[384,128]{1,0:T(8,128)(2,1)S(1)}, u32[]{:S(2)}, u32[]{:S(2)}) collective-permute-start(bf16[384,128]{1,0:T(8,128)(2,1)S(1)} %pad_maximum_fusion.6), channel_id=1, source_target_pairs={{0,2},{1,3},{2,0},{3,1},{4,6},{5,7},{6,4},{7,5},{8,10},{9,11},{10,... | collective-permute-start | bytes 294920 | tf_op jit(solution)/shard_map/ppermute | solution.py:23
  100.2 5.7 %collective-permute-start.20 = (bf16[128,768]{1,0:T(8,128)(2,1)S(1)}, bf16[128,768]{1,0:T(8,128)(2,1)S(1)}, u32[]{:S(2)}, u32[]{:S(2)}) collective-permute-start(bf16[128,768]{1,0:T(8,128)(2,1)S(1)} %get-tuple-element.92), channel_id=1, source_target_pairs={{0,2},{1,3},{2,0},{3,1},{4,6},{5,7},{6,4},{7,5},{8,10},{9,11},{10,... | collective-permute-start | bytes 589832 | tf_op jit(solution)/shard_map/ppermute | solution.py:23
  102.3 6.8 %collective-permute-start.41 = (bf16[128,768]{1,0:T(8,128)(2,1)S(1)}, bf16[128,768]{1,0:T(8,128)(2,1)S(1)}, u32[]{:S(2)}, u32[]{:S(2)}) collective-permute-start(bf16[128,768]{1,0:T(8,128)(2,1)S(1)} %copy-done.42), channel_id=1, source_target_pairs={{0,1},{1,0},{2,3},{3,2},{4,5},{5,4},{6,7},{7,6},{8,9},{9,8},{10,11... | collective-permute-start | bytes 589832 | tf_op jit(solution)/shard_map/ppermute | solution.py:23
  102.3 6.8 %collective-permute-start.39 = (bf16[128,768]{1,0:T(8,128)(2,1)S(1)}, bf16[128,768]{1,0:T(8,128)(2,1)S(1)}, u32[]{:S(2)}, u32[]{:S(2)}) collective-permute-start(bf16[128,768]{1,0:T(8,128)(2,1)S(1)} %get-tuple-element.121), channel_id=1, source_target_pairs={{0,1},{1,0},{2,3},{3,2},{4,5},{5,4},{6,7},{7,6},{8,9},{9,8},{10,11... | collective-permute-start | bytes 589832 | tf_op jit(solution)/shard_map/ppermute | solution.py:23
  102.8 6.3 %collective-permute-start.40 = (bf16[128,768]{1,0:T(8,128)(2,1)S(1)}, bf16[128,768]{1,0:T(8,128)(2,1)S(1)}, u32[]{:S(2)}, u32[]{:S(2)}) collective-permute-start(bf16[128,768]{1,0:T(8,128)(2,1)S(1)} %get-tuple-element.122), channel_id=1, source_target_pairs={{0,1},{1,0},{2,3},{3,2},{4,5},{5,4},{6,7},{7,6},{8,9},{9,8},{10,11... | collective-permute-start | bytes 589832 | tf_op jit(solution)/shard_map/ppermute | solution.py:23
  105.8 3.3 %collective-permute-start.42 = (bf16[128,768]{1,0:T(8,128)(2,1)S(1)}, bf16[128,768]{1,0:T(8,128)(2,1)S(1)}, u32[]{:S(2)}, u32[]{:S(2)}) collective-permute-start(bf16[128,768]{1,0:T(8,128)(2,1)S(1)} %collective-permute-done.19.grad_ffn.f1), channel_id=1, source_target_pairs={{0,1},{1,0},{2,3},{3,2},{4,5},{5,4},{6,7},{7,6},{8,9},{9,8},{10,11... | collective-permute-start | bytes 589832 | tf_op jit(solution)/shard_map/ppermute | solution.py:23
  108.6 5.3 %collective-permute-start.33 = (f32[9,768]{1,0:T(8,128)S(1)}, f32[9,768]{1,0:T(8,128)S(1)}, u32[]{:S(2)}, u32[]{:S(2)}) collective-permute-start(f32[9,768]{1,0:T(8,128)S(1)} %pad_maximum_fusion.8), channel_id=1, source_target_pairs={{0,1},{1,0},{2,3},{3,2},{4,5},{5,4},{6,7},{7,6},{8,9},{9,8},{10,11... | collective-permute-start | bytes 82952 | tf_op jit(solution)/shard_map/ppermute | solution.py:23
  112.5 5.0 %collective-permute-start.21 = (bf16[384,128]{1,0:T(8,128)(2,1)S(1)}, bf16[384,128]{1,0:T(8,128)(2,1)S(1)}, u32[]{:S(2)}, u32[]{:S(2)}) collective-permute-start(bf16[384,128]{1,0:T(8,128)(2,1)S(1)} %get-tuple-element.98), channel_id=1, source_target_pairs={{0,2},{1,3},{2,0},{3,1},{4,6},{5,7},{6,4},{7,5},{8,10},{9,11},{10,... | collective-permute-start | bytes 294920 | tf_op jit(solution)/shard_map/ppermute | solution.py:23
  113.9 3.9 %collective-permute-start.34 = (f32[8,768]{1,0:T(8,128)S(1)}, f32[8,768]{1,0:T(8,128)S(1)}, u32[]{:S(2)}, u32[]{:S(2)}) collective-permute-start(f32[8,768]{1,0:T(8,128)S(1)} %slice_add_fusion.4), channel_id=1, source_target_pairs={{0,2},{1,3},{2,0},{3,1},{4,6},{5,7},{6,4},{7,5},{8,10},{9,11},{10,... | collective-permute-start | bytes 73736 | tf_op jit(solution)/shard_map/ppermute | solution.py:23
  117.5 1.4 collective-permute-start.22
  128.3 7.6 %collective-permute-start.43 = (f32[12,768]{1,0:T(8,128)}, f32[12,768]{1,0:T(8,128)S(1)}, u32[]{:S(2)}, u32[]{:S(2)}) collective-permute-start(f32[12,768]{1,0:T(8,128)} %concatenate.170), channel_id=1, source_target_pairs={{0,4},{4,0},{8,12},{12,8},{16,20},{20,16},{24,28},{28,24},{1,5},{5... | collective-permute-start | bytes 110600 | tf_op jit(solution)/shard_map/ppermute | solution.py:23
  131.7 20.7 %collective-permute-start.52 = (bf16[384,768]{1,0:T(8,128)(2,1)}, bf16[384,768]{1,0:T(8,128)(2,1)S(1)}, u32[]{:S(2)}, u32[]{:S(2)}) collective-permute-start(bf16[384,768]{1,0:T(8,128)(2,1)} %copy-done.56), channel_id=1, source_target_pairs={{0,4},{4,0},{8,12},{12,8},{16,20},{20,16},{24,28},{28,24},{1,5},{5... | collective-permute-start | bytes 1769480 | tf_op jit(solution)/shard_map/ppermute | solution.py:23
  132.1 27.5 %collective-permute-start.46 = (bf16[384,768]{1,0:T(8,128)(2,1)}, bf16[384,768]{1,0:T(8,128)(2,1)S(1)}, u32[]{:S(2)}, u32[]{:S(2)}) collective-permute-start(bf16[384,768]{1,0:T(8,128)(2,1)} %copy-done.55), channel_id=1, source_target_pairs={{0,4},{4,0},{8,12},{12,8},{16,20},{20,16},{24,28},{28,24},{1,5},{5... | collective-permute-start | bytes 1769480 | tf_op jit(solution)/shard_map/ppermute | solution.py:23
  135.8 25.6 %collective-permute-start.25 = (bf16[384,768]{1,0:T(8,128)(2,1)S(1)}, bf16[384,768]{1,0:T(8,128)(2,1)S(1)}, u32[]{:S(2)}, u32[]{:S(2)}) collective-permute-start(bf16[384,768]{1,0:T(8,128)(2,1)S(1)} %get-tuple-element.109), channel_id=1, source_target_pairs={{0,1},{1,0},{2,3},{3,2},{4,5},{5,4},{6,7},{7,6},{8,9},{9,8},{10,11... | collective-permute-start | bytes 1769480 | tf_op jit(solution)/shard_map/ppermute | solution.py:23
  136.8 4.1 %collective-permute-start.44 = (f32[12,768]{1,0:T(8,128)S(1)}, f32[12,768]{1,0:T(8,128)S(1)}, u32[]{:S(2)}, u32[]{:S(2)}) collective-permute-start(f32[12,768]{1,0:T(8,128)S(1)} %add.166), channel_id=1, source_target_pairs={{0,8},{4,12},{8,0},{12,4},{16,24},{20,28},{24,16},{28,20},{1,9},{5... | collective-permute-start | bytes 110600 | tf_op jit(solution)/shard_map/ppermute | solution.py:23
  139.9 23.2 %collective-permute-start.23 = (bf16[384,512]{1,0:T(8,128)(2,1)S(1)}, bf16[384,512]{1,0:T(8,128)(2,1)S(1)}, u32[]{:S(2)}, u32[]{:S(2)}) collective-permute-start(bf16[384,512]{1,0:T(8,128)(2,1)S(1)} %get-tuple-element.103), channel_id=1, source_target_pairs={{0,1},{1,0},{2,3},{3,2},{4,5},{5,4},{6,7},{7,6},{8,9},{9,8},{10,11... | collective-permute-start | bytes 1179656 | tf_op jit(solution)/shard_map/ppermute | solution.py:23
  140.9 5.2 %collective-permute-start.45 = (f32[12,768]{1,0:T(8,128)S(1)}, f32[12,768]{1,0:T(8,128)S(1)}, u32[]{:S(2)}, u32[]{:S(2)}) collective-permute-start(f32[12,768]{1,0:T(8,128)S(1)} %add.167), channel_id=1, source_target_pairs={{0,16},{4,20},{8,24},{12,28},{16,0},{20,4},{24,8},{28,12},{1,17},{... | collective-permute-start | bytes 110600 | tf_op jit(solution)/shard_map/ppermute | solution.py:23
  152.5 11.4 %collective-permute-start.53 = (bf16[192,768]{1,0:T(8,128)(2,1)S(1)}, bf16[192,768]{1,0:T(8,128)(2,1)S(1)}, u32[]{:S(2)}, u32[]{:S(2)}) collective-permute-start(bf16[192,768]{1,0:T(8,128)(2,1)S(1)} %dynamic-slice_convert_fusion), channel_id=1, source_target_pairs={{0,8},{4,12},{8,0},{12,4},{16,24},{20,28},{24,16},{28,20},{1,9},{5... | collective-permute-start | bytes 884744 | tf_op jit(solution)/shard_map/ppermute | solution.py:23
  159.8 10.4 %collective-permute-start.47 = (bf16[192,768]{1,0:T(8,128)(2,1)S(1)}, bf16[192,768]{1,0:T(8,128)(2,1)S(1)}, u32[]{:S(2)}, u32[]{:S(2)}) collective-permute-start(bf16[192,768]{1,0:T(8,128)(2,1)S(1)} %dynamic-slice_convert_fusion.1), channel_id=1, source_target_pairs={{0,8},{4,12},{8,0},{12,4},{16,24},{20,28},{24,16},{28,20},{1,9},{5... | collective-permute-start | bytes 884744 | tf_op jit(solution)/shard_map/ppermute | solution.py:23
  161.6 10.7 %collective-permute-start.26 = (bf16[192,768]{1,0:T(8,128)(2,1)S(1)}, bf16[192,768]{1,0:T(8,128)(2,1)S(1)}, u32[]{:S(2)}, u32[]{:S(2)}) collective-permute-start(bf16[192,768]{1,0:T(8,128)(2,1)S(1)} %fusion.6), channel_id=1, source_target_pairs={{0,2},{1,3},{2,0},{3,1},{4,6},{5,7},{6,4},{7,5},{8,10},{9,11},{10,... | collective-permute-start | bytes 884744 | tf_op jit(solution)/shard_map/ppermute | solution.py:23
  163.3 58.9 %collective-permute-start.24 = (bf16[192,512]{1,0:T(8,128)(2,1)S(1)}, bf16[192,512]{1,0:T(8,128)(2,1)S(1)}, u32[]{:S(2)}, u32[]{:S(2)}) collective-permute-start(bf16[192,512]{1,0:T(8,128)(2,1)S(1)} %fusion.8), channel_id=1, source_target_pairs={{0,2},{1,3},{2,0},{3,1},{4,6},{5,7},{6,4},{7,5},{8,10},{9,11},{10,... | collective-permute-start | bytes 589832 | tf_op jit(solution)/shard_map/ppermute | solution.py:23
  164.0 11.2 %collective-permute-start.54 = (bf16[96,768]{1,0:T(8,128)(2,1)S(1)}, bf16[96,768]{1,0:T(8,128)(2,1)S(1)}, u32[]{:S(2)}, u32[]{:S(2)}) collective-permute-start(bf16[96,768]{1,0:T(8,128)(2,1)S(1)} %dynamic-slice_convert_fusion.3), channel_id=1, source_target_pairs={{0,16},{4,20},{8,24},{12,28},{16,0},{20,4},{24,8},{28,12},{1,17},{... | collective-permute-start | bytes 442376 | tf_op jit(solution)/shard_map/ppermute | solution.py:23
  170.3 9.0 %collective-permute-start.48 = (bf16[96,768]{1,0:T(8,128)(2,1)S(1)}, bf16[96,768]{1,0:T(8,128)(2,1)S(1)}, u32[]{:S(2)}, u32[]{:S(2)}) collective-permute-start(bf16[96,768]{1,0:T(8,128)(2,1)S(1)} %dynamic-slice_convert_fusion.4), channel_id=1, source_target_pairs={{0,16},{4,20},{8,24},{12,28},{16,0},{20,4},{24,8},{28,12},{1,17},{... | collective-permute-start | bytes 442376 | tf_op jit(solution)/shard_map/ppermute | solution.py:23
  172.7 11.8 %collective-permute-start.27 = (bf16[384,768]{1,0:T(8,128)(2,1)S(1)}, bf16[384,768]{1,0:T(8,128)(2,1)S(1)}, u32[]{:S(2)}, u32[]{:S(2)}) collective-permute-start(bf16[384,768]{1,0:T(8,128)(2,1)S(1)} %fusion.1), channel_id=1, source_target_pairs={{0,4},{4,0},{8,12},{12,8},{16,20},{20,16},{24,28},{28,24},{1,5},{5... | collective-permute-start | bytes 1769480 | tf_op jit(solution)/shard_map/ppermute | solution.py:23
  175.3 4.0 %collective-permute-start.55 = (bf16[48,768]{1,0:T(8,128)(2,1)S(1)}, bf16[48,768]{1,0:T(8,128)(2,1)S(1)}, u32[]{:S(2)}, u32[]{:S(2)}) collective-permute-start(bf16[48,768]{1,0:T(8,128)(2,1)S(1)} %pad_maximum_fusion.2), channel_id=1, source_target_pairs={{0,1},{1,0},{2,3},{3,2},{4,5},{5,4},{6,7},{7,6},{8,9},{9,8},{10,11... | collective-permute-start | bytes 221192 | tf_op jit(solution)/shard_map/ppermute | solution.py:23
  179.3 18.1 %collective-permute-start.49 = (bf16[96,768]{1,0:T(8,128)(2,1)S(1)}, bf16[96,768]{1,0:T(8,128)(2,1)S(1)}, u32[]{:S(2)}, u32[]{:S(2)}) collective-permute-start(bf16[96,768]{1,0:T(8,128)(2,1)S(1)} %add_convert_fusion), channel_id=1, source_target_pairs={{0,16},{4,20},{8,24},{12,28},{16,0},{20,4},{24,8},{28,12},{1,17},{... | collective-permute-start | bytes 442376 | tf_op jit(solution)/shard_map/ppermute | solution.py:23
  179.4 4.4 %collective-permute-start.56 = (bf16[48,768]{1,0:T(8,128)(2,1)S(1)}, bf16[48,768]{1,0:T(8,128)(2,1)S(1)}, u32[]{:S(2)}, u32[]{:S(2)}) collective-permute-start(bf16[48,768]{1,0:T(8,128)(2,1)S(1)} %pad_maximum_fusion.3), channel_id=1, source_target_pairs={{0,2},{1,3},{2,0},{3,1},{4,6},{5,7},{6,4},{7,5},{8,10},{9,11},{10,... | collective-permute-start | bytes 221192 | tf_op jit(solution)/shard_map/ppermute | solution.py:23
  184.9 11.8 %collective-permute-start.28 = (bf16[192,768]{1,0:T(8,128)(2,1)S(1)}, bf16[192,768]{1,0:T(8,128)(2,1)S(1)}, u32[]{:S(2)}, u32[]{:S(2)}) collective-permute-start(bf16[192,768]{1,0:T(8,128)(2,1)S(1)} %dynamic-slice_convert_fusion.2), channel_id=1, source_target_pairs={{0,8},{4,12},{8,0},{12,4},{16,24},{20,28},{24,16},{28,20},{1,9},{5... | collective-permute-start | bytes 884744 | tf_op jit(solution)/shard_map/ppermute | solution.py:23
  187.6 12.3 %collective-permute-start.57 = (bf16[96,768]{1,0:T(8,128)(2,1)S(1)}, bf16[96,768]{1,0:T(8,128)(2,1)S(1)}, u32[]{:S(2)}, u32[]{:S(2)}) collective-permute-start(bf16[96,768]{1,0:T(8,128)(2,1)S(1)} %fusion.11), channel_id=1, source_target_pairs={{0,16},{4,20},{8,24},{12,28},{16,0},{20,4},{24,8},{28,12},{1,17},{... | collective-permute-start | bytes 442376 | tf_op jit(solution)/shard_map/ppermute | solution.py:23
  196.8 9.3 %collective-permute-start.29 = (bf16[96,768]{1,0:T(8,128)(2,1)S(1)}, bf16[96,768]{1,0:T(8,128)(2,1)S(1)}, u32[]{:S(2)}, u32[]{:S(2)}) collective-permute-start(bf16[96,768]{1,0:T(8,128)(2,1)S(1)} %dynamic-slice_convert_fusion.5), channel_id=1, source_target_pairs={{0,16},{4,20},{8,24},{12,28},{16,0},{20,4},{24,8},{28,12},{1,17},{... | collective-permute-start | bytes 442376 | tf_op jit(solution)/shard_map/ppermute | solution.py:23
  197.4 16.7 %collective-permute-start.50 = (bf16[192,768]{1,0:T(8,128)(2,1)S(1)}, bf16[192,768]{1,0:T(8,128)(2,1)S(1)}, u32[]{:S(2)}, u32[]{:S(2)}) collective-permute-start(bf16[192,768]{1,0:T(8,128)(2,1)S(1)} %maximum_select_fusion.7), channel_id=1, source_target_pairs={{0,8},{4,12},{8,0},{12,4},{16,24},{20,28},{24,16},{28,20},{1,9},{5... | collective-permute-start | bytes 884744 | tf_op jit(solution)/shard_map/ppermute | solution.py:23
  200.0 19.0 %collective-permute-start.58 = (bf16[192,768]{1,0:T(8,128)(2,1)S(1)}, bf16[192,768]{1,0:T(8,128)(2,1)S(1)}, u32[]{:S(2)}, u32[]{:S(2)}) collective-permute-start(bf16[192,768]{1,0:T(8,128)(2,1)S(1)} %maximum_select_fusion.9), channel_id=1, source_target_pairs={{0,8},{4,12},{8,0},{12,4},{16,24},{20,28},{24,16},{28,20},{1,9},{5... | collective-permute-start | bytes 884744 | tf_op jit(solution)/shard_map/ppermute | solution.py:23
  206.1 14.1 %collective-permute-start.30 = (bf16[96,768]{1,0:T(8,128)(2,1)S(1)}, bf16[96,768]{1,0:T(8,128)(2,1)S(1)}, u32[]{:S(2)}, u32[]{:S(2)}) collective-permute-start(bf16[96,768]{1,0:T(8,128)(2,1)S(1)} %add_convert_fusion.1), channel_id=1, source_target_pairs={{0,16},{4,20},{8,24},{12,28},{16,0},{20,4},{24,8},{28,12},{1,17},{... | collective-permute-start | bytes 442376 | tf_op jit(solution)/shard_map/ppermute | solution.py:23
  214.3 14.9 %collective-permute-start.51 = (bf16[384,768]{1,0:T(8,128)(2,1)S(1)}, bf16[384,768]{1,0:T(8,128)(2,1)S(1)}, u32[]{:S(2)}, u32[]{:S(2)}) collective-permute-start(bf16[384,768]{1,0:T(8,128)(2,1)S(1)} %maximum_select_fusion.4), channel_id=1, source_target_pairs={{0,4},{4,0},{8,12},{12,8},{16,20},{20,16},{24,28},{28,24},{1,5},{5... | collective-permute-start | bytes 1769480 | tf_op jit(solution)/shard_map/ppermute | solution.py:23
  219.5 20.8 %collective-permute-start.59 = (bf16[384,768]{1,0:T(8,128)(2,1)S(1)}, bf16[384,768]{1,0:T(8,128)(2,1)S(1)}, u32[]{:S(2)}, u32[]{:S(2)}) collective-permute-start(bf16[384,768]{1,0:T(8,128)(2,1)S(1)} %maximum_select_fusion.5), channel_id=1, source_target_pairs={{0,4},{4,0},{8,12},{12,8},{16,20},{20,16},{24,28},{28,24},{1,5},{5... | collective-permute-start | bytes 1769480 | tf_op jit(solution)/shard_map/ppermute | solution.py:23
  220.2 7.4 %collective-permute-start.31 = (bf16[192,768]{1,0:T(8,128)(2,1)S(1)}, bf16[192,768]{1,0:T(8,128)(2,1)S(1)}, u32[]{:S(2)}, u32[]{:S(2)}) collective-permute-start(bf16[192,768]{1,0:T(8,128)(2,1)S(1)} %maximum_select_fusion.6), channel_id=1, source_target_pairs={{0,8},{4,12},{8,0},{12,4},{16,24},{20,28},{24,16},{28,20},{1,9},{5... | collective-permute-start | bytes 884744 | tf_op jit(solution)/shard_map/ppermute | solution.py:23
  227.8 21.7 %collective-permute-start.32 = (bf16[384,768]{1,0:T(8,128)(2,1)S(1)}, bf16[384,768]{1,0:T(8,128)(2,1)S(1)}, u32[]{:S(2)}, u32[]{:S(2)}) collective-permute-start(bf16[384,768]{1,0:T(8,128)(2,1)S(1)} %maximum_select_fusion.3), channel_id=1, source_target_pairs={{0,4},{4,0},{8,12},{12,8},{16,20},{20,16},{24,28},{28,24},{1,5},{5... | collective-permute-start | bytes 1769480 | tf_op jit(solution)/shard_map/ppermute | solution.py:23
  (76 other events, 420.6 us)

commit v2 on v1

v2 whole, which is shorter than its diff:
```python
import jax
import jax.numpy as jnp
from jax import lax
from jax.experimental import pallas as pl
from jax.experimental.pallas import tpu as pltpu
from jax.sharding import PartitionSpec as P

HEAD_DIM = 64
norm_eps = 1e-06
masked_score = -1e30
bf16 = jnp.bfloat16
f32 = jnp.float32
MIB = 1 << 20
HBM_BYTES_PER_MICRO = 3690000

SPECS = {
    "S": pl.BlockSpec(memory_space=pltpu.SMEM),
    "V": pl.BlockSpec(memory_space=pltpu.VMEM),
}


def swap(block, axis, bit):
    return lax.ppermute(block, axis, [(i, i ^ bit) for i in range(lax.axis_size(axis))])


def after(block, *others):
    return lax.optimization_barrier((block, *others))[0]


def sds(shape, dtype):
    return jax.ShapeDtypeStruct(shape, dtype)


def local_kernel(body, name, args, kinds, outs, scratch=(), micros=0.6, vmem=16):
    return pl.pallas_call(
        body,
        name=name,
        out_shape=outs,
        in_specs=[SPECS[k] for k in kinds],
        out_specs=[SPECS["V"]] * len(outs),
        scratch_shapes=list(scratch),
        compiler_params=pltpu.CompilerParams(vmem_limit_bytes=vmem * MIB),
        cost_estimate=pl.CostEstimate(
            flops=1, bytes_accessed=int(micros * HBM_BYTES_PER_MICRO), transcendentals=0
        ),
    )(*args)


def dot(left, right):
    return jnp.dot(left, right, preferred_element_type=f32)


def dot_nt(left, right):
    return lax.dot_general(left, right, (((1,), (1,)), ((), ())), preferred_element_type=f32)


def dot_tn(left, right):
    return lax.dot_general(left, right, (((0,), (0,)), ((), ())), preferred_element_type=f32)


def at(index, size):
    return pl.ds(pl.multiple_of(index * size, size), size)


def doc_bounds(lengths, query):
    start = jnp.zeros_like(query)
    stop = jnp.zeros_like(query)
    end = jnp.int32(0)
    for j in range(lengths.shape[1]):
        begin, end = end, end + lengths[0, j]
        inside = (query >= begin) & (query < end)
        start = jnp.where(inside, begin, start)
        stop = jnp.where(inside, end, stop)
    return start, stop


def same_doc(lengths, shape, offset):
    query = lax.broadcasted_iota(jnp.int32, (1, shape[1]), 1) + offset
    start, stop = doc_bounds(lengths, query)
    position = lax.broadcasted_iota(jnp.int32, shape, 0)
    return (position >= start) & (position < stop)


def attn_forward(
    lengths, gate, bias, x0, x1, x2, x3, w_qkv,
    x_all, qkv, logsum, mine, send_core, send_x, x_block, gated,
):
    me = lax.axis_index("hid")
    feats, toks = x0.shape
    block = toks // 4
    for k, piece in enumerate((x0, x1, x2, x3)):
        x_all[at(me ^ k, feats), :] = piece[...]
    x_block[...] = x_all[:, at(me, block)]
    cols = jnp.transpose(bias[...])
    for c in range(3):
        rows = dot(w_qkv[c], x_all[...])
        if c != 1:
            rows = rows + cols[:feats, c // 2 : c // 2 + 1]
        rows = rows.astype(bf16)
        if c == 0:
            rows = rows * jnp.asarray(HEAD_DIM ** (-0.5), bf16)
        qkv[c] = rows
    heads = feats // HEAD_DIM
    for head in range(heads):
        span = slice(head * HEAD_DIM, (head + 1) * HEAD_DIM)
        keys = jnp.transpose(qkv[1, span, :])
        values = qkv[2, span, :]
        for j in range(4):
            chunk = slice(j * block, (j + 1) * block)
            scores = dot(keys, qkv[0, span, chunk])
            scores = jnp.where(
                same_doc(lengths, scores.shape, j * block), scores, masked_score
            )
            peak = jnp.max(scores, axis=0, keepdims=True)
            expo = jnp.exp(scores - peak)
            total = jnp.sum(expo, axis=0, keepdims=True)
            probs = (expo * (1.0 / total)).astype(bf16)
            logsum[head : head + 1, chunk] = peak + jnp.log(total)
            gated[span, chunk] = (dot(values, probs) * gate[head]).astype(bf16)
    mine[...] = gated[:, at(me, block)]
    send_x[:feats, :] = gated[:, at(me ^ 2, block)]
    send_x[feats:, :] = gated[:, at(me ^ 3, block)]
    send_core[...] = gated[:, at(me ^ 1, block)]


def attn_backward(
    lengths, qkv, logsum, u0, u1, u2, u3, grads, head_sums, bias_sums, up
):
    me = lax.axis_index("hid")
    feats, block = u0.shape
    for k, piece in enumerate((u0, u1, u2.at[:feats, :], u3.at[feats:, :])):
        up[:, at(me ^ k, block)] = piece[...]
    heads = feats // HEAD_DIM
    head_sums[...] = jnp.zeros_like(head_sums)
    for head in range(heads):
        span = slice(head * HEAD_DIM, (head + 1) * HEAD_DIM)
        queries, keys_t, values_t = (qkv[c, span, :] for c in range(3))
        keys = jnp.transpose(keys_t)
        values = jnp.transpose(values_t)
        upstream = up[span, :]
        grad_k = jnp.zeros((HEAD_DIM, 4 * block), f32)
        grad_v = jnp.zeros((HEAD_DIM, 4 * block), f32)
        inner_sum = jnp.zeros((1, block), f32)
        for j in range(4):
            chunk = slice(j * block, (j + 1) * block)
            scores = dot(keys, queries[:, chunk])
            scores = jnp.where(
                same_doc(lengths, scores.shape, j * block), scores, masked_score
            )
            probs = jnp.exp(scores - logsum[head : head + 1, chunk])
            grad_p = dot(values, upstream[:, chunk])
            weighted = probs * grad_p
            inner = jnp.sum(weighted, axis=0, keepdims=True)
            inner_sum = inner_sum + inner
            grad_s = (weighted - probs * inner).astype(bf16)
            grad_v = grad_v + dot_nt(upstream[:, chunk], probs.astype(bf16))
            grad_k = grad_k + dot_nt(queries[:, chunk], grad_s)
            grads[span, chunk] = (dot(keys_t, grad_s) * HEAD_DIM ** (-0.5)).astype(bf16)
        for c, grad in ((1, grad_k), (2, grad_v)):
            rows = slice(c * feats + head * HEAD_DIM, c * feats + (head + 1) * HEAD_DIM)
            grads[rows, :] = grad.astype(bf16)
        head_sums[head : head + 1, :] = inner_sum
    ones = jnp.ones((8, 4 * block), bf16)
    bias_sums[...] = dot_nt(ones, grads[...])


def qk_weight_grad(grads, x_all, keep, send, full):
    parity = lax.axis_index("rows") & 1
    n = keep.shape[0]
    full[...] = dot_nt(grads[: 2 * n, :], x_all[...])
    send[...] = full[at(parity ^ 1, n), :].astype(bf16)
    keep[...] = full[at(parity, n), :]


def vo_weight_grad(grads, x_all, wo_mine, wo_core, wo_far, keep, send, full):
    parity = (lax.axis_index("rows") >> 1) & 1
    n = keep.shape[0]
    full[:n, :] = dot_nt(grads[2 * n :, :], x_all[...])
    full[n:, :] = wo_mine[...] + wo_core[:n, :].astype(f32) + wo_far[...].astype(f32)
    send[...] = full[at(parity ^ 1, n), :].astype(bf16)
    keep[...] = full[at(parity, n), :]


def add_low(mine, other, total):
    total[...] = (mine[...].astype(f32) + other[...].astype(f32)).astype(total.dtype)


def add_second(mine, other, total):
    n = mine.shape[0]
    total[...] = (mine[...] + other[n:, :].astype(f32)).astype(total.dtype)


def add_two(mine, first, second, total):
    n = mine.shape[0]
    both = first[:n, :].astype(f32) + second[...].astype(f32)
    total[...] = (mine[...] + both).astype(total.dtype)


def qkv_input_grad(grads, w_qkv, dres, mine, mine_x, send, full):
    me = lax.axis_index("hid")
    feats = mine.shape[0]
    block = dres.shape[0]
    total = None
    for c in range(3):
        part = dot(jnp.transpose(w_qkv[c]), grads[c * feats : (c + 1) * feats, :])
        total = part if total is None else total + part
    full[...] = total
    full[:, at(me, block)] += jnp.transpose(dres[...])
    send[:feats, :] = full[at(me ^ 1, feats), :].astype(bf16)
    send[feats:, :] = full[at(me ^ 3, feats), :].astype(bf16)
    mine[...] = full[at(me, feats), :]
    mine_x[...] = full[at(me ^ 2, feats), :]


def place_rows(own, from_core, from_x, far, whole):
    me, n = lax.axis_index("hid"), own.shape[0]
    for k, piece in enumerate((own, from_core, from_x, far)):
        whole[at(me ^ k, n), :] = piece[...]


def row_norm(values):
    mean = jnp.mean(values, axis=1, keepdims=True)
    centered = values - mean
    spread = jnp.mean(centered * centered, axis=1, keepdims=True)
    inv = lax.rsqrt(spread + norm_eps)
    return centered * inv, inv


def attn_out(
    branch, g0, g1, g2, g3, x_block, vecs, wo,
    normed, normed_low, hat, inv_out, pre, gated_rows, heads_all,
):
    me = lax.axis_index("hid")
    feats = g0.shape[0]
    for k, piece in enumerate((g0, g1, g2.at[:feats, :], g3.at[feats:, :])):
        heads_all[at(me ^ k, feats), :] = piece[...]
    gated = jnp.transpose(heads_all[...])
    gated_rows[...] = gated
    tokens = jnp.transpose(x_block[...].astype(f32))
    attn = dot_nt(gated, wo[...]) + vecs[0:1, :]
    pre[...] = attn
    resid = tokens + branch[0] * attn * vecs[3:4, :]
    x_hat, inv = row_norm(resid)
    value = x_hat * vecs[1:2, :] + vecs[2:3, :]
    normed_low[...] = value.astype(bf16)
    normed[...] = value
    hat[...] = x_hat
    inv_out[...] = jnp.broadcast_to(inv, inv_out.shape)


def attn_out_back(
    branch, part, recv, dres2, hat, inv, pre, vecs, wo,
    dres, grad_attn, sums, up_mine, up_core, up_x, ups,
):
    me = lax.axis_index("hid")
    feats = up_mine.shape[0]
    grad = part[...] + recv[...].astype(f32) + dres2[...]
    x_hat = hat[...]
    scaled = grad * vecs[1:2, :]
    mean_plain = jnp.mean(scaled, axis=1, keepdims=True)
    mean_along = jnp.mean(scaled * x_hat, axis=1, keepdims=True)
    grad_resid = inv[:, 0:1] * (scaled - mean_plain - x_hat * mean_along)
    dres[...] = grad_resid
    low = (grad_resid * (branch[0] * vecs[3:4, :])).astype(bf16)
    grad_attn[...] = low
    grad_gated = dot(low, wo[...])
    upstream = (grad_gated * vecs[7:8, :]).astype(bf16)
    ups[...] = jnp.transpose(upstream)
    up_mine[...] = ups[at(me, feats), :]
    up_core[...] = ups[at(me ^ 1, feats), :]
    up_x[:feats, :] = ups[at(me ^ 2, feats), :]
    up_x[feats:, :] = ups[at(me ^ 3, feats), :]
    sums[0:1, :] = jnp.sum(grad * x_hat, axis=0, keepdims=True)
    sums[1:2, :] = jnp.sum(grad, axis=0, keepdims=True)
    sums[2:3, :] = jnp.sum(low.astype(f32), axis=0, keepdims=True)
    sums[3:4, :] = jnp.sum(grad_resid * pre[...], axis=0, keepdims=True)


def out_weight_grad(grad_attn, gated_rows, mine, mine_x, send, full):
    me = lax.axis_index("hid")
    feats = mine.shape[0]
    full[...] = dot_tn(grad_attn[...], gated_rows[...])
    send[:feats, :] = full[at(me ^ 1, feats), :].astype(bf16)
    send[feats:, :] = full[at(me ^ 3, feats), :].astype(bf16)
    mine[...] = full[at(me, feats), :]
    mine_x[...] = full[at(me ^ 2, feats), :]


def cut_inputs(w_back, cotangent, back_half, cot_send):
    other, parity = 1 - lax.axis_index("hid") // 2, lax.axis_index("rows") & 1
    back_half[...] = w_back[:, at(2 * other + parity, back_half.shape[1])]
    cot_send[...] = cotangent[:, at(other, cot_send.shape[1])]


def place_units(wi_own, wi_core, own, core_rows, xa, xb, fa, fb, wi, wb):
    me, core, chip, parity = lax.axis_index("hid"), lax.axis_index("hid") & 1, lax.axis_index("hid") // 2, lax.axis_index("rows") & 1
    n, half = xa.shape
    units = wi_own.shape[1]
    wi[:, at(core, units)] = wi_own[...]
    wi[:, at(core ^ 1, units)] = wi_core[...]
    wb[at(me, n), :] = own[:, at(chip, 2 * half)]
    wb[at(me ^ 1, n), :] = core_rows[:, at(chip, 2 * half)]
    for owner, first, second in ((me ^ 2, xa, xb), (me ^ 3, fa, fb)):
        wb[at(owner, n), at(parity, half)] = first[...]
        wb[at(owner, n), at(parity ^ 1, half)] = second[...]


def ffn_forward(
    rows, unit_rows, wi, wb, act, slope, inter_mine, inter_core, part, inter,
):
    ffn_units(rows, unit_rows, wi, act, slope, inter_mine, inter_core, inter)
    part[...] = dot_nt(inter[...], wb[...])


def ffn_forward_far(
    rows, unit_rows, wi, wb, core_mine, act, slope, inter_mine, part, core_pair, inter,
):
    n = rows.shape[0]
    core_pair[:n, :] = core_mine[...]
    ffn_units(rows, unit_rows, wi, act, slope, inter_mine, core_pair.at[n:, :], inter)
    part[...] = dot_nt(inter[...], wb[...]).astype(part.dtype)


def ffn_units(rows, unit_rows, wi, act, slope, inter_mine, inter_core, inter):
    core = lax.axis_index("hid") & 1
    units = wi.shape[1]
    step = 256
    for j in range(units // step):
        cut = slice(j * step, (j + 1) * step)
        u = dot(rows[...], wi[:, cut]) + unit_rows[0:1, cut]
        cdf = 0.5 * (1.0 + lax.erf(u * 0.7071067811865476))
        value = u * cdf
        act[:, cut] = value
        slope[:, cut] = cdf + u * (jnp.exp(-0.5 * u * u) * 0.3989422804014327)
        inter[:, cut] = (value * unit_rows[1:2, cut]).astype(bf16)
    inter_mine[...] = inter[:, at(core, units // 2)]
    inter_core[...] = inter[:, at(core ^ 1, units // 2)]


def ffn_backward(
    rows, act, slope, unit_rows, wi, wb, gpre_mine, gpre_core, part, sums, gpre,
):
    ffn_units_back(rows, act, slope, unit_rows, wb, gpre_mine, gpre_core, sums, gpre)
    part[...] = dot_nt(gpre[...], wi[...])


def ffn_backward_far(
    rows, act, slope, unit_rows, wi, wb, core_mine,
    gpre_mine, part, sums, core_pair, gpre,
):
    n = rows.shape[0]
    core_pair[:n, :] = core_mine[...]
    ffn_units_back(
        rows, act, slope, unit_rows, wb, gpre_mine, core_pair.at[n:, :], sums, gpre
    )
    part[...] = dot_nt(gpre[...], wi[...]).astype(part.dtype)


def ffn_units_back(rows, act, slope, unit_rows, wb, gpre_mine, gpre_core, sums, gpre):
    core = lax.axis_index("hid") & 1
    units = wb.shape[1]
    step = 256
    for j in range(units // step):
        cut = slice(j * step, (j + 1) * step)
        ginter = dot(rows[...], wb[:, cut])
        sums[:, cut] = jnp.broadcast_to(
            jnp.sum(ginter * act[:, cut], axis=0, keepdims=True), (8, step)
        )
        gpre[:, cut] = (ginter * unit_rows[1:2, cut] * slope[:, cut]).astype(bf16)
    gpre_mine[...] = gpre[:, at(core, units // 2)]
    gpre_core[...] = gpre[:, at(core ^ 1, units // 2)]


def ffn_weight_grads(
    n0, n1, n2, n3, e0, e1, e_core, p0, p1, p_core, f0, f1, f2, f3,
    in_keep, in_send, back_keep, back_send, bias_sums, left, right, full,
):
    parity = lax.axis_index("rows") & 1
    in_parity = (lax.axis_index("rows") >> 1) & 1
    half = full.shape[0] // 2

    def fill(target, pieces):
        start = 0
        for piece in pieces:
            target[start : start + piece.shape[0], :] = piece[...]
            start += piece.shape[0]

    fill(left, (f0, f1, f2, f3))
    fill(right, (e0, e1, e_core))
    full[...] = dot_tn(left[...], right[...])
    owners, subs = 4, 8
    rows = full.shape[0] // (owners * subs)
    for q in range(subs // 2):
        for h in range(owners):
            to = slice((q * owners + h) * rows, (q * owners + h + 1) * rows)
            base = h * subs * rows + q * rows
            kept = base + parity * (subs // 2) * rows
            sent = base + (parity ^ 1) * (subs // 2) * rows
            back_keep[to, :] = full[pl.ds(pl.multiple_of(kept, rows), rows), :]
            left_rows = full[pl.ds(pl.multiple_of(sent, rows), rows), :]
            back_send[to, :] = left_rows.astype(bf16)
    fill(left, (n0, n1, n2, n3))
    fill(right, (p0, p1, p_core))
    full[...] = dot_tn(left[...], right[...])
    in_send[...] = full[at(in_parity ^ 1, half), :].astype(bf16)
    in_keep[...] = full[at(in_parity, half), :]
    bias_sums[...] = jnp.broadcast_to(
        jnp.sum(right[...].astype(f32), axis=0, keepdims=True), bias_sums.shape
    )


def second_norm(
    branch, part, recv, normed, cot0, cot1, cot2, cot3, vecs,
    grad_low, dres, sums, out_mine, out_x, out_send, cots, outs,
):
    me = lax.axis_index("hid")
    feats = cot0.shape[0]
    block = part.shape[0]
    core = me & 1
    cots[at(me, feats), :] = cot0[:, at(me, block)]
    cots[at(me ^ 1, feats), :] = cot1[:, at(me, block)]
    cots[at(me ^ 2, feats), :] = cot2[:, at(core, block)]
    cots[at(me ^ 3, feats), :] = cot3[:, at(core, block)]
    ffn = part[...] + recv[...].astype(f32) + vecs[4:5, :]
    resid = normed[...] + branch[1] * ffn * vecs[3:4, :]
    x_hat, inv = row_norm(resid)
    grad_out = jnp.transpose(cots[...].astype(f32))
    scaled = grad_out * vecs[5:6, :]
    mean_plain = jnp.mean(scaled, axis=1, keepdims=True)
    mean_along = jnp.mean(scaled * x_hat, axis=1, keepdims=True)
    grad_resid = inv * (scaled - mean_plain - x_hat * mean_along)
    low = (grad_resid * (branch[1] * vecs[3:4, :])).astype(bf16)
    grad_low[...] = low
    dres[...] = grad_resid
    value = x_hat * vecs[5:6, :] + vecs[6:7, :]
    outs[...] = jnp.transpose(value).astype(bf16)
    out_mine[...] = outs[at(me, feats), :]
    out_x[...] = outs[at(me ^ 2, feats), :]
    out_send[:feats, :] = outs[at(me ^ 1, feats), :]
    out_send[feats:, :] = outs[at(me ^ 3, feats), :]
    sums[0:1, :] = jnp.sum(grad_out * x_hat, axis=0, keepdims=True)
    sums[1:2, :] = jnp.sum(grad_out, axis=0, keepdims=True)
    sums[2:3, :] = jnp.sum(low.astype(f32), axis=0, keepdims=True)
    sums[3:4, :] = jnp.sum(grad_resid * ffn, axis=0, keepdims=True)


def pack_vectors(
    head_gate, b_out, gain, bias, hidden_gate, hidden_mask, b_back, b_in, inter_gate, b_qv,
    packed, qv,
):
    feats = b_out.shape[0]

    def row(ref):
        return ref[...].reshape(1, ref.shape[0])

    packed[...] = jnp.zeros_like(packed)
    packed[0:1, :feats] = row(b_out)
    packed[1:2, :feats] = gain[0:1, :]
    packed[2:3, :feats] = bias[0:1, :]
    packed[3:4, :feats] = row(hidden_gate) * row(hidden_mask).astype(f32)
    packed[4:5, :feats] = row(b_back)
    packed[5:6, :feats] = gain[1:2, :]
    packed[6:7, :feats] = bias[1:2, :]
    packed[7:8, :feats] = jnp.concatenate(
        [jnp.full((1, HEAD_DIM), head_gate[i], f32) for i in range(feats // HEAD_DIM)], axis=1
    )
    packed[0:1, 256:] = row(b_in)
    packed[1:2, 256:] = row(inter_gate)
    qv[...] = jnp.zeros_like(qv)
    qv[0:2, :feats] = b_qv[...]


def place_vectors(p0, p1, p2, p3, vecs, unit_rows, cols):
    me, core = lax.axis_index("hid"), lax.axis_index("hid") & 1
    feats = cols.shape[0] // 4
    units = p0.shape[1] - 256
    for k, piece in enumerate((p0, p1, p2, p3)):
        cols[at(me ^ k, feats), :] = jnp.transpose(piece[:, :256])[:feats, :]
    vecs[...] = jnp.transpose(cols[...])
    unit_rows[:, at(core, units)] = p0[0:2, 256:]
    unit_rows[:, at(core ^ 1, units)] = p1[0:2, 256:]


def pack_sums(sums1, sums2, ig0, ig1, bin_sum, keep, send):
    core = lax.axis_index("hid") & 1
    units = keep.shape[1]
    keep[0:4, :] = sums1[...]
    keep[4:8, :] = sums2[...]
    keep[8:, :] = jnp.zeros((keep.shape[0] - 8, units), f32)
    send[...] = keep[...]
    keep[8:9, :] = ig0[0:1, at(core, units)] + ig1[0:1, at(core, units)]
    send[8:9, :] = ig0[0:1, at(core ^ 1, units)] + ig1[0:1, at(core ^ 1, units)]
    keep[9:10, :] = bin_sum[0:1, :]


def add_rows(mine, other, total):
    total[...] = mine[...] + other[...]


def last_sums(shared, other, head_sums, bias_sums, total):
    total[...] = shared[...]
    total[0:8, :] += other[0:8, :]
    width = bias_sums.shape[1]
    total[10:11, :width] = bias_sums[0:1, :]
    heads = jnp.sum(jnp.transpose(head_sums[...]), axis=0, keepdims=True)
    total[11:12, :8] = heads


def vector_outputs(
    branch, head_gate, vec, vecs, hidden_mask,
    g_qv, g_bout, g_bin, g_bback, g_gain, g_bias, g_head, g_inter, g_branch, g_hidden, cols,
):
    me = lax.axis_index("hid")
    feats = g_bout.shape[0]
    cols[...] = jnp.transpose(vec[0:8, :])
    own = jnp.transpose(cols[at(me, feats), :])
    g_gain[0:1, :] = own[0:1, :]
    g_gain[1:2, :] = own[4:5, :]
    g_bias[0:1, :] = own[1:2, :]
    g_bias[1:2, :] = own[5:6, :]
    g_bout[...] = own[2, :]
    g_bback[...] = own[6, :]
    mask = hidden_mask[...].astype(f32)
    g_hidden[...] = (branch[0] * own[3, :] + branch[1] * own[7, :]) * mask
    g_inter[...] = vec[8, :]
    g_bin[...] = vec[9, :]
    g_qv[0:1, :] = vec[10:11, :feats]
    rolled = vec[10:11, 2 * feats : 3 * feats]
    g_qv[1:2, :] = rolled
    lane = lax.broadcasted_iota(jnp.int32, (1, 128), 1)
    gates = jnp.ones((1, 128), f32)
    for i in range(feats // HEAD_DIM):
        gates = jnp.where(lane == i, head_gate[i], gates)
    g_head[...] = (vec[11:12, :128] / gates)[0, : feats // HEAD_DIM]
    part0 = jnp.sum(vec[3:4, :] * vecs[3:4, :], axis=1, keepdims=True)
    part1 = jnp.sum(vec[7:8, :] * vecs[3:4, :], axis=1, keepdims=True)
    both = jnp.where(lane == 0, part0, part1)
    g_branch[...] = both[0, :2]


def row_step(k):
    def body(keep, recv, keep_next, send_next):
        bit = (lax.axis_index("rows") >> k) & 1
        n = keep_next.shape[0]
        sent = keep[at(bit ^ 1, n), :] + recv[at(bit ^ 1, n), :].astype(f32)
        send_next[...] = sent.astype(bf16)
        keep_next[...] = keep[at(bit, n), :] + recv[at(bit, n), :].astype(f32)

    return body


def along(block, bit):
    return swap(block, "rows", 1 << bit)


def reduce_step(keep, recv, bit, gate):
    n, width = keep.shape
    return local_kernel(
        row_step(bit),
        "row_step",
        (after(keep, *gate), recv),
        "VV",
        [sds((n // 2, width), f32), sds((n // 2, width), bf16)],
    )


def far_rows_sum(chunk):
    count = lax.axis_size("rows")
    if count == 8:
        return chunk
    groups = [[i + 8 * j for j in range(count // 8)] for i in range(8)]
    return lax.psum(chunk, "rows", axis_index_groups=groups)


def last_step(keep, recv, gate):
    kind = bf16 if lax.axis_size("rows") == 8 else f32
    (chunk,) = local_kernel(
        add_low, "last_step", (after(keep, *gate), recv), "VV", [sds(keep.shape, kind)]
    )
    return far_rows_sum(chunk).astype(bf16)


def in_order(k):
    def body(mine, other, both):
        bit = (lax.axis_index("rows") >> k) & 1
        n = mine.shape[0]
        both[at(bit, n), :] = mine[...]
        both[at(bit ^ 1, n), :] = other[...]

    return body


def join_step(mine, other, bit, gate):
    n, width = mine.shape
    (both,) = local_kernel(
        in_order(bit), "in_order", (after(mine, *gate), other), "VV", [sds((2 * n, width), bf16)]
    )
    return both


def in_gradient(k):
    def body(mine, other, grad):
        bit = (lax.axis_index("rows") >> k) & 1
        n = mine.shape[0]
        grad[at(bit, n), :] = mine[...].astype(f32)
        grad[at(bit ^ 1, n), :] = other[...].astype(f32)

    return body


def back_gradient(mine, other, grad, wide):
    bit = lax.axis_index("rows") & 1
    units = mine.shape[1]
    rows = grad.shape[0] // 8
    for side, half in ((bit, mine), (bit ^ 1, other)):
        wide[...] = half[...].astype(f32)
        for q in range(4):
            for owner in range(4):
                block = wide[(q * 4 + owner) * rows : (q * 4 + owner + 1) * rows, :]
                to = pl.ds(pl.multiple_of((side * 4 + q) * rows, rows), rows)
                grad[to, owner * units : (owner + 1) * units] = block


def attn_gradients(qk_mine, qk_other, vo_mine, vo_other, grad_qkv, grad_out):
    y, z = lax.axis_index("rows") & 1, (lax.axis_index("rows") >> 1) & 1
    n = qk_mine.shape[0]
    grad_qkv[at(y, n), :] = qk_mine[...].astype(f32)
    grad_qkv[at(y ^ 1, n), :] = qk_other[...].astype(f32)
    mine, other = vo_mine[...].astype(f32), vo_other[...].astype(f32)
    grad_qkv[2 * n :, :] = jnp.where(z == 0, mine, other)
    grad_out[...] = jnp.where(z == 0, other, mine)


def split_owners(keep, recv, mine, mine_x, send, full):
    me = lax.axis_index("hid")
    n = mine.shape[0]
    full[...] = keep[...] + recv[...].astype(f32)
    mine[...] = full[at(me, n), :]
    mine_x[...] = full[at(me ^ 2, n), :]
    send[:n, :] = full[at(me ^ 1, n), :]
    send[n:, :] = full[at(me ^ 3, n), :]


def join_owners(mine, from_core, from_x, chunk, full):
    me, n = lax.axis_index("hid"), mine.shape[0]
    full[at(me, n), :] = mine[...]
    full[at(me ^ 1, n), :] = from_core[:n, :]
    full[at(me ^ 2, n), :] = from_x[:n, :]
    full[at(me ^ 3, n), :] = from_x[n:, :]
    chunk[...] = full[...].astype(chunk.dtype)


def second_half(mine, recv, both):
    n = mine.shape[0]
    both[:n, :] = mine[...]
    both[n:, :] = recv[n:, :]


def place_blocks(mine, from_core, from_x, whole):
    me = lax.axis_index("hid")
    rows, n = mine.shape
    whole[:, at(me, n)] = mine[...]
    whole[:, at(me ^ 1, n)] = from_core[:rows, :]
    whole[:, at(me ^ 2, n)] = from_x[:rows, :]
    whole[:, at(me ^ 3, n)] = from_x[rows:, :]


def shards(
    tokens, w_qkv, b_qv, w_out, b_out, w_in, b_in, w_back, b_back, norm_gain, norm_bias,
    head_gate, inter_gate, branch_gate, hidden_gate, hidden_mask, doc_lengths, cotangent,
):
    feats, toks = tokens.shape
    width = 4 * feats
    units = w_in.shape[1]
    block = toks // 4
    tokens_x = swap(tokens, "hid", 2)
    tokens_core = swap(tokens, "hid", 1)
    out_x = swap(w_out, "hid", 2)
    back_half, cot_send = local_kernel(
        cut_inputs,
        "cut_inputs",
        (w_back, cotangent),
        "VV",
        [sds((feats, units), bf16), sds((feats, 2 * block), bf16)],
    )
    back_xa = swap(back_half, "hid", 2)
    wi_core = swap(w_in, "hid", 1)
    wo_core = swap(w_out, "hid", 1)
    cot_core = swap(cotangent, "hid", 1)
    back_core = swap(w_back, "hid", 1)
    packed, qv_rows = local_kernel(
        pack_vectors,
        "pack_vectors",
        (
            head_gate, b_out, norm_gain, norm_bias, hidden_gate, hidden_mask, b_back,
            b_in, inter_gate, b_qv,
        ),
        "S" + "V" * 9,
        [sds((8, 256 + units), f32), sds((8, 256), f32)],
    )
    tokens_far = swap(
        after(tokens_x, tokens_core, wi_core, wo_core, cot_core, back_core, back_half), "hid", 1
    )

    head_block = sds((feats, block), bf16)
    two_blocks = sds((2 * feats, block), bf16)
    x_all, qkv, logsum, g0, g_core, g_x, x_block = local_kernel(
        attn_forward,
        "attn_forward",
        (
            doc_lengths, head_gate, qv_rows,
            tokens, tokens_core, tokens_x, tokens_far, w_qkv,
        ),
        "SSVVVVVV",
        [
            sds((width, toks), bf16),
            sds((3, feats, toks), bf16),
            sds((8, toks), f32),
            head_block,
            head_block,
            two_blocks,
            sds((width, block), bf16),
        ],
        [pltpu.VMEM((feats, toks), bf16)],
        micros=5.4,
    )
    g2 = swap(g_x, "hid", 2)
    g1 = swap(g_core, "hid", 1)
    packed_x = swap(after(packed, g0), "hid", 2)
    packed_core = swap(after(packed, g0), "hid", 1)
    g3 = swap(after(g2, packed_x, packed_core), "hid", 1)
    packed_far = swap(packed_x, "hid", 1)
    out_far = swap(after(out_x, g0), "hid", 1)
    back_xb = swap(after(back_xa, g1), "rows", 1)
    back_fa = swap(after(back_xa, g1), "hid", 1)
    cot_x = swap(after(cot_send, g1), "hid", 2)
    (wo,) = local_kernel(
        place_rows,
        "place_rows",
        (w_out, wo_core, out_x, out_far),
        "VVVV",
        [sds((width, width), bf16)],
    )
    vecs, unit_rows = local_kernel(
        place_vectors,
        "place_vectors",
        (after(packed, cot_x), packed_core, packed_x, packed_far),
        "VVVV",
        [sds((8, width), f32), sds((2, 2 * units), f32)],
        [pltpu.VMEM((width, 8), f32)],
    )

    normed, normed_low, hat, inv, attn_pre, gated_rows = local_kernel(
        attn_out,
        "attn_out",
        (branch_gate, g0, g1, g2, g3, x_block, vecs, wo),
        "SVVVVVVV",
        [
            sds((block, width), f32),
            sds((block, width), bf16),
            sds((block, width), f32),
            sds((block, 128), f32),
            sds((block, width), f32),
            sds((block, width), bf16),
        ],
        [pltpu.VMEM((width, block), bf16)],
        micros=1.3,
    )

    normed_x = swap(normed_low, "hid", 2)
    n2 = swap(normed_low, "hid", 1)
    back_fb = swap(after(back_xb, normed_x), "hid", 1)
    wi, wb = local_kernel(
        place_units,
        "place_units",
        (w_in, wi_core, w_back, back_core, back_xa, back_xb, back_fa, back_fb),
        "V" * 8,
        [sds((width, 2 * units), bf16), sds((width, 2 * units), bf16)],
        micros=0.85,
    )

    act_block = sds((block, 2 * units), f32)
    half_block = sds((block, units), bf16)
    pair_block = sds((2 * block, units), bf16)
    rows_block = sds((block, width), bf16)
    ffn_scratch = [pltpu.VMEM((block, 2 * units), bf16)]
    act, slope, e0, inter_core, ffn_part = local_kernel(
        ffn_forward,
        "ffn_forward",
        (normed_low, unit_rows, wi, wb),
        "VVVV",
        [act_block, act_block, half_block, half_block, sds((block, width), f32)],
        ffn_scratch,
        micros=1.85,
    )
    act_x, slope_x, e1, ffn_send, e_pair = local_kernel(
        ffn_forward_far,
        "ffn_forward_far",
        (normed_x, unit_rows, wi, wb, inter_core),
        "VVVVV",
        [act_block, act_block, half_block, rows_block, pair_block],
        ffn_scratch,
        micros=1.85,
    )
    ffn_recv = swap(ffn_send, "hid", 2)
    cot_far = swap(after(cot_x, normed_x), "hid", 1)
    n3 = swap(after(normed_x, ffn_send), "hid", 1)
    e_core = swap(after(e_pair, ffn_send), "hid", 1)

    out_block = sds((feats, block), bf16)
    gffn, dres2, sums2, res_mine, res_x, res_send = local_kernel(
        second_norm,
        "second_norm",
        (
            branch_gate, after(ffn_part, n3, e_core), ffn_recv, normed,
            cotangent, cot_core, cot_x, cot_far, vecs,
        ),
        "S" + "V" * 8,
        [
            sds((block, width), bf16),
            sds((block, width), f32),
            sds((4, width), f32),
            out_block,
            out_block,
            sds((2 * feats, block), bf16),
        ],
        [pltpu.VMEM((width, block), bf16), pltpu.VMEM((width, block), bf16)],
        micros=1.2,
    )

    gffn_x = swap(gffn, "hid", 2)
    f2 = swap(gffn, "hid", 1)
    sums_block = sds((8, 2 * units), f32)
    p0, gpre_core, gn_part, ig_sum = local_kernel(
        ffn_backward,
        "ffn_backward",
        (gffn, act, slope, unit_rows, wi, wb),
        "VVVVVV",
        [half_block, half_block, sds((block, width), f32), sums_block],
        ffn_scratch,
        micros=1.85,
    )
    p1, gn_send, ig_sum_x, p_pair = local_kernel(
        ffn_backward_far,
        "ffn_backward_far",
        (after(gffn_x, f2), act_x, slope_x, unit_rows, wi, wb, gpre_core),
        "VVVVVVV",
        [half_block, rows_block, sums_block, pair_block],
        ffn_scratch,
        micros=1.85,
    )
    gn_recv = swap(gn_send, "hid", 2)
    f3 = swap(after(gffn_x, gn_send), "hid", 1)
    p_core = swap(p_pair, "hid", 1)
    in_keep, in_send, back_keep, back_send, bin_sum = local_kernel(
        ffn_weight_grads,
        "ffn_weight_grads",
        (
            normed_low, normed_x, n2, n3, e0, e1, e_core,
            p0, p1, p_core, gffn, gffn_x, f2, f3,
        ),
        "V" * 14,
        [
            sds((width // 2, units), f32),
            sds((width // 2, units), bf16),
            sds((width // 2, units), f32),
            sds((width // 2, units), bf16),
            sds((8, units), f32),
        ],
        [
            pltpu.VMEM((toks, width), bf16),
            pltpu.VMEM((toks, units), bf16),
            pltpu.VMEM((width, units), f32),
        ],
        micros=2.5,
    )

    back_recv = swap(after(back_send, gn_recv), "rows", 1)
    in_recv = swap(after(in_send, gn_recv), "rows", 2)

    dres1, gattn, sums1, u0, up_core, up_x = local_kernel(
        attn_out_back,
        "attn_out_back",
        (
            branch_gate, after(gn_part, in_send), gn_recv, dres2, hat, inv, attn_pre,
            vecs, wo,
        ),
        "S" + "V" * 8,
        [
            sds((block, width), f32),
            sds((block, width), bf16),
            sds((4, width), f32),
            head_block,
            head_block,
            two_blocks,
        ],
        [pltpu.VMEM((width, block), bf16)],
        micros=1.3,
    )
    u2 = swap(up_x, "hid", 2)
    u1 = swap(up_core, "hid", 1)
    u3 = swap(u2, "hid", 1)

    weight_block = sds((feats, width), f32)
    low_block = sds((feats, width), bf16)
    wo_mine, wo_keep, wo_send = local_kernel(
        out_weight_grad,
        "out_weight_grad",
        (gattn, gated_rows),
        "VV",
        [weight_block, weight_block, sds((2 * feats, width), bf16)],
        [pltpu.VMEM((width, width), f32)],
        micros=1.2,
    )
    wo_grad_core = swap(after(wo_send, u1), "hid", 1)

    grads, head_sums, bias_sums = local_kernel(
        attn_backward,
        "attn_backward",
        (doc_lengths, qkv, logsum, u0, u1, u2, u3),
        "SVVVVVV",
        [
            sds((3 * feats, toks), bf16),
            sds((8, block), f32),
            sds((8, 3 * feats), f32),
        ],
        [pltpu.VMEM((feats, toks), bf16)],
        micros=5.0,
    )
    (wo_low,) = local_kernel(add_second, "wo_low", (wo_keep, wo_grad_core), "VV", [low_block])
    wo_far = swap(after(wo_low, u3), "hid", 2)

    qk_keep, qk_send = local_kernel(
        qk_weight_grad,
        "qk_weight_grad",
        (grads, x_all),
        "VV",
        [weight_block, low_block],
        [pltpu.VMEM((2 * feats, width), f32)],
        micros=1.2,
    )
    vo_keep, vo_send = local_kernel(
        vo_weight_grad,
        "vo_weight_grad",
        (after(grads, qk_send), x_all, wo_mine, wo_grad_core, wo_far),
        "VVVVV",
        [weight_block, low_block],
        [pltpu.VMEM((2 * feats, width), f32)],
        micros=1.1,
    )
    gx_block = sds((feats, toks), f32)
    gx_low = sds((feats, toks), bf16)
    gx_mine, gx_x, gx_send = local_kernel(
        qkv_input_grad,
        "qkv_input_grad",
        (after(grads, vo_send), w_qkv, dres1),
        "VVV",
        [gx_block, gx_block, sds((2 * feats, toks), bf16)],
        [pltpu.VMEM((width, toks), f32)],
        micros=1.5,
    )
    gx_core = swap(gx_send, "hid", 1)
    (gx_send,) = local_kernel(add_second, "gx_send", (gx_x, gx_core), "VV", [gx_low])
    gx_far = swap(gx_send, "hid", 2)
    res_core = swap(after(res_send, grads), "hid", 1)
    (res_send,) = local_kernel(
        second_half, "out_join", (res_x, res_core), "VV", [sds((2 * feats, block), bf16)]
    )
    rows16 = sds((16, units), f32)
    vec_keep, vec_send = local_kernel(
        pack_sums,
        "pack_sums",
        (sums1, sums2, ig_sum, ig_sum_x, bin_sum),
        "VVVVV",
        [rows16, rows16],
    )

    def vector_step(vec, hop, body=add_rows, *more):
        (vec,) = local_kernel(body, body.__name__, (vec, hop) + more, "VV" + "V" * len(more), [rows16])
        return vec

    y, z, far = 0, 1, 2
    qk_recv = along(qk_send, y)
    vo_recv = along(vo_send, z)
    turn = (qk_send, vo_send)
    back_keep, back_send = reduce_step(back_keep, back_recv, z, turn)
    in_keep, in_send = reduce_step(in_keep, in_recv, y, turn)
    back_recv, in_recv = along(back_send, z), along(in_send, y)
    vec_hop = swap(after(vec_send, vo_send), "hid", 1)
    turn = (back_send, in_send, gx_core, vec_hop)
    qk_keep, qk_send = reduce_step(qk_keep, qk_recv, z, turn)
    vo_keep, vo_send = reduce_step(vo_keep, vo_recv, y, turn)
    qk_recv, vo_recv = along(qk_send, z), along(vo_send, y)
    vec = vector_step(vec_keep, vec_hop)
    vec_hop = swap(vec, "hid", 2)
    turn = (qk_send, vo_send, gx_far, vec_hop)
    back_keep, back_send = reduce_step(back_keep, back_recv, far, turn)
    in_keep, in_send = reduce_step(in_keep, in_recv, far, turn)
    back_recv, in_recv = along(back_send, far), along(in_send, far)
    vec = vector_step(vec, vec_hop, last_sums, head_sums, bias_sums)
    vec_hop = along(vec, y)
    res_far = swap(after(res_send, gx_far), "hid", 2)
    turn = (back_send, in_send, res_far)
    qk_keep, qk_send = reduce_step(qk_keep, qk_recv, far, turn)
    vo_keep, vo_send = reduce_step(vo_keep, vo_recv, far, turn)
    qk_recv, vo_recv = along(qk_send, far), along(vo_send, far)

    turn = (qk_send, vo_send, vec_hop)
    sub = sds((back_keep.shape[0] // 4, units), f32)
    two = sds((back_keep.shape[0] // 2, units), f32)
    back_keep = after(back_keep, *turn)
    if lax.axis_size("rows") > 8:
        back_keep = far_rows_sum(back_keep + back_recv.astype(f32))
        back_recv = jnp.zeros_like(back_recv)
    b_mine, b_x, b_send = local_kernel(
        split_owners,
        "split_owners",
        (back_keep, back_recv),
        "VV",
        [sub, sub, two],
        [pltpu.VMEM(back_keep.shape, f32)],
    )
    b_core = swap(b_send, "hid", 1)
    in_mine = last_step(in_keep, in_recv, turn)
    in_other = along(in_mine, far)
    (b_send,) = local_kernel(second_half, "back_join", (b_x, b_core), "VV", [two])
    b_far = swap(b_send, "hid", 2)
    vec = vector_step(vec, vec_hop)
    vec_hop = along(vec, z)
    turn = (in_mine, b_send)
    qk_mine = last_step(qk_keep, qk_recv, turn)
    vo_mine = last_step(vo_keep, vo_recv, turn)
    qk_other, vo_other = along(qk_mine, far), along(vo_mine, far)
    turn = (qk_mine, vo_mine, vec_hop)
    (back_mine,) = local_kernel(
        join_owners,
        "join_owners",
        (after(b_mine, *turn), b_core, b_far),
        "VVV",
        [sds(back_keep.shape, bf16)],
        [pltpu.VMEM(back_keep.shape, f32)],
    )
    back_other = along(back_mine, far)
    in_mine = join_step(in_mine, in_other, far, turn)
    in_other = along(in_mine, y)
    vec = vector_step(vec, vec_hop)
    vec_hop = along(vec, far)
    turn = (back_mine, in_mine)
    qk_mine = join_step(qk_mine, qk_other, far, turn)
    vo_mine = join_step(vo_mine, vo_other, far, turn)
    qk_other, vo_other = along(qk_mine, z), along(vo_mine, y)
    turn = (qk_mine, vo_mine, vec_hop)
    back_mine = join_step(back_mine, back_other, far, turn)
    back_other = along(back_mine, z)
    in_mine = join_step(in_mine, in_other, y, turn)
    in_other = along(in_mine, z)
    vec = vector_step(vec, vec_hop)
    turn = (back_mine, in_mine)
    qk_mine = join_step(qk_mine, qk_other, z, turn)
    vo_mine = join_step(vo_mine, vo_other, y, turn)
    qk_other, vo_other = along(qk_mine, y), along(vo_mine, z)
    turn = (qk_mine, vo_mine)
    back_mine = join_step(back_mine, back_other, z, turn)
    back_other = along(back_mine, y)
    (grad_w_in,) = local_kernel(
        in_gradient(z),
        "in_gradient",
        (in_mine, in_other),
        "VV",
        [sds((width, units), f32)],
        micros=2.1,
    )
    grad_qkv, grad_w_out = local_kernel(
        attn_gradients,
        "attn_gradients",
        (qk_mine, qk_other, vo_mine, vo_other),
        "VVVV",
        [sds((3 * feats, width), f32), weight_block],
        micros=2.1,
    )
    (grad_w_back,) = local_kernel(
        back_gradient,
        "back_gradient",
        (back_mine, back_other),
        "VV",
        [sds((feats, 4 * units), f32)],
        [pltpu.VMEM(back_mine.shape, f32)],
        micros=2.1,
    )
    grad_w_qkv = grad_qkv.reshape(3, feats, width)

    (grad_tokens,) = local_kernel(add_two, "grad_tokens", (gx_mine, gx_core, gx_far), "VVV", [gx_low])
    (output,) = local_kernel(
        place_blocks,
        "place_blocks",
        (res_mine, res_core, res_far),
        "VVV",
        [sds((feats, toks), bf16)],
        micros=1.2,
    )

    vec = far_rows_sum(vec)
    (
        grad_b_qv, grad_b_out, grad_b_in, grad_b_back, grad_norm_gain, grad_norm_bias,
        grad_head_gate, grad_inter_gate, grad_branch_gate, grad_hidden_gate,
    ) = local_kernel(
        vector_outputs,
        "vector_outputs",
        (branch_gate, head_gate, vec, vecs, hidden_mask),
        "SSVVV",
        [
            sds((2, feats), f32),
            sds((feats,), f32),
            sds((units,), f32),
            sds((feats,), f32),
            sds((2, feats), f32),
            sds((2, feats), f32),
            sds((feats // HEAD_DIM,), f32),
            sds((units,), f32),
            sds((2,), f32),
            sds((feats,), f32),
        ],
        [pltpu.VMEM((width, 8), f32)],
        micros=1.4,
    )
    return (
        output,
        grad_tokens,
        grad_w_qkv,
        grad_b_qv,
        grad_w_out,
        grad_b_out,
        grad_w_in,
        grad_b_in,
        grad_w_back,
        grad_b_back,
        grad_norm_gain,
        grad_norm_bias,
        grad_head_gate,
        grad_inter_gate,
        grad_branch_gate,
        grad_hidden_gate,
    )


def solution(mesh):
    return jax.shard_map(
        shards,
        mesh=mesh,
        in_specs=(
            P("hid", "rows"),
            P(None, "hid", None),
            P(None, "hid"),
            P("hid", None),
            P("hid"),
            P(None, "hid"),
            P("hid"),
            P("hid", None),
            P("hid"),
            P(None, "hid"),
            P(None, "hid"),
            P("hid"),
            P("hid"),
            P(),
            P("hid"),
            P("hid"),
            P("rows", None),
            P("hid", "rows"),
        ),
        out_specs=(
            P("hid", "rows"),
            P("hid", "rows"),
            P(None, "hid", None),
            P(None, "hid"),
            P("hid", None),
            P("hid"),
            P(None, "hid"),
            P("hid"),
            P("hid", None),
            P("hid"),
            P(None, "hid"),
            P(None, "hid"),
            P("hid"),
            P("hid"),
            P(),
            P("hid"),
        ),
        check_vma=False,
    )
```

time: 253 us -> 195 us (0.77)
  local copies, waits for them, and re-layouts: 40.9 us -> 2.96 us
  other arithmetic: 22.1 us -> 0 us
    unnamed x161 -> x40, local copies, waits for them, and re-layouts: 24.3 us -> 2.96 us
    slice x14 -> x0, local copies, waits for them, and re-layouts: 4.97 us -> none  [the longest x1 1.34 us: shards(): norm_bias[1]]
    select_n x15 -> x0, other arithmetic: 4.66 us -> none  [ordered(): jnp.where(bit == 0, jnp.concatenate([mine, other], axis=axis), jnp.concat...]
    add x16 -> x0, other arithmetic: 4.3 us -> none  [the longest x1 1.95 us: shards(): hidden = (branch_gate[0] * own[3] + branch_gate[1] * own[7]) * kept]
    another operation x6 -> x0, other arithmetic: 3.72 us -> none  [the longest x1 1.88 us: shards(): jnp.stack([jnp.sum(vec[3] * cols), jnp.sum(vec[7] * cols)])]
    convert_element_type x11 -> x0, other arithmetic: 3.28 us -> none  [the longest x2 1.85 us: gather_rows(): return chunk.astype(f32)]
    dynamic_slice x5 -> x0, local copies, waits for them, and re-layouts: 3.26 us -> none  [the longest x1 2.44 us: shards(): wb_chip = lax.dynamic_slice_in_dim(w_back, chip * 2 * units, 2 * units, 1)]
    concatenate x1 -> x0, local copies, waits for them, and re-layouts: 2.65 us -> none  [shards(): jnp.concatenate([shared, ig_mine, bin_sum[:1], jnp.pad(bias_sums[:1], ((0...]
  transfers between devices with their start and end apart: 60 -> 71, of which waited for: 28 -> 39; matrix products, arithmetic and copies ran while one was open for 12% -> 0% of each run, Pallas kernels for 9% -> 13%
where the time goes in v2:
time: 195 us; the launch traced here: 194 us
  waiting for transfers between devices  102 us (52%)
  starting transfers between devices  53.4 us (27%)
  Pallas kernels  34.4 us (18%)
  local copies, waits for them, and re-layouts  2.96 us (2%)
    ppermute x71, waiting for transfers between devices, swap(): lax.ppermute(block, axis, [(i, i ^ bit) for i in range(lax.axis_size(axis...  102 us
    ppermute x71, starting transfers between devices, swap(): lax.ppermute(block, axis, [(i, i ^ bit) for i in range(lax.axis_size(axis...  53.4 us
    pallas_call x56, Pallas kernels, local_kernel(): pl.pallas_call(body, name=name, out_shape=outs, in_specs=[SPECS[k] for k...  34.4 us
  transfers between devices with their start and end apart: 71, of which 39 were waited for; matrix products, arithmetic and copies ran while one was open for 0% of the time, Pallas kernels for 13%

profile of v2, /device:TPU:0, one launch (start us, length us, event | category | flops | bytes accessed | tf_op | source)
XLA Modules:
  0.0 194.4 jit_solution(11697978902191692380)
XLA Ops:
  1.8 2.9 %collective-permute-start.1 = (bf16[192,512]{1,0:T(8,128)(2,1)}, bf16[192,512]{1,0:T(8,128)(2,1)S(1)}, u32[]{:S(2)}, u32[]{:S(2)}) collective-permute-start(bf16[192,512]{1,0:T(8,128)(2,1)} %x0.1), channel_id=1, source_target_pairs={{0,2},{1,3},{2,0},{3,1},{4,6},{5,7},{6,4},{7,5},{8,10},{9,11},{10,... | collective-permute-start | bytes 589832 | tf_op jit(solution)/shard_map/ppermute | solution.py:23
  4.7 1.1 collective-permute-done.x1
  6.2 3.8 %collective-permute-done.1.x2 = bf16[192,512]{1,0:T(8,128)(2,1)S(1)} collective-permute-done((bf16[192,512]{1,0:T(8,128)(2,1)}, bf16[192,512]{1,0:T(8,128)(2,1)S(1)}, u32[]{:S(2)}, u32[]{:S(2)}) %collective-permute-start.1) | collective-permute-done | bytes 196640 | tf_op jit(solution)/shard_map/ppermute | solution.py:23
  10.0 1.7 collective-permute-start.14
  11.8 1.3 copy-done
  15.7 5.4 %attn_forward.1 = (bf16[768,512]{1,0:T(8,128)(2,1)S(1)}, bf16[3,192,512]{2,1,0:T(8,128)(2,1)S(1)}, f32[8,512]{1,0:T(8,128)S(1)}, bf16[192,128]{1,0:T(8,128)(2,1)...) custom-call(s32[1,4]{1,0:T(1,128)S(1)} %copy-done.13, ...), custom_call_target="tpu_custom_call" | custom-call | flops 1 | bytes 19926000 | tf_op jit(solution)/shard_map/attn_forward/pallas_call | solution.py:35
  21.3 1.4 collective-permute-start.8
  24.1 3.8 %collective-permute-done.9.p2 = f32[8,1024]{1,0:T(8,128)S(1)} collective-permute-done((f32[8,1024]{1,0:T(8,128)S(1)}, f32[8,1024]{1,0:T(8,128)S(1)}, u32[]{:S(2)}, u32[]{:S(2)}) %collective-permute-start.9) | collective-permute-done | bytes 32800 | tf_op jit(solution)/shard_map/ppermute | solution.py:23
  27.8 1.4 collective-permute-start.12
  29.3 1.6 collective-permute-start.17
  31.0 1.4 collective-permute-done.12.cot2
  33.4 1.3 attn_out.1
  34.8 1.5 collective-permute-start.19
  36.3 2.4 %collective-permute-done.17.xb = bf16[192,768]{1,0:T(8,128)(2,1)S(1)} collective-permute-done((bf16[192,768]{1,0:T(8,128)(2,1)S(1)}, bf16[192,768]{1,0:T(8,128)(2,1)S(1)}, u32[]{:S(2)}, u32[]{:S(2)}) %collective-permute-start.17) | collective-permute-done | bytes 294944 | tf_op jit(solution)/shard_map/ppermute | solution.py:23
  38.7 2.7 %collective-permute-done.19.rows.n1 = bf16[128,768]{1,0:T(8,128)(2,1)S(1)} collective-permute-done((bf16[128,768]{1,0:T(8,128)(2,1)S(1)}, bf16[128,768]{1,0:T(8,128)(2,1)S(1)}, u32[]{:S(2)}, u32[]{:S(2)}) %collective-permute-start.19) | collective-permute-done | bytes 196640 | tf_op jit(solution)/shard_map/ppermute | solution.py:23
  41.5 1.6 collective-permute-done.20.fb
  43.4 1.3 ffn_forward.1
  44.7 1.3 ffn_forward_far.1
  48.5 5.1 %collective-permute-done.23.recv = bf16[128,768]{1,0:T(8,128)(2,1)S(1)} collective-permute-done((bf16[128,768]{1,0:T(8,128)(2,1)S(1)}, bf16[128,768]{1,0:T(8,128)(2,1)S(1)}, u32[]{:S(2)}, u32[]{:S(2)}) %collective-permute-start.23) | collective-permute-done | bytes 196640 | tf_op jit(solution)/shard_map/ppermute | solution.py:23
  53.6 1.2 second_norm.1
  55.4 1.3 ffn_backward.1
  56.8 4.3 %collective-permute-done.26.rows.f1 = bf16[128,768]{1,0:T(8,128)(2,1)S(1)} collective-permute-done((bf16[128,768]{1,0:T(8,128)(2,1)S(1)}, bf16[128,768]{1,0:T(8,128)(2,1)S(1)}, u32[]{:S(2)}, u32[]{:S(2)}) %collective-permute-start.26) | collective-permute-done | bytes 196640 | tf_op jit(solution)/shard_map/ppermute | solution.py:23
  61.1 1.3 ffn_backward_far.1
  64.7 2.1 %ffn_weight_grads.1 = (f32[384,768]{1,0:T(8,128)S(1)}, bf16[384,768]{1,0:T(8,128)(2,1)S(1)}, f32[384,768]{1,0:T(8,128)S(1)}, bf16[384,768]{1,0:T(8,128)(2,1)S(1)}, f32[8,768]{1,0:T(8,128)S(1)}) custom-call(bf16[128,768]{1,0:T(8,128)(2,1)S(1)} %get-tuple-element.178.rows.n0, bf16[128,768]{1,0:T(8,128)(2,1)S(1)} %collective-permute-done.19.rows.n1, ...), custom_call_target="tpu_custom_call" | custom-call | flops 1 | bytes 9225000 | tf_op jit(solution)/shard_map/ffn_weight_grads/pallas_call | solution.py:35
  66.8 3.5 %collective-permute-done.30.recv = bf16[128,768]{1,0:T(8,128)(2,1)S(1)} collective-permute-done((bf16[128,768]{1,0:T(8,128)(2,1)S(1)}, bf16[128,768]{1,0:T(8,128)(2,1)S(1)}, u32[]{:S(2)}, u32[]{:S(2)}) %collective-permute-start.30) | collective-permute-done | bytes 196640 | tf_op jit(solution)/shard_map/ppermute | solution.py:23
  70.3 1.2 attn_out_back.1
  73.5 4.5 %collective-permute-done.32.u2 = bf16[384,128]{1,0:T(8,128)(2,1)S(1)} collective-permute-done((bf16[384,128]{1,0:T(8,128)(2,1)S(1)}, bf16[384,128]{1,0:T(8,128)(2,1)S(1)}, u32[]{:S(2)}, u32[]{:S(2)}) %collective-permute-start.32) | collective-permute-done | bytes 98336 | tf_op jit(solution)/shard_map/ppermute | solution.py:23
  78.1 1.2 collective-permute-done.33.u3
  79.9 1.5 collective-permute-start.40
  81.4 1.6 collective-permute-start.41
  82.9 4.9 %attn_backward.1 = (bf16[576,512]{1,0:T(8,128)(2,1)S(1)}, f32[8,128]{1,0:T(8,128)S(1)}, f32[8,576]{1,0:T(8,128)S(1)}) custom-call(s32[1,4]{1,0:T(1,128)S(1)} %copy-done.13, bf16[3,192,512]{2,1,0:T(8,128)(2,1)S(1)} %get-tuple-element.195.qkv, f32[8,512]{1,0:T(8,128)S(1)} %get-tuple-element.196.logsum, bf16[192,128]{1,0:T(8,128)(2,1)S(1)} %get-tuple-element.218.u0, ...), custom_call_target="tpu_custom_call" | custom-call | flops 1 | bytes 18450000 | tf_op jit(solution)/shard_map/attn_backward/pallas_call | solution.py:35
  90.8 1.4 collective-permute-start.44
  92.2 3.9 %collective-permute-done.40.recv = bf16[384,768]{1,0:T(8,128)(2,1)S(1)} collective-permute-done((bf16[384,768]{1,0:T(8,128)(2,1)S(1)}, bf16[384,768]{1,0:T(8,128)(2,1)S(1)}, u32[]{:S(2)}, u32[]{:S(2)}) %collective-permute-start.40) | collective-permute-done | bytes 589856 | tf_op jit(solution)/shard_map/ppermute | solution.py:23
  96.2 1.6 collective-permute-start.46
  97.9 1.5 collective-permute-start.38
  100.2 2.2 %collective-permute-done.43.recv = bf16[192,768]{1,0:T(8,128)(2,1)S(1)} collective-permute-done((bf16[192,768]{1,0:T(8,128)(2,1)S(1)}, bf16[192,768]{1,0:T(8,128)(2,1)S(1)}, u32[]{:S(2)}, u32[]{:S(2)}) %collective-permute-start.43) | collective-permute-done | bytes 294944 | tf_op jit(solution)/shard_map/ppermute | solution.py:23
  102.4 1.2 collective-permute-done.42.other
  103.9 1.4 collective-permute-start.45
  105.4 2.6 %collective-permute-done.45.other = f32[16,768]{1,0:T(8,128)S(1)} collective-permute-done((f32[16,768]{1,0:T(8,128)S(1)}, f32[16,768]{1,0:T(8,128)S(1)}, u32[]{:S(2)}, u32[]{:S(2)}) %collective-permute-start.45) | collective-permute-done | bytes 49184 | tf_op jit(solution)/shard_map/ppermute | solution.py:23
  108.0 1.4 collective-permute-start.49
  109.5 1.6 collective-permute-start.48
  111.2 2.6 %collective-permute-start.52 = (bf16[96,768]{1,0:T(8,128)(2,1)S(1)}, bf16[96,768]{1,0:T(8,128)(2,1)S(1)}, u32[]{:S(2)}, u32[]{:S(2)}) collective-permute-start(bf16[96,768]{1,0:T(8,128)(2,1)S(1)} %get-tuple-element.267), channel_id=1, source_target_pairs={{0,16},{4,20},{8,24},{12,28},{16,0},{20,4},{24,8},{28,12},{1,17},{... | collective-permute-start | bytes 442376 | tf_op jit(solution)/shard_map/ppermute | solution.py:23
  114.7 1.5 collective-permute-start.50
  116.2 2.4 %collective-permute-done.39.from_x = bf16[384,128]{1,0:T(8,128)(2,1)S(1)} collective-permute-done((bf16[384,128]{1,0:T(8,128)(2,1)S(1)}, bf16[384,128]{1,0:T(8,128)(2,1)S(1)}, u32[]{:S(2)}, u32[]{:S(2)}) %collective-permute-start.39) | collective-permute-done | bytes 98336 | tf_op jit(solution)/shard_map/ppermute | solution.py:23
  118.8 1.3 collective-permute-done.52.recv
  122.2 1.6 collective-permute-start.55
  123.8 1.3 collective-permute-start.54
  125.1 1.8 collective-permute-start.56
  126.9 6.7 %collective-permute-done.51.other = bf16[96,768]{1,0:T(8,128)(2,1)S(1)} collective-permute-done((bf16[96,768]{1,0:T(8,128)(2,1)S(1)}, bf16[96,768]{1,0:T(8,128)(2,1)S(1)}, u32[]{:S(2)}, u32[]{:S(2)}) %collective-permute-start.51) | collective-permute-done | bytes 147488 | tf_op jit(solution)/shard_map/ppermute | solution.py:23
  133.7 1.5 collective-permute-done.55.other
  135.2 12.1 %collective-permute-done.54.other = bf16[48,768]{1,0:T(8,128)(2,1)S(1)} collective-permute-done((bf16[48,768]{1,0:T(8,128)(2,1)S(1)}, bf16[48,768]{1,0:T(8,128)(2,1)S(1)}, u32[]{:S(2)}, u32[]{:S(2)}) %collective-permute-start.54) | collective-permute-done | bytes 73760 | tf_op jit(solution)/shard_map/ppermute | solution.py:23
  147.4 2.9 %collective-permute-start.60 = (bf16[48,768]{1,0:T(8,128)(2,1)S(1)}, bf16[48,768]{1,0:T(8,128)(2,1)S(1)}, u32[]{:S(2)}, u32[]{:S(2)}) collective-permute-start(bf16[48,768]{1,0:T(8,128)(2,1)S(1)} %last_step.5.mine), channel_id=1, source_target_pairs={{0,16},{4,20},{8,24},{12,28},{16,0},{20,4},{24,8},{28,12},{1,17},{... | collective-permute-start | bytes 221192 | tf_op jit(solution)/shard_map/ppermute | solution.py:23
  150.4 2.8 %collective-permute-start.61 = (f32[16,768]{1,0:T(8,128)S(1)}, f32[16,768]{1,0:T(8,128)S(1)}, u32[]{:S(2)}, u32[]{:S(2)}) collective-permute-start(f32[16,768]{1,0:T(8,128)S(1)} %add_rows.6.mine), channel_id=1, source_target_pairs={{0,16},{4,20},{8,24},{12,28},{16,0},{20,4},{24,8},{28,12},{1,17},{... | collective-permute-start | bytes 147464 | tf_op jit(solution)/shard_map/ppermute | solution.py:23
  153.9 2.7 %collective-permute-done.60.other = bf16[48,768]{1,0:T(8,128)(2,1)S(1)} collective-permute-done((bf16[48,768]{1,0:T(8,128)(2,1)S(1)}, bf16[48,768]{1,0:T(8,128)(2,1)S(1)}, u32[]{:S(2)}, u32[]{:S(2)}) %collective-permute-start.60) | collective-permute-done | bytes 73760 | tf_op jit(solution)/shard_map/ppermute | solution.py:23
  156.6 1.2 collective-permute-done.59.other
  159.0 1.9 %collective-permute-start.64 = (bf16[96,768]{1,0:T(8,128)(2,1)S(1)}, bf16[96,768]{1,0:T(8,128)(2,1)S(1)}, u32[]{:S(2)}, u32[]{:S(2)}) collective-permute-start(bf16[96,768]{1,0:T(8,128)(2,1)S(1)} %in_order.9.mine), channel_id=1, source_target_pairs={{0,8},{4,12},{8,0},{12,4},{16,24},{20,28},{24,16},{28,20},{1,9},{5... | collective-permute-start | bytes 442376 | tf_op jit(solution)/shard_map/ppermute | solution.py:23
  162.2 2.2 %collective-permute-done.66.other = bf16[96,768]{1,0:T(8,128)(2,1)S(1)} collective-permute-done((bf16[96,768]{1,0:T(8,128)(2,1)S(1)}, bf16[96,768]{1,0:T(8,128)(2,1)S(1)}, u32[]{:S(2)}, u32[]{:S(2)}) %collective-permute-start.66) | collective-permute-done | bytes 147488 | tf_op jit(solution)/shard_map/ppermute | solution.py:23
  164.4 7.1 %collective-permute-done.64.other = bf16[96,768]{1,0:T(8,128)(2,1)S(1)} collective-permute-done((bf16[96,768]{1,0:T(8,128)(2,1)S(1)}, bf16[96,768]{1,0:T(8,128)(2,1)S(1)}, u32[]{:S(2)}, u32[]{:S(2)}) %collective-permute-start.64) | collective-permute-done | bytes 147488 | tf_op jit(solution)/shard_map/ppermute | solution.py:23
  172.2 1.5 collective-permute-start.65
  173.8 1.4 vector_outputs.1
  176.6 12.0 %collective-permute-done.67.vo_other = bf16[192,768]{1,0:T(8,128)(2,1)S(1)} collective-permute-done((bf16[192,768]{1,0:T(8,128)(2,1)S(1)}, bf16[192,768]{1,0:T(8,128)(2,1)S(1)}, u32[]{:S(2)}, u32[]{:S(2)}) %collective-permute-start.67) | collective-permute-done | bytes 294944 | tf_op jit(solution)/shard_map/ppermute | solution.py:23
  189.7 1.6 attn_gradients.1
  191.2 1.6 in_gradient.1
  192.8 1.6 back_gradient.1
  (174 shorter events, 29.2 us)
Async XLA Ops:
  0.6 13.5 %collective-permute-start.2 = (bf16[768,768]{1,0:T(8,128)(2,1)}, bf16[768,768]{1,0:T(8,128)(2,1)S(1)}, u32[]{:S(2)}, u32[]{:S(2)}) collective-permute-start(bf16[768,768]{1,0:T(8,128)(2,1)} %wi_own.1), channel_id=1, source_target_pairs={{0,1},{1,0},{2,3},{3,2},{4,5},{5,4},{6,7},{7,6},{8,9},{9,8},{10,11... | collective-permute-start | bytes 3538952 | tf_op jit(solution)/shard_map/ppermute | solution.py:23
  1.2 13.0 %collective-permute-start.5 = (bf16[192,3072]{1,0:T(8,128)(2,1)}, bf16[192,3072]{1,0:T(8,128)(2,1)S(1)}, u32[]{:S(2)}, u32[]{:S(2)}) collective-permute-start(bf16[192,3072]{1,0:T(8,128)(2,1)} %own.3), channel_id=1, source_target_pairs={{0,1},{1,0},{2,3},{3,2},{4,5},{5,4},{6,7},{7,6},{8,9},{9,8},{10,11... | collective-permute-start | bytes 3538952 | tf_op jit(solution)/shard_map/ppermute | solution.py:23
  1.2 4.6 %collective-permute-start = (bf16[192,512]{1,0:T(8,128)(2,1)}, bf16[192,512]{1,0:T(8,128)(2,1)S(1)}, u32[]{:S(2)}, u32[]{:S(2)}) collective-permute-start(bf16[192,512]{1,0:T(8,128)(2,1)} %x0.1), channel_id=1, source_target_pairs={{0,1},{1,0},{2,3},{3,2},{4,5},{5,4},{6,7},{7,6},{8,9},{9,8},{10,11... | collective-permute-start | bytes 589832 | tf_op jit(solution)/shard_map/ppermute | solution.py:23
  1.7 12.5 %collective-permute-start.3 = (bf16[192,768]{1,0:T(8,128)(2,1)}, bf16[192,768]{1,0:T(8,128)(2,1)S(1)}, u32[]{:S(2)}, u32[]{:S(2)}) collective-permute-start(bf16[192,768]{1,0:T(8,128)(2,1)} %own.2), channel_id=1, source_target_pairs={{0,1},{1,0},{2,3},{3,2},{4,5},{5,4},{6,7},{7,6},{8,9},{9,8},{10,11... | collective-permute-start | bytes 884744 | tf_op jit(solution)/shard_map/ppermute | solution.py:23
  1.8 8.3 %collective-permute-start.1 = (bf16[192,512]{1,0:T(8,128)(2,1)}, bf16[192,512]{1,0:T(8,128)(2,1)S(1)}, u32[]{:S(2)}, u32[]{:S(2)}) collective-permute-start(bf16[192,512]{1,0:T(8,128)(2,1)} %x0.1), channel_id=1, source_target_pairs={{0,2},{1,3},{2,0},{3,1},{4,6},{5,7},{6,4},{7,5},{8,10},{9,11},{10,... | collective-permute-start | bytes 589832 | tf_op jit(solution)/shard_map/ppermute | solution.py:23
  5.8 8.3 %collective-permute-start.4 = (bf16[192,512]{1,0:T(8,128)(2,1)}, bf16[192,512]{1,0:T(8,128)(2,1)S(1)}, u32[]{:S(2)}, u32[]{:S(2)}) collective-permute-start(bf16[192,512]{1,0:T(8,128)(2,1)} %cot0.1), channel_id=1, source_target_pairs={{0,1},{1,0},{2,3},{3,2},{4,5},{5,4},{6,7},{7,6},{8,9},{9,8},{10,11... | collective-permute-start | bytes 589832 | tf_op jit(solution)/shard_map/ppermute | solution.py:23
  10.0 11.1 %collective-permute-start.14 = (bf16[192,768]{1,0:T(8,128)(2,1)}, bf16[192,768]{1,0:T(8,128)(2,1)S(1)}, u32[]{:S(2)}, u32[]{:S(2)}) collective-permute-start(bf16[192,768]{1,0:T(8,128)(2,1)} %own.2), channel_id=1, source_target_pairs={{0,2},{1,3},{2,0},{3,1},{4,6},{5,7},{6,4},{7,5},{8,10},{9,11},{10,... | collective-permute-start | bytes 884744 | tf_op jit(solution)/shard_map/ppermute | solution.py:23
  14.3 15.0 %collective-permute-start.16 = (bf16[192,768]{1,0:T(8,128)(2,1)S(1)}, bf16[192,768]{1,0:T(8,128)(2,1)S(1)}, u32[]{:S(2)}, u32[]{:S(2)}) collective-permute-start(bf16[192,768]{1,0:T(8,128)(2,1)S(1)} %get-tuple-element.164), channel_id=1, source_target_pairs={{0,2},{1,3},{2,0},{3,1},{4,6},{5,7},{6,4},{7,5},{8,10},{9,11},{10,... | collective-permute-start | bytes 884744 | tf_op jit(solution)/shard_map/ppermute | solution.py:23
  21.1 11.7 %collective-permute-start.15 = (bf16[192,768]{1,0:T(8,128)(2,1)S(1)}, bf16[192,768]{1,0:T(8,128)(2,1)S(1)}, u32[]{:S(2)}, u32[]{:S(2)}) collective-permute-start(bf16[192,768]{1,0:T(8,128)(2,1)S(1)} %collective-permute-done.14.from_x), channel_id=1, source_target_pairs={{0,1},{1,0},{2,3},{3,2},{4,5},{5,4},{6,7},{7,6},{8,9},{9,8},{10,11... | collective-permute-start | bytes 884744 | tf_op jit(solution)/shard_map/ppermute | solution.py:23
  21.3 8.0 %collective-permute-start.8 = (bf16[384,128]{1,0:T(8,128)(2,1)S(1)}, bf16[384,128]{1,0:T(8,128)(2,1)S(1)}, u32[]{:S(2)}, u32[]{:S(2)}) collective-permute-start(bf16[384,128]{1,0:T(8,128)(2,1)S(1)} %get-tuple-element.168), channel_id=1, source_target_pairs={{0,2},{1,3},{2,0},{3,1},{4,6},{5,7},{6,4},{7,5},{8,10},{9,11},{10,... | collective-permute-start | bytes 294920 | tf_op jit(solution)/shard_map/ppermute | solution.py:23
  22.7 5.1 %collective-permute-start.9 = (f32[8,1024]{1,0:T(8,128)S(1)}, f32[8,1024]{1,0:T(8,128)S(1)}, u32[]{:S(2)}, u32[]{:S(2)}) collective-permute-start(f32[8,1024]{1,0:T(8,128)S(1)} %get-tuple-element.175.p0), channel_id=1, source_target_pairs={{0,2},{1,3},{2,0},{3,1},{4,6},{5,7},{6,4},{7,5},{8,10},{9,11},{10,... | collective-permute-start | bytes 98312 | tf_op jit(solution)/shard_map/ppermute | solution.py:23
  23.9 5.4 %collective-permute-start.10 = (f32[8,1024]{1,0:T(8,128)S(1)}, f32[8,1024]{1,0:T(8,128)S(1)}, u32[]{:S(2)}, u32[]{:S(2)}) collective-permute-start(f32[8,1024]{1,0:T(8,128)S(1)} %get-tuple-element.175.p0), channel_id=1, source_target_pairs={{0,1},{1,0},{2,3},{3,2},{4,5},{5,4},{6,7},{7,6},{8,9},{9,8},{10,11... | collective-permute-start | bytes 98312 | tf_op jit(solution)/shard_map/ppermute | solution.py:23
  27.8 4.6 %collective-permute-start.12 = (bf16[192,256]{1,0:T(8,128)(2,1)S(1)}, bf16[192,256]{1,0:T(8,128)(2,1)S(1)}, u32[]{:S(2)}, u32[]{:S(2)}) collective-permute-start(bf16[192,256]{1,0:T(8,128)(2,1)S(1)} %get-tuple-element.174), channel_id=1, source_target_pairs={{0,2},{1,3},{2,0},{3,1},{4,6},{5,7},{6,4},{7,5},{8,10},{9,11},{10,... | collective-permute-start | bytes 294920 | tf_op jit(solution)/shard_map/ppermute | solution.py:23
  29.3 3.6 %collective-permute-start.11 = (bf16[384,128]{1,0:T(8,128)(2,1)S(1)}, bf16[384,128]{1,0:T(8,128)(2,1)S(1)}, u32[]{:S(2)}, u32[]{:S(2)}) collective-permute-start(bf16[384,128]{1,0:T(8,128)(2,1)S(1)} %collective-permute-done.8.g2), channel_id=1, source_target_pairs={{0,1},{1,0},{2,3},{3,2},{4,5},{5,4},{6,7},{7,6},{8,9},{9,8},{10,11... | collective-permute-start | bytes 294920 | tf_op jit(solution)/shard_map/ppermute | solution.py:23
  29.3 9.4 %collective-permute-start.17 = (bf16[192,768]{1,0:T(8,128)(2,1)S(1)}, bf16[192,768]{1,0:T(8,128)(2,1)S(1)}, u32[]{:S(2)}, u32[]{:S(2)}) collective-permute-start(bf16[192,768]{1,0:T(8,128)(2,1)S(1)} %collective-permute-done.16.xa), channel_id=1, source_target_pairs={{0,4},{4,0},{8,12},{12,8},{16,20},{20,16},{24,28},{28,24},{1,5},{5... | collective-permute-start | bytes 884744 | tf_op jit(solution)/shard_map/ppermute | solution.py:23
  30.9 1.6 collective-permute-start.13
  34.8 6.7 %collective-permute-start.19 = (bf16[128,768]{1,0:T(8,128)(2,1)S(1)}, bf16[128,768]{1,0:T(8,128)(2,1)S(1)}, u32[]{:S(2)}, u32[]{:S(2)}) collective-permute-start(bf16[128,768]{1,0:T(8,128)(2,1)S(1)} %get-tuple-element.178.rows.n0), channel_id=1, source_target_pairs={{0,2},{1,3},{2,0},{3,1},{4,6},{5,7},{6,4},{7,5},{8,10},{9,11},{10,... | collective-permute-start | bytes 589832 | tf_op jit(solution)/shard_map/ppermute | solution.py:23
  36.3 5.2 %collective-permute-start.18 = (bf16[192,768]{1,0:T(8,128)(2,1)S(1)}, bf16[192,768]{1,0:T(8,128)(2,1)S(1)}, u32[]{:S(2)}, u32[]{:S(2)}) collective-permute-start(bf16[192,768]{1,0:T(8,128)(2,1)S(1)} %collective-permute-done.16.xa), channel_id=1, source_target_pairs={{0,1},{1,0},{2,3},{3,2},{4,5},{5,4},{6,7},{7,6},{8,9},{9,8},{10,11... | collective-permute-start | bytes 884744 | tf_op jit(solution)/shard_map/ppermute | solution.py:23
  41.4 1.6 collective-permute-start.20
  46.0 2.1 %collective-permute-start.22 = (bf16[256,768]{1,0:T(8,128)(2,1)S(1)}, bf16[256,768]{1,0:T(8,128)(2,1)S(1)}, u32[]{:S(2)}, u32[]{:S(2)}) collective-permute-start(bf16[256,768]{1,0:T(8,128)(2,1)S(1)} %get-tuple-element.189), channel_id=1, source_target_pairs={{0,1},{1,0},{2,3},{3,2},{4,5},{5,4},{6,7},{7,6},{8,9},{9,8},{10,11... | collective-permute-start | bytes 1179656 | tf_op jit(solution)/shard_map/ppermute | solution.py:23
  46.3 1.8 collective-permute-start.21
  46.6 7.0 %collective-permute-start.23 = (bf16[128,768]{1,0:T(8,128)(2,1)S(1)}, bf16[128,768]{1,0:T(8,128)(2,1)S(1)}, u32[]{:S(2)}, u32[]{:S(2)}) collective-permute-start(bf16[128,768]{1,0:T(8,128)(2,1)S(1)} %get-tuple-element.186), channel_id=1, source_target_pairs={{0,2},{1,3},{2,0},{3,1},{4,6},{5,7},{6,4},{7,5},{8,10},{9,11},{10,... | collective-permute-start | bytes 589832 | tf_op jit(solution)/shard_map/ppermute | solution.py:23
  54.8 6.2 %collective-permute-start.26 = (bf16[128,768]{1,0:T(8,128)(2,1)S(1)}, bf16[128,768]{1,0:T(8,128)(2,1)S(1)}, u32[]{:S(2)}, u32[]{:S(2)}) collective-permute-start(bf16[128,768]{1,0:T(8,128)(2,1)S(1)} %get-tuple-element.197.rows.f0), channel_id=1, source_target_pairs={{0,2},{1,3},{2,0},{3,1},{4,6},{5,7},{6,4},{7,5},{8,10},{9,11},{10,... | collective-permute-start | bytes 589832 | tf_op jit(solution)/shard_map/ppermute | solution.py:23
  55.4 5.6 %collective-permute-start.27 = (bf16[128,768]{1,0:T(8,128)(2,1)S(1)}, bf16[128,768]{1,0:T(8,128)(2,1)S(1)}, u32[]{:S(2)}, u32[]{:S(2)}) collective-permute-start(bf16[128,768]{1,0:T(8,128)(2,1)S(1)} %get-tuple-element.197.rows.f0), channel_id=1, source_target_pairs={{0,1},{1,0},{2,3},{3,2},{4,5},{5,4},{6,7},{7,6},{8,9},{9,8},{10,11... | collective-permute-start | bytes 589832 | tf_op jit(solution)/shard_map/ppermute | solution.py:23
  62.4 2.4 %collective-permute-start.28 = (bf16[256,768]{1,0:T(8,128)(2,1)S(1)}, bf16[256,768]{1,0:T(8,128)(2,1)S(1)}, u32[]{:S(2)}, u32[]{:S(2)}) collective-permute-start(bf16[256,768]{1,0:T(8,128)(2,1)S(1)} %get-tuple-element.209), channel_id=1, source_target_pairs={{0,1},{1,0},{2,3},{3,2},{4,5},{5,4},{6,7},{7,6},{8,9},{9,8},{10,11... | collective-permute-start | bytes 1179656 | tf_op jit(solution)/shard_map/ppermute | solution.py:23
  62.4 2.0 %collective-permute-start.25 = (bf16[128,768]{1,0:T(8,128)(2,1)S(1)}, bf16[128,768]{1,0:T(8,128)(2,1)S(1)}, u32[]{:S(2)}, u32[]{:S(2)}) collective-permute-start(bf16[128,768]{1,0:T(8,128)(2,1)S(1)} %get-tuple-element.178.rows.n0), channel_id=1, source_target_pairs={{0,1},{1,0},{2,3},{3,2},{4,5},{5,4},{6,7},{7,6},{8,9},{9,8},{10,11... | collective-permute-start | bytes 589832 | tf_op jit(solution)/shard_map/ppermute | solution.py:23
  62.9 1.8 collective-permute-start.29
  63.0 7.3 %collective-permute-start.30 = (bf16[128,768]{1,0:T(8,128)(2,1)S(1)}, bf16[128,768]{1,0:T(8,128)(2,1)S(1)}, u32[]{:S(2)}, u32[]{:S(2)}) collective-permute-start(bf16[128,768]{1,0:T(8,128)(2,1)S(1)} %get-tuple-element.210), channel_id=1, source_target_pairs={{0,2},{1,3},{2,0},{3,1},{4,6},{5,7},{6,4},{7,5},{8,10},{9,11},{10,... | collective-permute-start | bytes 589832 | tf_op jit(solution)/shard_map/ppermute | solution.py:23
  72.8 5.2 %collective-permute-start.35 = (bf16[384,768]{1,0:T(8,128)(2,1)S(1)}, bf16[384,768]{1,0:T(8,128)(2,1)S(1)}, u32[]{:S(2)}, u32[]{:S(2)}) collective-permute-start(bf16[384,768]{1,0:T(8,128)(2,1)S(1)} %get-tuple-element.231), channel_id=1, source_target_pairs={{0,1},{1,0},{2,3},{3,2},{4,5},{5,4},{6,7},{7,6},{8,9},{9,8},{10,11... | collective-permute-start | bytes 1769480 | tf_op jit(solution)/shard_map/ppermute | solution.py:23
  73.0 5.0 %collective-permute-start.32 = (bf16[384,128]{1,0:T(8,128)(2,1)S(1)}, bf16[384,128]{1,0:T(8,128)(2,1)S(1)}, u32[]{:S(2)}, u32[]{:S(2)}) collective-permute-start(bf16[384,128]{1,0:T(8,128)(2,1)S(1)} %get-tuple-element.220), channel_id=1, source_target_pairs={{0,2},{1,3},{2,0},{3,1},{4,6},{5,7},{6,4},{7,5},{8,10},{9,11},{10,... | collective-permute-start | bytes 294920 | tf_op jit(solution)/shard_map/ppermute | solution.py:23
  79.3 9.2 %collective-permute-start.36 = (bf16[192,768]{1,0:T(8,128)(2,1)S(1)}, bf16[192,768]{1,0:T(8,128)(2,1)S(1)}, u32[]{:S(2)}, u32[]{:S(2)}) collective-permute-start(bf16[192,768]{1,0:T(8,128)(2,1)S(1)} %wo_low.1), channel_id=1, source_target_pairs={{0,2},{1,3},{2,0},{3,1},{4,6},{5,7},{6,4},{7,5},{8,10},{9,11},{10,... | collective-permute-start | bytes 884744 | tf_op jit(solution)/shard_map/ppermute | solution.py:23
  79.9 16.2 %collective-permute-start.40 = (bf16[384,768]{1,0:T(8,128)(2,1)S(1)}, bf16[384,768]{1,0:T(8,128)(2,1)S(1)}, u32[]{:S(2)}, u32[]{:S(2)}) collective-permute-start(bf16[384,768]{1,0:T(8,128)(2,1)S(1)} %get-tuple-element.245), channel_id=1, source_target_pairs={{0,4},{4,0},{8,12},{12,8},{16,20},{20,16},{24,28},{28,24},{1,5},{5... | collective-permute-start | bytes 1769480 | tf_op jit(solution)/shard_map/ppermute | solution.py:23
  81.4 18.1 %collective-permute-start.41 = (bf16[384,768]{1,0:T(8,128)(2,1)S(1)}, bf16[384,768]{1,0:T(8,128)(2,1)S(1)}, u32[]{:S(2)}, u32[]{:S(2)}) collective-permute-start(bf16[384,768]{1,0:T(8,128)(2,1)S(1)} %get-tuple-element.249), channel_id=1, source_target_pairs={{0,8},{4,12},{8,0},{12,4},{16,24},{20,28},{24,16},{28,20},{1,9},{5... | collective-permute-start | bytes 1769480 | tf_op jit(solution)/shard_map/ppermute | solution.py:23
  90.1 7.8 %collective-permute-start.37 = (bf16[384,512]{1,0:T(8,128)(2,1)S(1)}, bf16[384,512]{1,0:T(8,128)(2,1)S(1)}, u32[]{:S(2)}, u32[]{:S(2)}) collective-permute-start(bf16[384,512]{1,0:T(8,128)(2,1)S(1)} %get-tuple-element.238), channel_id=1, source_target_pairs={{0,1},{1,0},{2,3},{3,2},{4,5},{5,4},{6,7},{7,6},{8,9},{9,8},{10,11... | collective-permute-start | bytes 1179656 | tf_op jit(solution)/shard_map/ppermute | solution.py:23
  90.1 12.2 %collective-permute-start.43 = (bf16[192,768]{1,0:T(8,128)(2,1)S(1)}, bf16[192,768]{1,0:T(8,128)(2,1)S(1)}, u32[]{:S(2)}, u32[]{:S(2)}) collective-permute-start(bf16[192,768]{1,0:T(8,128)(2,1)S(1)} %get-tuple-element.225), channel_id=1, source_target_pairs={{0,4},{4,0},{8,12},{12,8},{16,20},{20,16},{24,28},{28,24},{1,5},{5... | collective-permute-start | bytes 884744 | tf_op jit(solution)/shard_map/ppermute | solution.py:23
  90.8 13.2 %collective-permute-start.44 = (bf16[192,768]{1,0:T(8,128)(2,1)S(1)}, bf16[192,768]{1,0:T(8,128)(2,1)S(1)}, u32[]{:S(2)}, u32[]{:S(2)}) collective-permute-start(bf16[192,768]{1,0:T(8,128)(2,1)S(1)} %get-tuple-element.234), channel_id=1, source_target_pairs={{0,8},{4,12},{8,0},{12,4},{16,24},{20,28},{24,16},{28,20},{1,9},{5... | collective-permute-start | bytes 884744 | tf_op jit(solution)/shard_map/ppermute | solution.py:23
  96.2 15.0 %collective-permute-start.46 = (bf16[192,768]{1,0:T(8,128)(2,1)S(1)}, bf16[192,768]{1,0:T(8,128)(2,1)S(1)}, u32[]{:S(2)}, u32[]{:S(2)}) collective-permute-start(bf16[192,768]{1,0:T(8,128)(2,1)S(1)} %get-tuple-element.246), channel_id=1, source_target_pairs={{0,8},{4,12},{8,0},{12,4},{16,24},{20,28},{24,16},{28,20},{1,9},{5... | collective-permute-start | bytes 884744 | tf_op jit(solution)/shard_map/ppermute | solution.py:23
  97.9 11.6 %collective-permute-start.38 = (bf16[192,512]{1,0:T(8,128)(2,1)S(1)}, bf16[192,512]{1,0:T(8,128)(2,1)S(1)}, u32[]{:S(2)}, u32[]{:S(2)}) collective-permute-start(bf16[192,512]{1,0:T(8,128)(2,1)S(1)} %gx_send.1), channel_id=1, source_target_pairs={{0,2},{1,3},{2,0},{3,1},{4,6},{5,7},{6,4},{7,5},{8,10},{9,11},{10,... | collective-permute-start | bytes 589832 | tf_op jit(solution)/shard_map/ppermute | solution.py:23
  99.6 15.1 %collective-permute-start.47 = (bf16[192,768]{1,0:T(8,128)(2,1)S(1)}, bf16[192,768]{1,0:T(8,128)(2,1)S(1)}, u32[]{:S(2)}, u32[]{:S(2)}) collective-permute-start(bf16[192,768]{1,0:T(8,128)(2,1)S(1)} %get-tuple-element.250), channel_id=1, source_target_pairs={{0,4},{4,0},{8,12},{12,8},{16,20},{20,16},{24,28},{28,24},{1,5},{5... | collective-permute-start | bytes 884744 | tf_op jit(solution)/shard_map/ppermute | solution.py:23
  103.6 10.3 %collective-permute-start.34 = (bf16[384,128]{1,0:T(8,128)(2,1)S(1)}, bf16[384,128]{1,0:T(8,128)(2,1)S(1)}, u32[]{:S(2)}, u32[]{:S(2)}) collective-permute-start(bf16[384,128]{1,0:T(8,128)(2,1)S(1)} %get-tuple-element.222), channel_id=1, source_target_pairs={{0,1},{1,0},{2,3},{3,2},{4,5},{5,4},{6,7},{7,6},{8,9},{9,8},{10,11... | collective-permute-start | bytes 294920 | tf_op jit(solution)/shard_map/ppermute | solution.py:23
  103.9 4.1 %collective-permute-start.45 = (f32[16,768]{1,0:T(8,128)S(1)}, f32[16,768]{1,0:T(8,128)S(1)}, u32[]{:S(2)}, u32[]{:S(2)}) collective-permute-start(f32[16,768]{1,0:T(8,128)S(1)} %add_rows.4.shared), channel_id=1, source_target_pairs={{0,2},{1,3},{2,0},{3,1},{4,6},{5,7},{6,4},{7,5},{8,10},{9,11},{10,... | collective-permute-start | bytes 147464 | tf_op jit(solution)/shard_map/ppermute | solution.py:23
  108.0 10.6 %collective-permute-start.49 = (bf16[96,768]{1,0:T(8,128)(2,1)S(1)}, bf16[96,768]{1,0:T(8,128)(2,1)S(1)}, u32[]{:S(2)}, u32[]{:S(2)}) collective-permute-start(bf16[96,768]{1,0:T(8,128)(2,1)S(1)} %get-tuple-element.264), channel_id=1, source_target_pairs={{0,4},{4,0},{8,12},{12,8},{16,20},{20,16},{24,28},{28,24},{1,5},{5... | collective-permute-start | bytes 442376 | tf_op jit(solution)/shard_map/ppermute | solution.py:23
  109.5 9.1 %collective-permute-start.48 = (bf16[96,768]{1,0:T(8,128)(2,1)S(1)}, bf16[96,768]{1,0:T(8,128)(2,1)S(1)}, u32[]{:S(2)}, u32[]{:S(2)}) collective-permute-start(bf16[96,768]{1,0:T(8,128)(2,1)S(1)} %get-tuple-element.261), channel_id=1, source_target_pairs={{0,8},{4,12},{8,0},{12,4},{16,24},{20,28},{24,16},{28,20},{1,9},{5... | collective-permute-start | bytes 442376 | tf_op jit(solution)/shard_map/ppermute | solution.py:23
  111.2 8.9 %collective-permute-start.52 = (bf16[96,768]{1,0:T(8,128)(2,1)S(1)}, bf16[96,768]{1,0:T(8,128)(2,1)S(1)}, u32[]{:S(2)}, u32[]{:S(2)}) collective-permute-start(bf16[96,768]{1,0:T(8,128)(2,1)S(1)} %get-tuple-element.267), channel_id=1, source_target_pairs={{0,16},{4,20},{8,24},{12,28},{16,0},{20,4},{24,8},{28,12},{1,17},{... | collective-permute-start | bytes 442376 | tf_op jit(solution)/shard_map/ppermute | solution.py:23
  113.9 4.7 %collective-permute-start.39 = (bf16[384,128]{1,0:T(8,128)(2,1)S(1)}, bf16[384,128]{1,0:T(8,128)(2,1)S(1)}, u32[]{:S(2)}, u32[]{:S(2)}) collective-permute-start(bf16[384,128]{1,0:T(8,128)(2,1)S(1)} %out_join.1), channel_id=1, source_target_pairs={{0,2},{1,3},{2,0},{3,1},{4,6},{5,7},{6,4},{7,5},{8,10},{9,11},{10,... | collective-permute-start | bytes 294920 | tf_op jit(solution)/shard_map/ppermute | solution.py:23
  114.7 4.2 %collective-permute-start.50 = (f32[16,768]{1,0:T(8,128)S(1)}, f32[16,768]{1,0:T(8,128)S(1)}, u32[]{:S(2)}, u32[]{:S(2)}) collective-permute-start(f32[16,768]{1,0:T(8,128)S(1)} %last_sums.1.mine), channel_id=1, source_target_pairs={{0,4},{4,0},{8,12},{12,8},{16,20},{20,16},{24,28},{28,24},{1,5},{5... | collective-permute-start | bytes 147464 | tf_op jit(solution)/shard_map/ppermute | solution.py:23
  120.2 13.3 %collective-permute-start.51 = (bf16[96,768]{1,0:T(8,128)(2,1)S(1)}, bf16[96,768]{1,0:T(8,128)(2,1)S(1)}, u32[]{:S(2)}, u32[]{:S(2)}) collective-permute-start(bf16[96,768]{1,0:T(8,128)(2,1)S(1)} %get-tuple-element.270), channel_id=1, source_target_pairs={{0,16},{4,20},{8,24},{12,28},{16,0},{20,4},{24,8},{28,12},{1,17},{... | collective-permute-start | bytes 442376 | tf_op jit(solution)/shard_map/ppermute | solution.py:23
  121.6 25.7 %collective-permute-start.57 = (f32[48,768]{1,0:T(8,128)S(1)}, f32[48,768]{1,0:T(8,128)S(1)}, u32[]{:S(2)}, u32[]{:S(2)}) collective-permute-start(f32[48,768]{1,0:T(8,128)S(1)} %back_join.1), channel_id=1, source_target_pairs={{0,2},{1,3},{2,0},{3,1},{4,6},{5,7},{6,4},{7,5},{8,10},{9,11},{10,... | collective-permute-start | bytes 442376 | tf_op jit(solution)/shard_map/ppermute | solution.py:23
  122.2 13.0 %collective-permute-start.55 = (bf16[48,768]{1,0:T(8,128)(2,1)S(1)}, bf16[48,768]{1,0:T(8,128)(2,1)S(1)}, u32[]{:S(2)}, u32[]{:S(2)}) collective-permute-start(bf16[48,768]{1,0:T(8,128)(2,1)S(1)} %get-tuple-element.277), channel_id=1, source_target_pairs={{0,16},{4,20},{8,24},{12,28},{16,0},{20,4},{24,8},{28,12},{1,17},{... | collective-permute-start | bytes 221192 | tf_op jit(solution)/shard_map/ppermute | solution.py:23
  123.8 23.4 %collective-permute-start.54 = (bf16[48,768]{1,0:T(8,128)(2,1)S(1)}, bf16[48,768]{1,0:T(8,128)(2,1)S(1)}, u32[]{:S(2)}, u32[]{:S(2)}) collective-permute-start(bf16[48,768]{1,0:T(8,128)(2,1)S(1)} %get-tuple-element.274), channel_id=1, source_target_pairs={{0,16},{4,20},{8,24},{12,28},{16,0},{20,4},{24,8},{28,12},{1,17},{... | collective-permute-start | bytes 221192 | tf_op jit(solution)/shard_map/ppermute | solution.py:23
  125.1 22.2 %collective-permute-start.56 = (f32[16,768]{1,0:T(8,128)S(1)}, f32[16,768]{1,0:T(8,128)S(1)}, u32[]{:S(2)}, u32[]{:S(2)}) collective-permute-start(f32[16,768]{1,0:T(8,128)S(1)} %add_rows.5.mine), channel_id=1, source_target_pairs={{0,8},{4,12},{8,0},{12,4},{16,24},{20,28},{24,16},{28,20},{1,9},{5... | collective-permute-start | bytes 147464 | tf_op jit(solution)/shard_map/ppermute | solution.py:23
  133.6 19.7 %collective-permute-start.58 = (bf16[96,768]{1,0:T(8,128)(2,1)S(1)}, bf16[96,768]{1,0:T(8,128)(2,1)S(1)}, u32[]{:S(2)}, u32[]{:S(2)}) collective-permute-start(bf16[96,768]{1,0:T(8,128)(2,1)S(1)} %last_step.3.mine), channel_id=1, source_target_pairs={{0,16},{4,20},{8,24},{12,28},{16,0},{20,4},{24,8},{28,12},{1,17},{... | collective-permute-start | bytes 442376 | tf_op jit(solution)/shard_map/ppermute | solution.py:23
  147.4 11.0 %collective-permute-start.62 = (bf16[96,768]{1,0:T(8,128)(2,1)S(1)}, bf16[96,768]{1,0:T(8,128)(2,1)S(1)}, u32[]{:S(2)}, u32[]{:S(2)}) collective-permute-start(bf16[96,768]{1,0:T(8,128)(2,1)S(1)} %join_owners.1.mine), channel_id=1, source_target_pairs={{0,16},{4,20},{8,24},{12,28},{16,0},{20,4},{24,8},{28,12},{1,17},{... | collective-permute-start | bytes 442376 | tf_op jit(solution)/shard_map/ppermute | solution.py:23
  147.4 9.2 %collective-permute-start.60 = (bf16[48,768]{1,0:T(8,128)(2,1)S(1)}, bf16[48,768]{1,0:T(8,128)(2,1)S(1)}, u32[]{:S(2)}, u32[]{:S(2)}) collective-permute-start(bf16[48,768]{1,0:T(8,128)(2,1)S(1)} %last_step.5.mine), channel_id=1, source_target_pairs={{0,16},{4,20},{8,24},{12,28},{16,0},{20,4},{24,8},{28,12},{1,17},{... | collective-permute-start | bytes 221192 | tf_op jit(solution)/shard_map/ppermute | solution.py:23
  150.4 7.4 %collective-permute-start.59 = (bf16[48,768]{1,0:T(8,128)(2,1)S(1)}, bf16[48,768]{1,0:T(8,128)(2,1)S(1)}, u32[]{:S(2)}, u32[]{:S(2)}) collective-permute-start(bf16[48,768]{1,0:T(8,128)(2,1)S(1)} %last_step.4.mine), channel_id=1, source_target_pairs={{0,16},{4,20},{8,24},{12,28},{16,0},{20,4},{24,8},{28,12},{1,17},{... | collective-permute-start | bytes 221192 | tf_op jit(solution)/shard_map/ppermute | solution.py:23
  150.4 7.9 %collective-permute-start.61 = (f32[16,768]{1,0:T(8,128)S(1)}, f32[16,768]{1,0:T(8,128)S(1)}, u32[]{:S(2)}, u32[]{:S(2)}) collective-permute-start(f32[16,768]{1,0:T(8,128)S(1)} %add_rows.6.mine), channel_id=1, source_target_pairs={{0,16},{4,20},{8,24},{12,28},{16,0},{20,4},{24,8},{28,12},{1,17},{... | collective-permute-start | bytes 147464 | tf_op jit(solution)/shard_map/ppermute | solution.py:23
  153.3 8.7 %collective-permute-start.63 = (bf16[192,768]{1,0:T(8,128)(2,1)S(1)}, bf16[192,768]{1,0:T(8,128)(2,1)S(1)}, u32[]{:S(2)}, u32[]{:S(2)}) collective-permute-start(bf16[192,768]{1,0:T(8,128)(2,1)S(1)} %in_order.8.mine), channel_id=1, source_target_pairs={{0,4},{4,0},{8,12},{12,8},{16,20},{20,16},{24,28},{28,24},{1,5},{5... | collective-permute-start | bytes 884744 | tf_op jit(solution)/shard_map/ppermute | solution.py:23
  158.4 13.2 %collective-permute-start.69 = (bf16[192,768]{1,0:T(8,128)(2,1)S(1)}, bf16[192,768]{1,0:T(8,128)(2,1)S(1)}, u32[]{:S(2)}, u32[]{:S(2)}) collective-permute-start(bf16[192,768]{1,0:T(8,128)(2,1)S(1)} %in_order.11.mine), channel_id=1, source_target_pairs={{0,8},{4,12},{8,0},{12,4},{16,24},{20,28},{24,16},{28,20},{1,9},{5... | collective-permute-start | bytes 884744 | tf_op jit(solution)/shard_map/ppermute | solution.py:23
  158.4 5.9 %collective-permute-start.66 = (bf16[96,768]{1,0:T(8,128)(2,1)S(1)}, bf16[96,768]{1,0:T(8,128)(2,1)S(1)}, u32[]{:S(2)}, u32[]{:S(2)}) collective-permute-start(bf16[96,768]{1,0:T(8,128)(2,1)S(1)} %in_order.10.mine), channel_id=1, source_target_pairs={{0,4},{4,0},{8,12},{12,8},{16,20},{20,16},{24,28},{28,24},{1,5},{5... | collective-permute-start | bytes 442376 | tf_op jit(solution)/shard_map/ppermute | solution.py:23
  159.0 12.5 %collective-permute-start.64 = (bf16[96,768]{1,0:T(8,128)(2,1)S(1)}, bf16[96,768]{1,0:T(8,128)(2,1)S(1)}, u32[]{:S(2)}, u32[]{:S(2)}) collective-permute-start(bf16[96,768]{1,0:T(8,128)(2,1)S(1)} %in_order.9.mine), channel_id=1, source_target_pairs={{0,8},{4,12},{8,0},{12,4},{16,24},{20,28},{24,16},{28,20},{1,9},{5... | collective-permute-start | bytes 442376 | tf_op jit(solution)/shard_map/ppermute | solution.py:23
  162.1 29.1 %collective-permute-start.68 = (bf16[384,768]{1,0:T(8,128)(2,1)S(1)}, bf16[384,768]{1,0:T(8,128)(2,1)S(1)}, u32[]{:S(2)}, u32[]{:S(2)}) collective-permute-start(bf16[384,768]{1,0:T(8,128)(2,1)S(1)} %in_order.12.mine), channel_id=1, source_target_pairs={{0,8},{4,12},{8,0},{12,4},{16,24},{20,28},{24,16},{28,20},{1,9},{5... | collective-permute-start | bytes 1769480 | tf_op jit(solution)/shard_map/ppermute | solution.py:23
  171.6 21.2 %collective-permute-start.70 = (bf16[384,768]{1,0:T(8,128)(2,1)S(1)}, bf16[384,768]{1,0:T(8,128)(2,1)S(1)}, u32[]{:S(2)}, u32[]{:S(2)}) collective-permute-start(bf16[384,768]{1,0:T(8,128)(2,1)S(1)} %in_order.15.mine), channel_id=1, source_target_pairs={{0,4},{4,0},{8,12},{12,8},{16,20},{20,16},{24,28},{28,24},{1,5},{5... | collective-permute-start | bytes 1769480 | tf_op jit(solution)/shard_map/ppermute | solution.py:23
  172.2 16.4 %collective-permute-start.67 = (bf16[192,768]{1,0:T(8,128)(2,1)S(1)}, bf16[192,768]{1,0:T(8,128)(2,1)S(1)}, u32[]{:S(2)}, u32[]{:S(2)}) collective-permute-start(bf16[192,768]{1,0:T(8,128)(2,1)S(1)} %in_order.14.vo_mine), channel_id=1, source_target_pairs={{0,8},{4,12},{8,0},{12,4},{16,24},{20,28},{24,16},{28,20},{1,9},{5... | collective-permute-start | bytes 884744 | tf_op jit(solution)/shard_map/ppermute | solution.py:23
  172.2 17.4 %collective-permute-start.65 = (bf16[192,768]{1,0:T(8,128)(2,1)S(1)}, bf16[192,768]{1,0:T(8,128)(2,1)S(1)}, u32[]{:S(2)}, u32[]{:S(2)}) collective-permute-start(bf16[192,768]{1,0:T(8,128)(2,1)S(1)} %in_order.13.qk_mine), channel_id=1, source_target_pairs={{0,4},{4,0},{8,12},{12,8},{16,20},{20,16},{24,28},{28,24},{1,5},{5... | collective-permute-start | bytes 884744 | tf_op jit(solution)/shard_map/ppermute | solution.py:23
  (27 other events, 72.3 us)

commit v3 on v2

v3 whole, which is shorter than its diff:
```python
import jax
import jax.numpy as jnp
from jax import lax
from jax.experimental import pallas as pl
from jax.experimental.pallas import tpu as pltpu
from jax.sharding import PartitionSpec as P

HEAD_DIM = 64
norm_eps = 1e-06
masked_score = -1e30
bf16 = jnp.bfloat16
f32 = jnp.float32
MIB = 1 << 20
WIDE = 512
HBM_BYTES_PER_MICRO = 3690000

SPECS = {
    "S": pl.BlockSpec(memory_space=pltpu.SMEM),
    "V": pl.BlockSpec(memory_space=pltpu.VMEM),
}


def swap(block, axis, bit):
    return lax.ppermute(block, axis, [(i, i ^ bit) for i in range(lax.axis_size(axis))])


def after(block, *others):
    return lax.optimization_barrier((block, *others))[0]


def sds(shape, dtype):
    return jax.ShapeDtypeStruct(shape, dtype)


def local_kernel(body, name, args, kinds, outs, scratch=(), micros=0.6, vmem=16):
    return pl.pallas_call(
        body,
        name=name,
        out_shape=outs,
        in_specs=[SPECS[k] for k in kinds],
        out_specs=[SPECS["V"]] * len(outs),
        scratch_shapes=list(scratch),
        compiler_params=pltpu.CompilerParams(vmem_limit_bytes=vmem * MIB),
        cost_estimate=pl.CostEstimate(
            flops=1, bytes_accessed=int(micros * HBM_BYTES_PER_MICRO), transcendentals=0
        ),
    )(*args)


def dot(left, right):
    return jnp.dot(left, right, preferred_element_type=f32)


def dot_nt(left, right):
    return lax.dot_general(left, right, (((1,), (1,)), ((), ())), preferred_element_type=f32)


def dot_tn(left, right):
    return lax.dot_general(left, right, (((0,), (0,)), ((), ())), preferred_element_type=f32)


def at(index, size):
    return pl.ds(pl.multiple_of(index * size, size), size)


def begin(given, w_out, w_back, bounds, small, out_half, back_half):
    toks = bounds.shape[1]
    query = lax.broadcasted_iota(jnp.int32, (1, toks), 1).astype(f32)
    start, stop = jnp.zeros_like(query), jnp.zeros_like(query)
    end = jnp.zeros((1, 1), f32)
    for j in range(4):
        first, end = end, end + given[3:4, j : j + 1]
        inside = (query >= first) & (query < end)
        start = jnp.where(inside, first, start)
        stop = jnp.where(inside, end, stop)
    bounds[0:1, :] = start.astype(jnp.int32)
    bounds[1:2, :] = stop.astype(jnp.int32)
    feats = given.shape[1]
    small[...] = jnp.zeros_like(small)
    small[0:2, :feats] = given[0:2, :]
    heads = feats // HEAD_DIM
    small[2:3, :feats] = jnp.concatenate(
        [jnp.broadcast_to(given[2:3, i : i + 1], (1, HEAD_DIM)) for i in range(heads)], axis=1
    )
    other, parity = 1 - lax.axis_index("hid") // 2, lax.axis_index("rows") & 1
    out_half[...] = w_out[at(parity, out_half.shape[0]), :]
    back_half[...] = w_back[:, at(2 * other + parity, back_half.shape[1])]


def fill_mask(bounds, mask):
    toks = mask.shape[0]
    for j in range(toks // WIDE):
        chunk = slice(j * WIDE, (j + 1) * WIDE)
        position = lax.broadcasted_iota(jnp.int32, (toks, WIDE), 0)
        same = (position >= bounds[0:1, chunk]) & (position < bounds[1:2, chunk])
        mask[:, chunk] = jnp.where(same, 0.0, masked_score)


def attn_forward(
    bounds, small, x0, x1, x2, x3, w_qkv,
    x_all, qkv, logsum, mine, send_core, send_x, x_block, gated, mask,
):
    me = lax.axis_index("hid")
    feats, toks = x0.shape
    block = toks // 4
    for k, piece in enumerate((x0, x1, x2, x3)):
        x_all[at(me ^ k, feats), :] = piece[...]
    x_block[...] = x_all[:, at(me, block)]
    cols = jnp.transpose(small[...])
    for c in range(3):
        rows = dot(w_qkv[c], x_all[...])
        if c != 1:
            rows = rows + cols[:feats, c // 2 : c // 2 + 1]
        rows = rows.astype(bf16)
        if c == 0:
            rows = rows * jnp.asarray(HEAD_DIM ** (-0.5), bf16)
        qkv[c] = rows
    fill_mask(bounds, mask)
    heads = feats // HEAD_DIM
    for head in range(heads):
        span = slice(head * HEAD_DIM, (head + 1) * HEAD_DIM)
        keys = jnp.transpose(qkv[1, span, :])
        values = qkv[2, span, :]
        for j in range(4 * block // WIDE):
            chunk = slice(j * WIDE, (j + 1) * WIDE)
            scores = dot(keys, qkv[0, span, chunk])
            scores = scores + mask[:, chunk]
            peak = jnp.max(scores, axis=0, keepdims=True)
            expo = jnp.exp(scores - peak)
            total = jnp.sum(expo, axis=0, keepdims=True)
            probs = (expo * (1.0 / total)).astype(bf16)
            logsum[head : head + 1, chunk] = peak + jnp.log(total)
            gated[span, chunk] = (dot(values, probs) * cols[span, 2:3]).astype(bf16)
    mine[...] = gated[:, at(me, block)]
    send_x[:feats, :] = gated[:, at(me ^ 2, block)]
    send_x[feats:, :] = gated[:, at(me ^ 3, block)]
    send_core[...] = gated[:, at(me ^ 1, block)]


def attn_backward(
    bounds, qkv, logsum, u0, u1, u2, u3, grads, head_sums, bias_sums, up, mask
):
    me = lax.axis_index("hid")
    feats, block = u0.shape
    pieces = (u0, u1.at[:feats, :], u2.at[:feats, :], u3.at[feats : 2 * feats, :])
    for k, piece in enumerate(pieces):
        up[:, at(me ^ k, block)] = piece[...]
    fill_mask(bounds, mask)
    heads = feats // HEAD_DIM
    head_sums[...] = jnp.zeros_like(head_sums)
    for head in range(heads):
        span = slice(head * HEAD_DIM, (head + 1) * HEAD_DIM)
        queries, keys_t, values_t = (qkv[c, span, :] for c in range(3))
        keys = jnp.transpose(keys_t)
        values = jnp.transpose(values_t)
        upstream = up[span, :]
        grad_k = jnp.zeros((HEAD_DIM, 4 * block), f32)
        grad_v = jnp.zeros((HEAD_DIM, 4 * block), f32)
        inner_sum = jnp.zeros((1, WIDE), f32)
        for j in range(4 * block // WIDE):
            chunk = slice(j * WIDE, (j + 1) * WIDE)
            scores = dot(keys, queries[:, chunk])
            scores = scores + mask[:, chunk]
            probs = jnp.exp(scores - logsum[head : head + 1, chunk])
            grad_p = dot(values, upstream[:, chunk])
            weighted = probs * grad_p
            inner = jnp.sum(weighted, axis=0, keepdims=True)
            inner_sum = inner_sum + inner
            grad_s = (weighted - probs * inner).astype(bf16)
            grad_v = grad_v + dot_nt(upstream[:, chunk], probs.astype(bf16))
            grad_k = grad_k + dot_nt(queries[:, chunk], grad_s)
            grads[span, chunk] = (dot(keys_t, grad_s) * HEAD_DIM ** (-0.5)).astype(bf16)
        for c, grad in ((1, grad_k), (2, grad_v)):
            rows = slice(c * feats + head * HEAD_DIM, c * feats + (head + 1) * HEAD_DIM)
            grads[rows, :] = grad.astype(bf16)
        head_sums[head : head + 1, :] = sum(
            inner_sum[:, k * block : (k + 1) * block] for k in range(WIDE // block)
        )
    ones = jnp.ones((8, 4 * block), bf16)
    bias_sums[...] = dot_nt(ones, grads[...])


def all_sums(sums, u1, u2, u3, ig_mine, p_core, bin_sum, head_sums, bias_sums, vec):
    blocks = sums.shape[1] // 128
    feats = (u2.shape[0] - 16 * blocks) // 2
    total = sums[...] + get_sums(u1, feats, 8, blocks)
    vec[0:8, :] = (total + get_sums(u2, 2 * feats, 8, blocks)) + get_sums(u3, 2 * feats, 8, blocks)
    vec[8:, :] = jnp.zeros((vec.shape[0] - 8, vec.shape[1]), f32)
    pair = p_core[p_core.shape[0] - 16 :, :].astype(f32)
    vec[8:9, :] = ig_mine[0:1, :] + (pair[0:1, :] + pair[8:9, :])
    vec[9:10, :] = bin_sum[0:1, :]
    width = bias_sums.shape[1]
    vec[10:11, :width] = bias_sums[0:1, :]
    vec[11:12, :8] = jnp.sum(jnp.transpose(head_sums[...]), axis=0, keepdims=True)


def pair_value(pair):
    n = pair.shape[0] // 2
    return pair[:n, :].astype(f32) + pair[n:, :].astype(f32)


def qk_weight_grad(
    grads, x_all, sums, u1, u2, u3, ig_mine, p_core, bin_sum, head_sums, bias_sums,
    keep, send, pair, full, vec,
):
    parity = lax.axis_index("rows") & 1
    n = keep.shape[0]
    full[...] = dot_nt(grads[: 2 * n, :], x_all[...])
    all_sums(sums, u1, u2, u3, ig_mine, p_core, bin_sum, head_sums, bias_sums, vec)
    send[:n, :] = full[at(parity ^ 1, n), :].astype(bf16)
    send[n:, :] = high_low(vec[...])
    pair[...] = high_low(vec[...])
    keep[...] = full[at(parity, n), :]


def vo_weight_grad(grads, x_all, wo_mine, wo_core, wo_far, keep, send, full):
    parity = lax.axis_index("rows") & 1
    n = keep.shape[0]
    full[:n, :] = dot_nt(grads[2 * n :, :], x_all[...])
    full[n:, :] = wo_mine[...] + wo_core[:n, :].astype(f32) + wo_far[...].astype(f32)
    send[...] = full[at(parity ^ 1, n), :].astype(bf16)
    keep[...] = full[at(parity, n), :]


def add_low(mine, other, total):
    total[...] = (mine[...].astype(f32) + other[...].astype(f32)).astype(total.dtype)


def add_second(mine, other, total):
    n = mine.shape[0]
    total[...] = (mine[...] + other[n:, :].astype(f32)).astype(total.dtype)


def tokens_step(mine, res_x, recv, send):
    n, toks = mine.shape
    block = res_x.shape[1]
    send[:, :toks] = (mine[...] + recv[n:, :toks].astype(f32)).astype(bf16)
    send[:, toks : toks + block] = res_x[...]
    send[:, toks + block :] = recv[n:, toks:]


def tokens_outputs(mine, res_mine, from_core, from_x, grad, output):
    me = lax.axis_index("hid")
    n, toks = mine.shape
    block = res_mine.shape[1]
    both = from_core[:n, :toks].astype(f32) + from_x[:, :toks].astype(f32)
    grad[...] = (mine[...] + both).astype(bf16)
    output[:, at(me, block)] = res_mine[...]
    output[:, at(me ^ 1, block)] = from_core[:n, toks:]
    output[:, at(me ^ 2, block)] = from_x[:, toks : toks + block]
    output[:, at(me ^ 3, block)] = from_x[:, toks + block :]


def qkv_input_grad(grads, w_qkv, dres, res_send, mine, mine_x, send, full):
    me = lax.axis_index("hid")
    feats = mine.shape[0]
    block = dres.shape[0]
    total = None
    for c in range(3):
        part = dot(jnp.transpose(w_qkv[c]), grads[c * feats : (c + 1) * feats, :])
        total = part if total is None else total + part
    full[...] = total
    full[:, at(me, block)] += jnp.transpose(dres[...])
    toks = full.shape[1]
    send[:feats, :toks] = full[at(me ^ 1, feats), :].astype(bf16)
    send[feats:, :toks] = full[at(me ^ 3, feats), :].astype(bf16)
    send[:, toks:] = res_send[...]
    mine[...] = full[at(me, feats), :]
    mine_x[...] = full[at(me ^ 2, feats), :]


def place_rows(own, core_rows, xa, xb, fa, fb, whole):
    me, parity = lax.axis_index("hid"), lax.axis_index("rows") & 1
    n = own.shape[0]
    half = n // 2
    whole[at(me, n), :] = own[...]
    whole[at(me ^ 1, n), :] = core_rows[...]
    for owner, first, second in ((me ^ 2, xa, xb), (me ^ 3, fa, fb)):
        whole[at(2 * owner + parity, half), :] = first[...]
        whole[at(2 * owner + (parity ^ 1), half), :] = second[...]


def row_norm(values):
    mean = jnp.mean(values, axis=1, keepdims=True)
    centered = values - mean
    spread = jnp.mean(centered * centered, axis=1, keepdims=True)
    inv = lax.rsqrt(spread + norm_eps)
    return centered * inv, inv


def attn_out(
    g0, g1, g2, g3, x_block, vecs, wo, cotangent,
    normed, send, hat, inv_out, pre, gated_rows, heads_all,
):
    me = lax.axis_index("hid")
    feats = g0.shape[0]
    for k, piece in enumerate((g0, g1.at[:feats, :], g2.at[:feats, :], g3.at[feats : 2 * feats, :])):
        heads_all[at(me ^ k, feats), :] = piece[...]
    gated = jnp.transpose(heads_all[...])
    gated_rows[...] = gated
    tokens = jnp.transpose(x_block[...].astype(f32))
    attn = dot_nt(gated, wo[...]) + vecs[0:1, :]
    pre[...] = attn
    n = normed.shape[0]
    resid = tokens + attn * vecs[8:9, :]
    x_hat, inv = row_norm(resid)
    value = x_hat * vecs[1:2, :] + vecs[2:3, :]
    send[:n, :] = value.astype(bf16)
    rows = feats // 3
    for k in range(3):
        piece = cotangent[k * rows : (k + 1) * rows, at(1 - me // 2, 2 * n)]
        send[n:, k * 2 * n : (k + 1) * 2 * n] = piece
    normed[...] = value
    hat[...] = x_hat
    inv_out[...] = jnp.broadcast_to(inv, inv_out.shape)


def high_low(values):
    high = values.astype(bf16).astype(f32)
    return jnp.concatenate([high, values - high], axis=0).astype(bf16)


def put_sums(sums, ref, start):
    pairs = high_low(sums)
    count = pairs.shape[0]
    for t in range(sums.shape[1] // 128):
        ref[start + t * count : start + (t + 1) * count, :] = pairs[:, t * 128 : (t + 1) * 128]


def get_sums(ref, start, count, blocks):
    parts = []
    for t in range(blocks):
        pair = ref[start + 2 * count * t : start + 2 * count * (t + 1), :].astype(f32)
        parts.append(pair[:count, :] + pair[count:, :])
    return jnp.concatenate(parts, axis=1)


def attn_out_back(
    part, recv, dres2, hat, inv, pre, vecs, wo, sums2,
    dres, grad_attn, sums, up_mine, up_core, up_x, ups,
):
    me = lax.axis_index("hid")
    feats = up_mine.shape[0]
    grad = part[...] + recv[...].astype(f32) + dres2[...]
    x_hat = hat[...]
    scaled = grad * vecs[1:2, :]
    mean_plain = jnp.mean(scaled, axis=1, keepdims=True)
    mean_along = jnp.mean(scaled * x_hat, axis=1, keepdims=True)
    grad_resid = inv[:, 0:1] * (scaled - mean_plain - x_hat * mean_along)
    dres[...] = grad_resid
    low = (grad_resid * vecs[8:9, :]).astype(bf16)
    grad_attn[...] = low
    grad_gated = dot(low, wo[...])
    upstream = (grad_gated * vecs[7:8, :]).astype(bf16)
    ups[...] = jnp.transpose(upstream)
    up_mine[...] = ups[at(me, feats), :]
    up_core[:feats, :] = ups[at(me ^ 1, feats), :]
    up_x[:feats, :] = ups[at(me ^ 2, feats), :]
    up_x[feats : 2 * feats, :] = ups[at(me ^ 3, feats), :]
    sums[0:1, :] = jnp.sum(grad * x_hat, axis=0, keepdims=True)
    sums[1:2, :] = jnp.sum(grad, axis=0, keepdims=True)
    sums[2:3, :] = jnp.sum(low.astype(f32), axis=0, keepdims=True)
    sums[3:4, :] = jnp.sum(grad_resid * pre[...], axis=0, keepdims=True)
    sums[4:8, :] = sums2[...]
    for ref, start in ((up_core, feats), (up_x, 2 * feats)):
        put_sums(sums[...], ref, start)


def out_weight_grad(grad_attn, gated_rows, mine, mine_x, send, full):
    me = lax.axis_index("hid")
    feats = mine.shape[0]
    full[...] = dot_tn(grad_attn[...], gated_rows[...])
    send[:feats, :] = full[at(me ^ 1, feats), :].astype(bf16)
    send[feats:, :] = full[at(me ^ 3, feats), :].astype(bf16)
    mine[...] = full[at(me, feats), :]
    mine_x[...] = full[at(me ^ 2, feats), :]


def place_units(wi_own, wi_core, own, core_rows, xa, xb, fa, fb, wi, wb):
    me, core, chip, parity = lax.axis_index("hid"), lax.axis_index("hid") & 1, lax.axis_index("hid") // 2, lax.axis_index("rows") & 1
    n, half = xa.shape
    units = wi_own.shape[1]
    wi[:, at(core, units)] = wi_own[...]
    wi[:, at(core ^ 1, units)] = wi_core[...]
    wb[at(me, n), :] = own[:, at(chip, 2 * half)]
    wb[at(me ^ 1, n), :] = core_rows[:, at(chip, 2 * half)]
    for owner, first, second in ((me ^ 2, xa, xb), (me ^ 3, fa, fb)):
        wb[at(owner, n), at(parity, half)] = first[...]
        wb[at(owner, n), at(parity ^ 1, half)] = second[...]


def ffn_forward(
    rows, unit_rows, wi, wb, core_far, act, slope, inter_mine, part, core_pair, inter
):
    n = part.shape[0]
    core_pair[n:, :] = core_far[...]
    ffn_units(rows[: part.shape[0], :], unit_rows, wi, act, slope, inter_mine, core_pair.at[:n, :], inter)
    part[...] = dot_nt(inter[...], wb[...])


def ffn_forward_far(
    rows, unit_rows, wi, wb, act, slope, inter_mine, inter_core, part, inter
):
    ffn_units(rows[: part.shape[0], :], unit_rows, wi, act, slope, inter_mine, inter_core, inter)
    part[...] = dot_nt(inter[...], wb[...]).astype(part.dtype)


def ffn_units(rows, unit_rows, wi, act, slope, inter_mine, inter_core, inter):
    core = lax.axis_index("hid") & 1
    units = wi.shape[1]
    step = 256
    for j in range(units // step):
        cut = slice(j * step, (j + 1) * step)
        u = dot(rows, wi[:, cut]) + unit_rows[0:1, cut]
        cdf = 0.5 * (1.0 + lax.erf(u * 0.7071067811865476))
        value = u * cdf
        act[:, cut] = value
        slope[:, cut] = cdf + u * (jnp.exp(-0.5 * u * u) * 0.3989422804014327)
        inter[:, cut] = (value * unit_rows[1:2, cut]).astype(bf16)
    inter_mine[...] = inter[:, at(core, units // 2)]
    inter_core[...] = inter[:, at(core ^ 1, units // 2)]


def ffn_backward(
    rows, act, slope, unit_rows, wi, wb, gpre_mine, gpre_core, part, sums, gpre,
):
    ffn_units_back(rows, act, slope, unit_rows, wb, gpre_mine, gpre_core, sums, gpre)
    part[...] = dot_nt(gpre[...], wi[...])


def ffn_backward_far(
    rows, act, slope, unit_rows, wi, wb, core_mine, sums_mine,
    gpre_mine, part, sums, core_pair, gpre, all_sums,
):
    core, n = lax.axis_index("hid") & 1, rows.shape[0]
    units = gpre_mine.shape[1]
    core_pair[:n, :] = core_mine[...]
    ffn_units_back(
        rows, act, slope, unit_rows, wb, gpre_mine, core_pair.at[n : 2 * n, :], all_sums, gpre
    )
    part[...] = dot_nt(gpre[...], wi[...]).astype(part.dtype)
    all_sums[...] += sums_mine[...]
    sums[...] = all_sums[:, at(core, units)]
    core_pair[2 * n :, :] = high_low(all_sums[:, at(core ^ 1, units)])


def ffn_units_back(rows, act, slope, unit_rows, wb, gpre_mine, gpre_core, sums, gpre):
    core = lax.axis_index("hid") & 1
    units = wb.shape[1]
    step = 256
    for j in range(units // step):
        cut = slice(j * step, (j + 1) * step)
        ginter = dot(rows[...], wb[:, cut])
        sums[:, cut] = jnp.broadcast_to(
            jnp.sum(ginter * act[:, cut], axis=0, keepdims=True), (8, step)
        )
        gpre[:, cut] = (ginter * unit_rows[1:2, cut] * slope[:, cut]).astype(bf16)
    gpre_mine[...] = gpre[:, at(core, units // 2)]
    gpre_core[...] = gpre[:, at(core ^ 1, units // 2)]


def ffn_weight_grads(
    n0, n1, n2, n3, e0, e1, e_core, p0, p1, p_core, f0, f1, f2, f3,
    back0_keep, back0_send, back1_keep, back1_send, in0_keep, in0_send, in1_keep, in1_send,
    bias_sums, left, right, full,
):
    parity = lax.axis_index("rows") & 1

    def fill(target, pieces):
        start = 0
        for piece in pieces:
            count = piece.shape[0] // 128 * 128
            target[start : start + count, :] = piece[:count, :]
            start += count

    fill(left, (f0, f1, f2, f3))
    fill(right, (e0, e1, e_core))
    full[...] = dot_tn(left[...], right[...])
    owners, parts = 4, 4
    rows = full.shape[0] // (owners * parts)
    for k, (keep, send) in enumerate(((back0_keep, back0_send), (back1_keep, back1_send))):
        for h in range(owners):
            to = slice(h * rows, (h + 1) * rows)
            send[to, :] = full[at(h * parts + 2 * k + (parity ^ 1), rows), :].astype(bf16)
            keep[to, :] = full[at(h * parts + 2 * k + parity, rows), :]
    fill(left, (n0, n1, n2, n3))
    fill(right, (p0, p1, p_core))
    full[...] = dot_tn(left[...], right[...])
    rows = full.shape[0] // 4
    for k, (keep, send) in enumerate(((in0_keep, in0_send), (in1_keep, in1_send))):
        send[...] = full[at(2 * k + (parity ^ 1), rows), :].astype(bf16)
        keep[...] = full[at(2 * k + parity, rows), :]
    bias_sums[...] = jnp.broadcast_to(
        jnp.sum(right[...].astype(f32), axis=0, keepdims=True), bias_sums.shape
    )


def second_norm(
    part, recv, normed, cot0, cot1, n_x, n_far, vecs,
    grad_low, dres, sums, out_mine, out_x, out_send, cots, outs,
):
    me = lax.axis_index("hid")
    feats = cot0.shape[0]
    block = part.shape[0]
    core = me & 1
    cots[at(me, feats), :] = cot0[:, at(me, block)]
    cots[at(me ^ 1, feats), :] = cot1[:, at(me, block)]
    rows = feats // 3
    for owner, pieces in ((me ^ 2, n_x), (me ^ 3, n_far)):
        for k in range(3):
            to = pl.ds(pl.multiple_of(owner * feats + k * rows, rows), rows)
            cots[to, :] = pieces[block:, at(2 * k + core, block)]
    ffn = part[...] + recv[...].astype(f32) + vecs[4:5, :]
    resid = normed[...] + ffn * vecs[9:10, :]
    x_hat, inv = row_norm(resid)
    grad_out = jnp.transpose(cots[...].astype(f32))
    scaled = grad_out * vecs[5:6, :]
    mean_plain = jnp.mean(scaled, axis=1, keepdims=True)
    mean_along = jnp.mean(scaled * x_hat, axis=1, keepdims=True)
    grad_resid = inv * (scaled - mean_plain - x_hat * mean_along)
    low = (grad_resid * vecs[9:10, :]).astype(bf16)
    grad_low[...] = low
    dres[...] = grad_resid
    value = x_hat * vecs[5:6, :] + vecs[6:7, :]
    outs[...] = jnp.transpose(value).astype(bf16)
    out_mine[...] = outs[at(me, feats), :]
    out_x[...] = outs[at(me ^ 2, feats), :]
    out_send[:feats, :] = outs[at(me ^ 1, feats), :]
    out_send[feats:, :] = outs[at(me ^ 3, feats), :]
    sums[0:1, :] = jnp.sum(grad_out * x_hat, axis=0, keepdims=True)
    sums[1:2, :] = jnp.sum(grad_out, axis=0, keepdims=True)
    sums[2:3, :] = jnp.sum(low.astype(f32), axis=0, keepdims=True)
    sums[3:4, :] = jnp.sum(grad_resid * ffn, axis=0, keepdims=True)


VECTORS = 16


def add_vectors(
    head_gate, branch, b_out, gain, bias, hidden_gate, hidden_mask, b_back, ctx_core, ctx_x,
    send_core, send_x, columns, rows,
):
    feats = b_out.shape[0]

    def row(ref):
        return ref[...].reshape(1, ref.shape[0])

    cols = row(hidden_gate) * row(hidden_mask).astype(f32)
    rows[...] = jnp.zeros_like(rows)
    rows[0:1, :feats] = row(b_out)
    rows[1:2, :feats] = gain[0:1, :]
    rows[2:3, :feats] = bias[0:1, :]
    rows[3:4, :feats] = cols
    rows[4:5, :feats] = row(b_back)
    rows[5:6, :feats] = gain[1:2, :]
    rows[6:7, :feats] = bias[1:2, :]
    rows[7:8, :feats] = jnp.concatenate(
        [jnp.full((1, HEAD_DIM), head_gate[i], f32) for i in range(feats // HEAD_DIM)], axis=1
    )
    rows[8:9, :feats] = branch[0] * cols
    rows[9:10, :feats] = branch[1] * cols
    rest = jnp.transpose(rows[...])[:feats, :]
    columns[...] = jnp.zeros_like(columns)
    for k in range(3):
        low = rest.astype(bf16)
        columns[:, k * VECTORS : (k + 1) * VECTORS] = low
        rest = rest - low.astype(f32)
    for send, ctx in ((send_core, ctx_core), (send_x, ctx_x)):
        n = ctx.shape[0]
        send[:n, :] = ctx[...]
        send[n:, :] = columns[...]


def place_vectors(p0, p1, p2, p3, b_in, gate, b_in_core, gate_core, vecs, unit_rows, cols):
    me, core = lax.axis_index("hid"), lax.axis_index("hid") & 1
    feats = cols.shape[0] // 4
    units = b_in.shape[0]
    for k, piece in enumerate((p0, p1.at[feats:, :], p2.at[2 * feats :, :], p3.at[2 * feats :, :])):
        parts = piece[...].astype(f32)
        cols[at(me ^ k, feats), :] = (
            parts[:, :VECTORS] + parts[:, VECTORS : 2 * VECTORS]
        ) + parts[:, 2 * VECTORS : 3 * VECTORS]
    vecs[...] = jnp.transpose(cols[...])
    for k, (one, two) in enumerate(((b_in, gate), (b_in_core, gate_core))):
        unit_rows[0:1, at(core ^ k, units)] = one[...].reshape(1, units)
        unit_rows[1:2, at(core ^ k, units)] = two[...].reshape(1, units)


def vector_outputs(
    branch, head_gate, vec, vecs, hidden_mask,
    g_qv, g_bout, g_bin, g_bback, g_gain, g_bias, g_head, g_inter, g_branch, g_hidden, cols,
):
    me = lax.axis_index("hid")
    feats = g_bout.shape[0]
    cols[...] = jnp.transpose(vec[0:8, :])
    own = jnp.transpose(cols[at(me, feats), :])
    g_gain[0:1, :] = own[0:1, :]
    g_gain[1:2, :] = own[4:5, :]
    g_bias[0:1, :] = own[1:2, :]
    g_bias[1:2, :] = own[5:6, :]
    g_bout[...] = own[2, :]
    g_bback[...] = own[6, :]
    mask = hidden_mask[...].astype(f32)
    g_hidden[...] = (branch[0] * own[3, :] + branch[1] * own[7, :]) * mask
    g_inter[...] = vec[8, :]
    g_bin[...] = vec[9, :]
    g_qv[0:1, :] = vec[10:11, :feats]
    rolled = vec[10:11, 2 * feats : 3 * feats]
    g_qv[1:2, :] = rolled
    lane = lax.broadcasted_iota(jnp.int32, (1, 128), 1)
    gates = jnp.ones((1, 128), f32)
    for i in range(feats // HEAD_DIM):
        gates = jnp.where(lane == i, head_gate[i], gates)
    g_head[...] = (vec[11:12, :128] / gates)[0, : feats // HEAD_DIM]
    part0 = jnp.sum(vec[3:4, :] * vecs[3:4, :], axis=1, keepdims=True)
    part1 = jnp.sum(vec[7:8, :] * vecs[3:4, :], axis=1, keepdims=True)
    both = jnp.where(lane == 0, part0, part1)
    g_branch[...] = both[0, :2]


def row_place():
    row = lax.axis_index("rows")
    return row & 1, (row >> 1) & 3


def first_add(keep, recv, total, send):
    total[...] = keep[...] + recv[...].astype(f32)
    send[...] = total[...].astype(bf16)


def first_add_pair(keep, pair, recv, total, send):
    n = keep.shape[0]
    total[...] = keep[...] + recv[:n, :].astype(f32)
    send[:n, :] = total[...].astype(bf16)
    send[n:, :] = high_low(pair_value(pair) + pair_value(recv[n:, :]))


def second_add(keep, recv, send):
    send[...] = (keep[...] + recv[...].astype(f32)).astype(bf16)


def second_add_pair(keep, mine, recv, send):
    n = keep.shape[0]
    send[:n, :] = (keep[...] + recv[:n, :].astype(f32)).astype(bf16)
    send[n:, :] = high_low(pair_value(mine[n:, :]) + pair_value(recv[n:, :]))


def third_add(mine, recv, total):
    total[...] = (mine[...].astype(f32) + recv[...].astype(f32)).astype(bf16)


def third_add_pair(mine, recv, total):
    n = mine.shape[0] - 32
    total[:n, :] = (mine[:n, :].astype(f32) + recv[:n, :].astype(f32)).astype(bf16)
    total[n:, :] = high_low(pair_value(mine[n:, :]) + pair_value(recv[n:, :]))


def choose(mine, recv, total):
    z = row_place()[1]
    outer = (z == 0) | (z == 3)
    total[...] = jnp.where(outer, recv[...], mine[...])


def choose_pair(mine, recv, total, vec):
    n = total.shape[0]
    z = row_place()[1]
    outer = (z == 0) | (z == 3)
    total[...] = jnp.where(outer, recv[:n, :], mine[:n, :])
    vec[...] = jnp.where(outer, pair_value(recv[n:, :]), pair_value(mine[n:, :]))


def split_owners(mine, recv, own, own_x, send):
    me = lax.axis_index("hid")
    n = own.shape[0]

    def rows(k):
        total = mine[at(me ^ k, n), :].astype(f32) + recv[at(me ^ k, n), :].astype(f32)
        return total.astype(bf16)

    own[...] = rows(0)
    own_x[...] = rows(2)
    send[:n, :] = rows(1)
    send[n:, :] = rows(3)


def join_owners(mine, from_core, from_x, chunk):
    me, n = lax.axis_index("hid"), mine.shape[0]
    chunk[at(me, n), :] = mine[...]
    chunk[at(me ^ 1, n), :] = from_core[:n, :]
    chunk[at(me ^ 2, n), :] = from_x[:n, :]
    chunk[at(me ^ 3, n), :] = from_x[n:, :]


def in_gradient(mine0, other0, mine1, other1, grad):
    y = row_place()[0]
    n = mine0.shape[0]
    for k, (mine, other) in enumerate(((mine0, other0), (mine1, other1))):
        grad[at(2 * k + y, n), :] = mine[...].astype(f32)
        grad[at(2 * k + (y ^ 1), n), :] = other[...].astype(f32)


def back_gradient(mine0, other0, mine1, other1, grad):
    y = row_place()[0]
    units = mine0.shape[1]
    n = mine0.shape[0] // 4
    for k, (mine, other) in enumerate(((mine0, other0), (mine1, other1))):
        for side, half in ((y, mine), (y ^ 1, other)):
            for owner in range(4):
                block = half[owner * n : (owner + 1) * n, :].astype(f32)
                grad[at(2 * k + side, n), owner * units : (owner + 1) * units] = block


def attn_gradients(qk_mine, qk_other, vo_mine, vo_other, grad_qkv, grad_out):
    y = row_place()[0]
    n = qk_mine.shape[0]
    grad_qkv[at(y, n), :] = qk_mine[...].astype(f32)
    grad_qkv[at(y ^ 1, n), :] = qk_other[...].astype(f32)
    mine, other = vo_mine[...].astype(f32), vo_other[...].astype(f32)
    grad_qkv[2 * n :, :] = jnp.where(y == 0, mine, other)
    grad_out[...] = jnp.where(y == 0, other, mine)


def second_half(mine, recv, both):
    n = mine.shape[0]
    both[:n, :] = mine[...]
    both[n:, :] = recv[n:, :]


EARLY_TURNS = "313"
TURNS = "41q3v2413241v2341q122vg132q4v12q4vg2qegvq"
FIRST = ("in0", "back0")


def along(block, way="y"):
    pairs = []
    for i in range(lax.axis_size("rows")):
        z = (i >> 1) & 3
        step = {
            "y": 1 - 2 * (i & 1),
            "in": {0: 2, 3: -2}.get(z),
            "mid": {1: 2, 2: -2}.get(z),
            "out": {1: -2, 2: 2}.get(z),
        }[way]
        if step is not None:
            pairs.append((i, i + step))
    return lax.ppermute(block, "rows", pairs)


class Turns:
    def __init__(self):
        self.last = ()

    def held(self, block):
        return after(block, *self.last) if self.last else block

    def mark(self, *blocks):
        self.last = blocks


def far_rows_sum(chunk):
    count = lax.axis_size("rows")
    if count == 8:
        return chunk
    groups = [[i + 8 * j for j in range(count // 8)] for i in range(8)]
    return lax.psum(chunk.astype(f32), "rows", axis_index_groups=groups).astype(chunk.dtype)


def shards(
    tokens, w_qkv, b_qv, w_out, b_out, w_in, b_in, w_back, b_back, norm_gain, norm_bias,
    head_gate, inter_gate, branch_gate, hidden_gate, hidden_mask, doc_lengths, cotangent,
):
    feats, toks = tokens.shape
    width = 4 * feats
    units = w_in.shape[1]
    block = toks // 4
    given = jnp.concatenate(
        [
            b_qv,
            jnp.pad(head_gate, (0, feats - head_gate.shape[0]))[None],
            jnp.pad(doc_lengths.astype(f32), ((0, 0), (0, feats - doc_lengths.shape[1]))),
        ],
        0,
    )
    bounds, small, out_half, back_half = local_kernel(
        begin,
        "begin",
        (given, w_out, w_back),
        "VVV",
        [
            sds((8, toks), jnp.int32),
            sds((8, 256), f32),
            sds((feats // 2, width), bf16),
            sds((feats, units), bf16),
        ],
    )
    tokens_x = swap(tokens, "hid", 2)
    tokens_core = swap(tokens, "hid", 1)
    x_own = swap(tokens_core, "hid", 1)
    out_xa = swap(out_half, "hid", 2)
    back_xa = swap(back_half, "hid", 2)
    wi_core = swap(w_in, "hid", 1)
    wo_core = swap(w_out, "hid", 1)
    cot_core = swap(after(cotangent, back_half), "hid", 1)
    b_in_core = swap(b_in, "hid", 1)
    gate_core = swap(inter_gate, "hid", 1)
    back_core = swap(w_back, "hid", 1)
    tokens_far = swap(
        after(tokens_x, tokens_core, wi_core, wo_core, cot_core, back_core, back_half), "hid", 1
    )

    head_block = sds((feats, block), bf16)
    two_blocks = sds((2 * feats, block), bf16)
    x_all, qkv, logsum, g0, g_core, g_x, x_block = local_kernel(
        attn_forward,
        "attn_forward",
        (
            bounds, small, x_own, tokens_core, tokens_x, tokens_far, w_qkv,
        ),
        "V" * 7,
        [
            sds((width, toks), bf16),
            sds((3, feats, toks), bf16),
            sds((8, toks), f32),
            head_block,
            head_block,
            two_blocks,
            sds((width, block), bf16),
        ],
        [pltpu.VMEM((feats, toks), bf16), pltpu.VMEM((toks, toks), f32)],
        micros=5.4,
    )
    send_core, send_x, columns = local_kernel(
        add_vectors,
        "add_vectors",
        (
            head_gate, branch_gate, after(b_out, x_block), norm_gain, norm_bias, hidden_gate,
            hidden_mask, b_back, g_core, g_x,
        ),
        "SS" + "V" * 8,
        [two_blocks, sds((3 * feats, block), bf16), head_block],
        [pltpu.VMEM((VECTORS, 256), f32)],
    )
    g2 = swap(send_x, "hid", 2)
    g1 = swap(send_core, "hid", 1)
    g3 = swap(after(g2, g1, b_in_core, gate_core), "hid", 1)
    out_xb = swap(after(out_xa, g0), "rows", 1)
    out_fa = swap(after(out_xa, g0), "hid", 1)
    out_fb = swap(out_xb, "hid", 1)
    back_xb = swap(after(back_xa, g1), "rows", 1)
    back_fa = swap(after(back_xa, g1), "hid", 1)
    (wo,) = local_kernel(
        place_rows,
        "place_rows",
        (w_out, wo_core, out_xa, out_xb, out_fa, out_fb),
        "VVVVVV",
        [sds((width, width), bf16)],
    )
    vecs, unit_rows = local_kernel(
        place_vectors,
        "place_vectors",
        (columns, g1, g2, g3, b_in, inter_gate, b_in_core, gate_core),
        "V" * 8,
        [sds((VECTORS, width), f32), sds((2, 2 * units), f32)],
        [pltpu.VMEM((width, VECTORS), f32)],
    )

    normed, n_send, hat, inv, attn_pre, gated_rows = local_kernel(
        attn_out,
        "attn_out",
        (g0, g1, g2, g3, x_block, vecs, wo, cotangent),
        "VVVVVVVV",
        [
            sds((block, width), f32),
            sds((block + feats // 3, width), bf16),
            sds((block, width), f32),
            sds((block, 128), f32),
            sds((block, width), f32),
            sds((block, width), bf16),
        ],
        [pltpu.VMEM((width, block), bf16)],
        micros=1.3,
    )

    n_x = swap(n_send, "hid", 2)
    n_core = swap(n_send, "hid", 1)
    back_fb = swap(after(back_xb, n_x), "hid", 1)
    wi, wb = local_kernel(
        place_units,
        "place_units",
        (w_in, wi_core, w_back, back_core, back_xa, back_xb, back_fa, back_fb),
        "V" * 8,
        [sds((width, 2 * units), bf16), sds((width, 2 * units), bf16)],
        micros=0.85,
    )

    act_block = sds((block, 2 * units), f32)
    half_block = sds((block, units), bf16)
    pair_block = sds((2 * block, units), bf16)
    rows_block = sds((block, width), bf16)
    ffn_scratch = [pltpu.VMEM((block, 2 * units), bf16)]
    act_x, slope_x, e1, inter_core, ffn_send = local_kernel(
        ffn_forward_far,
        "ffn_forward_far",
        (n_x, unit_rows, wi, wb),
        "VVVV",
        [act_block, act_block, half_block, half_block, rows_block],
        ffn_scratch,
        micros=1.85,
    )
    ffn_recv = swap(ffn_send, "hid", 2)
    act, slope, e0, ffn_part, e_pair = local_kernel(
        ffn_forward,
        "ffn_forward",
        (after(n_send, ffn_send), unit_rows, wi, wb, inter_core),
        "VVVVV",
        [act_block, act_block, half_block, sds((block, width), f32), pair_block],
        ffn_scratch,
        micros=1.85,
    )
    n_far = swap(after(n_x, ffn_send), "hid", 1)

    out_block = sds((feats, block), bf16)
    gffn, dres2, sums2, res_mine, res_x, res_send = local_kernel(
        second_norm,
        "second_norm",
        (
            after(ffn_part, n_core), ffn_recv, normed, cotangent, cot_core, n_x, n_far, vecs,
        ),
        "V" * 8,
        [
            sds((block, width), bf16),
            sds((block, width), f32),
            sds((4, width), f32),
            out_block,
            out_block,
            sds((2 * feats, block), bf16),
        ],
        [pltpu.VMEM((width, block), bf16), pltpu.VMEM((width, block), bf16)],
        micros=1.2,
    )

    gffn_x = swap(gffn, "hid", 2)
    e_core = swap(after(e_pair, gffn), "hid", 1)
    f2 = swap(gffn, "hid", 1)
    sums_block = sds((8, 2 * units), f32)
    p0, gpre_core, gn_part, ig_sum = local_kernel(
        ffn_backward,
        "ffn_backward",
        (gffn, act, slope, unit_rows, wi, wb),
        "VVVVVV",
        [half_block, half_block, sds((block, width), f32), sums_block],
        ffn_scratch,
        micros=1.85,
    )
    p1, gn_send, ig_mine, p_pair = local_kernel(
        ffn_backward_far,
        "ffn_backward_far",
        (after(gffn_x, f2, e_core), act_x, slope_x, unit_rows, wi, wb, gpre_core, ig_sum),
        "VVVVVVVV",
        [half_block, rows_block, sds((8, units), f32), sds((2 * block + 16, units), bf16)],
        ffn_scratch + [pltpu.VMEM((8, 2 * units), f32)],
        micros=1.85,
    )
    gn_recv = swap(gn_send, "hid", 2)
    f3 = swap(after(gffn_x, gn_send), "hid", 1)
    p_core = swap(p_pair, "hid", 1)
    *pieces, bin_sum = local_kernel(
        ffn_weight_grads,
        "ffn_weight_grads",
        (
            n_send, n_x, n_core, n_far, e0, e1, e_core,
            p0, p1, p_core, gffn, gffn_x, f2, f3,
        ),
        "V" * 14,
        [
            sds((feats, units), f32),
            sds((feats, units), bf16),
            sds((feats, units), f32),
            sds((feats, units), bf16),
            sds((feats, units), f32),
            sds((feats, units), bf16),
            sds((feats, units), f32),
            sds((feats, units), bf16),
            sds((8, units), f32),
        ],
        [
            pltpu.VMEM((toks, width), bf16),
            pltpu.VMEM((toks, units), bf16),
            pltpu.VMEM((width, units), f32),
        ],
        micros=2.5,
    )

    pieces = dict(zip(("back0", "back1", "in0", "in1"), zip(pieces[0::2], pieces[1::2])))
    early = {name: along(after(pieces[name][1], gn_recv)) for name in FIRST}

    sum_rows = 16 * width // 128
    dres1, gattn, sums1, u0, up_core, up_x = local_kernel(
        attn_out_back,
        "attn_out_back",
        (
            after(gn_part, pieces["in1"][1]), gn_recv, dres2, hat, inv, attn_pre,
            vecs, wo, sums2,
        ),
        "V" * 9,
        [
            sds((block, width), f32),
            sds((block, width), bf16),
            sds((8, width), f32),
            head_block,
            sds((feats + sum_rows, block), bf16),
            sds((2 * feats + sum_rows, block), bf16),
        ],
        [pltpu.VMEM((width, block), bf16)],
        micros=1.3,
    )
    u2 = swap(up_x, "hid", 2)
    u1 = swap(up_core, "hid", 1)
    u3 = swap(u2, "hid", 1)

    weight_block = sds((feats, width), f32)
    low_block = sds((feats, width), bf16)
    wo_mine, wo_keep, wo_send = local_kernel(
        out_weight_grad,
        "out_weight_grad",
        (gattn, gated_rows),
        "VV",
        [weight_block, weight_block, sds((2 * feats, width), bf16)],
        [pltpu.VMEM((width, width), f32)],
        micros=1.2,
    )
    wo_grad_core = swap(after(wo_send, u1), "hid", 1)

    turns = Turns()
    results = {}
    whole_block = sds((feats, width), f32)

    def step(body, args, outs, **more):
        outs = local_kernel(
            body, body.__name__, (turns.held(args[0]),) + args[1:], "V" * len(args), outs, **more
        )
        turns.mark(*outs[-1:])
        return outs

    def sum_chain(name, keep, send, recv=None):
        if recv is None:
            recv = along(turns.held(send))
        yield
        keep, send = step(first_add, (keep, recv), [whole_block, low_block])
        recv = along(send, "in")
        yield
        (mine,) = step(second_add, (keep, recv), [low_block])
        recv = along(mine, "mid")
        yield
        if name.startswith("back"):
            part = sds((feats // 4, units), bf16)
            two = sds((feats // 2, units), bf16)
            mine, mine_x, send = step(split_owners, (mine, recv), [part, part, two])
            from_core = swap(send, "hid", 1)
            yield
            (send,) = step(second_half, (mine_x, from_core), [two])
            from_x = swap(send, "hid", 2)
            yield
            (mine,) = step(join_owners, (mine, from_core, from_x), [low_block])
        else:
            (mine,) = step(third_add, (mine, recv), [low_block])
        recv = along(mine, "out")
        yield
        (mine,) = step(choose, (mine, recv), [low_block])
        yield from last_part(name, mine)

    def last_part(name, mine):
        mine = far_rows_sum(mine)
        other = along(mine)
        yield
        results[name] = (mine, other)
        if name in ("in0", "in1") and "in0" in results and "in1" in results:
            (results["w_in"],) = step(
                in_gradient,
                results["in0"] + results["in1"],
                [sds((width, units), f32)],
                micros=2.1,
            )
        if name in ("back0", "back1") and "back0" in results and "back1" in results:
            (results["w_back"],) = step(
                back_gradient,
                results["back0"] + results["back1"],
                [sds((feats, 4 * units), f32)],
                micros=2.1,
            )
        if name in ("qk", "vo") and "qk" in results and "vo" in results:
            results["w_qkv"], results["w_out"] = step(
                attn_gradients,
                results["qk"] + results["vo"],
                [sds((3 * feats, width), f32), weight_block],
                micros=2.1,
            )

    chains = {
        key: sum_chain(name, *pieces[name], early.get(name))
        for key, name in zip("1234", ("back0", "back1", "in0", "in1"))
    }
    turns.mark(u1)
    for turn in EARLY_TURNS:
        next(chains[turn], None)
    grads, head_sums, bias_sums = local_kernel(
        attn_backward,
        "attn_backward",
        (bounds, turns.held(qkv), logsum, u0, u1, u2, u3),
        "V" * 7,
        [
            sds((3 * feats, toks), bf16),
            sds((8, block), f32),
            sds((8, 3 * feats), f32),
        ],
        [pltpu.VMEM((feats, toks), bf16), pltpu.VMEM((toks, toks), f32)],
        micros=5.0,
    )
    (wo_low,) = local_kernel(add_second, "wo_low", (wo_keep, wo_grad_core), "VV", [low_block])
    wo_far = swap(after(wo_low, u3), "hid", 2)

    gx_block = sds((feats, toks), f32)
    gx_low = sds((feats, toks), bf16)

    def qk_chain():
        with_pair = sds((feats + 32, width), bf16)
        keep, send, pair = local_kernel(
            qk_weight_grad,
            "qk_weight_grad",
            (
                turns.held(grads), x_all, sums1, u1, u2, u3, ig_mine, p_core, bin_sum,
                head_sums, bias_sums,
            ),
            "V" * 11,
            [weight_block, with_pair, sds((32, width), bf16)],
            [pltpu.VMEM((2 * feats, width), f32), pltpu.VMEM((16, width), f32)],
            micros=1.2,
        )
        turns.mark(send)
        recv = along(send)
        yield
        keep, send = step(first_add_pair, (keep, pair, recv), [weight_block, with_pair])
        recv = along(send, "in")
        yield
        (mine,) = step(second_add_pair, (keep, send, recv), [with_pair])
        recv = along(mine, "mid")
        yield
        (mine,) = step(third_add_pair, (mine, recv), [with_pair])
        recv = along(mine, "out")
        yield
        mine, results["sums"] = step(
            choose_pair, (mine, recv), [low_block, sds((16, width), f32)]
        )
        yield from last_part("qk", mine)

    def vo_chain():
        keep, send = local_kernel(
            vo_weight_grad,
            "vo_weight_grad",
            (turns.held(grads), x_all, wo_mine, wo_grad_core, wo_far),
            "VVVVV",
            [weight_block, low_block],
            [pltpu.VMEM((2 * feats, width), f32)],
            micros=1.1,
        )
        turns.mark(send)
        yield from sum_chain("vo", keep, send, along(send))

    def tokens_chain():
        mine, mine_x, send = local_kernel(
            qkv_input_grad,
            "qkv_input_grad",
            (turns.held(grads), w_qkv, dres1, res_send),
            "VVVV",
            [gx_block, gx_block, sds((2 * feats, toks + block), bf16)],
            [pltpu.VMEM((width, toks), f32)],
            micros=1.5,
        )
        turns.mark(send)
        from_core = swap(send, "hid", 1)
        yield
        (send,) = local_kernel(
            tokens_step,
            "tokens_step",
            (turns.held(mine_x), res_x, from_core),
            "VVV",
            [sds((feats, toks + 2 * block), bf16)],
        )
        turns.mark(send)
        from_x = swap(send, "hid", 2)
        yield
        results["tokens"], results["output"] = local_kernel(
            tokens_outputs,
            "tokens_outputs",
            (turns.held(mine), res_mine, from_core, from_x),
            "VVVV",
            [gx_low, gx_low],
            micros=1.2,
        )
        turns.mark(results["tokens"])

    def vector_chain():
        results["vectors"] = local_kernel(
            vector_outputs,
            "vector_outputs",
            (branch_gate, head_gate, far_rows_sum(turns.held(results["sums"])), vecs, hidden_mask),
            "SSVVV",
            [
                sds((2, feats), f32),
                sds((feats,), f32),
                sds((units,), f32),
                sds((feats,), f32),
                sds((2, feats), f32),
                sds((2, feats), f32),
                sds((feats // HEAD_DIM,), f32),
                sds((units,), f32),
                sds((2,), f32),
                sds((feats,), f32),
            ],
            [pltpu.VMEM((width, 8), f32)],
            micros=1.4,
        )
        turns.mark(results["vectors"][0])
        yield

    chains.update(q=qk_chain(), v=vo_chain(), g=tokens_chain(), e=vector_chain())
    turns.mark(grads)
    for turn in TURNS:
        next(chains[turn], None)
    (
        grad_b_qv, grad_b_out, grad_b_in, grad_b_back, grad_norm_gain, grad_norm_bias,
        grad_head_gate, grad_inter_gate, grad_branch_gate, grad_hidden_gate,
    ) = results["vectors"]
    output, grad_tokens = results["output"], results["tokens"]
    grad_w_qkv = results["w_qkv"].reshape(3, feats, width)
    grad_w_out, grad_w_in, grad_w_back = results["w_out"], results["w_in"], results["w_back"]
    return (
        output,
        grad_tokens,
        grad_w_qkv,
        grad_b_qv,
        grad_w_out,
        grad_b_out,
        grad_w_in,
        grad_b_in,
        grad_w_back,
        grad_b_back,
        grad_norm_gain,
        grad_norm_bias,
        grad_head_gate,
        grad_inter_gate,
        grad_branch_gate,
        grad_hidden_gate,
    )


def solution(mesh):
    return jax.shard_map(
        shards,
        mesh=mesh,
        in_specs=(
            P("hid", "rows"),
            P(None, "hid", None),
            P(None, "hid"),
            P("hid", None),
            P("hid"),
            P(None, "hid"),
            P("hid"),
            P("hid", None),
            P("hid"),
            P(None, "hid"),
            P(None, "hid"),
            P("hid"),
            P("hid"),
            P(),
            P("hid"),
            P("hid"),
            P("rows", None),
            P("hid", "rows"),
        ),
        out_specs=(
            P("hid", "rows"),
            P("hid", "rows"),
            P(None, "hid", None),
            P(None, "hid"),
            P("hid", None),
            P("hid"),
            P(None, "hid"),
            P("hid"),
            P("hid", None),
            P("hid"),
            P(None, "hid"),
            P(None, "hid"),
            P("hid"),
            P("hid"),
            P(),
            P("hid"),
        ),
        check_vma=False,
    )
```

time: 195 us -> 178 us (0.913)
  waiting for transfers between devices: 102 us -> 75.5 us
  starting transfers between devices: 53.4 us -> 68 us
  Pallas kernels: 34.4 us -> 27.9 us
    ppermute x71 -> x42, waiting for transfers between devices: 102 us -> 33.6 us  [swap(): lax.ppermute(block, axis, [(i, i ^ bit) for i in range(lax.axis_size(axis...]
    ppermute x0 -> x30, waiting for transfers between devices: none -> 41.9 us  [along(): return lax.ppermute(block, 'rows', pairs)]
    ppermute x0 -> x30, starting transfers between devices: none -> 39.9 us  [along(): return lax.ppermute(block, 'rows', pairs)]
    ppermute x71 -> x42, starting transfers between devices: 53.4 us -> 28 us  [swap(): lax.ppermute(block, axis, [(i, i ^ bit) for i in range(lax.axis_size(axis...]
    pallas_call x56 -> x54, Pallas kernels: 34.4 us -> 27.9 us  [local_kernel(): pl.pallas_call(body, name=name, out_shape=outs, in_specs=[SPECS[k] for k...]
  transfers between devices with their start and end apart: 71 -> 72, of which waited for: 39 -> 30; matrix products, arithmetic and copies ran while one was open for 0% -> 1% of each run, Pallas kernels for 13% -> 13%
where the time goes in v3:
time: 178 us; the launch traced here: 177 us
  waiting for transfers between devices  75.5 us (42%)
  starting transfers between devices  68 us (38%)
  Pallas kernels  27.9 us (16%)
  local copies, waits for them, and re-layouts  2.95 us (2%)
    ppermute x30, waiting for transfers between devices, along(): return lax.ppermute(block, 'rows', pairs)  41.9 us
    ppermute x30, starting transfers between devices, along(): return lax.ppermute(block, 'rows', pairs)  39.9 us
    ppermute x42, waiting for transfers between devices, swap(): lax.ppermute(block, axis, [(i, i ^ bit) for i in range(lax.axis_size(axis...  33.6 us
    ppermute x42, starting transfers between devices, swap(): lax.ppermute(block, axis, [(i, i ^ bit) for i in range(lax.axis_size(axis...  28 us
    pallas_call x54, Pallas kernels, local_kernel(): pl.pallas_call(body, name=name, out_shape=outs, in_specs=[SPECS[k] for k...  27.9 us
  transfers between devices with their start and end apart: 72, of which 30 were waited for; matrix products, arithmetic and copies ran while one was open for 1% of the time, Pallas kernels for 13%

profile of v3, /device:TPU:0, one launch (start us, length us, event | category | flops | bytes accessed | tf_op | source)
XLA Modules:
  0.0 177.2 jit_solution(3572187404053574073)
XLA Ops:
  1.3 2.9 %collective-permute-start.2 = (bf16[192,512]{1,0:T(8,128)(2,1)}, bf16[192,512]{1,0:T(8,128)(2,1)S(1)}, u32[]{:S(2)}, u32[]{:S(2)}) collective-permute-start(bf16[192,512]{1,0:T(8,128)(2,1)} %param.18), channel_id=1, source_target_pairs={{0,2},{1,3},{2,0},{3,1},{4,6},{5,7},{6,4},{7,5},{8,10},{9,11},{10,... | collective-permute-start | bytes 589832 | tf_op jit(solution)/shard_map/ppermute | solution.py:24
  6.8 1.3 copy-done
  10.1 1.3 collective-permute-done.5.cot1
  11.7 1.8 %collective-permute-start.13 = (bf16[96,768]{1,0:T(8,128)(2,1)S(1)}, bf16[96,768]{1,0:T(8,128)(2,1)S(1)}, u32[]{:S(2)}, u32[]{:S(2)}) collective-permute-start(bf16[96,768]{1,0:T(8,128)(2,1)S(1)} %get-tuple-element.200), channel_id=1, source_target_pairs={{0,2},{1,3},{2,0},{3,1},{4,6},{5,7},{6,4},{7,5},{8,10},{9,11},{10,... | collective-permute-start | bytes 442376 | tf_op jit(solution)/shard_map/ppermute | solution.py:24
  13.7 2.6 %attn_forward.1 = (bf16[768,512]{1,0:T(8,128)(2,1)S(1)}, bf16[3,192,512]{2,1,0:T(8,128)(2,1)S(1)}, f32[8,512]{1,0:T(8,128)S(1)}, bf16[192,128]{1,0:T(8,128)(2,1)...) custom-call(s32[8,512]{1,0:T(8,128)S(1)} %get-tuple-element.184.bounds, ...), custom_call_target="tpu_custom_call" | custom-call | flops 1 | bytes 19926000 | tf_op jit(solution)/shard_map/attn_forward/pallas_call | solution.py:36
  17.1 1.8 %collective-permute-start.9 = (bf16[576,128]{1,0:T(8,128)(2,1)S(1)}, bf16[576,128]{1,0:T(8,128)(2,1)S(1)}, u32[]{:S(2)}, u32[]{:S(2)}) collective-permute-start(bf16[576,128]{1,0:T(8,128)(2,1)S(1)} %get-tuple-element.196), channel_id=1, source_target_pairs={{0,2},{1,3},{2,0},{3,1},{4,6},{5,7},{6,4},{7,5},{8,10},{9,11},{10,... | collective-permute-start | bytes 442376 | tf_op jit(solution)/shard_map/ppermute | solution.py:24
  19.0 1.5 collective-permute-start.14
  23.0 4.3 %collective-permute-done.9.p2.g2 = bf16[576,128]{1,0:T(8,128)(2,1)S(1)} collective-permute-done((bf16[576,128]{1,0:T(8,128)(2,1)S(1)}, bf16[576,128]{1,0:T(8,128)(2,1)S(1)}, u32[]{:S(2)}, u32[]{:S(2)}) %collective-permute-start.9) | collective-permute-done | bytes 147488 | tf_op jit(solution)/shard_map/ppermute | solution.py:24
  27.8 1.8 %collective-permute-start.20 = (bf16[192,768]{1,0:T(8,128)(2,1)S(1)}, bf16[192,768]{1,0:T(8,128)(2,1)S(1)}, u32[]{:S(2)}, u32[]{:S(2)}) collective-permute-start(bf16[192,768]{1,0:T(8,128)(2,1)S(1)} %collective-permute-done.19.xa), channel_id=1, source_target_pairs={{0,4},{4,0},{8,12},{12,8},{16,20},{20,16},{24,28},{28,24},{1,5},{5... | collective-permute-start | bytes 884744 | tf_op jit(solution)/shard_map/ppermute | solution.py:24
  30.9 1.6 collective-permute-start.17
  32.4 4.8 %collective-permute-done.20.xb = bf16[192,768]{1,0:T(8,128)(2,1)S(1)} collective-permute-done((bf16[192,768]{1,0:T(8,128)(2,1)S(1)}, bf16[192,768]{1,0:T(8,128)(2,1)S(1)}, u32[]{:S(2)}, u32[]{:S(2)}) %collective-permute-start.20) | collective-permute-done | bytes 294944 | tf_op jit(solution)/shard_map/ppermute | solution.py:24
  37.2 2.8 %collective-permute-done.17.rows.n_x.n1 = bf16[192,768]{1,0:T(8,128)(2,1)S(1)} collective-permute-done((bf16[192,768]{1,0:T(8,128)(2,1)S(1)}, bf16[192,768]{1,0:T(8,128)(2,1)S(1)}, u32[]{:S(2)}, u32[]{:S(2)}) %collective-permute-start.17) | collective-permute-done | bytes 294944 | tf_op jit(solution)/shard_map/ppermute | solution.py:24
  40.5 1.1 collective-permute-done.22.fb
  42.0 1.3 ffn_forward_far.1
  43.5 1.5 collective-permute-start.24
  45.0 1.3 ffn_forward.1
  46.3 4.3 %collective-permute-done.24.recv = bf16[128,768]{1,0:T(8,128)(2,1)S(1)} collective-permute-done((bf16[128,768]{1,0:T(8,128)(2,1)S(1)}, bf16[128,768]{1,0:T(8,128)(2,1)S(1)}, u32[]{:S(2)}, u32[]{:S(2)}) %collective-permute-start.24) | collective-permute-done | bytes 196640 | tf_op jit(solution)/shard_map/ppermute | solution.py:24
  51.9 1.5 collective-permute-start.26
  53.4 1.3 ffn_backward.1
  54.7 4.1 %collective-permute-done.26.rows.f1 = bf16[128,768]{1,0:T(8,128)(2,1)S(1)} collective-permute-done((bf16[128,768]{1,0:T(8,128)(2,1)S(1)}, bf16[128,768]{1,0:T(8,128)(2,1)S(1)}, u32[]{:S(2)}, u32[]{:S(2)}) %collective-permute-start.26) | collective-permute-done | bytes 196640 | tf_op jit(solution)/shard_map/ppermute | solution.py:24
  58.8 1.3 ffn_backward_far.1
  60.7 1.5 collective-permute-start.30
  62.2 1.9 %ffn_weight_grads.1 = (f32[192,768]{1,0:T(8,128)S(1)}, bf16[192,768]{1,0:T(8,128)(2,1)S(1)}, f32[192,768]{1,0:T(8,128)S(1)}, bf16[192,768]{1,0:T(8,128)(2,1)S(1)...) custom-call(bf16[192,768]{1,0:T(8,128)(2,1)S(1)} %get-tuple-element., ...), custom_call_target="tpu_custom_call" | custom-call | flops 1 | bytes 9225000 | tf_op jit(solution)/shard_map/ffn_weight_grads/pallas_call | solution.py:36
  64.1 3.5 %collective-permute-done.30.recv = bf16[128,768]{1,0:T(8,128)(2,1)S(1)} collective-permute-done((bf16[128,768]{1,0:T(8,128)(2,1)S(1)}, bf16[128,768]{1,0:T(8,128)(2,1)S(1)}, u32[]{:S(2)}, u32[]{:S(2)}) %collective-permute-start.30) | collective-permute-done | bytes 196640 | tf_op jit(solution)/shard_map/ppermute | solution.py:24
  70.9 1.5 collective-permute-start.33
  72.4 3.8 %collective-permute-done.33.u2 = bf16[480,128]{1,0:T(8,128)(2,1)S(1)} collective-permute-done((bf16[480,128]{1,0:T(8,128)(2,1)S(1)}, bf16[480,128]{1,0:T(8,128)(2,1)S(1)}, u32[]{:S(2)}, u32[]{:S(2)}) %collective-permute-start.33) | collective-permute-done | bytes 122912 | tf_op jit(solution)/shard_map/ppermute | solution.py:24
  76.2 1.0 collective-permute-start.35
  77.2 1.9 %collective-permute-done.32.recv = bf16[192,768]{1,0:T(8,128)(2,1)S(1)} collective-permute-done((bf16[192,768]{1,0:T(8,128)(2,1)S(1)}, bf16[192,768]{1,0:T(8,128)(2,1)S(1)}, u32[]{:S(2)}, u32[]{:S(2)}) %collective-permute-start.32) | collective-permute-done | bytes 294944 | tf_op jit(solution)/shard_map/ppermute | solution.py:746
  79.3 3.5 %collective-permute-start.36 = (bf16[192,768]{1,0:T(8,128)(2,1)S(1)}, bf16[192,768]{1,0:T(8,128)(2,1)S(1)}, u32[]{:S(2)}, u32[]{:S(2)}) collective-permute-start(bf16[192,768]{1,0:T(8,128)(2,1)S(1)} %get-tuple-element.245), channel_id=1, source_target_pairs={{0,8},{4,12},{24,16},{28,20},{1,9},{5,13},{25,17},{29,21},{2,10},{... | collective-permute-start | bytes 884744 | tf_op jit(solution)/shard_map/ppermute | solution.py:746
  82.9 1.6 collective-permute-start.38
  84.5 2.6 %attn_backward.1 = (bf16[576,512]{1,0:T(8,128)(2,1)S(1)}, f32[8,128]{1,0:T(8,128)S(1)}, f32[8,576]{1,0:T(8,128)S(1)}) custom-call(s32[8,512]{1,0:T(8,128)S(1)} %get-tuple-element.184.bounds, bf16[3,192,512]{2,1,0:T(8,128)(2,1)S(1)} %get-tuple-element.246.qkv, f32[8,512]{1,0:T(8,128)S(1)} %get-tuple-element.247.logsum, ...), custom_call_target="tpu_custom_call" | custom-call | flops 1 | bytes 18450000 | tf_op jit(solution)/shard_map/attn_backward/pallas_call | solution.py:36
  88.2 1.3 collective-permute-start.40
  92.7 4.0 %collective-permute-done.39.recv = bf16[192,768]{1,0:T(8,128)(2,1)S(1)} collective-permute-done((bf16[192,768]{1,0:T(8,128)(2,1)S(1)}, bf16[192,768]{1,0:T(8,128)(2,1)S(1)}, u32[]{:S(2)}, u32[]{:S(2)}) %collective-permute-start.39) | collective-permute-done | bytes 294944 | tf_op jit(solution)/shard_map/ppermute | solution.py:746
  96.8 1.6 collective-permute-start.43
  99.2 1.1 collective-permute-start.45
  100.4 2.6 %collective-permute-done.42.recv = bf16[192,768]{1,0:T(8,128)(2,1)S(1)} collective-permute-done((bf16[192,768]{1,0:T(8,128)(2,1)S(1)}, bf16[192,768]{1,0:T(8,128)(2,1)S(1)}, u32[]{:S(2)}, u32[]{:S(2)}) %collective-permute-start.42) | collective-permute-done | bytes 294944 | tf_op jit(solution)/shard_map/ppermute | solution.py:746
  103.1 1.9 %collective-permute-start.46 = (bf16[192,768]{1,0:T(8,128)(2,1)S(1)}, bf16[192,768]{1,0:T(8,128)(2,1)S(1)}, u32[]{:S(2)}, u32[]{:S(2)}) collective-permute-start(bf16[192,768]{1,0:T(8,128)(2,1)S(1)} %get-tuple-element.288), channel_id=1, source_target_pairs={{0,8},{4,12},{24,16},{28,20},{1,9},{5,13},{25,17},{29,21},{2,10},{... | collective-permute-start | bytes 884744 | tf_op jit(solution)/shard_map/ppermute | solution.py:746
  105.0 1.3 collective-permute-start.47
  110.0 3.7 %collective-permute-done.47.recv = bf16[192,768]{1,0:T(8,128)(2,1)S(1)} collective-permute-done((bf16[192,768]{1,0:T(8,128)(2,1)S(1)}, bf16[192,768]{1,0:T(8,128)(2,1)S(1)}, u32[]{:S(2)}, u32[]{:S(2)}) %collective-permute-start.47) | collective-permute-done | bytes 294944 | tf_op jit(solution)/shard_map/ppermute | solution.py:746
  113.8 1.4 collective-permute-start.51
  115.2 5.8 %collective-permute-start.54 = (bf16[192,768]{1,0:T(8,128)(2,1)S(1)}, bf16[192,768]{1,0:T(8,128)(2,1)S(1)}, u32[]{:S(2)}, u32[]{:S(2)}) collective-permute-start(bf16[192,768]{1,0:T(8,128)(2,1)S(1)} %get-tuple-element.295), channel_id=1, source_target_pairs={{0,8},{4,12},{24,16},{28,20},{1,9},{5,13},{25,17},{29,21},{2,10},{... | collective-permute-start | bytes 884744 | tf_op jit(solution)/shard_map/ppermute | solution.py:746
  121.1 1.3 collective-permute-start.57
  122.5 1.3 collective-permute-start.55
  123.9 1.3 collective-permute-start.58
  126.2 2.2 %collective-permute-done.54.recv = bf16[192,768]{1,0:T(8,128)(2,1)S(1)} collective-permute-done((bf16[192,768]{1,0:T(8,128)(2,1)S(1)}, bf16[192,768]{1,0:T(8,128)(2,1)S(1)}, u32[]{:S(2)}, u32[]{:S(2)}) %collective-permute-start.54) | collective-permute-done | bytes 294944 | tf_op jit(solution)/shard_map/ppermute | solution.py:746
  129.1 1.1 qkv_input_grad.1
  130.2 3.8 %collective-permute-done.55.recv = bf16[192,768]{1,0:T(8,128)(2,1)S(1)} collective-permute-done((bf16[192,768]{1,0:T(8,128)(2,1)S(1)}, bf16[192,768]{1,0:T(8,128)(2,1)S(1)}, u32[]{:S(2)}, u32[]{:S(2)}) %collective-permute-start.55) | collective-permute-done | bytes 294944 | tf_op jit(solution)/shard_map/ppermute | solution.py:746
  134.9 1.3 collective-permute-start.60
  136.2 1.2 collective-permute-start.62
  138.0 1.1 collective-permute-start.63
  139.2 5.4 %collective-permute-done.60.recv = bf16[192,768]{1,0:T(8,128)(2,1)S(1)} collective-permute-done((bf16[192,768]{1,0:T(8,128)(2,1)S(1)}, bf16[192,768]{1,0:T(8,128)(2,1)S(1)}, u32[]{:S(2)}, u32[]{:S(2)}) %collective-permute-start.60) | collective-permute-done | bytes 294944 | tf_op jit(solution)/shard_map/ppermute | solution.py:746
  144.7 1.3 collective-permute-start.68
  146.0 1.3 collective-permute-start.64
  148.4 1.7 collective-permute-done.63.other1
  150.0 1.1 collective-permute-start.67
  151.1 1.6 in_gradient.1
  152.7 9.1 %collective-permute-done.64.recv = bf16[192,768]{1,0:T(8,128)(2,1)S(1)} collective-permute-done((bf16[192,768]{1,0:T(8,128)(2,1)S(1)}, bf16[192,768]{1,0:T(8,128)(2,1)S(1)}, u32[]{:S(2)}, u32[]{:S(2)}) %collective-permute-start.64) | collective-permute-done | bytes 294944 | tf_op jit(solution)/shard_map/ppermute | solution.py:746
  161.9 1.1 collective-permute-start.69
  163.9 1.6 back_gradient.1
  165.5 1.2 collective-permute-start.70
  166.7 1.4 vector_outputs.1
  169.6 2.8 %collective-permute-done.71.vo_other = bf16[192,768]{1,0:T(8,128)(2,1)S(1)} collective-permute-done((bf16[192,768]{1,0:T(8,128)(2,1)S(1)}, bf16[192,768]{1,0:T(8,128)(2,1)S(1)}, u32[]{:S(2)}, u32[]{:S(2)}) %collective-permute-start.71) | collective-permute-done | bytes 294944 | tf_op jit(solution)/shard_map/ppermute | solution.py:746
  172.4 3.2 %collective-permute-done.70.qk_other = bf16[192,768]{1,0:T(8,128)(2,1)S(1)} collective-permute-done((bf16[192,768]{1,0:T(8,128)(2,1)S(1)}, bf16[192,768]{1,0:T(8,128)(2,1)S(1)}, u32[]{:S(2)}, u32[]{:S(2)}) %collective-permute-start.70) | collective-permute-done | bytes 294944 | tf_op jit(solution)/shard_map/ppermute | solution.py:746
  175.6 1.6 attn_gradients.1
  (171 shorter events, 33.3 us)
Async XLA Ops:
  0.7 10.7 %collective-permute-start.3 = (bf16[768,768]{1,0:T(8,128)(2,1)}, bf16[768,768]{1,0:T(8,128)(2,1)S(1)}, u32[]{:S(2)}, u32[]{:S(2)}) collective-permute-start(bf16[768,768]{1,0:T(8,128)(2,1)} %wi_own.1), channel_id=1, source_target_pairs={{0,1},{1,0},{2,3},{3,2},{4,5},{5,4},{6,7},{7,6},{8,9},{9,8},{10,11... | collective-permute-start | bytes 3538952 | tf_op jit(solution)/shard_map/ppermute | solution.py:24
  1.2 10.2 %collective-permute-start.6 = (bf16[192,3072]{1,0:T(8,128)(2,1)}, bf16[192,3072]{1,0:T(8,128)(2,1)S(1)}, u32[]{:S(2)}, u32[]{:S(2)}) collective-permute-start(bf16[192,3072]{1,0:T(8,128)(2,1)} %own.3), channel_id=1, source_target_pairs={{0,1},{1,0},{2,3},{3,2},{4,5},{5,4},{6,7},{7,6},{8,9},{9,8},{10,11... | collective-permute-start | bytes 3538952 | tf_op jit(solution)/shard_map/ppermute | solution.py:24
  1.3 8.3 %collective-permute-start.2 = (bf16[192,512]{1,0:T(8,128)(2,1)}, bf16[192,512]{1,0:T(8,128)(2,1)S(1)}, u32[]{:S(2)}, u32[]{:S(2)}) collective-permute-start(bf16[192,512]{1,0:T(8,128)(2,1)} %param.18), channel_id=1, source_target_pairs={{0,2},{1,3},{2,0},{3,1},{4,6},{5,7},{6,4},{7,5},{8,10},{9,11},{10,... | collective-permute-start | bytes 589832 | tf_op jit(solution)/shard_map/ppermute | solution.py:24
  4.2 7.2 %collective-permute-start.4 = (bf16[192,768]{1,0:T(8,128)(2,1)}, bf16[192,768]{1,0:T(8,128)(2,1)S(1)}, u32[]{:S(2)}, u32[]{:S(2)}) collective-permute-start(bf16[192,768]{1,0:T(8,128)(2,1)} %own.2), channel_id=1, source_target_pairs={{0,1},{1,0},{2,3},{3,2},{4,5},{5,4},{6,7},{7,6},{8,9},{9,8},{10,11... | collective-permute-start | bytes 884744 | tf_op jit(solution)/shard_map/ppermute | solution.py:24
  6.2 3.4 %collective-permute-start = (bf16[192,512]{1,0:T(8,128)(2,1)}, bf16[192,512]{1,0:T(8,128)(2,1)S(1)}, u32[]{:S(2)}, u32[]{:S(2)}) collective-permute-start(bf16[192,512]{1,0:T(8,128)(2,1)} %param.18), channel_id=1, source_target_pairs={{0,1},{1,0},{2,3},{3,2},{4,5},{5,4},{6,7},{7,6},{8,9},{9,8},{10,11... | collective-permute-start | bytes 589832 | tf_op jit(solution)/shard_map/ppermute | solution.py:24
  9.6 4.1 %collective-permute-start.1 = (bf16[192,512]{1,0:T(8,128)(2,1)S(1)}, bf16[192,512]{1,0:T(8,128)(2,1)S(1)}, u32[]{:S(2)}, u32[]{:S(2)}) collective-permute-start(bf16[192,512]{1,0:T(8,128)(2,1)S(1)} %collective-permute-done.x1), channel_id=1, source_target_pairs={{0,1},{1,0},{2,3},{3,2},{4,5},{5,4},{6,7},{7,6},{8,9},{9,8},{10,11... | collective-permute-start | bytes 589832 | tf_op jit(solution)/shard_map/ppermute | solution.py:24
  11.5 2.2 %collective-permute-start.7 = (bf16[192,512]{1,0:T(8,128)(2,1)S(1)}, bf16[192,512]{1,0:T(8,128)(2,1)S(1)}, u32[]{:S(2)}, u32[]{:S(2)}) collective-permute-start(bf16[192,512]{1,0:T(8,128)(2,1)S(1)} %collective-permute-done.2.x2), channel_id=1, source_target_pairs={{0,1},{1,0},{2,3},{3,2},{4,5},{5,4},{6,7},{7,6},{8,9},{9,8},{10,11... | collective-permute-start | bytes 589832 | tf_op jit(solution)/shard_map/ppermute | solution.py:24
  11.7 7.3 %collective-permute-start.13 = (bf16[96,768]{1,0:T(8,128)(2,1)S(1)}, bf16[96,768]{1,0:T(8,128)(2,1)S(1)}, u32[]{:S(2)}, u32[]{:S(2)}) collective-permute-start(bf16[96,768]{1,0:T(8,128)(2,1)S(1)} %get-tuple-element.200), channel_id=1, source_target_pairs={{0,2},{1,3},{2,0},{3,1},{4,6},{5,7},{6,4},{7,5},{8,10},{9,11},{10,... | collective-permute-start | bytes 442376 | tf_op jit(solution)/shard_map/ppermute | solution.py:24
  13.4 14.4 %collective-permute-start.19 = (bf16[192,768]{1,0:T(8,128)(2,1)S(1)}, bf16[192,768]{1,0:T(8,128)(2,1)S(1)}, u32[]{:S(2)}, u32[]{:S(2)}) collective-permute-start(bf16[192,768]{1,0:T(8,128)(2,1)S(1)} %get-tuple-element.186), channel_id=1, source_target_pairs={{0,2},{1,3},{2,0},{3,1},{4,6},{5,7},{6,4},{7,5},{8,10},{9,11},{10,... | collective-permute-start | bytes 884744 | tf_op jit(solution)/shard_map/ppermute | solution.py:24
  17.1 10.1 %collective-permute-start.9 = (bf16[576,128]{1,0:T(8,128)(2,1)S(1)}, bf16[576,128]{1,0:T(8,128)(2,1)S(1)}, u32[]{:S(2)}, u32[]{:S(2)}) collective-permute-start(bf16[576,128]{1,0:T(8,128)(2,1)S(1)} %get-tuple-element.196), channel_id=1, source_target_pairs={{0,2},{1,3},{2,0},{3,1},{4,6},{5,7},{6,4},{7,5},{8,10},{9,11},{10,... | collective-permute-start | bytes 442376 | tf_op jit(solution)/shard_map/ppermute | solution.py:24
  19.0 8.8 %collective-permute-start.14 = (bf16[96,768]{1,0:T(8,128)(2,1)S(1)}, bf16[96,768]{1,0:T(8,128)(2,1)S(1)}, u32[]{:S(2)}, u32[]{:S(2)}) collective-permute-start(bf16[96,768]{1,0:T(8,128)(2,1)S(1)} %collective-permute-done.13.xa), channel_id=1, source_target_pairs={{0,4},{4,0},{8,12},{12,8},{16,20},{20,16},{24,28},{28,24},{1,5},{5... | collective-permute-start | bytes 442376 | tf_op jit(solution)/shard_map/ppermute | solution.py:24
  20.5 2.5 %collective-permute-start.8 = (bf16[384,128]{1,0:T(8,128)(2,1)S(1)}, bf16[384,128]{1,0:T(8,128)(2,1)S(1)}, u32[]{:S(2)}, u32[]{:S(2)}) collective-permute-start(bf16[384,128]{1,0:T(8,128)(2,1)S(1)} %get-tuple-element.195), channel_id=1, source_target_pairs={{0,1},{1,0},{2,3},{3,2},{4,5},{5,4},{6,7},{7,6},{8,9},{9,8},{10,11... | collective-permute-start | bytes 294920 | tf_op jit(solution)/shard_map/ppermute | solution.py:24
  27.3 2.4 %collective-permute-start.12 = (bf16[576,128]{1,0:T(8,128)(2,1)S(1)}, bf16[576,128]{1,0:T(8,128)(2,1)S(1)}, u32[]{:S(2)}, u32[]{:S(2)}) collective-permute-start(bf16[576,128]{1,0:T(8,128)(2,1)S(1)} %collective-permute-done.9.p2.g2), channel_id=1, source_target_pairs={{0,1},{1,0},{2,3},{3,2},{4,5},{5,4},{6,7},{7,6},{8,9},{9,8},{10,11... | collective-permute-start | bytes 442376 | tf_op jit(solution)/shard_map/ppermute | solution.py:24
  27.3 2.7 %collective-permute-start.15 = (bf16[96,768]{1,0:T(8,128)(2,1)S(1)}, bf16[96,768]{1,0:T(8,128)(2,1)S(1)}, u32[]{:S(2)}, u32[]{:S(2)}) collective-permute-start(bf16[96,768]{1,0:T(8,128)(2,1)S(1)} %collective-permute-done.13.xa), channel_id=1, source_target_pairs={{0,1},{1,0},{2,3},{3,2},{4,5},{5,4},{6,7},{7,6},{8,9},{9,8},{10,11... | collective-permute-start | bytes 442376 | tf_op jit(solution)/shard_map/ppermute | solution.py:24
  27.8 2.2 %collective-permute-start.16 = (bf16[96,768]{1,0:T(8,128)(2,1)S(1)}, bf16[96,768]{1,0:T(8,128)(2,1)S(1)}, u32[]{:S(2)}, u32[]{:S(2)}) collective-permute-start(bf16[96,768]{1,0:T(8,128)(2,1)S(1)} %collective-permute-done.14.xb), channel_id=1, source_target_pairs={{0,1},{1,0},{2,3},{3,2},{4,5},{5,4},{6,7},{7,6},{8,9},{9,8},{10,11... | collective-permute-start | bytes 442376 | tf_op jit(solution)/shard_map/ppermute | solution.py:24
  27.8 9.4 %collective-permute-start.20 = (bf16[192,768]{1,0:T(8,128)(2,1)S(1)}, bf16[192,768]{1,0:T(8,128)(2,1)S(1)}, u32[]{:S(2)}, u32[]{:S(2)}) collective-permute-start(bf16[192,768]{1,0:T(8,128)(2,1)S(1)} %collective-permute-done.19.xa), channel_id=1, source_target_pairs={{0,4},{4,0},{8,12},{12,8},{16,20},{20,16},{24,28},{28,24},{1,5},{5... | collective-permute-start | bytes 884744 | tf_op jit(solution)/shard_map/ppermute | solution.py:24
  30.9 9.1 %collective-permute-start.17 = (bf16[192,768]{1,0:T(8,128)(2,1)S(1)}, bf16[192,768]{1,0:T(8,128)(2,1)S(1)}, u32[]{:S(2)}, u32[]{:S(2)}) collective-permute-start(bf16[192,768]{1,0:T(8,128)(2,1)S(1)} %get-tuple-element.210.rows.n0), channel_id=1, source_target_pairs={{0,2},{1,3},{2,0},{3,1},{4,6},{5,7},{6,4},{7,5},{8,10},{9,11},{10,... | collective-permute-start | bytes 884744 | tf_op jit(solution)/shard_map/ppermute | solution.py:24
  32.4 8.1 %collective-permute-start.21 = (bf16[192,768]{1,0:T(8,128)(2,1)S(1)}, bf16[192,768]{1,0:T(8,128)(2,1)S(1)}, u32[]{:S(2)}, u32[]{:S(2)}) collective-permute-start(bf16[192,768]{1,0:T(8,128)(2,1)S(1)} %collective-permute-done.19.xa), channel_id=1, source_target_pairs={{0,1},{1,0},{2,3},{3,2},{4,5},{5,4},{6,7},{7,6},{8,9},{9,8},{10,11... | collective-permute-start | bytes 884744 | tf_op jit(solution)/shard_map/ppermute | solution.py:24
  40.0 6.3 %collective-permute-start.18 = (bf16[192,768]{1,0:T(8,128)(2,1)S(1)}, bf16[192,768]{1,0:T(8,128)(2,1)S(1)}, u32[]{:S(2)}, u32[]{:S(2)}) collective-permute-start(bf16[192,768]{1,0:T(8,128)(2,1)S(1)} %get-tuple-element.210.rows.n0), channel_id=1, source_target_pairs={{0,1},{1,0},{2,3},{3,2},{4,5},{5,4},{6,7},{7,6},{8,9},{9,8},{10,11... | collective-permute-start | bytes 884744 | tf_op jit(solution)/shard_map/ppermute | solution.py:24
  43.3 7.4 %collective-permute-start.23 = (bf16[192,768]{1,0:T(8,128)(2,1)S(1)}, bf16[192,768]{1,0:T(8,128)(2,1)S(1)}, u32[]{:S(2)}, u32[]{:S(2)}) collective-permute-start(bf16[192,768]{1,0:T(8,128)(2,1)S(1)} %collective-permute-done.17.rows.n_x.n1), channel_id=1, source_target_pairs={{0,1},{1,0},{2,3},{3,2},{4,5},{5,4},{6,7},{7,6},{8,9},{9,8},{10,11... | collective-permute-start | bytes 884744 | tf_op jit(solution)/shard_map/ppermute | solution.py:24
  43.5 7.2 %collective-permute-start.24 = (bf16[128,768]{1,0:T(8,128)(2,1)S(1)}, bf16[128,768]{1,0:T(8,128)(2,1)S(1)}, u32[]{:S(2)}, u32[]{:S(2)}) collective-permute-start(bf16[128,768]{1,0:T(8,128)(2,1)S(1)} %get-tuple-element.208), channel_id=1, source_target_pairs={{0,2},{1,3},{2,0},{3,1},{4,6},{5,7},{6,4},{7,5},{8,10},{9,11},{10,... | collective-permute-start | bytes 589832 | tf_op jit(solution)/shard_map/ppermute | solution.py:24
  51.3 7.5 %collective-permute-start.25 = (bf16[256,768]{1,0:T(8,128)(2,1)S(1)}, bf16[256,768]{1,0:T(8,128)(2,1)S(1)}, u32[]{:S(2)}, u32[]{:S(2)}) collective-permute-start(bf16[256,768]{1,0:T(8,128)(2,1)S(1)} %get-tuple-element.219), channel_id=1, source_target_pairs={{0,1},{1,0},{2,3},{3,2},{4,5},{5,4},{6,7},{7,6},{8,9},{9,8},{10,11... | collective-permute-start | bytes 1179656 | tf_op jit(solution)/shard_map/ppermute | solution.py:24
  51.4 3.3 %collective-permute-start.27 = (bf16[128,768]{1,0:T(8,128)(2,1)S(1)}, bf16[128,768]{1,0:T(8,128)(2,1)S(1)}, u32[]{:S(2)}, u32[]{:S(2)}) collective-permute-start(bf16[128,768]{1,0:T(8,128)(2,1)S(1)} %get-tuple-element.218.rows.f0), channel_id=1, source_target_pairs={{0,1},{1,0},{2,3},{3,2},{4,5},{5,4},{6,7},{7,6},{8,9},{9,8},{10,11... | collective-permute-start | bytes 589832 | tf_op jit(solution)/shard_map/ppermute | solution.py:24
  51.9 6.9 %collective-permute-start.26 = (bf16[128,768]{1,0:T(8,128)(2,1)S(1)}, bf16[128,768]{1,0:T(8,128)(2,1)S(1)}, u32[]{:S(2)}, u32[]{:S(2)}) collective-permute-start(bf16[128,768]{1,0:T(8,128)(2,1)S(1)} %get-tuple-element.218.rows.f0), channel_id=1, source_target_pairs={{0,2},{1,3},{2,0},{3,1},{4,6},{5,7},{6,4},{7,5},{8,10},{9,11},{10,... | collective-permute-start | bytes 589832 | tf_op jit(solution)/shard_map/ppermute | solution.py:24
  60.7 6.9 %collective-permute-start.30 = (bf16[128,768]{1,0:T(8,128)(2,1)S(1)}, bf16[128,768]{1,0:T(8,128)(2,1)S(1)}, u32[]{:S(2)}, u32[]{:S(2)}) collective-permute-start(bf16[128,768]{1,0:T(8,128)(2,1)S(1)} %get-tuple-element.230), channel_id=1, source_target_pairs={{0,2},{1,3},{2,0},{3,1},{4,6},{5,7},{6,4},{7,5},{8,10},{9,11},{10,... | collective-permute-start | bytes 589832 | tf_op jit(solution)/shard_map/ppermute | solution.py:24
  69.8 13.0 %collective-permute-start.37 = (bf16[384,768]{1,0:T(8,128)(2,1)S(1)}, bf16[384,768]{1,0:T(8,128)(2,1)S(1)}, u32[]{:S(2)}, u32[]{:S(2)}) collective-permute-start(bf16[384,768]{1,0:T(8,128)(2,1)S(1)} %get-tuple-element.271), channel_id=1, source_target_pairs={{0,1},{1,0},{2,3},{3,2},{4,5},{5,4},{6,7},{7,6},{8,9},{9,8},{10,11... | collective-permute-start | bytes 1769480 | tf_op jit(solution)/shard_map/ppermute | solution.py:24
  69.9 9.3 %collective-permute-start.32 = (bf16[192,768]{1,0:T(8,128)(2,1)S(1)}, bf16[192,768]{1,0:T(8,128)(2,1)S(1)}, u32[]{:S(2)}, u32[]{:S(2)}) collective-permute-start(bf16[192,768]{1,0:T(8,128)(2,1)S(1)} %get-tuple-element.244), channel_id=1, source_target_pairs={{0,4},{4,0},{8,12},{12,8},{16,20},{20,16},{24,28},{28,24},{1,5},{5... | collective-permute-start | bytes 884744 | tf_op jit(solution)/shard_map/ppermute | solution.py:746
  70.9 5.3 %collective-permute-start.33 = (bf16[480,128]{1,0:T(8,128)(2,1)S(1)}, bf16[480,128]{1,0:T(8,128)(2,1)S(1)}, u32[]{:S(2)}, u32[]{:S(2)}) collective-permute-start(bf16[480,128]{1,0:T(8,128)(2,1)S(1)} %get-tuple-element.249), channel_id=1, source_target_pairs={{0,2},{1,3},{2,0},{3,1},{4,6},{5,7},{6,4},{7,5},{8,10},{9,11},{10,... | collective-permute-start | bytes 368648 | tf_op jit(solution)/shard_map/ppermute | solution.py:24
  76.2 6.7 %collective-permute-start.34 = (bf16[480,128]{1,0:T(8,128)(2,1)S(1)}, bf16[480,128]{1,0:T(8,128)(2,1)S(1)}, u32[]{:S(2)}, u32[]{:S(2)}) collective-permute-start(bf16[480,128]{1,0:T(8,128)(2,1)S(1)} %collective-permute-done.33.u2), channel_id=1, source_target_pairs={{0,1},{1,0},{2,3},{3,2},{4,5},{5,4},{6,7},{7,6},{8,9},{9,8},{10,11... | collective-permute-start | bytes 368648 | tf_op jit(solution)/shard_map/ppermute | solution.py:24
  76.2 11.9 %collective-permute-start.35 = (bf16[192,768]{1,0:T(8,128)(2,1)S(1)}, bf16[192,768]{1,0:T(8,128)(2,1)S(1)}, u32[]{:S(2)}, u32[]{:S(2)}) collective-permute-start(bf16[192,768]{1,0:T(8,128)(2,1)S(1)} %get-tuple-element.255), channel_id=1, source_target_pairs={{0,4},{4,0},{8,12},{12,8},{16,20},{20,16},{24,28},{28,24},{1,5},{5... | collective-permute-start | bytes 884744 | tf_op jit(solution)/shard_map/ppermute | solution.py:746
  79.3 10.9 %collective-permute-start.36 = (bf16[192,768]{1,0:T(8,128)(2,1)S(1)}, bf16[192,768]{1,0:T(8,128)(2,1)S(1)}, u32[]{:S(2)}, u32[]{:S(2)}) collective-permute-start(bf16[192,768]{1,0:T(8,128)(2,1)S(1)} %get-tuple-element.245), channel_id=1, source_target_pairs={{0,8},{4,12},{24,16},{28,20},{1,9},{5,13},{25,17},{29,21},{2,10},{... | collective-permute-start | bytes 884744 | tf_op jit(solution)/shard_map/ppermute | solution.py:746
  82.9 8.2 %collective-permute-start.38 = (bf16[192,768]{1,0:T(8,128)(2,1)S(1)}, bf16[192,768]{1,0:T(8,128)(2,1)S(1)}, u32[]{:S(2)}, u32[]{:S(2)}) collective-permute-start(bf16[192,768]{1,0:T(8,128)(2,1)S(1)} %wo_low.1), channel_id=1, source_target_pairs={{0,2},{1,3},{2,0},{3,1},{4,6},{5,7},{6,4},{7,5},{8,10},{9,11},{10,... | collective-permute-start | bytes 884744 | tf_op jit(solution)/shard_map/ppermute | solution.py:24
  87.1 9.6 %collective-permute-start.39 = (bf16[192,768]{1,0:T(8,128)(2,1)S(1)}, bf16[192,768]{1,0:T(8,128)(2,1)S(1)}, u32[]{:S(2)}, u32[]{:S(2)}) collective-permute-start(bf16[192,768]{1,0:T(8,128)(2,1)S(1)} %get-tuple-element.279), channel_id=1, source_target_pairs={{0,4},{4,0},{8,12},{12,8},{16,20},{20,16},{24,28},{28,24},{1,5},{5... | collective-permute-start | bytes 884744 | tf_op jit(solution)/shard_map/ppermute | solution.py:746
  88.2 10.2 %collective-permute-start.40 = (bf16[192,768]{1,0:T(8,128)(2,1)S(1)}, bf16[192,768]{1,0:T(8,128)(2,1)S(1)}, u32[]{:S(2)}, u32[]{:S(2)}) collective-permute-start(bf16[192,768]{1,0:T(8,128)(2,1)S(1)} %get-tuple-element.256), channel_id=1, source_target_pairs={{0,8},{4,12},{24,16},{28,20},{1,9},{5,13},{25,17},{29,21},{2,10},{... | collective-permute-start | bytes 884744 | tf_op jit(solution)/shard_map/ppermute | solution.py:746
  90.3 10.0 %collective-permute-start.41 = (bf16[192,768]{1,0:T(8,128)(2,1)S(1)}, bf16[192,768]{1,0:T(8,128)(2,1)S(1)}, u32[]{:S(2)}, u32[]{:S(2)}) collective-permute-start(bf16[192,768]{1,0:T(8,128)(2,1)S(1)} %second_add.5.mine), channel_id=1, source_target_pairs={{8,16},{12,20},{16,8},{20,12},{9,17},{13,21},{17,9},{21,13},{10,18... | collective-permute-start | bytes 884744 | tf_op jit(solution)/shard_map/ppermute | solution.py:746
  91.7 11.3 %collective-permute-start.42 = (bf16[192,768]{1,0:T(8,128)(2,1)S(1)}, bf16[192,768]{1,0:T(8,128)(2,1)S(1)}, u32[]{:S(2)}, u32[]{:S(2)}) collective-permute-start(bf16[192,768]{1,0:T(8,128)(2,1)S(1)} %get-tuple-element.287), channel_id=1, source_target_pairs={{0,4},{4,0},{8,12},{12,8},{16,20},{20,16},{24,28},{28,24},{1,5},{5... | collective-permute-start | bytes 884744 | tf_op jit(solution)/shard_map/ppermute | solution.py:746
  96.8 9.5 %collective-permute-start.43 = (bf16[192,768]{1,0:T(8,128)(2,1)S(1)}, bf16[192,768]{1,0:T(8,128)(2,1)S(1)}, u32[]{:S(2)}, u32[]{:S(2)}) collective-permute-start(bf16[192,768]{1,0:T(8,128)(2,1)S(1)} %get-tuple-element.280), channel_id=1, source_target_pairs={{0,8},{4,12},{24,16},{28,20},{1,9},{5,13},{25,17},{29,21},{2,10},{... | collective-permute-start | bytes 884744 | tf_op jit(solution)/shard_map/ppermute | solution.py:746
  98.5 8.6 %collective-permute-start.44 = (bf16[192,768]{1,0:T(8,128)(2,1)S(1)}, bf16[192,768]{1,0:T(8,128)(2,1)S(1)}, u32[]{:S(2)}, u32[]{:S(2)}) collective-permute-start(bf16[192,768]{1,0:T(8,128)(2,1)S(1)} %second_add.6.mine), channel_id=1, source_target_pairs={{8,16},{12,20},{16,8},{20,12},{9,17},{13,21},{17,9},{21,13},{10,18... | collective-permute-start | bytes 884744 | tf_op jit(solution)/shard_map/ppermute | solution.py:746
  99.2 9.1 %collective-permute-start.45 = (bf16[192,768]{1,0:T(8,128)(2,1)S(1)}, bf16[192,768]{1,0:T(8,128)(2,1)S(1)}, u32[]{:S(2)}, u32[]{:S(2)}) collective-permute-start(bf16[192,768]{1,0:T(8,128)(2,1)S(1)} %get-tuple-element.277), channel_id=1, source_target_pairs={{0,4},{4,0},{8,12},{12,8},{16,20},{20,16},{24,28},{28,24},{1,5},{5... | collective-permute-start | bytes 884744 | tf_op jit(solution)/shard_map/ppermute | solution.py:746
  103.1 6.1 %collective-permute-start.46 = (bf16[192,768]{1,0:T(8,128)(2,1)S(1)}, bf16[192,768]{1,0:T(8,128)(2,1)S(1)}, u32[]{:S(2)}, u32[]{:S(2)}) collective-permute-start(bf16[192,768]{1,0:T(8,128)(2,1)S(1)} %get-tuple-element.288), channel_id=1, source_target_pairs={{0,8},{4,12},{24,16},{28,20},{1,9},{5,13},{25,17},{29,21},{2,10},{... | collective-permute-start | bytes 884744 | tf_op jit(solution)/shard_map/ppermute | solution.py:746
  105.0 8.6 %collective-permute-start.47 = (bf16[192,768]{1,0:T(8,128)(2,1)S(1)}, bf16[192,768]{1,0:T(8,128)(2,1)S(1)}, u32[]{:S(2)}, u32[]{:S(2)}) collective-permute-start(bf16[192,768]{1,0:T(8,128)(2,1)S(1)} %third_add.3.mine), channel_id=1, source_target_pairs={{8,0},{12,4},{16,24},{20,28},{9,1},{13,5},{17,25},{21,29},{10,2},{... | collective-permute-start | bytes 884744 | tf_op jit(solution)/shard_map/ppermute | solution.py:746
  106.4 7.3 %collective-permute-start.48 = (bf16[192,768]{1,0:T(8,128)(2,1)S(1)}, bf16[192,768]{1,0:T(8,128)(2,1)S(1)}, u32[]{:S(2)}, u32[]{:S(2)}) collective-permute-start(bf16[192,768]{1,0:T(8,128)(2,1)S(1)} %second_add.7.mine), channel_id=1, source_target_pairs={{8,16},{12,20},{16,8},{20,12},{9,17},{13,21},{17,9},{21,13},{10,18... | collective-permute-start | bytes 884744 | tf_op jit(solution)/shard_map/ppermute | solution.py:746
  107.1 13.8 %collective-permute-start.50 = (bf16[224,768]{1,0:T(8,128)(2,1)S(1)}, bf16[224,768]{1,0:T(8,128)(2,1)S(1)}, u32[]{:S(2)}, u32[]{:S(2)}) collective-permute-start(bf16[224,768]{1,0:T(8,128)(2,1)S(1)} %get-tuple-element.264), channel_id=1, source_target_pairs={{0,4},{4,0},{8,12},{12,8},{16,20},{20,16},{24,28},{28,24},{1,5},{5... | collective-permute-start | bytes 1032200 | tf_op jit(solution)/shard_map/ppermute | solution.py:746
  108.2 5.6 %collective-permute-start.49 = (bf16[96,768]{1,0:T(8,128)(2,1)S(1)}, bf16[96,768]{1,0:T(8,128)(2,1)S(1)}, u32[]{:S(2)}, u32[]{:S(2)}) collective-permute-start(bf16[96,768]{1,0:T(8,128)(2,1)S(1)} %get-tuple-element.291), channel_id=1, source_target_pairs={{0,1},{1,0},{2,3},{3,2},{4,5},{5,4},{6,7},{7,6},{8,9},{9,8},{10,11... | collective-permute-start | bytes 442376 | tf_op jit(solution)/shard_map/ppermute | solution.py:24
  109.3 14.5 %collective-permute-start.52 = (bf16[192,768]{1,0:T(8,128)(2,1)S(1)}, bf16[192,768]{1,0:T(8,128)(2,1)S(1)}, u32[]{:S(2)}, u32[]{:S(2)}) collective-permute-start(bf16[192,768]{1,0:T(8,128)(2,1)S(1)} %second_add.8.mine), channel_id=1, source_target_pairs={{8,16},{12,20},{16,8},{20,12},{9,17},{13,21},{17,9},{21,13},{10,18... | collective-permute-start | bytes 884744 | tf_op jit(solution)/shard_map/ppermute | solution.py:746
  113.8 8.6 %collective-permute-start.51 = (bf16[96,768]{1,0:T(8,128)(2,1)S(1)}, bf16[96,768]{1,0:T(8,128)(2,1)S(1)}, u32[]{:S(2)}, u32[]{:S(2)}) collective-permute-start(bf16[96,768]{1,0:T(8,128)(2,1)S(1)} %second_half.2), channel_id=1, source_target_pairs={{0,2},{1,3},{2,0},{3,1},{4,6},{5,7},{6,4},{7,5},{8,10},{9,11},{10,... | collective-permute-start | bytes 442376 | tf_op jit(solution)/shard_map/ppermute | solution.py:24
  115.2 13.2 %collective-permute-start.54 = (bf16[192,768]{1,0:T(8,128)(2,1)S(1)}, bf16[192,768]{1,0:T(8,128)(2,1)S(1)}, u32[]{:S(2)}, u32[]{:S(2)}) collective-permute-start(bf16[192,768]{1,0:T(8,128)(2,1)S(1)} %get-tuple-element.295), channel_id=1, source_target_pairs={{0,8},{4,12},{24,16},{28,20},{1,9},{5,13},{25,17},{29,21},{2,10},{... | collective-permute-start | bytes 884744 | tf_op jit(solution)/shard_map/ppermute | solution.py:746
  121.1 13.0 %collective-permute-start.57 = (bf16[224,768]{1,0:T(8,128)(2,1)S(1)}, bf16[224,768]{1,0:T(8,128)(2,1)S(1)}, u32[]{:S(2)}, u32[]{:S(2)}) collective-permute-start(bf16[224,768]{1,0:T(8,128)(2,1)S(1)} %get-tuple-element.305.mine), channel_id=1, source_target_pairs={{0,8},{4,12},{24,16},{28,20},{1,9},{5,13},{25,17},{29,21},{2,10},{... | collective-permute-start | bytes 1032200 | tf_op jit(solution)/shard_map/ppermute | solution.py:746
  122.5 11.5 %collective-permute-start.55 = (bf16[192,768]{1,0:T(8,128)(2,1)S(1)}, bf16[192,768]{1,0:T(8,128)(2,1)S(1)}, u32[]{:S(2)}, u32[]{:S(2)}) collective-permute-start(bf16[192,768]{1,0:T(8,128)(2,1)S(1)} %join_owners.2.mine), channel_id=1, source_target_pairs={{8,0},{12,4},{16,24},{20,28},{9,1},{13,5},{17,25},{21,29},{10,2},{... | collective-permute-start | bytes 884744 | tf_op jit(solution)/shard_map/ppermute | solution.py:746
  123.9 14.0 %collective-permute-start.58 = (bf16[192,768]{1,0:T(8,128)(2,1)S(1)}, bf16[192,768]{1,0:T(8,128)(2,1)S(1)}, u32[]{:S(2)}, u32[]{:S(2)}) collective-permute-start(bf16[192,768]{1,0:T(8,128)(2,1)S(1)} %third_add.4.mine), channel_id=1, source_target_pairs={{8,0},{12,4},{16,24},{20,28},{9,1},{13,5},{17,25},{21,29},{10,2},{... | collective-permute-start | bytes 884744 | tf_op jit(solution)/shard_map/ppermute | solution.py:746
  125.3 8.7 %collective-permute-start.56 = (bf16[96,768]{1,0:T(8,128)(2,1)S(1)}, bf16[96,768]{1,0:T(8,128)(2,1)S(1)}, u32[]{:S(2)}, u32[]{:S(2)}) collective-permute-start(bf16[96,768]{1,0:T(8,128)(2,1)S(1)} %second_half.3), channel_id=1, source_target_pairs={{0,2},{1,3},{2,0},{3,1},{4,6},{5,7},{6,4},{7,5},{8,10},{9,11},{10,... | collective-permute-start | bytes 442376 | tf_op jit(solution)/shard_map/ppermute | solution.py:24
  128.4 10.7 %collective-permute-start.59 = (bf16[192,768]{1,0:T(8,128)(2,1)S(1)}, bf16[192,768]{1,0:T(8,128)(2,1)S(1)}, u32[]{:S(2)}, u32[]{:S(2)}) collective-permute-start(bf16[192,768]{1,0:T(8,128)(2,1)S(1)} %second_add.9.mine), channel_id=1, source_target_pairs={{8,16},{12,20},{16,8},{20,12},{9,17},{13,21},{17,9},{21,13},{10,18... | collective-permute-start | bytes 884744 | tf_op jit(solution)/shard_map/ppermute | solution.py:746
  134.2 10.4 %collective-permute-start.61 = (bf16[224,768]{1,0:T(8,128)(2,1)S(1)}, bf16[224,768]{1,0:T(8,128)(2,1)S(1)}, u32[]{:S(2)}, u32[]{:S(2)}) collective-permute-start(bf16[224,768]{1,0:T(8,128)(2,1)S(1)} %second_add_pair.1.mine), channel_id=1, source_target_pairs={{8,16},{12,20},{16,8},{20,12},{9,17},{13,21},{17,9},{21,13},{10,18... | collective-permute-start | bytes 1032200 | tf_op jit(solution)/shard_map/ppermute | solution.py:746
  134.9 9.7 %collective-permute-start.60 = (bf16[192,768]{1,0:T(8,128)(2,1)S(1)}, bf16[192,768]{1,0:T(8,128)(2,1)S(1)}, u32[]{:S(2)}, u32[]{:S(2)}) collective-permute-start(bf16[192,768]{1,0:T(8,128)(2,1)S(1)} %join_owners.3.mine), channel_id=1, source_target_pairs={{8,0},{12,4},{16,24},{20,28},{9,1},{13,5},{17,25},{21,29},{10,2},{... | collective-permute-start | bytes 884744 | tf_op jit(solution)/shard_map/ppermute | solution.py:746
  136.2 11.2 %collective-permute-start.62 = (bf16[192,768]{1,0:T(8,128)(2,1)S(1)}, bf16[192,768]{1,0:T(8,128)(2,1)S(1)}, u32[]{:S(2)}, u32[]{:S(2)}) collective-permute-start(bf16[192,768]{1,0:T(8,128)(2,1)S(1)} %choose.5.mine0), channel_id=1, source_target_pairs={{0,4},{4,0},{8,12},{12,8},{16,20},{20,16},{24,28},{28,24},{1,5},{5... | collective-permute-start | bytes 884744 | tf_op jit(solution)/shard_map/ppermute | solution.py:746
  138.0 12.0 %collective-permute-start.63 = (bf16[192,768]{1,0:T(8,128)(2,1)S(1)}, bf16[192,768]{1,0:T(8,128)(2,1)S(1)}, u32[]{:S(2)}, u32[]{:S(2)}) collective-permute-start(bf16[192,768]{1,0:T(8,128)(2,1)S(1)} %choose.7.mine1), channel_id=1, source_target_pairs={{0,4},{4,0},{8,12},{12,8},{16,20},{20,16},{24,28},{28,24},{1,5},{5... | collective-permute-start | bytes 884744 | tf_op jit(solution)/shard_map/ppermute | solution.py:746
  139.1 22.7 %collective-permute-start.65 = (bf16[384,640]{1,0:T(8,128)(2,1)S(1)}, bf16[384,640]{1,0:T(8,128)(2,1)S(1)}, u32[]{:S(2)}, u32[]{:S(2)}) collective-permute-start(bf16[384,640]{1,0:T(8,128)(2,1)S(1)} %get-tuple-element.318), channel_id=1, source_target_pairs={{0,1},{1,0},{2,3},{3,2},{4,5},{5,4},{6,7},{7,6},{8,9},{9,8},{10,11... | collective-permute-start | bytes 1474568 | tf_op jit(solution)/shard_map/ppermute | solution.py:24
  144.7 20.7 %collective-permute-start.68 = (bf16[224,768]{1,0:T(8,128)(2,1)S(1)}, bf16[224,768]{1,0:T(8,128)(2,1)S(1)}, u32[]{:S(2)}, u32[]{:S(2)}) collective-permute-start(bf16[224,768]{1,0:T(8,128)(2,1)S(1)} %third_add_pair.1.mine), channel_id=1, source_target_pairs={{8,0},{12,4},{16,24},{20,28},{9,1},{13,5},{17,25},{21,29},{10,2},{... | collective-permute-start | bytes 1032200 | tf_op jit(solution)/shard_map/ppermute | solution.py:746
  146.0 15.8 %collective-permute-start.64 = (bf16[192,768]{1,0:T(8,128)(2,1)S(1)}, bf16[192,768]{1,0:T(8,128)(2,1)S(1)}, u32[]{:S(2)}, u32[]{:S(2)}) collective-permute-start(bf16[192,768]{1,0:T(8,128)(2,1)S(1)} %third_add.5.mine), channel_id=1, source_target_pairs={{8,0},{12,4},{16,24},{20,28},{9,1},{13,5},{17,25},{21,29},{10,2},{... | collective-permute-start | bytes 884744 | tf_op jit(solution)/shard_map/ppermute | solution.py:746
  147.3 16.5 %collective-permute-start.66 = (bf16[192,768]{1,0:T(8,128)(2,1)S(1)}, bf16[192,768]{1,0:T(8,128)(2,1)S(1)}, u32[]{:S(2)}, u32[]{:S(2)}) collective-permute-start(bf16[192,768]{1,0:T(8,128)(2,1)S(1)} %choose.6.mine0), channel_id=1, source_target_pairs={{0,4},{4,0},{8,12},{12,8},{16,20},{20,16},{24,28},{28,24},{1,5},{5... | collective-permute-start | bytes 884744 | tf_op jit(solution)/shard_map/ppermute | solution.py:746
  150.0 13.9 %collective-permute-start.67 = (bf16[192,768]{1,0:T(8,128)(2,1)S(1)}, bf16[192,768]{1,0:T(8,128)(2,1)S(1)}, u32[]{:S(2)}, u32[]{:S(2)}) collective-permute-start(bf16[192,768]{1,0:T(8,128)(2,1)S(1)} %choose.8.mine1), channel_id=1, source_target_pairs={{0,4},{4,0},{8,12},{12,8},{16,20},{20,16},{24,28},{28,24},{1,5},{5... | collective-permute-start | bytes 884744 | tf_op jit(solution)/shard_map/ppermute | solution.py:746
  161.9 6.9 %collective-permute-start.69 = (bf16[192,768]{1,0:T(8,128)(2,1)S(1)}, bf16[192,768]{1,0:T(8,128)(2,1)S(1)}, u32[]{:S(2)}, u32[]{:S(2)}) collective-permute-start(bf16[192,768]{1,0:T(8,128)(2,1)S(1)} %tokens_step.1), channel_id=1, source_target_pairs={{0,2},{1,3},{2,0},{3,1},{4,6},{5,7},{6,4},{7,5},{8,10},{9,11},{10,... | collective-permute-start | bytes 884744 | tf_op jit(solution)/shard_map/ppermute | solution.py:24
  163.0 9.4 %collective-permute-start.71 = (bf16[192,768]{1,0:T(8,128)(2,1)S(1)}, bf16[192,768]{1,0:T(8,128)(2,1)S(1)}, u32[]{:S(2)}, u32[]{:S(2)}) collective-permute-start(bf16[192,768]{1,0:T(8,128)(2,1)S(1)} %choose.9.vo_mine), channel_id=1, source_target_pairs={{0,4},{4,0},{8,12},{12,8},{16,20},{20,16},{24,28},{28,24},{1,5},{5... | collective-permute-start | bytes 884744 | tf_op jit(solution)/shard_map/ppermute | solution.py:746
  165.5 10.1 %collective-permute-start.70 = (bf16[192,768]{1,0:T(8,128)(2,1)S(1)}, bf16[192,768]{1,0:T(8,128)(2,1)S(1)}, u32[]{:S(2)}, u32[]{:S(2)}) collective-permute-start(bf16[192,768]{1,0:T(8,128)(2,1)S(1)} %get-tuple-element.340.qk_mine), channel_id=1, source_target_pairs={{0,4},{4,0},{8,12},{12,8},{16,20},{20,16},{24,28},{28,24},{1,5},{5... | collective-permute-start | bytes 884744 | tf_op jit(solution)/shard_map/ppermute | solution.py:746
  (25 other events, 218.8 us)

commit v4 on v3

--- a/solution.py
+++ b/solution.py
@@ -795,17 +795,16 @@
     )
     tokens_x = swap(tokens, "hid", 2)
     tokens_core = swap(tokens, "hid", 1)
-    x_own = swap(tokens_core, "hid", 1)
+    x_own = swap(after(tokens_core, back_half), "hid", 1)
     out_xa = swap(out_half, "hid", 2)
     back_xa = swap(back_half, "hid", 2)
     wi_core = swap(w_in, "hid", 1)
     wo_core = swap(w_out, "hid", 1)
-    cot_core = swap(after(cotangent, back_half), "hid", 1)
     b_in_core = swap(b_in, "hid", 1)
     gate_core = swap(inter_gate, "hid", 1)
     back_core = swap(w_back, "hid", 1)
     tokens_far = swap(
-        after(tokens_x, tokens_core, wi_core, wo_core, cot_core, back_core, back_half), "hid", 1
+        after(tokens_x, tokens_core, wi_core, wo_core, back_core, back_half), "hid", 1
     )
 
     head_block = sds((feats, block), bf16)
@@ -829,6 +828,7 @@
         [pltpu.VMEM((feats, toks), bf16), pltpu.VMEM((toks, toks), f32)],
         micros=5.4,
     )
+    cot_core = swap(after(cotangent, x_block), "hid", 1)
     send_core, send_x, columns = local_kernel(
         add_vectors,
         "add_vectors",

time: 178 us -> 177 us (level)
  transfers between devices with their start and end apart: 72 -> 72, of which waited for: 30 -> 29; matrix products, arithmetic and copies ran while one was open for 1% -> 1% of each run, Pallas kernels for 13% -> 13%
where the time goes in v4:
time: 177 us; the launch traced here: 176 us
  waiting for transfers between devices  74.5 us (42%)
  starting transfers between devices  67.7 us (38%)
  Pallas kernels  27.9 us (16%)
  local copies, waits for them, and re-layouts  2.95 us (2%)
    ppermute x30, waiting for transfers between devices, along(): return lax.ppermute(block, 'rows', pairs)  42 us
    ppermute x30, starting transfers between devices, along(): return lax.ppermute(block, 'rows', pairs)  39.9 us
    ppermute x42, waiting for transfers between devices, swap(): lax.ppermute(block, axis, [(i, i ^ bit) for i in range(lax.axis_size(axis...  32.5 us
    pallas_call x54, Pallas kernels, local_kernel(): pl.pallas_call(body, name=name, out_shape=outs, in_specs=[SPECS[k] for k...  27.9 us
    ppermute x42, starting transfers between devices, swap(): lax.ppermute(block, axis, [(i, i ^ bit) for i in range(lax.axis_size(axis...  27.9 us
  transfers between devices with their start and end apart: 72, of which 29 were waited for; matrix products, arithmetic and copies ran while one was open for 1% of the time, Pallas kernels for 13%

profile of v4, /device:TPU:0, one launch (start us, length us, event | category | flops | bytes accessed | tf_op | source)
XLA Modules:
  0.0 176.0 jit_solution(15351175300526854514)
XLA Ops:
  1.8 2.9 %collective-permute-start.2 = (bf16[192,512]{1,0:T(8,128)(2,1)}, bf16[192,512]{1,0:T(8,128)(2,1)S(1)}, u32[]{:S(2)}, u32[]{:S(2)}) collective-permute-start(bf16[192,512]{1,0:T(8,128)(2,1)} %param.18), channel_id=1, source_target_pairs={{0,2},{1,3},{2,0},{3,1},{4,6},{5,7},{6,4},{7,5},{8,10},{9,11},{10,... | collective-permute-start | bytes 589832 | tf_op jit(solution)/shard_map/ppermute | solution.py:24
  6.8 1.3 copy-done
  10.2 1.8 %collective-permute-start.12 = (bf16[96,768]{1,0:T(8,128)(2,1)S(1)}, bf16[96,768]{1,0:T(8,128)(2,1)S(1)}, u32[]{:S(2)}, u32[]{:S(2)}) collective-permute-start(bf16[96,768]{1,0:T(8,128)(2,1)S(1)} %get-tuple-element.201), channel_id=1, source_target_pairs={{0,2},{1,3},{2,0},{3,1},{4,6},{5,7},{6,4},{7,5},{8,10},{9,11},{10,... | collective-permute-start | bytes 442376 | tf_op jit(solution)/shard_map/ppermute | solution.py:24
  12.3 2.6 %attn_forward.1 = (bf16[768,512]{1,0:T(8,128)(2,1)S(1)}, bf16[3,192,512]{2,1,0:T(8,128)(2,1)S(1)}, f32[8,512]{1,0:T(8,128)S(1)}, bf16[192,128]{1,0:T(8,128)(2,1)...) custom-call(s32[8,512]{1,0:T(8,128)S(1)} %get-tuple-element.185.bounds, ...), custom_call_target="tpu_custom_call" | custom-call | flops 1 | bytes 19926000 | tf_op jit(solution)/shard_map/attn_forward/pallas_call | solution.py:36
  15.7 1.8 %collective-permute-start.8 = (bf16[576,128]{1,0:T(8,128)(2,1)S(1)}, bf16[576,128]{1,0:T(8,128)(2,1)S(1)}, u32[]{:S(2)}, u32[]{:S(2)}) collective-permute-start(bf16[576,128]{1,0:T(8,128)(2,1)S(1)} %get-tuple-element.197), channel_id=1, source_target_pairs={{0,2},{1,3},{2,0},{3,1},{4,6},{5,7},{6,4},{7,5},{8,10},{9,11},{10,... | collective-permute-start | bytes 442376 | tf_op jit(solution)/shard_map/ppermute | solution.py:24
  17.6 1.5 collective-permute-start.13
  21.6 4.4 %collective-permute-done.8.p2.g2 = bf16[576,128]{1,0:T(8,128)(2,1)S(1)} collective-permute-done((bf16[576,128]{1,0:T(8,128)(2,1)S(1)}, bf16[576,128]{1,0:T(8,128)(2,1)S(1)}, u32[]{:S(2)}, u32[]{:S(2)}) %collective-permute-start.8) | collective-permute-done | bytes 147488 | tf_op jit(solution)/shard_map/ppermute | solution.py:24
  26.5 1.8 %collective-permute-start.19 = (bf16[192,768]{1,0:T(8,128)(2,1)S(1)}, bf16[192,768]{1,0:T(8,128)(2,1)S(1)}, u32[]{:S(2)}, u32[]{:S(2)}) collective-permute-start(bf16[192,768]{1,0:T(8,128)(2,1)S(1)} %collective-permute-done.18.xa), channel_id=1, source_target_pairs={{0,4},{4,0},{8,12},{12,8},{16,20},{20,16},{24,28},{28,24},{1,5},{5... | collective-permute-start | bytes 884744 | tf_op jit(solution)/shard_map/ppermute | solution.py:24
  29.6 1.6 collective-permute-start.16
  31.1 4.8 %collective-permute-done.19.xb = bf16[192,768]{1,0:T(8,128)(2,1)S(1)} collective-permute-done((bf16[192,768]{1,0:T(8,128)(2,1)S(1)}, bf16[192,768]{1,0:T(8,128)(2,1)S(1)}, u32[]{:S(2)}, u32[]{:S(2)}) %collective-permute-start.19) | collective-permute-done | bytes 294944 | tf_op jit(solution)/shard_map/ppermute | solution.py:24
  35.9 2.8 %collective-permute-done.16.rows.n_x.n1 = bf16[192,768]{1,0:T(8,128)(2,1)S(1)} collective-permute-done((bf16[192,768]{1,0:T(8,128)(2,1)S(1)}, bf16[192,768]{1,0:T(8,128)(2,1)S(1)}, u32[]{:S(2)}, u32[]{:S(2)}) %collective-permute-start.16) | collective-permute-done | bytes 294944 | tf_op jit(solution)/shard_map/ppermute | solution.py:24
  39.2 1.1 collective-permute-done.21.fb
  40.6 1.3 ffn_forward_far.1
  42.5 1.5 collective-permute-start.23
  44.0 1.3 ffn_forward.1
  45.4 4.1 %collective-permute-done.23.recv = bf16[128,768]{1,0:T(8,128)(2,1)S(1)} collective-permute-done((bf16[128,768]{1,0:T(8,128)(2,1)S(1)}, bf16[128,768]{1,0:T(8,128)(2,1)S(1)}, u32[]{:S(2)}, u32[]{:S(2)}) %collective-permute-start.23) | collective-permute-done | bytes 196640 | tf_op jit(solution)/shard_map/ppermute | solution.py:24
  50.7 1.5 collective-permute-start.26
  52.2 1.3 ffn_backward.1
  53.6 4.0 %collective-permute-done.26.rows.f1 = bf16[128,768]{1,0:T(8,128)(2,1)S(1)} collective-permute-done((bf16[128,768]{1,0:T(8,128)(2,1)S(1)}, bf16[128,768]{1,0:T(8,128)(2,1)S(1)}, u32[]{:S(2)}, u32[]{:S(2)}) %collective-permute-start.26) | collective-permute-done | bytes 196640 | tf_op jit(solution)/shard_map/ppermute | solution.py:24
  57.6 1.3 ffn_backward_far.1
  59.5 1.5 collective-permute-start.30
  61.0 1.9 %ffn_weight_grads.1 = (f32[192,768]{1,0:T(8,128)S(1)}, bf16[192,768]{1,0:T(8,128)(2,1)S(1)}, f32[192,768]{1,0:T(8,128)S(1)}, bf16[192,768]{1,0:T(8,128)(2,1)S(1)...) custom-call(bf16[192,768]{1,0:T(8,128)(2,1)S(1)} %get-tuple-element., ...), custom_call_target="tpu_custom_call" | custom-call | flops 1 | bytes 9225000 | tf_op jit(solution)/shard_map/ffn_weight_grads/pallas_call | solution.py:36
  62.9 3.5 %collective-permute-done.30.recv = bf16[128,768]{1,0:T(8,128)(2,1)S(1)} collective-permute-done((bf16[128,768]{1,0:T(8,128)(2,1)S(1)}, bf16[128,768]{1,0:T(8,128)(2,1)S(1)}, u32[]{:S(2)}, u32[]{:S(2)}) %collective-permute-start.30) | collective-permute-done | bytes 196640 | tf_op jit(solution)/shard_map/ppermute | solution.py:24
  69.7 1.5 collective-permute-start.33
  71.2 3.8 %collective-permute-done.33.u2 = bf16[480,128]{1,0:T(8,128)(2,1)S(1)} collective-permute-done((bf16[480,128]{1,0:T(8,128)(2,1)S(1)}, bf16[480,128]{1,0:T(8,128)(2,1)S(1)}, u32[]{:S(2)}, u32[]{:S(2)}) %collective-permute-start.33) | collective-permute-done | bytes 122912 | tf_op jit(solution)/shard_map/ppermute | solution.py:24
  76.1 1.9 %collective-permute-done.32.recv = bf16[192,768]{1,0:T(8,128)(2,1)S(1)} collective-permute-done((bf16[192,768]{1,0:T(8,128)(2,1)S(1)}, bf16[192,768]{1,0:T(8,128)(2,1)S(1)}, u32[]{:S(2)}, u32[]{:S(2)}) %collective-permute-start.32) | collective-permute-done | bytes 294944 | tf_op jit(solution)/shard_map/ppermute | solution.py:746
  78.1 3.5 %collective-permute-start.36 = (bf16[192,768]{1,0:T(8,128)(2,1)S(1)}, bf16[192,768]{1,0:T(8,128)(2,1)S(1)}, u32[]{:S(2)}, u32[]{:S(2)}) collective-permute-start(bf16[192,768]{1,0:T(8,128)(2,1)S(1)} %get-tuple-element.247), channel_id=1, source_target_pairs={{0,8},{4,12},{24,16},{28,20},{1,9},{5,13},{25,17},{29,21},{2,10},{... | collective-permute-start | bytes 884744 | tf_op jit(solution)/shard_map/ppermute | solution.py:746
  81.7 1.6 collective-permute-start.38
  83.3 2.6 %attn_backward.1 = (bf16[576,512]{1,0:T(8,128)(2,1)S(1)}, f32[8,128]{1,0:T(8,128)S(1)}, f32[8,576]{1,0:T(8,128)S(1)}) custom-call(s32[8,512]{1,0:T(8,128)S(1)} %get-tuple-element.185.bounds, bf16[3,192,512]{2,1,0:T(8,128)(2,1)S(1)} %get-tuple-element.248.qkv, f32[8,512]{1,0:T(8,128)S(1)} %get-tuple-element.249.logsum, ...), custom_call_target="tpu_custom_call" | custom-call | flops 1 | bytes 18450000 | tf_op jit(solution)/shard_map/attn_backward/pallas_call | solution.py:36
  85.9 1.0 collective-permute-start.39
  87.1 1.3 collective-permute-start.40
  91.5 4.0 %collective-permute-done.39.recv = bf16[192,768]{1,0:T(8,128)(2,1)S(1)} collective-permute-done((bf16[192,768]{1,0:T(8,128)(2,1)S(1)}, bf16[192,768]{1,0:T(8,128)(2,1)S(1)}, u32[]{:S(2)}, u32[]{:S(2)}) %collective-permute-start.39) | collective-permute-done | bytes 294944 | tf_op jit(solution)/shard_map/ppermute | solution.py:746
  95.6 1.6 collective-permute-start.43
  98.0 1.1 collective-permute-start.45
  99.2 2.6 %collective-permute-done.42.recv = bf16[192,768]{1,0:T(8,128)(2,1)S(1)} collective-permute-done((bf16[192,768]{1,0:T(8,128)(2,1)S(1)}, bf16[192,768]{1,0:T(8,128)(2,1)S(1)}, u32[]{:S(2)}, u32[]{:S(2)}) %collective-permute-start.42) | collective-permute-done | bytes 294944 | tf_op jit(solution)/shard_map/ppermute | solution.py:746
  102.0 1.9 %collective-permute-start.46 = (bf16[192,768]{1,0:T(8,128)(2,1)S(1)}, bf16[192,768]{1,0:T(8,128)(2,1)S(1)}, u32[]{:S(2)}, u32[]{:S(2)}) collective-permute-start(bf16[192,768]{1,0:T(8,128)(2,1)S(1)} %get-tuple-element.290), channel_id=1, source_target_pairs={{0,8},{4,12},{24,16},{28,20},{1,9},{5,13},{25,17},{29,21},{2,10},{... | collective-permute-start | bytes 884744 | tf_op jit(solution)/shard_map/ppermute | solution.py:746
  103.8 1.3 collective-permute-start.47
  108.8 3.7 %collective-permute-done.47.recv = bf16[192,768]{1,0:T(8,128)(2,1)S(1)} collective-permute-done((bf16[192,768]{1,0:T(8,128)(2,1)S(1)}, bf16[192,768]{1,0:T(8,128)(2,1)S(1)}, u32[]{:S(2)}, u32[]{:S(2)}) %collective-permute-start.47) | collective-permute-done | bytes 294944 | tf_op jit(solution)/shard_map/ppermute | solution.py:746
  112.6 1.4 collective-permute-start.51
  114.0 5.8 %collective-permute-start.54 = (bf16[192,768]{1,0:T(8,128)(2,1)S(1)}, bf16[192,768]{1,0:T(8,128)(2,1)S(1)}, u32[]{:S(2)}, u32[]{:S(2)}) collective-permute-start(bf16[192,768]{1,0:T(8,128)(2,1)S(1)} %get-tuple-element.297), channel_id=1, source_target_pairs={{0,8},{4,12},{24,16},{28,20},{1,9},{5,13},{25,17},{29,21},{2,10},{... | collective-permute-start | bytes 884744 | tf_op jit(solution)/shard_map/ppermute | solution.py:746
  119.9 1.3 collective-permute-start.57
  121.3 1.3 collective-permute-start.55
  122.8 1.3 collective-permute-start.58
  125.0 2.2 %collective-permute-done.54.recv = bf16[192,768]{1,0:T(8,128)(2,1)S(1)} collective-permute-done((bf16[192,768]{1,0:T(8,128)(2,1)S(1)}, bf16[192,768]{1,0:T(8,128)(2,1)S(1)}, u32[]{:S(2)}, u32[]{:S(2)}) %collective-permute-start.54) | collective-permute-done | bytes 294944 | tf_op jit(solution)/shard_map/ppermute | solution.py:746
  127.9 1.1 qkv_input_grad.1
  129.0 3.8 %collective-permute-done.55.recv = bf16[192,768]{1,0:T(8,128)(2,1)S(1)} collective-permute-done((bf16[192,768]{1,0:T(8,128)(2,1)S(1)}, bf16[192,768]{1,0:T(8,128)(2,1)S(1)}, u32[]{:S(2)}, u32[]{:S(2)}) %collective-permute-start.55) | collective-permute-done | bytes 294944 | tf_op jit(solution)/shard_map/ppermute | solution.py:746
  133.7 1.3 collective-permute-start.60
  135.0 1.2 collective-permute-start.62
  136.8 1.1 collective-permute-start.63
  138.0 5.4 %collective-permute-done.60.recv = bf16[192,768]{1,0:T(8,128)(2,1)S(1)} collective-permute-done((bf16[192,768]{1,0:T(8,128)(2,1)S(1)}, bf16[192,768]{1,0:T(8,128)(2,1)S(1)}, u32[]{:S(2)}, u32[]{:S(2)}) %collective-permute-start.60) | collective-permute-done | bytes 294944 | tf_op jit(solution)/shard_map/ppermute | solution.py:746
  143.6 1.3 collective-permute-start.68
  144.9 1.3 collective-permute-start.64
  146.2 1.0 collective-permute-start.66
  147.2 1.6 collective-permute-done.63.other1
  148.8 1.1 collective-permute-start.67
  149.9 1.6 in_gradient.1
  151.5 9.1 %collective-permute-done.64.recv = bf16[192,768]{1,0:T(8,128)(2,1)S(1)} collective-permute-done((bf16[192,768]{1,0:T(8,128)(2,1)S(1)}, bf16[192,768]{1,0:T(8,128)(2,1)S(1)}, u32[]{:S(2)}, u32[]{:S(2)}) %collective-permute-start.64) | collective-permute-done | bytes 294944 | tf_op jit(solution)/shard_map/ppermute | solution.py:746
  160.7 1.2 collective-permute-start.69
  162.7 1.6 back_gradient.1
  164.4 1.2 collective-permute-start.70
  165.5 1.4 vector_outputs.1
  168.3 2.9 %collective-permute-done.71.vo_other = bf16[192,768]{1,0:T(8,128)(2,1)S(1)} collective-permute-done((bf16[192,768]{1,0:T(8,128)(2,1)S(1)}, bf16[192,768]{1,0:T(8,128)(2,1)S(1)}, u32[]{:S(2)}, u32[]{:S(2)}) %collective-permute-start.71) | collective-permute-done | bytes 294944 | tf_op jit(solution)/shard_map/ppermute | solution.py:746
  171.2 3.2 %collective-permute-done.70.qk_other = bf16[192,768]{1,0:T(8,128)(2,1)S(1)} collective-permute-done((bf16[192,768]{1,0:T(8,128)(2,1)S(1)}, bf16[192,768]{1,0:T(8,128)(2,1)S(1)}, u32[]{:S(2)}, u32[]{:S(2)}) %collective-permute-start.70) | collective-permute-done | bytes 294944 | tf_op jit(solution)/shard_map/ppermute | solution.py:746
  174.4 1.6 attn_gradients.1
  (171 shorter events, 32.4 us)
Async XLA Ops:
  0.7 9.4 %collective-permute-start.3 = (bf16[768,768]{1,0:T(8,128)(2,1)}, bf16[768,768]{1,0:T(8,128)(2,1)S(1)}, u32[]{:S(2)}, u32[]{:S(2)}) collective-permute-start(bf16[768,768]{1,0:T(8,128)(2,1)} %wi_own.1), channel_id=1, source_target_pairs={{0,1},{1,0},{2,3},{3,2},{4,5},{5,4},{6,7},{7,6},{8,9},{9,8},{10,11... | collective-permute-start | bytes 3538952 | tf_op jit(solution)/shard_map/ppermute | solution.py:24
  1.2 8.9 %collective-permute-start.5 = (bf16[192,3072]{1,0:T(8,128)(2,1)}, bf16[192,3072]{1,0:T(8,128)(2,1)S(1)}, u32[]{:S(2)}, u32[]{:S(2)}) collective-permute-start(bf16[192,3072]{1,0:T(8,128)(2,1)} %own.3), channel_id=1, source_target_pairs={{0,1},{1,0},{2,3},{3,2},{4,5},{5,4},{6,7},{7,6},{8,9},{9,8},{10,11... | collective-permute-start | bytes 3538952 | tf_op jit(solution)/shard_map/ppermute | solution.py:24
  1.3 8.8 %collective-permute-start.4 = (bf16[192,768]{1,0:T(8,128)(2,1)}, bf16[192,768]{1,0:T(8,128)(2,1)S(1)}, u32[]{:S(2)}, u32[]{:S(2)}) collective-permute-start(bf16[192,768]{1,0:T(8,128)(2,1)} %own.2), channel_id=1, source_target_pairs={{0,1},{1,0},{2,3},{3,2},{4,5},{5,4},{6,7},{7,6},{8,9},{9,8},{10,11... | collective-permute-start | bytes 884744 | tf_op jit(solution)/shard_map/ppermute | solution.py:24
  1.8 7.4 %collective-permute-start = (bf16[192,512]{1,0:T(8,128)(2,1)}, bf16[192,512]{1,0:T(8,128)(2,1)S(1)}, u32[]{:S(2)}, u32[]{:S(2)}) collective-permute-start(bf16[192,512]{1,0:T(8,128)(2,1)} %param.18), channel_id=1, source_target_pairs={{0,1},{1,0},{2,3},{3,2},{4,5},{5,4},{6,7},{7,6},{8,9},{9,8},{10,11... | collective-permute-start | bytes 589832 | tf_op jit(solution)/shard_map/ppermute | solution.py:24
  1.8 8.3 %collective-permute-start.2 = (bf16[192,512]{1,0:T(8,128)(2,1)}, bf16[192,512]{1,0:T(8,128)(2,1)S(1)}, u32[]{:S(2)}, u32[]{:S(2)}) collective-permute-start(bf16[192,512]{1,0:T(8,128)(2,1)} %param.18), channel_id=1, source_target_pairs={{0,2},{1,3},{2,0},{3,1},{4,6},{5,7},{6,4},{7,5},{8,10},{9,11},{10,... | collective-permute-start | bytes 589832 | tf_op jit(solution)/shard_map/ppermute | solution.py:24
  9.2 3.1 %collective-permute-start.1 = (bf16[192,512]{1,0:T(8,128)(2,1)S(1)}, bf16[192,512]{1,0:T(8,128)(2,1)S(1)}, u32[]{:S(2)}, u32[]{:S(2)}) collective-permute-start(bf16[192,512]{1,0:T(8,128)(2,1)S(1)} %collective-permute-done.x1), channel_id=1, source_target_pairs={{0,1},{1,0},{2,3},{3,2},{4,5},{5,4},{6,7},{7,6},{8,9},{9,8},{10,11... | collective-permute-start | bytes 589832 | tf_op jit(solution)/shard_map/ppermute | solution.py:24
  10.1 2.2 %collective-permute-start.6 = (bf16[192,512]{1,0:T(8,128)(2,1)S(1)}, bf16[192,512]{1,0:T(8,128)(2,1)S(1)}, u32[]{:S(2)}, u32[]{:S(2)}) collective-permute-start(bf16[192,512]{1,0:T(8,128)(2,1)S(1)} %collective-permute-done.2.x2), channel_id=1, source_target_pairs={{0,1},{1,0},{2,3},{3,2},{4,5},{5,4},{6,7},{7,6},{8,9},{9,8},{10,11... | collective-permute-start | bytes 589832 | tf_op jit(solution)/shard_map/ppermute | solution.py:24
  10.2 7.4 %collective-permute-start.12 = (bf16[96,768]{1,0:T(8,128)(2,1)S(1)}, bf16[96,768]{1,0:T(8,128)(2,1)S(1)}, u32[]{:S(2)}, u32[]{:S(2)}) collective-permute-start(bf16[96,768]{1,0:T(8,128)(2,1)S(1)} %get-tuple-element.201), channel_id=1, source_target_pairs={{0,2},{1,3},{2,0},{3,1},{4,6},{5,7},{6,4},{7,5},{8,10},{9,11},{10,... | collective-permute-start | bytes 442376 | tf_op jit(solution)/shard_map/ppermute | solution.py:24
  12.0 14.5 %collective-permute-start.18 = (bf16[192,768]{1,0:T(8,128)(2,1)S(1)}, bf16[192,768]{1,0:T(8,128)(2,1)S(1)}, u32[]{:S(2)}, u32[]{:S(2)}) collective-permute-start(bf16[192,768]{1,0:T(8,128)(2,1)S(1)} %get-tuple-element.187), channel_id=1, source_target_pairs={{0,2},{1,3},{2,0},{3,1},{4,6},{5,7},{6,4},{7,5},{8,10},{9,11},{10,... | collective-permute-start | bytes 884744 | tf_op jit(solution)/shard_map/ppermute | solution.py:24
  15.7 10.2 %collective-permute-start.8 = (bf16[576,128]{1,0:T(8,128)(2,1)S(1)}, bf16[576,128]{1,0:T(8,128)(2,1)S(1)}, u32[]{:S(2)}, u32[]{:S(2)}) collective-permute-start(bf16[576,128]{1,0:T(8,128)(2,1)S(1)} %get-tuple-element.197), channel_id=1, source_target_pairs={{0,2},{1,3},{2,0},{3,1},{4,6},{5,7},{6,4},{7,5},{8,10},{9,11},{10,... | collective-permute-start | bytes 442376 | tf_op jit(solution)/shard_map/ppermute | solution.py:24
  17.6 8.9 %collective-permute-start.13 = (bf16[96,768]{1,0:T(8,128)(2,1)S(1)}, bf16[96,768]{1,0:T(8,128)(2,1)S(1)}, u32[]{:S(2)}, u32[]{:S(2)}) collective-permute-start(bf16[96,768]{1,0:T(8,128)(2,1)S(1)} %collective-permute-done.12.xa), channel_id=1, source_target_pairs={{0,4},{4,0},{8,12},{12,8},{16,20},{20,16},{24,28},{28,24},{1,5},{5... | collective-permute-start | bytes 442376 | tf_op jit(solution)/shard_map/ppermute | solution.py:24
  19.1 2.5 %collective-permute-start.7 = (bf16[384,128]{1,0:T(8,128)(2,1)S(1)}, bf16[384,128]{1,0:T(8,128)(2,1)S(1)}, u32[]{:S(2)}, u32[]{:S(2)}) collective-permute-start(bf16[384,128]{1,0:T(8,128)(2,1)S(1)} %get-tuple-element.196), channel_id=1, source_target_pairs={{0,1},{1,0},{2,3},{3,2},{4,5},{5,4},{6,7},{7,6},{8,9},{9,8},{10,11... | collective-permute-start | bytes 294920 | tf_op jit(solution)/shard_map/ppermute | solution.py:24
  25.9 2.4 %collective-permute-start.11 = (bf16[576,128]{1,0:T(8,128)(2,1)S(1)}, bf16[576,128]{1,0:T(8,128)(2,1)S(1)}, u32[]{:S(2)}, u32[]{:S(2)}) collective-permute-start(bf16[576,128]{1,0:T(8,128)(2,1)S(1)} %collective-permute-done.8.p2.g2), channel_id=1, source_target_pairs={{0,1},{1,0},{2,3},{3,2},{4,5},{5,4},{6,7},{7,6},{8,9},{9,8},{10,11... | collective-permute-start | bytes 442376 | tf_op jit(solution)/shard_map/ppermute | solution.py:24
  25.9 2.7 %collective-permute-start.14 = (bf16[96,768]{1,0:T(8,128)(2,1)S(1)}, bf16[96,768]{1,0:T(8,128)(2,1)S(1)}, u32[]{:S(2)}, u32[]{:S(2)}) collective-permute-start(bf16[96,768]{1,0:T(8,128)(2,1)S(1)} %collective-permute-done.12.xa), channel_id=1, source_target_pairs={{0,1},{1,0},{2,3},{3,2},{4,5},{5,4},{6,7},{7,6},{8,9},{9,8},{10,11... | collective-permute-start | bytes 442376 | tf_op jit(solution)/shard_map/ppermute | solution.py:24
  26.5 9.4 %collective-permute-start.19 = (bf16[192,768]{1,0:T(8,128)(2,1)S(1)}, bf16[192,768]{1,0:T(8,128)(2,1)S(1)}, u32[]{:S(2)}, u32[]{:S(2)}) collective-permute-start(bf16[192,768]{1,0:T(8,128)(2,1)S(1)} %collective-permute-done.18.xa), channel_id=1, source_target_pairs={{0,4},{4,0},{8,12},{12,8},{16,20},{20,16},{24,28},{28,24},{1,5},{5... | collective-permute-start | bytes 884744 | tf_op jit(solution)/shard_map/ppermute | solution.py:24
  29.6 9.1 %collective-permute-start.16 = (bf16[192,768]{1,0:T(8,128)(2,1)S(1)}, bf16[192,768]{1,0:T(8,128)(2,1)S(1)}, u32[]{:S(2)}, u32[]{:S(2)}) collective-permute-start(bf16[192,768]{1,0:T(8,128)(2,1)S(1)} %get-tuple-element.211.rows.n0), channel_id=1, source_target_pairs={{0,2},{1,3},{2,0},{3,1},{4,6},{5,7},{6,4},{7,5},{8,10},{9,11},{10,... | collective-permute-start | bytes 884744 | tf_op jit(solution)/shard_map/ppermute | solution.py:24
  31.1 8.1 %collective-permute-start.20 = (bf16[192,768]{1,0:T(8,128)(2,1)S(1)}, bf16[192,768]{1,0:T(8,128)(2,1)S(1)}, u32[]{:S(2)}, u32[]{:S(2)}) collective-permute-start(bf16[192,768]{1,0:T(8,128)(2,1)S(1)} %collective-permute-done.18.xa), channel_id=1, source_target_pairs={{0,1},{1,0},{2,3},{3,2},{4,5},{5,4},{6,7},{7,6},{8,9},{9,8},{10,11... | collective-permute-start | bytes 884744 | tf_op jit(solution)/shard_map/ppermute | solution.py:24
  38.7 6.6 %collective-permute-start.17 = (bf16[192,768]{1,0:T(8,128)(2,1)S(1)}, bf16[192,768]{1,0:T(8,128)(2,1)S(1)}, u32[]{:S(2)}, u32[]{:S(2)}) collective-permute-start(bf16[192,768]{1,0:T(8,128)(2,1)S(1)} %get-tuple-element.211.rows.n0), channel_id=1, source_target_pairs={{0,1},{1,0},{2,3},{3,2},{4,5},{5,4},{6,7},{7,6},{8,9},{9,8},{10,11... | collective-permute-start | bytes 884744 | tf_op jit(solution)/shard_map/ppermute | solution.py:24
  41.9 7.5 %collective-permute-start.22 = (bf16[192,768]{1,0:T(8,128)(2,1)S(1)}, bf16[192,768]{1,0:T(8,128)(2,1)S(1)}, u32[]{:S(2)}, u32[]{:S(2)}) collective-permute-start(bf16[192,768]{1,0:T(8,128)(2,1)S(1)} %collective-permute-done.16.rows.n_x.n1), channel_id=1, source_target_pairs={{0,1},{1,0},{2,3},{3,2},{4,5},{5,4},{6,7},{7,6},{8,9},{9,8},{10,11... | collective-permute-start | bytes 884744 | tf_op jit(solution)/shard_map/ppermute | solution.py:24
  42.2 3.2 %collective-permute-start.24 = (bf16[192,512]{1,0:T(8,128)(2,1)S(1)}, bf16[192,512]{1,0:T(8,128)(2,1)S(1)}, u32[]{:S(2)}, u32[]{:S(2)}) collective-permute-start(bf16[192,512]{1,0:T(8,128)(2,1)S(1)} %copy-done.6), channel_id=1, source_target_pairs={{0,1},{1,0},{2,3},{3,2},{4,5},{5,4},{6,7},{7,6},{8,9},{9,8},{10,11... | collective-permute-start | bytes 589832 | tf_op jit(solution)/shard_map/ppermute | solution.py:24
  42.5 7.0 %collective-permute-start.23 = (bf16[128,768]{1,0:T(8,128)(2,1)S(1)}, bf16[128,768]{1,0:T(8,128)(2,1)S(1)}, u32[]{:S(2)}, u32[]{:S(2)}) collective-permute-start(bf16[128,768]{1,0:T(8,128)(2,1)S(1)} %get-tuple-element.209), channel_id=1, source_target_pairs={{0,2},{1,3},{2,0},{3,1},{4,6},{5,7},{6,4},{7,5},{8,10},{9,11},{10,... | collective-permute-start | bytes 589832 | tf_op jit(solution)/shard_map/ppermute | solution.py:24
  50.2 7.5 %collective-permute-start.25 = (bf16[256,768]{1,0:T(8,128)(2,1)S(1)}, bf16[256,768]{1,0:T(8,128)(2,1)S(1)}, u32[]{:S(2)}, u32[]{:S(2)}) collective-permute-start(bf16[256,768]{1,0:T(8,128)(2,1)S(1)} %get-tuple-element.221), channel_id=1, source_target_pairs={{0,1},{1,0},{2,3},{3,2},{4,5},{5,4},{6,7},{7,6},{8,9},{9,8},{10,11... | collective-permute-start | bytes 1179656 | tf_op jit(solution)/shard_map/ppermute | solution.py:24
  50.2 3.3 %collective-permute-start.27 = (bf16[128,768]{1,0:T(8,128)(2,1)S(1)}, bf16[128,768]{1,0:T(8,128)(2,1)S(1)}, u32[]{:S(2)}, u32[]{:S(2)}) collective-permute-start(bf16[128,768]{1,0:T(8,128)(2,1)S(1)} %get-tuple-element.220.rows.f0), channel_id=1, source_target_pairs={{0,1},{1,0},{2,3},{3,2},{4,5},{5,4},{6,7},{7,6},{8,9},{9,8},{10,11... | collective-permute-start | bytes 589832 | tf_op jit(solution)/shard_map/ppermute | solution.py:24
  50.7 6.9 %collective-permute-start.26 = (bf16[128,768]{1,0:T(8,128)(2,1)S(1)}, bf16[128,768]{1,0:T(8,128)(2,1)S(1)}, u32[]{:S(2)}, u32[]{:S(2)}) collective-permute-start(bf16[128,768]{1,0:T(8,128)(2,1)S(1)} %get-tuple-element.220.rows.f0), channel_id=1, source_target_pairs={{0,2},{1,3},{2,0},{3,1},{4,6},{5,7},{6,4},{7,5},{8,10},{9,11},{10,... | collective-permute-start | bytes 589832 | tf_op jit(solution)/shard_map/ppermute | solution.py:24
  59.5 6.9 %collective-permute-start.30 = (bf16[128,768]{1,0:T(8,128)(2,1)S(1)}, bf16[128,768]{1,0:T(8,128)(2,1)S(1)}, u32[]{:S(2)}, u32[]{:S(2)}) collective-permute-start(bf16[128,768]{1,0:T(8,128)(2,1)S(1)} %get-tuple-element.232), channel_id=1, source_target_pairs={{0,2},{1,3},{2,0},{3,1},{4,6},{5,7},{6,4},{7,5},{8,10},{9,11},{10,... | collective-permute-start | bytes 589832 | tf_op jit(solution)/shard_map/ppermute | solution.py:24
  68.6 13.1 %collective-permute-start.37 = (bf16[384,768]{1,0:T(8,128)(2,1)S(1)}, bf16[384,768]{1,0:T(8,128)(2,1)S(1)}, u32[]{:S(2)}, u32[]{:S(2)}) collective-permute-start(bf16[384,768]{1,0:T(8,128)(2,1)S(1)} %get-tuple-element.273), channel_id=1, source_target_pairs={{0,1},{1,0},{2,3},{3,2},{4,5},{5,4},{6,7},{7,6},{8,9},{9,8},{10,11... | collective-permute-start | bytes 1769480 | tf_op jit(solution)/shard_map/ppermute | solution.py:24
  68.7 9.3 %collective-permute-start.32 = (bf16[192,768]{1,0:T(8,128)(2,1)S(1)}, bf16[192,768]{1,0:T(8,128)(2,1)S(1)}, u32[]{:S(2)}, u32[]{:S(2)}) collective-permute-start(bf16[192,768]{1,0:T(8,128)(2,1)S(1)} %get-tuple-element.246), channel_id=1, source_target_pairs={{0,4},{4,0},{8,12},{12,8},{16,20},{20,16},{24,28},{28,24},{1,5},{5... | collective-permute-start | bytes 884744 | tf_op jit(solution)/shard_map/ppermute | solution.py:746
  69.7 5.3 %collective-permute-start.33 = (bf16[480,128]{1,0:T(8,128)(2,1)S(1)}, bf16[480,128]{1,0:T(8,128)(2,1)S(1)}, u32[]{:S(2)}, u32[]{:S(2)}) collective-permute-start(bf16[480,128]{1,0:T(8,128)(2,1)S(1)} %get-tuple-element.251), channel_id=1, source_target_pairs={{0,2},{1,3},{2,0},{3,1},{4,6},{5,7},{6,4},{7,5},{8,10},{9,11},{10,... | collective-permute-start | bytes 368648 | tf_op jit(solution)/shard_map/ppermute | solution.py:24
  75.0 6.7 %collective-permute-start.34 = (bf16[480,128]{1,0:T(8,128)(2,1)S(1)}, bf16[480,128]{1,0:T(8,128)(2,1)S(1)}, u32[]{:S(2)}, u32[]{:S(2)}) collective-permute-start(bf16[480,128]{1,0:T(8,128)(2,1)S(1)} %collective-permute-done.33.u2), channel_id=1, source_target_pairs={{0,1},{1,0},{2,3},{3,2},{4,5},{5,4},{6,7},{7,6},{8,9},{9,8},{10,11... | collective-permute-start | bytes 368648 | tf_op jit(solution)/shard_map/ppermute | solution.py:24
  75.1 11.9 %collective-permute-start.35 = (bf16[192,768]{1,0:T(8,128)(2,1)S(1)}, bf16[192,768]{1,0:T(8,128)(2,1)S(1)}, u32[]{:S(2)}, u32[]{:S(2)}) collective-permute-start(bf16[192,768]{1,0:T(8,128)(2,1)S(1)} %get-tuple-element.257), channel_id=1, source_target_pairs={{0,4},{4,0},{8,12},{12,8},{16,20},{20,16},{24,28},{28,24},{1,5},{5... | collective-permute-start | bytes 884744 | tf_op jit(solution)/shard_map/ppermute | solution.py:746
  78.1 10.9 %collective-permute-start.36 = (bf16[192,768]{1,0:T(8,128)(2,1)S(1)}, bf16[192,768]{1,0:T(8,128)(2,1)S(1)}, u32[]{:S(2)}, u32[]{:S(2)}) collective-permute-start(bf16[192,768]{1,0:T(8,128)(2,1)S(1)} %get-tuple-element.247), channel_id=1, source_target_pairs={{0,8},{4,12},{24,16},{28,20},{1,9},{5,13},{25,17},{29,21},{2,10},{... | collective-permute-start | bytes 884744 | tf_op jit(solution)/shard_map/ppermute | solution.py:746
  81.7 8.2 %collective-permute-start.38 = (bf16[192,768]{1,0:T(8,128)(2,1)S(1)}, bf16[192,768]{1,0:T(8,128)(2,1)S(1)}, u32[]{:S(2)}, u32[]{:S(2)}) collective-permute-start(bf16[192,768]{1,0:T(8,128)(2,1)S(1)} %wo_low.1), channel_id=1, source_target_pairs={{0,2},{1,3},{2,0},{3,1},{4,6},{5,7},{6,4},{7,5},{8,10},{9,11},{10,... | collective-permute-start | bytes 884744 | tf_op jit(solution)/shard_map/ppermute | solution.py:24
  85.9 9.6 %collective-permute-start.39 = (bf16[192,768]{1,0:T(8,128)(2,1)S(1)}, bf16[192,768]{1,0:T(8,128)(2,1)S(1)}, u32[]{:S(2)}, u32[]{:S(2)}) collective-permute-start(bf16[192,768]{1,0:T(8,128)(2,1)S(1)} %get-tuple-element.281), channel_id=1, source_target_pairs={{0,4},{4,0},{8,12},{12,8},{16,20},{20,16},{24,28},{28,24},{1,5},{5... | collective-permute-start | bytes 884744 | tf_op jit(solution)/shard_map/ppermute | solution.py:746
  87.1 10.2 %collective-permute-start.40 = (bf16[192,768]{1,0:T(8,128)(2,1)S(1)}, bf16[192,768]{1,0:T(8,128)(2,1)S(1)}, u32[]{:S(2)}, u32[]{:S(2)}) collective-permute-start(bf16[192,768]{1,0:T(8,128)(2,1)S(1)} %get-tuple-element.258), channel_id=1, source_target_pairs={{0,8},{4,12},{24,16},{28,20},{1,9},{5,13},{25,17},{29,21},{2,10},{... | collective-permute-start | bytes 884744 | tf_op jit(solution)/shard_map/ppermute | solution.py:746
  89.1 10.0 %collective-permute-start.41 = (bf16[192,768]{1,0:T(8,128)(2,1)S(1)}, bf16[192,768]{1,0:T(8,128)(2,1)S(1)}, u32[]{:S(2)}, u32[]{:S(2)}) collective-permute-start(bf16[192,768]{1,0:T(8,128)(2,1)S(1)} %second_add.5.mine), channel_id=1, source_target_pairs={{8,16},{12,20},{16,8},{20,12},{9,17},{13,21},{17,9},{21,13},{10,18... | collective-permute-start | bytes 884744 | tf_op jit(solution)/shard_map/ppermute | solution.py:746
  90.5 11.3 %collective-permute-start.42 = (bf16[192,768]{1,0:T(8,128)(2,1)S(1)}, bf16[192,768]{1,0:T(8,128)(2,1)S(1)}, u32[]{:S(2)}, u32[]{:S(2)}) collective-permute-start(bf16[192,768]{1,0:T(8,128)(2,1)S(1)} %get-tuple-element.289), channel_id=1, source_target_pairs={{0,4},{4,0},{8,12},{12,8},{16,20},{20,16},{24,28},{28,24},{1,5},{5... | collective-permute-start | bytes 884744 | tf_op jit(solution)/shard_map/ppermute | solution.py:746
  95.6 9.5 %collective-permute-start.43 = (bf16[192,768]{1,0:T(8,128)(2,1)S(1)}, bf16[192,768]{1,0:T(8,128)(2,1)S(1)}, u32[]{:S(2)}, u32[]{:S(2)}) collective-permute-start(bf16[192,768]{1,0:T(8,128)(2,1)S(1)} %get-tuple-element.282), channel_id=1, source_target_pairs={{0,8},{4,12},{24,16},{28,20},{1,9},{5,13},{25,17},{29,21},{2,10},{... | collective-permute-start | bytes 884744 | tf_op jit(solution)/shard_map/ppermute | solution.py:746
  97.3 8.6 %collective-permute-start.44 = (bf16[192,768]{1,0:T(8,128)(2,1)S(1)}, bf16[192,768]{1,0:T(8,128)(2,1)S(1)}, u32[]{:S(2)}, u32[]{:S(2)}) collective-permute-start(bf16[192,768]{1,0:T(8,128)(2,1)S(1)} %second_add.6.mine), channel_id=1, source_target_pairs={{8,16},{12,20},{16,8},{20,12},{9,17},{13,21},{17,9},{21,13},{10,18... | collective-permute-start | bytes 884744 | tf_op jit(solution)/shard_map/ppermute | solution.py:746
  98.0 9.1 %collective-permute-start.45 = (bf16[192,768]{1,0:T(8,128)(2,1)S(1)}, bf16[192,768]{1,0:T(8,128)(2,1)S(1)}, u32[]{:S(2)}, u32[]{:S(2)}) collective-permute-start(bf16[192,768]{1,0:T(8,128)(2,1)S(1)} %get-tuple-element.279), channel_id=1, source_target_pairs={{0,4},{4,0},{8,12},{12,8},{16,20},{20,16},{24,28},{28,24},{1,5},{5... | collective-permute-start | bytes 884744 | tf_op jit(solution)/shard_map/ppermute | solution.py:746
  102.0 6.1 %collective-permute-start.46 = (bf16[192,768]{1,0:T(8,128)(2,1)S(1)}, bf16[192,768]{1,0:T(8,128)(2,1)S(1)}, u32[]{:S(2)}, u32[]{:S(2)}) collective-permute-start(bf16[192,768]{1,0:T(8,128)(2,1)S(1)} %get-tuple-element.290), channel_id=1, source_target_pairs={{0,8},{4,12},{24,16},{28,20},{1,9},{5,13},{25,17},{29,21},{2,10},{... | collective-permute-start | bytes 884744 | tf_op jit(solution)/shard_map/ppermute | solution.py:746
  103.8 8.6 %collective-permute-start.47 = (bf16[192,768]{1,0:T(8,128)(2,1)S(1)}, bf16[192,768]{1,0:T(8,128)(2,1)S(1)}, u32[]{:S(2)}, u32[]{:S(2)}) collective-permute-start(bf16[192,768]{1,0:T(8,128)(2,1)S(1)} %third_add.3.mine), channel_id=1, source_target_pairs={{8,0},{12,4},{16,24},{20,28},{9,1},{13,5},{17,25},{21,29},{10,2},{... | collective-permute-start | bytes 884744 | tf_op jit(solution)/shard_map/ppermute | solution.py:746
  105.2 7.3 %collective-permute-start.48 = (bf16[192,768]{1,0:T(8,128)(2,1)S(1)}, bf16[192,768]{1,0:T(8,128)(2,1)S(1)}, u32[]{:S(2)}, u32[]{:S(2)}) collective-permute-start(bf16[192,768]{1,0:T(8,128)(2,1)S(1)} %second_add.7.mine), channel_id=1, source_target_pairs={{8,16},{12,20},{16,8},{20,12},{9,17},{13,21},{17,9},{21,13},{10,18... | collective-permute-start | bytes 884744 | tf_op jit(solution)/shard_map/ppermute | solution.py:746
  105.9 13.9 %collective-permute-start.50 = (bf16[224,768]{1,0:T(8,128)(2,1)S(1)}, bf16[224,768]{1,0:T(8,128)(2,1)S(1)}, u32[]{:S(2)}, u32[]{:S(2)}) collective-permute-start(bf16[224,768]{1,0:T(8,128)(2,1)S(1)} %get-tuple-element.266), channel_id=1, source_target_pairs={{0,4},{4,0},{8,12},{12,8},{16,20},{20,16},{24,28},{28,24},{1,5},{5... | collective-permute-start | bytes 1032200 | tf_op jit(solution)/shard_map/ppermute | solution.py:746
  107.1 5.5 %collective-permute-start.49 = (bf16[96,768]{1,0:T(8,128)(2,1)S(1)}, bf16[96,768]{1,0:T(8,128)(2,1)S(1)}, u32[]{:S(2)}, u32[]{:S(2)}) collective-permute-start(bf16[96,768]{1,0:T(8,128)(2,1)S(1)} %get-tuple-element.293), channel_id=1, source_target_pairs={{0,1},{1,0},{2,3},{3,2},{4,5},{5,4},{6,7},{7,6},{8,9},{9,8},{10,11... | collective-permute-start | bytes 442376 | tf_op jit(solution)/shard_map/ppermute | solution.py:24
  108.1 14.5 %collective-permute-start.52 = (bf16[192,768]{1,0:T(8,128)(2,1)S(1)}, bf16[192,768]{1,0:T(8,128)(2,1)S(1)}, u32[]{:S(2)}, u32[]{:S(2)}) collective-permute-start(bf16[192,768]{1,0:T(8,128)(2,1)S(1)} %second_add.8.mine), channel_id=1, source_target_pairs={{8,16},{12,20},{16,8},{20,12},{9,17},{13,21},{17,9},{21,13},{10,18... | collective-permute-start | bytes 884744 | tf_op jit(solution)/shard_map/ppermute | solution.py:746
  112.6 8.6 %collective-permute-start.51 = (bf16[96,768]{1,0:T(8,128)(2,1)S(1)}, bf16[96,768]{1,0:T(8,128)(2,1)S(1)}, u32[]{:S(2)}, u32[]{:S(2)}) collective-permute-start(bf16[96,768]{1,0:T(8,128)(2,1)S(1)} %second_half.2), channel_id=1, source_target_pairs={{0,2},{1,3},{2,0},{3,1},{4,6},{5,7},{6,4},{7,5},{8,10},{9,11},{10,... | collective-permute-start | bytes 442376 | tf_op jit(solution)/shard_map/ppermute | solution.py:24
  114.0 13.2 %collective-permute-start.54 = (bf16[192,768]{1,0:T(8,128)(2,1)S(1)}, bf16[192,768]{1,0:T(8,128)(2,1)S(1)}, u32[]{:S(2)}, u32[]{:S(2)}) collective-permute-start(bf16[192,768]{1,0:T(8,128)(2,1)S(1)} %get-tuple-element.297), channel_id=1, source_target_pairs={{0,8},{4,12},{24,16},{28,20},{1,9},{5,13},{25,17},{29,21},{2,10},{... | collective-permute-start | bytes 884744 | tf_op jit(solution)/shard_map/ppermute | solution.py:746
  119.9 13.0 %collective-permute-start.57 = (bf16[224,768]{1,0:T(8,128)(2,1)S(1)}, bf16[224,768]{1,0:T(8,128)(2,1)S(1)}, u32[]{:S(2)}, u32[]{:S(2)}) collective-permute-start(bf16[224,768]{1,0:T(8,128)(2,1)S(1)} %get-tuple-element.307.mine), channel_id=1, source_target_pairs={{0,8},{4,12},{24,16},{28,20},{1,9},{5,13},{25,17},{29,21},{2,10},{... | collective-permute-start | bytes 1032200 | tf_op jit(solution)/shard_map/ppermute | solution.py:746
  121.3 11.6 %collective-permute-start.55 = (bf16[192,768]{1,0:T(8,128)(2,1)S(1)}, bf16[192,768]{1,0:T(8,128)(2,1)S(1)}, u32[]{:S(2)}, u32[]{:S(2)}) collective-permute-start(bf16[192,768]{1,0:T(8,128)(2,1)S(1)} %join_owners.2.mine), channel_id=1, source_target_pairs={{8,0},{12,4},{16,24},{20,28},{9,1},{13,5},{17,25},{21,29},{10,2},{... | collective-permute-start | bytes 884744 | tf_op jit(solution)/shard_map/ppermute | solution.py:746
  122.8 14.0 %collective-permute-start.58 = (bf16[192,768]{1,0:T(8,128)(2,1)S(1)}, bf16[192,768]{1,0:T(8,128)(2,1)S(1)}, u32[]{:S(2)}, u32[]{:S(2)}) collective-permute-start(bf16[192,768]{1,0:T(8,128)(2,1)S(1)} %third_add.4.mine), channel_id=1, source_target_pairs={{8,0},{12,4},{16,24},{20,28},{9,1},{13,5},{17,25},{21,29},{10,2},{... | collective-permute-start | bytes 884744 | tf_op jit(solution)/shard_map/ppermute | solution.py:746
  124.1 8.7 %collective-permute-start.56 = (bf16[96,768]{1,0:T(8,128)(2,1)S(1)}, bf16[96,768]{1,0:T(8,128)(2,1)S(1)}, u32[]{:S(2)}, u32[]{:S(2)}) collective-permute-start(bf16[96,768]{1,0:T(8,128)(2,1)S(1)} %second_half.3), channel_id=1, source_target_pairs={{0,2},{1,3},{2,0},{3,1},{4,6},{5,7},{6,4},{7,5},{8,10},{9,11},{10,... | collective-permute-start | bytes 442376 | tf_op jit(solution)/shard_map/ppermute | solution.py:24
  127.3 10.7 %collective-permute-start.59 = (bf16[192,768]{1,0:T(8,128)(2,1)S(1)}, bf16[192,768]{1,0:T(8,128)(2,1)S(1)}, u32[]{:S(2)}, u32[]{:S(2)}) collective-permute-start(bf16[192,768]{1,0:T(8,128)(2,1)S(1)} %second_add.9.mine), channel_id=1, source_target_pairs={{8,16},{12,20},{16,8},{20,12},{9,17},{13,21},{17,9},{21,13},{10,18... | collective-permute-start | bytes 884744 | tf_op jit(solution)/shard_map/ppermute | solution.py:746
  133.0 10.4 %collective-permute-start.61 = (bf16[224,768]{1,0:T(8,128)(2,1)S(1)}, bf16[224,768]{1,0:T(8,128)(2,1)S(1)}, u32[]{:S(2)}, u32[]{:S(2)}) collective-permute-start(bf16[224,768]{1,0:T(8,128)(2,1)S(1)} %second_add_pair.1.mine), channel_id=1, source_target_pairs={{8,16},{12,20},{16,8},{20,12},{9,17},{13,21},{17,9},{21,13},{10,18... | collective-permute-start | bytes 1032200 | tf_op jit(solution)/shard_map/ppermute | solution.py:746
  133.7 9.7 %collective-permute-start.60 = (bf16[192,768]{1,0:T(8,128)(2,1)S(1)}, bf16[192,768]{1,0:T(8,128)(2,1)S(1)}, u32[]{:S(2)}, u32[]{:S(2)}) collective-permute-start(bf16[192,768]{1,0:T(8,128)(2,1)S(1)} %join_owners.3.mine), channel_id=1, source_target_pairs={{8,0},{12,4},{16,24},{20,28},{9,1},{13,5},{17,25},{21,29},{10,2},{... | collective-permute-start | bytes 884744 | tf_op jit(solution)/shard_map/ppermute | solution.py:746
  135.0 11.1 %collective-permute-start.62 = (bf16[192,768]{1,0:T(8,128)(2,1)S(1)}, bf16[192,768]{1,0:T(8,128)(2,1)S(1)}, u32[]{:S(2)}, u32[]{:S(2)}) collective-permute-start(bf16[192,768]{1,0:T(8,128)(2,1)S(1)} %choose.5.mine0), channel_id=1, source_target_pairs={{0,4},{4,0},{8,12},{12,8},{16,20},{20,16},{24,28},{28,24},{1,5},{5... | collective-permute-start | bytes 884744 | tf_op jit(solution)/shard_map/ppermute | solution.py:746
  136.8 12.0 %collective-permute-start.63 = (bf16[192,768]{1,0:T(8,128)(2,1)S(1)}, bf16[192,768]{1,0:T(8,128)(2,1)S(1)}, u32[]{:S(2)}, u32[]{:S(2)}) collective-permute-start(bf16[192,768]{1,0:T(8,128)(2,1)S(1)} %choose.7.mine1), channel_id=1, source_target_pairs={{0,4},{4,0},{8,12},{12,8},{16,20},{20,16},{24,28},{28,24},{1,5},{5... | collective-permute-start | bytes 884744 | tf_op jit(solution)/shard_map/ppermute | solution.py:746
  137.9 22.7 %collective-permute-start.65 = (bf16[384,640]{1,0:T(8,128)(2,1)S(1)}, bf16[384,640]{1,0:T(8,128)(2,1)S(1)}, u32[]{:S(2)}, u32[]{:S(2)}) collective-permute-start(bf16[384,640]{1,0:T(8,128)(2,1)S(1)} %get-tuple-element.320), channel_id=1, source_target_pairs={{0,1},{1,0},{2,3},{3,2},{4,5},{5,4},{6,7},{7,6},{8,9},{9,8},{10,11... | collective-permute-start | bytes 1474568 | tf_op jit(solution)/shard_map/ppermute | solution.py:24
  143.6 20.7 %collective-permute-start.68 = (bf16[224,768]{1,0:T(8,128)(2,1)S(1)}, bf16[224,768]{1,0:T(8,128)(2,1)S(1)}, u32[]{:S(2)}, u32[]{:S(2)}) collective-permute-start(bf16[224,768]{1,0:T(8,128)(2,1)S(1)} %third_add_pair.1.mine), channel_id=1, source_target_pairs={{8,0},{12,4},{16,24},{20,28},{9,1},{13,5},{17,25},{21,29},{10,2},{... | collective-permute-start | bytes 1032200 | tf_op jit(solution)/shard_map/ppermute | solution.py:746
  144.9 15.7 %collective-permute-start.64 = (bf16[192,768]{1,0:T(8,128)(2,1)S(1)}, bf16[192,768]{1,0:T(8,128)(2,1)S(1)}, u32[]{:S(2)}, u32[]{:S(2)}) collective-permute-start(bf16[192,768]{1,0:T(8,128)(2,1)S(1)} %third_add.5.mine), channel_id=1, source_target_pairs={{8,0},{12,4},{16,24},{20,28},{9,1},{13,5},{17,25},{21,29},{10,2},{... | collective-permute-start | bytes 884744 | tf_op jit(solution)/shard_map/ppermute | solution.py:746
  146.2 16.6 %collective-permute-start.66 = (bf16[192,768]{1,0:T(8,128)(2,1)S(1)}, bf16[192,768]{1,0:T(8,128)(2,1)S(1)}, u32[]{:S(2)}, u32[]{:S(2)}) collective-permute-start(bf16[192,768]{1,0:T(8,128)(2,1)S(1)} %choose.6.mine0), channel_id=1, source_target_pairs={{0,4},{4,0},{8,12},{12,8},{16,20},{20,16},{24,28},{28,24},{1,5},{5... | collective-permute-start | bytes 884744 | tf_op jit(solution)/shard_map/ppermute | solution.py:746
  148.8 13.9 %collective-permute-start.67 = (bf16[192,768]{1,0:T(8,128)(2,1)S(1)}, bf16[192,768]{1,0:T(8,128)(2,1)S(1)}, u32[]{:S(2)}, u32[]{:S(2)}) collective-permute-start(bf16[192,768]{1,0:T(8,128)(2,1)S(1)} %choose.8.mine1), channel_id=1, source_target_pairs={{0,4},{4,0},{8,12},{12,8},{16,20},{20,16},{24,28},{28,24},{1,5},{5... | collective-permute-start | bytes 884744 | tf_op jit(solution)/shard_map/ppermute | solution.py:746
  160.7 6.9 %collective-permute-start.69 = (bf16[192,768]{1,0:T(8,128)(2,1)S(1)}, bf16[192,768]{1,0:T(8,128)(2,1)S(1)}, u32[]{:S(2)}, u32[]{:S(2)}) collective-permute-start(bf16[192,768]{1,0:T(8,128)(2,1)S(1)} %tokens_step.1), channel_id=1, source_target_pairs={{0,2},{1,3},{2,0},{3,1},{4,6},{5,7},{6,4},{7,5},{8,10},{9,11},{10,... | collective-permute-start | bytes 884744 | tf_op jit(solution)/shard_map/ppermute | solution.py:24
  161.8 9.4 %collective-permute-start.71 = (bf16[192,768]{1,0:T(8,128)(2,1)S(1)}, bf16[192,768]{1,0:T(8,128)(2,1)S(1)}, u32[]{:S(2)}, u32[]{:S(2)}) collective-permute-start(bf16[192,768]{1,0:T(8,128)(2,1)S(1)} %choose.9.vo_mine), channel_id=1, source_target_pairs={{0,4},{4,0},{8,12},{12,8},{16,20},{20,16},{24,28},{28,24},{1,5},{5... | collective-permute-start | bytes 884744 | tf_op jit(solution)/shard_map/ppermute | solution.py:746
  164.4 10.0 %collective-permute-start.70 = (bf16[192,768]{1,0:T(8,128)(2,1)S(1)}, bf16[192,768]{1,0:T(8,128)(2,1)S(1)}, u32[]{:S(2)}, u32[]{:S(2)}) collective-permute-start(bf16[192,768]{1,0:T(8,128)(2,1)S(1)} %get-tuple-element.342.qk_mine), channel_id=1, source_target_pairs={{0,4},{4,0},{8,12},{12,8},{16,20},{20,16},{24,28},{28,24},{1,5},{5... | collective-permute-start | bytes 884744 | tf_op jit(solution)/shard_map/ppermute | solution.py:746
  (25 other events, 202.6 us)

commit v5 on v4

--- a/solution.py
+++ b/solution.py
@@ -727,7 +727,7 @@
 
 
 EARLY_TURNS = "313"
-TURNS = "41q3v2413241v2341q122vg132q4v12q4vg2qegvq"
+TURNS = "413vq2413241v3241q122vg13q24v12q4vg2qegvq"
 FIRST = ("in0", "back0")
 
 

time: 177 us -> 175 us (0.989)
  waiting for transfers between devices: 74.5 us -> 69.4 us
  starting transfers between devices: 67.7 us -> 69.8 us
    ppermute x30, waiting for transfers between devices: 42 us -> 36.6 us  [along(): return lax.ppermute(block, 'rows', pairs)]
    ppermute x30, starting transfers between devices: 39.9 us -> 42.5 us  [along(): return lax.ppermute(block, 'rows', pairs)]
  transfers between devices with their start and end apart: 72 -> 72, of which waited for: 29 -> 29; matrix products, arithmetic and copies ran while one was open for 1% -> 1% of each run, Pallas kernels for 13% -> 14%
where the time goes in v5:
time: 175 us; the launch traced here: 173 us
  starting transfers between devices  69.8 us (40%)
  waiting for transfers between devices  69.4 us (40%)
  Pallas kernels  27.9 us (16%)
  local copies, waits for them, and re-layouts  2.95 us (2%)
    ppermute x30, starting transfers between devices, along(): return lax.ppermute(block, 'rows', pairs)  42.5 us
    ppermute x30, waiting for transfers between devices, along(): return lax.ppermute(block, 'rows', pairs)  36.6 us
    ppermute x42, waiting for transfers between devices, swap(): lax.ppermute(block, axis, [(i, i ^ bit) for i in range(lax.axis_size(axis...  32.8 us
    pallas_call x54, Pallas kernels, local_kernel(): pl.pallas_call(body, name=name, out_shape=outs, in_specs=[SPECS[k] for k...  27.9 us
    ppermute x42, starting transfers between devices, swap(): lax.ppermute(block, axis, [(i, i ^ bit) for i in range(lax.axis_size(axis...  27.3 us
  transfers between devices with their start and end apart: 72, of which 29 were waited for; matrix products, arithmetic and copies ran while one was open for 1% of the time, Pallas kernels for 14%

profile of v5, /device:TPU:0, one launch (start us, length us, event | category | flops | bytes accessed | tf_op | source)
XLA Modules:
  0.0 172.9 jit_solution(6912137686378935679)
XLA Ops:
  1.8 2.9 %collective-permute-start.2 = (bf16[192,512]{1,0:T(8,128)(2,1)}, bf16[192,512]{1,0:T(8,128)(2,1)S(1)}, u32[]{:S(2)}, u32[]{:S(2)}) collective-permute-start(bf16[192,512]{1,0:T(8,128)(2,1)} %param.18), channel_id=1, source_target_pairs={{0,2},{1,3},{2,0},{3,1},{4,6},{5,7},{6,4},{7,5},{8,10},{9,11},{10,... | collective-permute-start | bytes 589832 | tf_op jit(solution)/shard_map/ppermute | solution.py:24
  6.8 1.3 copy-done
  10.2 1.8 %collective-permute-start.12 = (bf16[96,768]{1,0:T(8,128)(2,1)S(1)}, bf16[96,768]{1,0:T(8,128)(2,1)S(1)}, u32[]{:S(2)}, u32[]{:S(2)}) collective-permute-start(bf16[96,768]{1,0:T(8,128)(2,1)S(1)} %get-tuple-element.201), channel_id=1, source_target_pairs={{0,2},{1,3},{2,0},{3,1},{4,6},{5,7},{6,4},{7,5},{8,10},{9,11},{10,... | collective-permute-start | bytes 442376 | tf_op jit(solution)/shard_map/ppermute | solution.py:24
  12.3 2.6 %attn_forward.1 = (bf16[768,512]{1,0:T(8,128)(2,1)S(1)}, bf16[3,192,512]{2,1,0:T(8,128)(2,1)S(1)}, f32[8,512]{1,0:T(8,128)S(1)}, bf16[192,128]{1,0:T(8,128)(2,1)...) custom-call(s32[8,512]{1,0:T(8,128)S(1)} %get-tuple-element.185.bounds, ...), custom_call_target="tpu_custom_call" | custom-call | flops 1 | bytes 19926000 | tf_op jit(solution)/shard_map/attn_forward/pallas_call | solution.py:36
  15.7 1.8 %collective-permute-start.8 = (bf16[576,128]{1,0:T(8,128)(2,1)S(1)}, bf16[576,128]{1,0:T(8,128)(2,1)S(1)}, u32[]{:S(2)}, u32[]{:S(2)}) collective-permute-start(bf16[576,128]{1,0:T(8,128)(2,1)S(1)} %get-tuple-element.197), channel_id=1, source_target_pairs={{0,2},{1,3},{2,0},{3,1},{4,6},{5,7},{6,4},{7,5},{8,10},{9,11},{10,... | collective-permute-start | bytes 442376 | tf_op jit(solution)/shard_map/ppermute | solution.py:24
  17.6 1.5 collective-permute-start.13
  21.6 4.4 %collective-permute-done.8.p2.g2 = bf16[576,128]{1,0:T(8,128)(2,1)S(1)} collective-permute-done((bf16[576,128]{1,0:T(8,128)(2,1)S(1)}, bf16[576,128]{1,0:T(8,128)(2,1)S(1)}, u32[]{:S(2)}, u32[]{:S(2)}) %collective-permute-start.8) | collective-permute-done | bytes 147488 | tf_op jit(solution)/shard_map/ppermute | solution.py:24
  26.5 1.8 %collective-permute-start.19 = (bf16[192,768]{1,0:T(8,128)(2,1)S(1)}, bf16[192,768]{1,0:T(8,128)(2,1)S(1)}, u32[]{:S(2)}, u32[]{:S(2)}) collective-permute-start(bf16[192,768]{1,0:T(8,128)(2,1)S(1)} %collective-permute-done.18.xa), channel_id=1, source_target_pairs={{0,4},{4,0},{8,12},{12,8},{16,20},{20,16},{24,28},{28,24},{1,5},{5... | collective-permute-start | bytes 884744 | tf_op jit(solution)/shard_map/ppermute | solution.py:24
  29.6 1.6 collective-permute-start.16
  31.1 4.8 %collective-permute-done.19.xb = bf16[192,768]{1,0:T(8,128)(2,1)S(1)} collective-permute-done((bf16[192,768]{1,0:T(8,128)(2,1)S(1)}, bf16[192,768]{1,0:T(8,128)(2,1)S(1)}, u32[]{:S(2)}, u32[]{:S(2)}) %collective-permute-start.19) | collective-permute-done | bytes 294944 | tf_op jit(solution)/shard_map/ppermute | solution.py:24
  35.9 2.8 %collective-permute-done.16.rows.n_x.n1 = bf16[192,768]{1,0:T(8,128)(2,1)S(1)} collective-permute-done((bf16[192,768]{1,0:T(8,128)(2,1)S(1)}, bf16[192,768]{1,0:T(8,128)(2,1)S(1)}, u32[]{:S(2)}, u32[]{:S(2)}) %collective-permute-start.16) | collective-permute-done | bytes 294944 | tf_op jit(solution)/shard_map/ppermute | solution.py:24
  39.2 1.1 collective-permute-done.21.fb
  40.6 1.3 ffn_forward_far.1
  42.5 1.5 collective-permute-start.23
  44.0 1.3 ffn_forward.1
  45.4 4.1 %collective-permute-done.23.recv = bf16[128,768]{1,0:T(8,128)(2,1)S(1)} collective-permute-done((bf16[128,768]{1,0:T(8,128)(2,1)S(1)}, bf16[128,768]{1,0:T(8,128)(2,1)S(1)}, u32[]{:S(2)}, u32[]{:S(2)}) %collective-permute-start.23) | collective-permute-done | bytes 196640 | tf_op jit(solution)/shard_map/ppermute | solution.py:24
  50.7 1.5 collective-permute-start.26
  52.2 1.3 ffn_backward.1
  53.6 4.0 %collective-permute-done.26.rows.f1 = bf16[128,768]{1,0:T(8,128)(2,1)S(1)} collective-permute-done((bf16[128,768]{1,0:T(8,128)(2,1)S(1)}, bf16[128,768]{1,0:T(8,128)(2,1)S(1)}, u32[]{:S(2)}, u32[]{:S(2)}) %collective-permute-start.26) | collective-permute-done | bytes 196640 | tf_op jit(solution)/shard_map/ppermute | solution.py:24
  57.6 1.3 ffn_backward_far.1
  59.5 1.5 collective-permute-start.30
  61.0 1.9 %ffn_weight_grads.1 = (f32[192,768]{1,0:T(8,128)S(1)}, bf16[192,768]{1,0:T(8,128)(2,1)S(1)}, f32[192,768]{1,0:T(8,128)S(1)}, bf16[192,768]{1,0:T(8,128)(2,1)S(1)...) custom-call(bf16[192,768]{1,0:T(8,128)(2,1)S(1)} %get-tuple-element., ...), custom_call_target="tpu_custom_call" | custom-call | flops 1 | bytes 9225000 | tf_op jit(solution)/shard_map/ffn_weight_grads/pallas_call | solution.py:36
  62.9 3.5 %collective-permute-done.30.recv = bf16[128,768]{1,0:T(8,128)(2,1)S(1)} collective-permute-done((bf16[128,768]{1,0:T(8,128)(2,1)S(1)}, bf16[128,768]{1,0:T(8,128)(2,1)S(1)}, u32[]{:S(2)}, u32[]{:S(2)}) %collective-permute-start.30) | collective-permute-done | bytes 196640 | tf_op jit(solution)/shard_map/ppermute | solution.py:24
  69.7 1.5 collective-permute-start.33
  71.2 1.0 collective-permute-start.35
  72.3 2.8 %collective-permute-done.33.u2 = bf16[480,128]{1,0:T(8,128)(2,1)S(1)} collective-permute-done((bf16[480,128]{1,0:T(8,128)(2,1)S(1)}, bf16[480,128]{1,0:T(8,128)(2,1)S(1)}, u32[]{:S(2)}, u32[]{:S(2)}) %collective-permute-start.33) | collective-permute-done | bytes 122912 | tf_op jit(solution)/shard_map/ppermute | solution.py:24
  75.1 3.5 %collective-permute-done.32.recv = bf16[192,768]{1,0:T(8,128)(2,1)S(1)} collective-permute-done((bf16[192,768]{1,0:T(8,128)(2,1)S(1)}, bf16[192,768]{1,0:T(8,128)(2,1)S(1)}, u32[]{:S(2)}, u32[]{:S(2)}) %collective-permute-start.32) | collective-permute-done | bytes 294944 | tf_op jit(solution)/shard_map/ppermute | solution.py:746
  78.7 3.5 %collective-permute-start.36 = (bf16[192,768]{1,0:T(8,128)(2,1)S(1)}, bf16[192,768]{1,0:T(8,128)(2,1)S(1)}, u32[]{:S(2)}, u32[]{:S(2)}) collective-permute-start(bf16[192,768]{1,0:T(8,128)(2,1)S(1)} %get-tuple-element.247), channel_id=1, source_target_pairs={{0,8},{4,12},{24,16},{28,20},{1,9},{5,13},{25,17},{29,21},{2,10},{... | collective-permute-start | bytes 884744 | tf_op jit(solution)/shard_map/ppermute | solution.py:746
  82.3 1.6 collective-permute-start.38
  83.8 2.6 %attn_backward.1 = (bf16[576,512]{1,0:T(8,128)(2,1)S(1)}, f32[8,128]{1,0:T(8,128)S(1)}, f32[8,576]{1,0:T(8,128)S(1)}) custom-call(s32[8,512]{1,0:T(8,128)S(1)} %get-tuple-element.185.bounds, bf16[3,192,512]{2,1,0:T(8,128)(2,1)S(1)} %get-tuple-element.248.qkv, f32[8,512]{1,0:T(8,128)S(1)} %get-tuple-element.249.logsum, ...), custom_call_target="tpu_custom_call" | custom-call | flops 1 | bytes 18450000 | tf_op jit(solution)/shard_map/attn_backward/pallas_call | solution.py:36
  86.5 1.0 collective-permute-start.39
  87.6 1.3 collective-permute-start.40
  91.1 1.0 collective-permute-start.42
  92.2 3.7 %collective-permute-done.39.recv = bf16[192,768]{1,0:T(8,128)(2,1)S(1)} collective-permute-done((bf16[192,768]{1,0:T(8,128)(2,1)S(1)}, bf16[192,768]{1,0:T(8,128)(2,1)S(1)}, u32[]{:S(2)}, u32[]{:S(2)}) %collective-permute-start.39) | collective-permute-done | bytes 294944 | tf_op jit(solution)/shard_map/ppermute | solution.py:746
  95.9 1.9 %collective-permute-start.43 = (bf16[192,768]{1,0:T(8,128)(2,1)S(1)}, bf16[192,768]{1,0:T(8,128)(2,1)S(1)}, u32[]{:S(2)}, u32[]{:S(2)}) collective-permute-start(bf16[192,768]{1,0:T(8,128)(2,1)S(1)} %get-tuple-element.282), channel_id=1, source_target_pairs={{0,8},{4,12},{24,16},{28,20},{1,9},{5,13},{25,17},{29,21},{2,10},{... | collective-permute-start | bytes 884744 | tf_op jit(solution)/shard_map/ppermute | solution.py:746
  98.7 1.1 collective-permute-start.45
  99.8 1.3 collective-permute-start.46
  101.9 4.0 %collective-permute-start.47 = (bf16[192,768]{1,0:T(8,128)(2,1)S(1)}, bf16[192,768]{1,0:T(8,128)(2,1)S(1)}, u32[]{:S(2)}, u32[]{:S(2)}) collective-permute-start(bf16[192,768]{1,0:T(8,128)(2,1)S(1)} %get-tuple-element.290), channel_id=1, source_target_pairs={{0,8},{4,12},{24,16},{28,20},{1,9},{5,13},{25,17},{29,21},{2,10},{... | collective-permute-start | bytes 884744 | tf_op jit(solution)/shard_map/ppermute | solution.py:746
  106.6 1.1 collective-permute-start.50
  108.5 1.6 collective-permute-done.47.recv
  110.9 1.6 collective-permute-start.51
  112.5 6.1 %collective-permute-start.54 = (bf16[192,768]{1,0:T(8,128)(2,1)S(1)}, bf16[192,768]{1,0:T(8,128)(2,1)S(1)}, u32[]{:S(2)}, u32[]{:S(2)}) collective-permute-start(bf16[192,768]{1,0:T(8,128)(2,1)S(1)} %get-tuple-element.297), channel_id=1, source_target_pairs={{0,8},{4,12},{24,16},{28,20},{1,9},{5,13},{25,17},{29,21},{2,10},{... | collective-permute-start | bytes 884744 | tf_op jit(solution)/shard_map/ppermute | solution.py:746
  118.7 1.3 collective-permute-start.56
  120.1 1.3 collective-permute-start.55
  121.6 1.3 collective-permute-start.58
  122.9 3.1 %collective-permute-done.54.recv = bf16[192,768]{1,0:T(8,128)(2,1)S(1)} collective-permute-done((bf16[192,768]{1,0:T(8,128)(2,1)S(1)}, bf16[192,768]{1,0:T(8,128)(2,1)S(1)}, u32[]{:S(2)}, u32[]{:S(2)}) %collective-permute-start.54) | collective-permute-done | bytes 294944 | tf_op jit(solution)/shard_map/ppermute | solution.py:746
  127.6 1.1 qkv_input_grad.1
  128.7 1.9 %collective-permute-done.55.recv = bf16[192,768]{1,0:T(8,128)(2,1)S(1)} collective-permute-done((bf16[192,768]{1,0:T(8,128)(2,1)S(1)}, bf16[192,768]{1,0:T(8,128)(2,1)S(1)}, u32[]{:S(2)}, u32[]{:S(2)}) %collective-permute-start.55) | collective-permute-done | bytes 294944 | tf_op jit(solution)/shard_map/ppermute | solution.py:746
  132.0 1.3 collective-permute-start.60
  133.3 1.0 collective-permute-start.62
  135.1 1.0 collective-permute-start.63
  136.2 6.3 %collective-permute-done.60.recv = bf16[192,768]{1,0:T(8,128)(2,1)S(1)} collective-permute-done((bf16[192,768]{1,0:T(8,128)(2,1)S(1)}, bf16[192,768]{1,0:T(8,128)(2,1)S(1)}, u32[]{:S(2)}, u32[]{:S(2)}) %collective-permute-start.60) | collective-permute-done | bytes 294944 | tf_op jit(solution)/shard_map/ppermute | solution.py:746
  142.7 1.3 collective-permute-start.68
  144.0 1.3 collective-permute-start.64
  145.3 1.1 collective-permute-start.66
  147.5 1.6 in_gradient.1
  149.1 9.7 %collective-permute-done.64.recv = bf16[192,768]{1,0:T(8,128)(2,1)S(1)} collective-permute-done((bf16[192,768]{1,0:T(8,128)(2,1)S(1)}, bf16[192,768]{1,0:T(8,128)(2,1)S(1)}, u32[]{:S(2)}, u32[]{:S(2)}) %collective-permute-start.64) | collective-permute-done | bytes 294944 | tf_op jit(solution)/shard_map/ppermute | solution.py:746
  159.3 1.1 collective-permute-start.71
  160.5 1.6 back_gradient.1
  163.0 1.4 vector_outputs.1
  164.4 1.3 collective-permute-done.69.from_x
  166.5 1.7 collective-permute-done.71.vo_other
  168.2 3.2 %collective-permute-done.70.qk_other = bf16[192,768]{1,0:T(8,128)(2,1)S(1)} collective-permute-done((bf16[192,768]{1,0:T(8,128)(2,1)S(1)}, bf16[192,768]{1,0:T(8,128)(2,1)S(1)}, u32[]{:S(2)}, u32[]{:S(2)}) %collective-permute-start.70) | collective-permute-done | bytes 294944 | tf_op jit(solution)/shard_map/ppermute | solution.py:746
  171.4 1.6 attn_gradients.1
  (171 shorter events, 31.4 us)
Async XLA Ops:
  0.7 9.4 %collective-permute-start.3 = (bf16[768,768]{1,0:T(8,128)(2,1)}, bf16[768,768]{1,0:T(8,128)(2,1)S(1)}, u32[]{:S(2)}, u32[]{:S(2)}) collective-permute-start(bf16[768,768]{1,0:T(8,128)(2,1)} %wi_own.1), channel_id=1, source_target_pairs={{0,1},{1,0},{2,3},{3,2},{4,5},{5,4},{6,7},{7,6},{8,9},{9,8},{10,11... | collective-permute-start | bytes 3538952 | tf_op jit(solution)/shard_map/ppermute | solution.py:24
  1.2 8.9 %collective-permute-start.5 = (bf16[192,3072]{1,0:T(8,128)(2,1)}, bf16[192,3072]{1,0:T(8,128)(2,1)S(1)}, u32[]{:S(2)}, u32[]{:S(2)}) collective-permute-start(bf16[192,3072]{1,0:T(8,128)(2,1)} %own.3), channel_id=1, source_target_pairs={{0,1},{1,0},{2,3},{3,2},{4,5},{5,4},{6,7},{7,6},{8,9},{9,8},{10,11... | collective-permute-start | bytes 3538952 | tf_op jit(solution)/shard_map/ppermute | solution.py:24
  1.3 8.8 %collective-permute-start.4 = (bf16[192,768]{1,0:T(8,128)(2,1)}, bf16[192,768]{1,0:T(8,128)(2,1)S(1)}, u32[]{:S(2)}, u32[]{:S(2)}) collective-permute-start(bf16[192,768]{1,0:T(8,128)(2,1)} %own.2), channel_id=1, source_target_pairs={{0,1},{1,0},{2,3},{3,2},{4,5},{5,4},{6,7},{7,6},{8,9},{9,8},{10,11... | collective-permute-start | bytes 884744 | tf_op jit(solution)/shard_map/ppermute | solution.py:24
  1.8 7.4 %collective-permute-start = (bf16[192,512]{1,0:T(8,128)(2,1)}, bf16[192,512]{1,0:T(8,128)(2,1)S(1)}, u32[]{:S(2)}, u32[]{:S(2)}) collective-permute-start(bf16[192,512]{1,0:T(8,128)(2,1)} %param.18), channel_id=1, source_target_pairs={{0,1},{1,0},{2,3},{3,2},{4,5},{5,4},{6,7},{7,6},{8,9},{9,8},{10,11... | collective-permute-start | bytes 589832 | tf_op jit(solution)/shard_map/ppermute | solution.py:24
  1.8 8.3 %collective-permute-start.2 = (bf16[192,512]{1,0:T(8,128)(2,1)}, bf16[192,512]{1,0:T(8,128)(2,1)S(1)}, u32[]{:S(2)}, u32[]{:S(2)}) collective-permute-start(bf16[192,512]{1,0:T(8,128)(2,1)} %param.18), channel_id=1, source_target_pairs={{0,2},{1,3},{2,0},{3,1},{4,6},{5,7},{6,4},{7,5},{8,10},{9,11},{10,... | collective-permute-start | bytes 589832 | tf_op jit(solution)/shard_map/ppermute | solution.py:24
  9.2 3.1 %collective-permute-start.1 = (bf16[192,512]{1,0:T(8,128)(2,1)S(1)}, bf16[192,512]{1,0:T(8,128)(2,1)S(1)}, u32[]{:S(2)}, u32[]{:S(2)}) collective-permute-start(bf16[192,512]{1,0:T(8,128)(2,1)S(1)} %collective-permute-done.x1), channel_id=1, source_target_pairs={{0,1},{1,0},{2,3},{3,2},{4,5},{5,4},{6,7},{7,6},{8,9},{9,8},{10,11... | collective-permute-start | bytes 589832 | tf_op jit(solution)/shard_map/ppermute | solution.py:24
  10.1 2.2 %collective-permute-start.6 = (bf16[192,512]{1,0:T(8,128)(2,1)S(1)}, bf16[192,512]{1,0:T(8,128)(2,1)S(1)}, u32[]{:S(2)}, u32[]{:S(2)}) collective-permute-start(bf16[192,512]{1,0:T(8,128)(2,1)S(1)} %collective-permute-done.2.x2), channel_id=1, source_target_pairs={{0,1},{1,0},{2,3},{3,2},{4,5},{5,4},{6,7},{7,6},{8,9},{9,8},{10,11... | collective-permute-start | bytes 589832 | tf_op jit(solution)/shard_map/ppermute | solution.py:24
  10.2 7.4 %collective-permute-start.12 = (bf16[96,768]{1,0:T(8,128)(2,1)S(1)}, bf16[96,768]{1,0:T(8,128)(2,1)S(1)}, u32[]{:S(2)}, u32[]{:S(2)}) collective-permute-start(bf16[96,768]{1,0:T(8,128)(2,1)S(1)} %get-tuple-element.201), channel_id=1, source_target_pairs={{0,2},{1,3},{2,0},{3,1},{4,6},{5,7},{6,4},{7,5},{8,10},{9,11},{10,... | collective-permute-start | bytes 442376 | tf_op jit(solution)/shard_map/ppermute | solution.py:24
  12.0 14.5 %collective-permute-start.18 = (bf16[192,768]{1,0:T(8,128)(2,1)S(1)}, bf16[192,768]{1,0:T(8,128)(2,1)S(1)}, u32[]{:S(2)}, u32[]{:S(2)}) collective-permute-start(bf16[192,768]{1,0:T(8,128)(2,1)S(1)} %get-tuple-element.187), channel_id=1, source_target_pairs={{0,2},{1,3},{2,0},{3,1},{4,6},{5,7},{6,4},{7,5},{8,10},{9,11},{10,... | collective-permute-start | bytes 884744 | tf_op jit(solution)/shard_map/ppermute | solution.py:24
  15.7 10.2 %collective-permute-start.8 = (bf16[576,128]{1,0:T(8,128)(2,1)S(1)}, bf16[576,128]{1,0:T(8,128)(2,1)S(1)}, u32[]{:S(2)}, u32[]{:S(2)}) collective-permute-start(bf16[576,128]{1,0:T(8,128)(2,1)S(1)} %get-tuple-element.197), channel_id=1, source_target_pairs={{0,2},{1,3},{2,0},{3,1},{4,6},{5,7},{6,4},{7,5},{8,10},{9,11},{10,... | collective-permute-start | bytes 442376 | tf_op jit(solution)/shard_map/ppermute | solution.py:24
  17.6 8.9 %collective-permute-start.13 = (bf16[96,768]{1,0:T(8,128)(2,1)S(1)}, bf16[96,768]{1,0:T(8,128)(2,1)S(1)}, u32[]{:S(2)}, u32[]{:S(2)}) collective-permute-start(bf16[96,768]{1,0:T(8,128)(2,1)S(1)} %collective-permute-done.12.xa), channel_id=1, source_target_pairs={{0,4},{4,0},{8,12},{12,8},{16,20},{20,16},{24,28},{28,24},{1,5},{5... | collective-permute-start | bytes 442376 | tf_op jit(solution)/shard_map/ppermute | solution.py:24
  19.1 2.5 %collective-permute-start.7 = (bf16[384,128]{1,0:T(8,128)(2,1)S(1)}, bf16[384,128]{1,0:T(8,128)(2,1)S(1)}, u32[]{:S(2)}, u32[]{:S(2)}) collective-permute-start(bf16[384,128]{1,0:T(8,128)(2,1)S(1)} %get-tuple-element.196), channel_id=1, source_target_pairs={{0,1},{1,0},{2,3},{3,2},{4,5},{5,4},{6,7},{7,6},{8,9},{9,8},{10,11... | collective-permute-start | bytes 294920 | tf_op jit(solution)/shard_map/ppermute | solution.py:24
  25.9 2.4 %collective-permute-start.11 = (bf16[576,128]{1,0:T(8,128)(2,1)S(1)}, bf16[576,128]{1,0:T(8,128)(2,1)S(1)}, u32[]{:S(2)}, u32[]{:S(2)}) collective-permute-start(bf16[576,128]{1,0:T(8,128)(2,1)S(1)} %collective-permute-done.8.p2.g2), channel_id=1, source_target_pairs={{0,1},{1,0},{2,3},{3,2},{4,5},{5,4},{6,7},{7,6},{8,9},{9,8},{10,11... | collective-permute-start | bytes 442376 | tf_op jit(solution)/shard_map/ppermute | solution.py:24
  25.9 2.7 %collective-permute-start.14 = (bf16[96,768]{1,0:T(8,128)(2,1)S(1)}, bf16[96,768]{1,0:T(8,128)(2,1)S(1)}, u32[]{:S(2)}, u32[]{:S(2)}) collective-permute-start(bf16[96,768]{1,0:T(8,128)(2,1)S(1)} %collective-permute-done.12.xa), channel_id=1, source_target_pairs={{0,1},{1,0},{2,3},{3,2},{4,5},{5,4},{6,7},{7,6},{8,9},{9,8},{10,11... | collective-permute-start | bytes 442376 | tf_op jit(solution)/shard_map/ppermute | solution.py:24
  26.5 9.4 %collective-permute-start.19 = (bf16[192,768]{1,0:T(8,128)(2,1)S(1)}, bf16[192,768]{1,0:T(8,128)(2,1)S(1)}, u32[]{:S(2)}, u32[]{:S(2)}) collective-permute-start(bf16[192,768]{1,0:T(8,128)(2,1)S(1)} %collective-permute-done.18.xa), channel_id=1, source_target_pairs={{0,4},{4,0},{8,12},{12,8},{16,20},{20,16},{24,28},{28,24},{1,5},{5... | collective-permute-start | bytes 884744 | tf_op jit(solution)/shard_map/ppermute | solution.py:24
  29.6 9.1 %collective-permute-start.16 = (bf16[192,768]{1,0:T(8,128)(2,1)S(1)}, bf16[192,768]{1,0:T(8,128)(2,1)S(1)}, u32[]{:S(2)}, u32[]{:S(2)}) collective-permute-start(bf16[192,768]{1,0:T(8,128)(2,1)S(1)} %get-tuple-element.211.rows.n0), channel_id=1, source_target_pairs={{0,2},{1,3},{2,0},{3,1},{4,6},{5,7},{6,4},{7,5},{8,10},{9,11},{10,... | collective-permute-start | bytes 884744 | tf_op jit(solution)/shard_map/ppermute | solution.py:24
  31.1 8.1 %collective-permute-start.20 = (bf16[192,768]{1,0:T(8,128)(2,1)S(1)}, bf16[192,768]{1,0:T(8,128)(2,1)S(1)}, u32[]{:S(2)}, u32[]{:S(2)}) collective-permute-start(bf16[192,768]{1,0:T(8,128)(2,1)S(1)} %collective-permute-done.18.xa), channel_id=1, source_target_pairs={{0,1},{1,0},{2,3},{3,2},{4,5},{5,4},{6,7},{7,6},{8,9},{9,8},{10,11... | collective-permute-start | bytes 884744 | tf_op jit(solution)/shard_map/ppermute | solution.py:24
  38.7 6.6 %collective-permute-start.17 = (bf16[192,768]{1,0:T(8,128)(2,1)S(1)}, bf16[192,768]{1,0:T(8,128)(2,1)S(1)}, u32[]{:S(2)}, u32[]{:S(2)}) collective-permute-start(bf16[192,768]{1,0:T(8,128)(2,1)S(1)} %get-tuple-element.211.rows.n0), channel_id=1, source_target_pairs={{0,1},{1,0},{2,3},{3,2},{4,5},{5,4},{6,7},{7,6},{8,9},{9,8},{10,11... | collective-permute-start | bytes 884744 | tf_op jit(solution)/shard_map/ppermute | solution.py:24
  41.9 7.5 %collective-permute-start.22 = (bf16[192,768]{1,0:T(8,128)(2,1)S(1)}, bf16[192,768]{1,0:T(8,128)(2,1)S(1)}, u32[]{:S(2)}, u32[]{:S(2)}) collective-permute-start(bf16[192,768]{1,0:T(8,128)(2,1)S(1)} %collective-permute-done.16.rows.n_x.n1), channel_id=1, source_target_pairs={{0,1},{1,0},{2,3},{3,2},{4,5},{5,4},{6,7},{7,6},{8,9},{9,8},{10,11... | collective-permute-start | bytes 884744 | tf_op jit(solution)/shard_map/ppermute | solution.py:24
  42.2 3.2 %collective-permute-start.24 = (bf16[192,512]{1,0:T(8,128)(2,1)S(1)}, bf16[192,512]{1,0:T(8,128)(2,1)S(1)}, u32[]{:S(2)}, u32[]{:S(2)}) collective-permute-start(bf16[192,512]{1,0:T(8,128)(2,1)S(1)} %copy-done.6), channel_id=1, source_target_pairs={{0,1},{1,0},{2,3},{3,2},{4,5},{5,4},{6,7},{7,6},{8,9},{9,8},{10,11... | collective-permute-start | bytes 589832 | tf_op jit(solution)/shard_map/ppermute | solution.py:24
  42.5 7.0 %collective-permute-start.23 = (bf16[128,768]{1,0:T(8,128)(2,1)S(1)}, bf16[128,768]{1,0:T(8,128)(2,1)S(1)}, u32[]{:S(2)}, u32[]{:S(2)}) collective-permute-start(bf16[128,768]{1,0:T(8,128)(2,1)S(1)} %get-tuple-element.209), channel_id=1, source_target_pairs={{0,2},{1,3},{2,0},{3,1},{4,6},{5,7},{6,4},{7,5},{8,10},{9,11},{10,... | collective-permute-start | bytes 589832 | tf_op jit(solution)/shard_map/ppermute | solution.py:24
  50.2 7.5 %collective-permute-start.25 = (bf16[256,768]{1,0:T(8,128)(2,1)S(1)}, bf16[256,768]{1,0:T(8,128)(2,1)S(1)}, u32[]{:S(2)}, u32[]{:S(2)}) collective-permute-start(bf16[256,768]{1,0:T(8,128)(2,1)S(1)} %get-tuple-element.221), channel_id=1, source_target_pairs={{0,1},{1,0},{2,3},{3,2},{4,5},{5,4},{6,7},{7,6},{8,9},{9,8},{10,11... | collective-permute-start | bytes 1179656 | tf_op jit(solution)/shard_map/ppermute | solution.py:24
  50.2 3.3 %collective-permute-start.27 = (bf16[128,768]{1,0:T(8,128)(2,1)S(1)}, bf16[128,768]{1,0:T(8,128)(2,1)S(1)}, u32[]{:S(2)}, u32[]{:S(2)}) collective-permute-start(bf16[128,768]{1,0:T(8,128)(2,1)S(1)} %get-tuple-element.220.rows.f0), channel_id=1, source_target_pairs={{0,1},{1,0},{2,3},{3,2},{4,5},{5,4},{6,7},{7,6},{8,9},{9,8},{10,11... | collective-permute-start | bytes 589832 | tf_op jit(solution)/shard_map/ppermute | solution.py:24
  50.7 6.9 %collective-permute-start.26 = (bf16[128,768]{1,0:T(8,128)(2,1)S(1)}, bf16[128,768]{1,0:T(8,128)(2,1)S(1)}, u32[]{:S(2)}, u32[]{:S(2)}) collective-permute-start(bf16[128,768]{1,0:T(8,128)(2,1)S(1)} %get-tuple-element.220.rows.f0), channel_id=1, source_target_pairs={{0,2},{1,3},{2,0},{3,1},{4,6},{5,7},{6,4},{7,5},{8,10},{9,11},{10,... | collective-permute-start | bytes 589832 | tf_op jit(solution)/shard_map/ppermute | solution.py:24
  59.5 6.9 %collective-permute-start.30 = (bf16[128,768]{1,0:T(8,128)(2,1)S(1)}, bf16[128,768]{1,0:T(8,128)(2,1)S(1)}, u32[]{:S(2)}, u32[]{:S(2)}) collective-permute-start(bf16[128,768]{1,0:T(8,128)(2,1)S(1)} %get-tuple-element.232), channel_id=1, source_target_pairs={{0,2},{1,3},{2,0},{3,1},{4,6},{5,7},{6,4},{7,5},{8,10},{9,11},{10,... | collective-permute-start | bytes 589832 | tf_op jit(solution)/shard_map/ppermute | solution.py:24
  68.6 13.6 %collective-permute-start.37 = (bf16[384,768]{1,0:T(8,128)(2,1)S(1)}, bf16[384,768]{1,0:T(8,128)(2,1)S(1)}, u32[]{:S(2)}, u32[]{:S(2)}) collective-permute-start(bf16[384,768]{1,0:T(8,128)(2,1)S(1)} %get-tuple-element.266), channel_id=1, source_target_pairs={{0,1},{1,0},{2,3},{3,2},{4,5},{5,4},{6,7},{7,6},{8,9},{9,8},{10,11... | collective-permute-start | bytes 1769480 | tf_op jit(solution)/shard_map/ppermute | solution.py:24
  68.7 9.8 %collective-permute-start.32 = (bf16[192,768]{1,0:T(8,128)(2,1)S(1)}, bf16[192,768]{1,0:T(8,128)(2,1)S(1)}, u32[]{:S(2)}, u32[]{:S(2)}) collective-permute-start(bf16[192,768]{1,0:T(8,128)(2,1)S(1)} %get-tuple-element.246), channel_id=1, source_target_pairs={{0,4},{4,0},{8,12},{12,8},{16,20},{20,16},{24,28},{28,24},{1,5},{5... | collective-permute-start | bytes 884744 | tf_op jit(solution)/shard_map/ppermute | solution.py:746
  69.7 5.3 %collective-permute-start.33 = (bf16[480,128]{1,0:T(8,128)(2,1)S(1)}, bf16[480,128]{1,0:T(8,128)(2,1)S(1)}, u32[]{:S(2)}, u32[]{:S(2)}) collective-permute-start(bf16[480,128]{1,0:T(8,128)(2,1)S(1)} %get-tuple-element.251), channel_id=1, source_target_pairs={{0,2},{1,3},{2,0},{3,1},{4,6},{5,7},{6,4},{7,5},{8,10},{9,11},{10,... | collective-permute-start | bytes 368648 | tf_op jit(solution)/shard_map/ppermute | solution.py:24
  71.2 16.3 %collective-permute-start.35 = (bf16[192,768]{1,0:T(8,128)(2,1)S(1)}, bf16[192,768]{1,0:T(8,128)(2,1)S(1)}, u32[]{:S(2)}, u32[]{:S(2)}) collective-permute-start(bf16[192,768]{1,0:T(8,128)(2,1)S(1)} %get-tuple-element.257), channel_id=1, source_target_pairs={{0,4},{4,0},{8,12},{12,8},{16,20},{20,16},{24,28},{28,24},{1,5},{5... | collective-permute-start | bytes 884744 | tf_op jit(solution)/shard_map/ppermute | solution.py:746
  75.0 7.2 %collective-permute-start.34 = (bf16[480,128]{1,0:T(8,128)(2,1)S(1)}, bf16[480,128]{1,0:T(8,128)(2,1)S(1)}, u32[]{:S(2)}, u32[]{:S(2)}) collective-permute-start(bf16[480,128]{1,0:T(8,128)(2,1)S(1)} %collective-permute-done.33.u2), channel_id=1, source_target_pairs={{0,1},{1,0},{2,3},{3,2},{4,5},{5,4},{6,7},{7,6},{8,9},{9,8},{10,11... | collective-permute-start | bytes 368648 | tf_op jit(solution)/shard_map/ppermute | solution.py:24
  78.7 10.3 %collective-permute-start.36 = (bf16[192,768]{1,0:T(8,128)(2,1)S(1)}, bf16[192,768]{1,0:T(8,128)(2,1)S(1)}, u32[]{:S(2)}, u32[]{:S(2)}) collective-permute-start(bf16[192,768]{1,0:T(8,128)(2,1)S(1)} %get-tuple-element.247), channel_id=1, source_target_pairs={{0,8},{4,12},{24,16},{28,20},{1,9},{5,13},{25,17},{29,21},{2,10},{... | collective-permute-start | bytes 884744 | tf_op jit(solution)/shard_map/ppermute | solution.py:746
  82.3 7.7 %collective-permute-start.38 = (bf16[192,768]{1,0:T(8,128)(2,1)S(1)}, bf16[192,768]{1,0:T(8,128)(2,1)S(1)}, u32[]{:S(2)}, u32[]{:S(2)}) collective-permute-start(bf16[192,768]{1,0:T(8,128)(2,1)S(1)} %wo_low.1), channel_id=1, source_target_pairs={{0,2},{1,3},{2,0},{3,1},{4,6},{5,7},{6,4},{7,5},{8,10},{9,11},{10,... | collective-permute-start | bytes 884744 | tf_op jit(solution)/shard_map/ppermute | solution.py:24
  86.5 9.3 %collective-permute-start.39 = (bf16[192,768]{1,0:T(8,128)(2,1)S(1)}, bf16[192,768]{1,0:T(8,128)(2,1)S(1)}, u32[]{:S(2)}, u32[]{:S(2)}) collective-permute-start(bf16[192,768]{1,0:T(8,128)(2,1)S(1)} %get-tuple-element.281), channel_id=1, source_target_pairs={{0,4},{4,0},{8,12},{12,8},{16,20},{20,16},{24,28},{28,24},{1,5},{5... | collective-permute-start | bytes 884744 | tf_op jit(solution)/shard_map/ppermute | solution.py:746
  87.6 10.3 %collective-permute-start.40 = (bf16[192,768]{1,0:T(8,128)(2,1)S(1)}, bf16[192,768]{1,0:T(8,128)(2,1)S(1)}, u32[]{:S(2)}, u32[]{:S(2)}) collective-permute-start(bf16[192,768]{1,0:T(8,128)(2,1)S(1)} %get-tuple-element.258), channel_id=1, source_target_pairs={{0,8},{4,12},{24,16},{28,20},{1,9},{5,13},{25,17},{29,21},{2,10},{... | collective-permute-start | bytes 884744 | tf_op jit(solution)/shard_map/ppermute | solution.py:746
  89.0 10.7 %collective-permute-start.41 = (bf16[192,768]{1,0:T(8,128)(2,1)S(1)}, bf16[192,768]{1,0:T(8,128)(2,1)S(1)}, u32[]{:S(2)}, u32[]{:S(2)}) collective-permute-start(bf16[192,768]{1,0:T(8,128)(2,1)S(1)} %second_add.5.mine), channel_id=1, source_target_pairs={{8,16},{12,20},{16,8},{20,12},{9,17},{13,21},{17,9},{21,13},{10,18... | collective-permute-start | bytes 884744 | tf_op jit(solution)/shard_map/ppermute | solution.py:746
  91.1 10.6 %collective-permute-start.42 = (bf16[192,768]{1,0:T(8,128)(2,1)S(1)}, bf16[192,768]{1,0:T(8,128)(2,1)S(1)}, u32[]{:S(2)}, u32[]{:S(2)}) collective-permute-start(bf16[192,768]{1,0:T(8,128)(2,1)S(1)} %get-tuple-element.289), channel_id=1, source_target_pairs={{0,4},{4,0},{8,12},{12,8},{16,20},{20,16},{24,28},{28,24},{1,5},{5... | collective-permute-start | bytes 884744 | tf_op jit(solution)/shard_map/ppermute | solution.py:746
  95.9 9.9 %collective-permute-start.43 = (bf16[192,768]{1,0:T(8,128)(2,1)S(1)}, bf16[192,768]{1,0:T(8,128)(2,1)S(1)}, u32[]{:S(2)}, u32[]{:S(2)}) collective-permute-start(bf16[192,768]{1,0:T(8,128)(2,1)S(1)} %get-tuple-element.282), channel_id=1, source_target_pairs={{0,8},{4,12},{24,16},{28,20},{1,9},{5,13},{25,17},{29,21},{2,10},{... | collective-permute-start | bytes 884744 | tf_op jit(solution)/shard_map/ppermute | solution.py:746
  98.0 8.6 %collective-permute-start.44 = (bf16[192,768]{1,0:T(8,128)(2,1)S(1)}, bf16[192,768]{1,0:T(8,128)(2,1)S(1)}, u32[]{:S(2)}, u32[]{:S(2)}) collective-permute-start(bf16[192,768]{1,0:T(8,128)(2,1)S(1)} %second_add.6.mine), channel_id=1, source_target_pairs={{8,16},{12,20},{16,8},{20,12},{9,17},{13,21},{17,9},{21,13},{10,18... | collective-permute-start | bytes 884744 | tf_op jit(solution)/shard_map/ppermute | solution.py:746
  98.7 9.1 %collective-permute-start.45 = (bf16[192,768]{1,0:T(8,128)(2,1)S(1)}, bf16[192,768]{1,0:T(8,128)(2,1)S(1)}, u32[]{:S(2)}, u32[]{:S(2)}) collective-permute-start(bf16[192,768]{1,0:T(8,128)(2,1)S(1)} %get-tuple-element.272), channel_id=1, source_target_pairs={{0,4},{4,0},{8,12},{12,8},{16,20},{20,16},{24,28},{28,24},{1,5},{5... | collective-permute-start | bytes 884744 | tf_op jit(solution)/shard_map/ppermute | solution.py:746
  99.8 8.6 %collective-permute-start.46 = (bf16[192,768]{1,0:T(8,128)(2,1)S(1)}, bf16[192,768]{1,0:T(8,128)(2,1)S(1)}, u32[]{:S(2)}, u32[]{:S(2)}) collective-permute-start(bf16[192,768]{1,0:T(8,128)(2,1)S(1)} %third_add.3.mine), channel_id=1, source_target_pairs={{8,0},{12,4},{16,24},{20,28},{9,1},{13,5},{17,25},{21,29},{10,2},{... | collective-permute-start | bytes 884744 | tf_op jit(solution)/shard_map/ppermute | solution.py:746
  101.9 8.2 %collective-permute-start.47 = (bf16[192,768]{1,0:T(8,128)(2,1)S(1)}, bf16[192,768]{1,0:T(8,128)(2,1)S(1)}, u32[]{:S(2)}, u32[]{:S(2)}) collective-permute-start(bf16[192,768]{1,0:T(8,128)(2,1)S(1)} %get-tuple-element.290), channel_id=1, source_target_pairs={{0,8},{4,12},{24,16},{28,20},{1,9},{5,13},{25,17},{29,21},{2,10},{... | collective-permute-start | bytes 884744 | tf_op jit(solution)/shard_map/ppermute | solution.py:746
  105.9 4.9 %collective-permute-start.48 = (bf16[192,768]{1,0:T(8,128)(2,1)S(1)}, bf16[192,768]{1,0:T(8,128)(2,1)S(1)}, u32[]{:S(2)}, u32[]{:S(2)}) collective-permute-start(bf16[192,768]{1,0:T(8,128)(2,1)S(1)} %second_add.7.mine), channel_id=1, source_target_pairs={{8,16},{12,20},{16,8},{20,12},{9,17},{13,21},{17,9},{21,13},{10,18... | collective-permute-start | bytes 884744 | tf_op jit(solution)/shard_map/ppermute | solution.py:746
  106.6 12.0 %collective-permute-start.50 = (bf16[224,768]{1,0:T(8,128)(2,1)S(1)}, bf16[224,768]{1,0:T(8,128)(2,1)S(1)}, u32[]{:S(2)}, u32[]{:S(2)}) collective-permute-start(bf16[224,768]{1,0:T(8,128)(2,1)S(1)} %get-tuple-element.279), channel_id=1, source_target_pairs={{0,4},{4,0},{8,12},{12,8},{16,20},{20,16},{24,28},{28,24},{1,5},{5... | collective-permute-start | bytes 1032200 | tf_op jit(solution)/shard_map/ppermute | solution.py:746
  107.8 3.1 %collective-permute-start.49 = (bf16[96,768]{1,0:T(8,128)(2,1)S(1)}, bf16[96,768]{1,0:T(8,128)(2,1)S(1)}, u32[]{:S(2)}, u32[]{:S(2)}) collective-permute-start(bf16[96,768]{1,0:T(8,128)(2,1)S(1)} %get-tuple-element.293), channel_id=1, source_target_pairs={{0,1},{1,0},{2,3},{3,2},{4,5},{5,4},{6,7},{7,6},{8,9},{9,8},{10,11... | collective-permute-start | bytes 442376 | tf_op jit(solution)/shard_map/ppermute | solution.py:24
  110.1 11.3 %collective-permute-start.52 = (bf16[192,768]{1,0:T(8,128)(2,1)S(1)}, bf16[192,768]{1,0:T(8,128)(2,1)S(1)}, u32[]{:S(2)}, u32[]{:S(2)}) collective-permute-start(bf16[192,768]{1,0:T(8,128)(2,1)S(1)} %second_add.8.mine), channel_id=1, source_target_pairs={{8,16},{12,20},{16,8},{20,12},{9,17},{13,21},{17,9},{21,13},{10,18... | collective-permute-start | bytes 884744 | tf_op jit(solution)/shard_map/ppermute | solution.py:746
  110.9 9.1 %collective-permute-start.51 = (bf16[96,768]{1,0:T(8,128)(2,1)S(1)}, bf16[96,768]{1,0:T(8,128)(2,1)S(1)}, u32[]{:S(2)}, u32[]{:S(2)}) collective-permute-start(bf16[96,768]{1,0:T(8,128)(2,1)S(1)} %second_half.2), channel_id=1, source_target_pairs={{0,2},{1,3},{2,0},{3,1},{4,6},{5,7},{6,4},{7,5},{8,10},{9,11},{10,... | collective-permute-start | bytes 442376 | tf_op jit(solution)/shard_map/ppermute | solution.py:24
  112.5 13.5 %collective-permute-start.54 = (bf16[192,768]{1,0:T(8,128)(2,1)S(1)}, bf16[192,768]{1,0:T(8,128)(2,1)S(1)}, u32[]{:S(2)}, u32[]{:S(2)}) collective-permute-start(bf16[192,768]{1,0:T(8,128)(2,1)S(1)} %get-tuple-element.297), channel_id=1, source_target_pairs={{0,8},{4,12},{24,16},{28,20},{1,9},{5,13},{25,17},{29,21},{2,10},{... | collective-permute-start | bytes 884744 | tf_op jit(solution)/shard_map/ppermute | solution.py:746
  118.7 11.9 %collective-permute-start.56 = (bf16[224,768]{1,0:T(8,128)(2,1)S(1)}, bf16[224,768]{1,0:T(8,128)(2,1)S(1)}, u32[]{:S(2)}, u32[]{:S(2)}) collective-permute-start(bf16[224,768]{1,0:T(8,128)(2,1)S(1)} %get-tuple-element.307.mine), channel_id=1, source_target_pairs={{0,8},{4,12},{24,16},{28,20},{1,9},{5,13},{25,17},{29,21},{2,10},{... | collective-permute-start | bytes 1032200 | tf_op jit(solution)/shard_map/ppermute | solution.py:746
  120.1 10.4 %collective-permute-start.55 = (bf16[192,768]{1,0:T(8,128)(2,1)S(1)}, bf16[192,768]{1,0:T(8,128)(2,1)S(1)}, u32[]{:S(2)}, u32[]{:S(2)}) collective-permute-start(bf16[192,768]{1,0:T(8,128)(2,1)S(1)} %join_owners.2.mine), channel_id=1, source_target_pairs={{8,0},{12,4},{16,24},{20,28},{9,1},{13,5},{17,25},{21,29},{10,2},{... | collective-permute-start | bytes 884744 | tf_op jit(solution)/shard_map/ppermute | solution.py:746
  121.6 13.5 %collective-permute-start.58 = (bf16[192,768]{1,0:T(8,128)(2,1)S(1)}, bf16[192,768]{1,0:T(8,128)(2,1)S(1)}, u32[]{:S(2)}, u32[]{:S(2)}) collective-permute-start(bf16[192,768]{1,0:T(8,128)(2,1)S(1)} %third_add.4.mine), channel_id=1, source_target_pairs={{8,0},{12,4},{16,24},{20,28},{9,1},{13,5},{17,25},{21,29},{10,2},{... | collective-permute-start | bytes 884744 | tf_op jit(solution)/shard_map/ppermute | solution.py:746
  126.1 10.0 %collective-permute-start.59 = (bf16[192,768]{1,0:T(8,128)(2,1)S(1)}, bf16[192,768]{1,0:T(8,128)(2,1)S(1)}, u32[]{:S(2)}, u32[]{:S(2)}) collective-permute-start(bf16[192,768]{1,0:T(8,128)(2,1)S(1)} %second_add.9.mine), channel_id=1, source_target_pairs={{8,16},{12,20},{16,8},{20,12},{9,17},{13,21},{17,9},{21,13},{10,18... | collective-permute-start | bytes 884744 | tf_op jit(solution)/shard_map/ppermute | solution.py:746
  126.8 5.2 %collective-permute-start.57 = (bf16[96,768]{1,0:T(8,128)(2,1)S(1)}, bf16[96,768]{1,0:T(8,128)(2,1)S(1)}, u32[]{:S(2)}, u32[]{:S(2)}) collective-permute-start(bf16[96,768]{1,0:T(8,128)(2,1)S(1)} %second_half.3), channel_id=1, source_target_pairs={{0,2},{1,3},{2,0},{3,1},{4,6},{5,7},{6,4},{7,5},{8,10},{9,11},{10,... | collective-permute-start | bytes 442376 | tf_op jit(solution)/shard_map/ppermute | solution.py:24
  130.7 11.9 %collective-permute-start.61 = (bf16[224,768]{1,0:T(8,128)(2,1)S(1)}, bf16[224,768]{1,0:T(8,128)(2,1)S(1)}, u32[]{:S(2)}, u32[]{:S(2)}) collective-permute-start(bf16[224,768]{1,0:T(8,128)(2,1)S(1)} %second_add_pair.1.mine), channel_id=1, source_target_pairs={{8,16},{12,20},{16,8},{20,12},{9,17},{13,21},{17,9},{21,13},{10,18... | collective-permute-start | bytes 1032200 | tf_op jit(solution)/shard_map/ppermute | solution.py:746
  132.0 10.5 %collective-permute-start.60 = (bf16[192,768]{1,0:T(8,128)(2,1)S(1)}, bf16[192,768]{1,0:T(8,128)(2,1)S(1)}, u32[]{:S(2)}, u32[]{:S(2)}) collective-permute-start(bf16[192,768]{1,0:T(8,128)(2,1)S(1)} %join_owners.3.mine), channel_id=1, source_target_pairs={{8,0},{12,4},{16,24},{20,28},{9,1},{13,5},{17,25},{21,29},{10,2},{... | collective-permute-start | bytes 884744 | tf_op jit(solution)/shard_map/ppermute | solution.py:746
  133.3 12.0 %collective-permute-start.62 = (bf16[192,768]{1,0:T(8,128)(2,1)S(1)}, bf16[192,768]{1,0:T(8,128)(2,1)S(1)}, u32[]{:S(2)}, u32[]{:S(2)}) collective-permute-start(bf16[192,768]{1,0:T(8,128)(2,1)S(1)} %choose.5.mine0), channel_id=1, source_target_pairs={{0,4},{4,0},{8,12},{12,8},{16,20},{20,16},{24,28},{28,24},{1,5},{5... | collective-permute-start | bytes 884744 | tf_op jit(solution)/shard_map/ppermute | solution.py:746
  135.1 11.5 %collective-permute-start.63 = (bf16[192,768]{1,0:T(8,128)(2,1)S(1)}, bf16[192,768]{1,0:T(8,128)(2,1)S(1)}, u32[]{:S(2)}, u32[]{:S(2)}) collective-permute-start(bf16[192,768]{1,0:T(8,128)(2,1)S(1)} %choose.7.mine1), channel_id=1, source_target_pairs={{0,4},{4,0},{8,12},{12,8},{16,20},{20,16},{24,28},{28,24},{1,5},{5... | collective-permute-start | bytes 884744 | tf_op jit(solution)/shard_map/ppermute | solution.py:746
  136.1 22.8 %collective-permute-start.65 = (bf16[384,640]{1,0:T(8,128)(2,1)S(1)}, bf16[384,640]{1,0:T(8,128)(2,1)S(1)}, u32[]{:S(2)}, u32[]{:S(2)}) collective-permute-start(bf16[384,640]{1,0:T(8,128)(2,1)S(1)} %get-tuple-element.319), channel_id=1, source_target_pairs={{0,1},{1,0},{2,3},{3,2},{4,5},{5,4},{6,7},{7,6},{8,9},{9,8},{10,11... | collective-permute-start | bytes 1474568 | tf_op jit(solution)/shard_map/ppermute | solution.py:24
  142.7 19.4 %collective-permute-start.68 = (bf16[224,768]{1,0:T(8,128)(2,1)S(1)}, bf16[224,768]{1,0:T(8,128)(2,1)S(1)}, u32[]{:S(2)}, u32[]{:S(2)}) collective-permute-start(bf16[224,768]{1,0:T(8,128)(2,1)S(1)} %third_add_pair.1.mine), channel_id=1, source_target_pairs={{8,0},{12,4},{16,24},{20,28},{9,1},{13,5},{17,25},{21,29},{10,2},{... | collective-permute-start | bytes 1032200 | tf_op jit(solution)/shard_map/ppermute | solution.py:746
  144.0 14.9 %collective-permute-start.64 = (bf16[192,768]{1,0:T(8,128)(2,1)S(1)}, bf16[192,768]{1,0:T(8,128)(2,1)S(1)}, u32[]{:S(2)}, u32[]{:S(2)}) collective-permute-start(bf16[192,768]{1,0:T(8,128)(2,1)S(1)} %third_add.5.mine), channel_id=1, source_target_pairs={{8,0},{12,4},{16,24},{20,28},{9,1},{13,5},{17,25},{21,29},{10,2},{... | collective-permute-start | bytes 884744 | tf_op jit(solution)/shard_map/ppermute | solution.py:746
  145.3 15.2 %collective-permute-start.66 = (bf16[192,768]{1,0:T(8,128)(2,1)S(1)}, bf16[192,768]{1,0:T(8,128)(2,1)S(1)}, u32[]{:S(2)}, u32[]{:S(2)}) collective-permute-start(bf16[192,768]{1,0:T(8,128)(2,1)S(1)} %choose.6.mine0), channel_id=1, source_target_pairs={{0,4},{4,0},{8,12},{12,8},{16,20},{20,16},{24,28},{28,24},{1,5},{5... | collective-permute-start | bytes 884744 | tf_op jit(solution)/shard_map/ppermute | solution.py:746
  146.6 13.9 %collective-permute-start.67 = (bf16[192,768]{1,0:T(8,128)(2,1)S(1)}, bf16[192,768]{1,0:T(8,128)(2,1)S(1)}, u32[]{:S(2)}, u32[]{:S(2)}) collective-permute-start(bf16[192,768]{1,0:T(8,128)(2,1)S(1)} %choose.8.mine1), channel_id=1, source_target_pairs={{0,4},{4,0},{8,12},{12,8},{16,20},{20,16},{24,28},{28,24},{1,5},{5... | collective-permute-start | bytes 884744 | tf_op jit(solution)/shard_map/ppermute | solution.py:746
  158.9 6.8 %collective-permute-start.69 = (bf16[192,768]{1,0:T(8,128)(2,1)S(1)}, bf16[192,768]{1,0:T(8,128)(2,1)S(1)}, u32[]{:S(2)}, u32[]{:S(2)}) collective-permute-start(bf16[192,768]{1,0:T(8,128)(2,1)S(1)} %tokens_step.1), channel_id=1, source_target_pairs={{0,2},{1,3},{2,0},{3,1},{4,6},{5,7},{6,4},{7,5},{8,10},{9,11},{10,... | collective-permute-start | bytes 884744 | tf_op jit(solution)/shard_map/ppermute | solution.py:24
  159.3 8.9 %collective-permute-start.71 = (bf16[192,768]{1,0:T(8,128)(2,1)S(1)}, bf16[192,768]{1,0:T(8,128)(2,1)S(1)}, u32[]{:S(2)}, u32[]{:S(2)}) collective-permute-start(bf16[192,768]{1,0:T(8,128)(2,1)S(1)} %choose.9.vo_mine), channel_id=1, source_target_pairs={{0,4},{4,0},{8,12},{12,8},{16,20},{20,16},{24,28},{28,24},{1,5},{5... | collective-permute-start | bytes 884744 | tf_op jit(solution)/shard_map/ppermute | solution.py:746
  162.1 9.3 %collective-permute-start.70 = (bf16[192,768]{1,0:T(8,128)(2,1)S(1)}, bf16[192,768]{1,0:T(8,128)(2,1)S(1)}, u32[]{:S(2)}, u32[]{:S(2)}) collective-permute-start(bf16[192,768]{1,0:T(8,128)(2,1)S(1)} %get-tuple-element.342.qk_mine), channel_id=1, source_target_pairs={{0,4},{4,0},{8,12},{12,8},{16,20},{20,16},{24,28},{28,24},{1,5},{5... | collective-permute-start | bytes 884744 | tf_op jit(solution)/shard_map/ppermute | solution.py:746
  (25 other events, 202.6 us)

commit v6 on v5

--- a/solution.py
+++ b/solution.py
@@ -727,7 +727,7 @@
 
 
 EARLY_TURNS = "313"
-TURNS = "413vq2413241v3241q122vg13q24v12q4vg2qegvq"
+TURNS = "413vq2413241v3241q122v13gq24vq124vg2qegvq"
 FIRST = ("in0", "back0")
 
 

time: 175 us -> 174 us (level)
  transfers between devices with their start and end apart: 72 -> 72, of which waited for: 29 -> 28; matrix products, arithmetic and copies ran while one was open for 1% -> 1% of each run, Pallas kernels for 14% -> 14%
where the time goes in v6:
time: 174 us
  waiting for transfers between devices  70 us (40%)
  starting transfers between devices  69.8 us (40%)
  Pallas kernels  27.9 us (16%)
  local copies, waits for them, and re-layouts  2.95 us (2%)
    ppermute x30, starting transfers between devices, along(): return lax.ppermute(block, 'rows', pairs)  42.4 us
    ppermute x30, waiting for transfers between devices, along(): return lax.ppermute(block, 'rows', pairs)  37.9 us
    ppermute x42, waiting for transfers between devices, swap(): lax.ppermute(block, axis, [(i, i ^ bit) for i in range(lax.axis_size(axis...  32.2 us
    pallas_call x54, Pallas kernels, local_kernel(): pl.pallas_call(body, name=name, out_shape=outs, in_specs=[SPECS[k] for k...  27.9 us
    ppermute x42, starting transfers between devices, swap(): lax.ppermute(block, axis, [(i, i ^ bit) for i in range(lax.axis_size(axis...  27.3 us
  transfers between devices with their start and end apart: 72, of which 28 were waited for; matrix products, arithmetic and copies ran while one was open for 1% of the time, Pallas kernels for 14%

profile of v6, /device:TPU:0, one launch (start us, length us, event | category | flops | bytes accessed | tf_op | source)
XLA Modules:
  0.0 173.5 jit_solution(16242352360684391275)
XLA Ops:
  1.8 2.9 %collective-permute-start.2 = (bf16[192,512]{1,0:T(8,128)(2,1)}, bf16[192,512]{1,0:T(8,128)(2,1)S(1)}, u32[]{:S(2)}, u32[]{:S(2)}) collective-permute-start(bf16[192,512]{1,0:T(8,128)(2,1)} %param.18), channel_id=1, source_target_pairs={{0,2},{1,3},{2,0},{3,1},{4,6},{5,7},{6,4},{7,5},{8,10},{9,11},{10,... | collective-permute-start | bytes 589832 | tf_op jit(solution)/shard_map/ppermute | solution.py:24
  6.8 1.3 copy-done
  10.2 1.8 %collective-permute-start.12 = (bf16[96,768]{1,0:T(8,128)(2,1)S(1)}, bf16[96,768]{1,0:T(8,128)(2,1)S(1)}, u32[]{:S(2)}, u32[]{:S(2)}) collective-permute-start(bf16[96,768]{1,0:T(8,128)(2,1)S(1)} %get-tuple-element.201), channel_id=1, source_target_pairs={{0,2},{1,3},{2,0},{3,1},{4,6},{5,7},{6,4},{7,5},{8,10},{9,11},{10,... | collective-permute-start | bytes 442376 | tf_op jit(solution)/shard_map/ppermute | solution.py:24
  12.3 2.6 %attn_forward.1 = (bf16[768,512]{1,0:T(8,128)(2,1)S(1)}, bf16[3,192,512]{2,1,0:T(8,128)(2,1)S(1)}, f32[8,512]{1,0:T(8,128)S(1)}, bf16[192,128]{1,0:T(8,128)(2,1)...) custom-call(s32[8,512]{1,0:T(8,128)S(1)} %get-tuple-element.185.bounds, ...), custom_call_target="tpu_custom_call" | custom-call | flops 1 | bytes 19926000 | tf_op jit(solution)/shard_map/attn_forward/pallas_call | solution.py:36
  15.7 1.8 %collective-permute-start.8 = (bf16[576,128]{1,0:T(8,128)(2,1)S(1)}, bf16[576,128]{1,0:T(8,128)(2,1)S(1)}, u32[]{:S(2)}, u32[]{:S(2)}) collective-permute-start(bf16[576,128]{1,0:T(8,128)(2,1)S(1)} %get-tuple-element.197), channel_id=1, source_target_pairs={{0,2},{1,3},{2,0},{3,1},{4,6},{5,7},{6,4},{7,5},{8,10},{9,11},{10,... | collective-permute-start | bytes 442376 | tf_op jit(solution)/shard_map/ppermute | solution.py:24
  17.6 1.5 collective-permute-start.13
  21.6 4.4 %collective-permute-done.8.p2.g2 = bf16[576,128]{1,0:T(8,128)(2,1)S(1)} collective-permute-done((bf16[576,128]{1,0:T(8,128)(2,1)S(1)}, bf16[576,128]{1,0:T(8,128)(2,1)S(1)}, u32[]{:S(2)}, u32[]{:S(2)}) %collective-permute-start.8) | collective-permute-done | bytes 147488 | tf_op jit(solution)/shard_map/ppermute | solution.py:24
  26.5 1.8 %collective-permute-start.19 = (bf16[192,768]{1,0:T(8,128)(2,1)S(1)}, bf16[192,768]{1,0:T(8,128)(2,1)S(1)}, u32[]{:S(2)}, u32[]{:S(2)}) collective-permute-start(bf16[192,768]{1,0:T(8,128)(2,1)S(1)} %collective-permute-done.18.xa), channel_id=1, source_target_pairs={{0,4},{4,0},{8,12},{12,8},{16,20},{20,16},{24,28},{28,24},{1,5},{5... | collective-permute-start | bytes 884744 | tf_op jit(solution)/shard_map/ppermute | solution.py:24
  29.6 1.6 collective-permute-start.16
  31.1 4.8 %collective-permute-done.19.xb = bf16[192,768]{1,0:T(8,128)(2,1)S(1)} collective-permute-done((bf16[192,768]{1,0:T(8,128)(2,1)S(1)}, bf16[192,768]{1,0:T(8,128)(2,1)S(1)}, u32[]{:S(2)}, u32[]{:S(2)}) %collective-permute-start.19) | collective-permute-done | bytes 294944 | tf_op jit(solution)/shard_map/ppermute | solution.py:24
  35.9 2.8 %collective-permute-done.16.rows.n_x.n1 = bf16[192,768]{1,0:T(8,128)(2,1)S(1)} collective-permute-done((bf16[192,768]{1,0:T(8,128)(2,1)S(1)}, bf16[192,768]{1,0:T(8,128)(2,1)S(1)}, u32[]{:S(2)}, u32[]{:S(2)}) %collective-permute-start.16) | collective-permute-done | bytes 294944 | tf_op jit(solution)/shard_map/ppermute | solution.py:24
  39.2 1.1 collective-permute-done.21.fb
  40.6 1.3 ffn_forward_far.1
  42.5 1.5 collective-permute-start.23
  44.0 1.3 ffn_forward.1
  45.4 4.1 %collective-permute-done.23.recv = bf16[128,768]{1,0:T(8,128)(2,1)S(1)} collective-permute-done((bf16[128,768]{1,0:T(8,128)(2,1)S(1)}, bf16[128,768]{1,0:T(8,128)(2,1)S(1)}, u32[]{:S(2)}, u32[]{:S(2)}) %collective-permute-start.23) | collective-permute-done | bytes 196640 | tf_op jit(solution)/shard_map/ppermute | solution.py:24
  50.7 1.5 collective-permute-start.26
  52.2 1.3 ffn_backward.1
  53.6 4.0 %collective-permute-done.26.rows.f1 = bf16[128,768]{1,0:T(8,128)(2,1)S(1)} collective-permute-done((bf16[128,768]{1,0:T(8,128)(2,1)S(1)}, bf16[128,768]{1,0:T(8,128)(2,1)S(1)}, u32[]{:S(2)}, u32[]{:S(2)}) %collective-permute-start.26) | collective-permute-done | bytes 196640 | tf_op jit(solution)/shard_map/ppermute | solution.py:24
  57.6 1.3 ffn_backward_far.1
  59.5 1.5 collective-permute-start.30
  61.0 1.9 %ffn_weight_grads.1 = (f32[192,768]{1,0:T(8,128)S(1)}, bf16[192,768]{1,0:T(8,128)(2,1)S(1)}, f32[192,768]{1,0:T(8,128)S(1)}, bf16[192,768]{1,0:T(8,128)(2,1)S(1)...) custom-call(bf16[192,768]{1,0:T(8,128)(2,1)S(1)} %get-tuple-element., ...), custom_call_target="tpu_custom_call" | custom-call | flops 1 | bytes 9225000 | tf_op jit(solution)/shard_map/ffn_weight_grads/pallas_call | solution.py:36
  62.9 3.5 %collective-permute-done.30.recv = bf16[128,768]{1,0:T(8,128)(2,1)S(1)} collective-permute-done((bf16[128,768]{1,0:T(8,128)(2,1)S(1)}, bf16[128,768]{1,0:T(8,128)(2,1)S(1)}, u32[]{:S(2)}, u32[]{:S(2)}) %collective-permute-start.30) | collective-permute-done | bytes 196640 | tf_op jit(solution)/shard_map/ppermute | solution.py:24
  69.7 1.5 collective-permute-start.33
  71.2 1.0 collective-permute-start.35
  72.3 2.8 %collective-permute-done.33.u2 = bf16[480,128]{1,0:T(8,128)(2,1)S(1)} collective-permute-done((bf16[480,128]{1,0:T(8,128)(2,1)S(1)}, bf16[480,128]{1,0:T(8,128)(2,1)S(1)}, u32[]{:S(2)}, u32[]{:S(2)}) %collective-permute-start.33) | collective-permute-done | bytes 122912 | tf_op jit(solution)/shard_map/ppermute | solution.py:24
  75.1 3.5 %collective-permute-done.32.recv = bf16[192,768]{1,0:T(8,128)(2,1)S(1)} collective-permute-done((bf16[192,768]{1,0:T(8,128)(2,1)S(1)}, bf16[192,768]{1,0:T(8,128)(2,1)S(1)}, u32[]{:S(2)}, u32[]{:S(2)}) %collective-permute-start.32) | collective-permute-done | bytes 294944 | tf_op jit(solution)/shard_map/ppermute | solution.py:746
  78.7 3.5 %collective-permute-start.36 = (bf16[192,768]{1,0:T(8,128)(2,1)S(1)}, bf16[192,768]{1,0:T(8,128)(2,1)S(1)}, u32[]{:S(2)}, u32[]{:S(2)}) collective-permute-start(bf16[192,768]{1,0:T(8,128)(2,1)S(1)} %get-tuple-element.247), channel_id=1, source_target_pairs={{0,8},{4,12},{24,16},{28,20},{1,9},{5,13},{25,17},{29,21},{2,10},{... | collective-permute-start | bytes 884744 | tf_op jit(solution)/shard_map/ppermute | solution.py:746
  82.3 1.6 collective-permute-start.38
  83.8 2.6 %attn_backward.1 = (bf16[576,512]{1,0:T(8,128)(2,1)S(1)}, f32[8,128]{1,0:T(8,128)S(1)}, f32[8,576]{1,0:T(8,128)S(1)}) custom-call(s32[8,512]{1,0:T(8,128)S(1)} %get-tuple-element.185.bounds, bf16[3,192,512]{2,1,0:T(8,128)(2,1)S(1)} %get-tuple-element.248.qkv, f32[8,512]{1,0:T(8,128)S(1)} %get-tuple-element.249.logsum, ...), custom_call_target="tpu_custom_call" | custom-call | flops 1 | bytes 18450000 | tf_op jit(solution)/shard_map/attn_backward/pallas_call | solution.py:36
  87.6 1.3 collective-permute-start.40
  91.1 1.0 collective-permute-start.42
  92.2 3.7 %collective-permute-done.39.recv = bf16[192,768]{1,0:T(8,128)(2,1)S(1)} collective-permute-done((bf16[192,768]{1,0:T(8,128)(2,1)S(1)}, bf16[192,768]{1,0:T(8,128)(2,1)S(1)}, u32[]{:S(2)}, u32[]{:S(2)}) %collective-permute-start.39) | collective-permute-done | bytes 294944 | tf_op jit(solution)/shard_map/ppermute | solution.py:746
  95.9 1.9 %collective-permute-start.43 = (bf16[192,768]{1,0:T(8,128)(2,1)S(1)}, bf16[192,768]{1,0:T(8,128)(2,1)S(1)}, u32[]{:S(2)}, u32[]{:S(2)}) collective-permute-start(bf16[192,768]{1,0:T(8,128)(2,1)S(1)} %get-tuple-element.281), channel_id=1, source_target_pairs={{0,8},{4,12},{24,16},{28,20},{1,9},{5,13},{25,17},{29,21},{2,10},{... | collective-permute-start | bytes 884744 | tf_op jit(solution)/shard_map/ppermute | solution.py:746
  98.7 1.1 collective-permute-start.45
  99.8 1.3 collective-permute-start.46
  101.9 4.0 %collective-permute-start.47 = (bf16[192,768]{1,0:T(8,128)(2,1)S(1)}, bf16[192,768]{1,0:T(8,128)(2,1)S(1)}, u32[]{:S(2)}, u32[]{:S(2)}) collective-permute-start(bf16[192,768]{1,0:T(8,128)(2,1)S(1)} %get-tuple-element.289), channel_id=1, source_target_pairs={{0,8},{4,12},{24,16},{28,20},{1,9},{5,13},{25,17},{29,21},{2,10},{... | collective-permute-start | bytes 884744 | tf_op jit(solution)/shard_map/ppermute | solution.py:746
  106.6 1.1 collective-permute-start.50
  108.5 1.6 collective-permute-done.47.recv
  110.9 1.6 collective-permute-start.51
  112.5 6.1 %collective-permute-start.54 = (bf16[192,768]{1,0:T(8,128)(2,1)S(1)}, bf16[192,768]{1,0:T(8,128)(2,1)S(1)}, u32[]{:S(2)}, u32[]{:S(2)}) collective-permute-start(bf16[192,768]{1,0:T(8,128)(2,1)S(1)} %get-tuple-element.299), channel_id=1, source_target_pairs={{0,8},{4,12},{24,16},{28,20},{1,9},{5,13},{25,17},{29,21},{2,10},{... | collective-permute-start | bytes 884744 | tf_op jit(solution)/shard_map/ppermute | solution.py:746
  118.7 1.3 collective-permute-start.56
  120.1 1.3 collective-permute-start.55
  121.6 1.3 collective-permute-start.58
  122.9 3.1 %collective-permute-done.54.recv = bf16[192,768]{1,0:T(8,128)(2,1)S(1)} collective-permute-done((bf16[192,768]{1,0:T(8,128)(2,1)S(1)}, bf16[192,768]{1,0:T(8,128)(2,1)S(1)}, u32[]{:S(2)}, u32[]{:S(2)}) %collective-permute-start.54) | collective-permute-done | bytes 294944 | tf_op jit(solution)/shard_map/ppermute | solution.py:746
  127.6 3.0 %collective-permute-done.55.recv = bf16[192,768]{1,0:T(8,128)(2,1)S(1)} collective-permute-done((bf16[192,768]{1,0:T(8,128)(2,1)S(1)}, bf16[192,768]{1,0:T(8,128)(2,1)S(1)}, u32[]{:S(2)}, u32[]{:S(2)}) %collective-permute-start.55) | collective-permute-done | bytes 294944 | tf_op jit(solution)/shard_map/ppermute | solution.py:746
  130.6 1.1 qkv_input_grad.1
  132.5 1.3 collective-permute-start.61
  133.8 1.0 collective-permute-start.62
  135.1 1.0 collective-permute-start.63
  136.3 1.3 collective-permute-start.68
  137.6 4.9 %collective-permute-done.61.recv = bf16[192,768]{1,0:T(8,128)(2,1)S(1)} collective-permute-done((bf16[192,768]{1,0:T(8,128)(2,1)S(1)}, bf16[192,768]{1,0:T(8,128)(2,1)S(1)}, u32[]{:S(2)}, u32[]{:S(2)}) %collective-permute-start.61) | collective-permute-done | bytes 294944 | tf_op jit(solution)/shard_map/ppermute | solution.py:746
  142.5 1.3 collective-permute-start.64
  143.8 1.1 collective-permute-start.66
  144.9 3.1 %collective-permute-done.63.other1 = bf16[192,768]{1,0:T(8,128)(2,1)S(1)} collective-permute-done((bf16[192,768]{1,0:T(8,128)(2,1)S(1)}, bf16[192,768]{1,0:T(8,128)(2,1)S(1)}, u32[]{:S(2)}, u32[]{:S(2)}) %collective-permute-start.63) | collective-permute-done | bytes 294944 | tf_op jit(solution)/shard_map/ppermute | solution.py:746
  149.0 1.6 in_gradient.1
  150.5 8.3 %collective-permute-done.64.recv = bf16[192,768]{1,0:T(8,128)(2,1)S(1)} collective-permute-done((bf16[192,768]{1,0:T(8,128)(2,1)S(1)}, bf16[192,768]{1,0:T(8,128)(2,1)S(1)}, u32[]{:S(2)}, u32[]{:S(2)}) %collective-permute-start.64) | collective-permute-done | bytes 294944 | tf_op jit(solution)/shard_map/ppermute | solution.py:746
  159.3 1.1 collective-permute-start.71
  160.4 1.6 back_gradient.1
  163.0 1.4 vector_outputs.1
  164.4 1.3 collective-permute-done.69.from_x
  166.5 2.3 %collective-permute-done.71.vo_other = bf16[192,768]{1,0:T(8,128)(2,1)S(1)} collective-permute-done((bf16[192,768]{1,0:T(8,128)(2,1)S(1)}, bf16[192,768]{1,0:T(8,128)(2,1)S(1)}, u32[]{:S(2)}, u32[]{:S(2)}) %collective-permute-start.71) | collective-permute-done | bytes 294944 | tf_op jit(solution)/shard_map/ppermute | solution.py:746
  168.8 3.2 %collective-permute-done.70.qk_other = bf16[192,768]{1,0:T(8,128)(2,1)S(1)} collective-permute-done((bf16[192,768]{1,0:T(8,128)(2,1)S(1)}, bf16[192,768]{1,0:T(8,128)(2,1)S(1)}, u32[]{:S(2)}, u32[]{:S(2)}) %collective-permute-start.70) | collective-permute-done | bytes 294944 | tf_op jit(solution)/shard_map/ppermute | solution.py:746
  172.0 1.6 attn_gradients.1
  (171 shorter events, 31.1 us)
Async XLA Ops:
  0.7 9.4 %collective-permute-start.3 = (bf16[768,768]{1,0:T(8,128)(2,1)}, bf16[768,768]{1,0:T(8,128)(2,1)S(1)}, u32[]{:S(2)}, u32[]{:S(2)}) collective-permute-start(bf16[768,768]{1,0:T(8,128)(2,1)} %wi_own.1), channel_id=1, source_target_pairs={{0,1},{1,0},{2,3},{3,2},{4,5},{5,4},{6,7},{7,6},{8,9},{9,8},{10,11... | collective-permute-start | bytes 3538952 | tf_op jit(solution)/shard_map/ppermute | solution.py:24
  1.2 8.9 %collective-permute-start.5 = (bf16[192,3072]{1,0:T(8,128)(2,1)}, bf16[192,3072]{1,0:T(8,128)(2,1)S(1)}, u32[]{:S(2)}, u32[]{:S(2)}) collective-permute-start(bf16[192,3072]{1,0:T(8,128)(2,1)} %own.3), channel_id=1, source_target_pairs={{0,1},{1,0},{2,3},{3,2},{4,5},{5,4},{6,7},{7,6},{8,9},{9,8},{10,11... | collective-permute-start | bytes 3538952 | tf_op jit(solution)/shard_map/ppermute | solution.py:24
  1.3 8.8 %collective-permute-start.4 = (bf16[192,768]{1,0:T(8,128)(2,1)}, bf16[192,768]{1,0:T(8,128)(2,1)S(1)}, u32[]{:S(2)}, u32[]{:S(2)}) collective-permute-start(bf16[192,768]{1,0:T(8,128)(2,1)} %own.2), channel_id=1, source_target_pairs={{0,1},{1,0},{2,3},{3,2},{4,5},{5,4},{6,7},{7,6},{8,9},{9,8},{10,11... | collective-permute-start | bytes 884744 | tf_op jit(solution)/shard_map/ppermute | solution.py:24
  1.8 7.4 %collective-permute-start = (bf16[192,512]{1,0:T(8,128)(2,1)}, bf16[192,512]{1,0:T(8,128)(2,1)S(1)}, u32[]{:S(2)}, u32[]{:S(2)}) collective-permute-start(bf16[192,512]{1,0:T(8,128)(2,1)} %param.18), channel_id=1, source_target_pairs={{0,1},{1,0},{2,3},{3,2},{4,5},{5,4},{6,7},{7,6},{8,9},{9,8},{10,11... | collective-permute-start | bytes 589832 | tf_op jit(solution)/shard_map/ppermute | solution.py:24
  1.8 8.3 %collective-permute-start.2 = (bf16[192,512]{1,0:T(8,128)(2,1)}, bf16[192,512]{1,0:T(8,128)(2,1)S(1)}, u32[]{:S(2)}, u32[]{:S(2)}) collective-permute-start(bf16[192,512]{1,0:T(8,128)(2,1)} %param.18), channel_id=1, source_target_pairs={{0,2},{1,3},{2,0},{3,1},{4,6},{5,7},{6,4},{7,5},{8,10},{9,11},{10,... | collective-permute-start | bytes 589832 | tf_op jit(solution)/shard_map/ppermute | solution.py:24
  9.2 3.1 %collective-permute-start.1 = (bf16[192,512]{1,0:T(8,128)(2,1)S(1)}, bf16[192,512]{1,0:T(8,128)(2,1)S(1)}, u32[]{:S(2)}, u32[]{:S(2)}) collective-permute-start(bf16[192,512]{1,0:T(8,128)(2,1)S(1)} %collective-permute-done.x1), channel_id=1, source_target_pairs={{0,1},{1,0},{2,3},{3,2},{4,5},{5,4},{6,7},{7,6},{8,9},{9,8},{10,11... | collective-permute-start | bytes 589832 | tf_op jit(solution)/shard_map/ppermute | solution.py:24
  10.1 2.2 %collective-permute-start.6 = (bf16[192,512]{1,0:T(8,128)(2,1)S(1)}, bf16[192,512]{1,0:T(8,128)(2,1)S(1)}, u32[]{:S(2)}, u32[]{:S(2)}) collective-permute-start(bf16[192,512]{1,0:T(8,128)(2,1)S(1)} %collective-permute-done.2.x2), channel_id=1, source_target_pairs={{0,1},{1,0},{2,3},{3,2},{4,5},{5,4},{6,7},{7,6},{8,9},{9,8},{10,11... | collective-permute-start | bytes 589832 | tf_op jit(solution)/shard_map/ppermute | solution.py:24
  10.2 7.4 %collective-permute-start.12 = (bf16[96,768]{1,0:T(8,128)(2,1)S(1)}, bf16[96,768]{1,0:T(8,128)(2,1)S(1)}, u32[]{:S(2)}, u32[]{:S(2)}) collective-permute-start(bf16[96,768]{1,0:T(8,128)(2,1)S(1)} %get-tuple-element.201), channel_id=1, source_target_pairs={{0,2},{1,3},{2,0},{3,1},{4,6},{5,7},{6,4},{7,5},{8,10},{9,11},{10,... | collective-permute-start | bytes 442376 | tf_op jit(solution)/shard_map/ppermute | solution.py:24
  12.0 14.5 %collective-permute-start.18 = (bf16[192,768]{1,0:T(8,128)(2,1)S(1)}, bf16[192,768]{1,0:T(8,128)(2,1)S(1)}, u32[]{:S(2)}, u32[]{:S(2)}) collective-permute-start(bf16[192,768]{1,0:T(8,128)(2,1)S(1)} %get-tuple-element.187), channel_id=1, source_target_pairs={{0,2},{1,3},{2,0},{3,1},{4,6},{5,7},{6,4},{7,5},{8,10},{9,11},{10,... | collective-permute-start | bytes 884744 | tf_op jit(solution)/shard_map/ppermute | solution.py:24
  15.7 10.2 %collective-permute-start.8 = (bf16[576,128]{1,0:T(8,128)(2,1)S(1)}, bf16[576,128]{1,0:T(8,128)(2,1)S(1)}, u32[]{:S(2)}, u32[]{:S(2)}) collective-permute-start(bf16[576,128]{1,0:T(8,128)(2,1)S(1)} %get-tuple-element.197), channel_id=1, source_target_pairs={{0,2},{1,3},{2,0},{3,1},{4,6},{5,7},{6,4},{7,5},{8,10},{9,11},{10,... | collective-permute-start | bytes 442376 | tf_op jit(solution)/shard_map/ppermute | solution.py:24
  17.6 8.9 %collective-permute-start.13 = (bf16[96,768]{1,0:T(8,128)(2,1)S(1)}, bf16[96,768]{1,0:T(8,128)(2,1)S(1)}, u32[]{:S(2)}, u32[]{:S(2)}) collective-permute-start(bf16[96,768]{1,0:T(8,128)(2,1)S(1)} %collective-permute-done.12.xa), channel_id=1, source_target_pairs={{0,4},{4,0},{8,12},{12,8},{16,20},{20,16},{24,28},{28,24},{1,5},{5... | collective-permute-start | bytes 442376 | tf_op jit(solution)/shard_map/ppermute | solution.py:24
  19.1 2.5 %collective-permute-start.7 = (bf16[384,128]{1,0:T(8,128)(2,1)S(1)}, bf16[384,128]{1,0:T(8,128)(2,1)S(1)}, u32[]{:S(2)}, u32[]{:S(2)}) collective-permute-start(bf16[384,128]{1,0:T(8,128)(2,1)S(1)} %get-tuple-element.196), channel_id=1, source_target_pairs={{0,1},{1,0},{2,3},{3,2},{4,5},{5,4},{6,7},{7,6},{8,9},{9,8},{10,11... | collective-permute-start | bytes 294920 | tf_op jit(solution)/shard_map/ppermute | solution.py:24
  25.9 2.4 %collective-permute-start.11 = (bf16[576,128]{1,0:T(8,128)(2,1)S(1)}, bf16[576,128]{1,0:T(8,128)(2,1)S(1)}, u32[]{:S(2)}, u32[]{:S(2)}) collective-permute-start(bf16[576,128]{1,0:T(8,128)(2,1)S(1)} %collective-permute-done.8.p2.g2), channel_id=1, source_target_pairs={{0,1},{1,0},{2,3},{3,2},{4,5},{5,4},{6,7},{7,6},{8,9},{9,8},{10,11... | collective-permute-start | bytes 442376 | tf_op jit(solution)/shard_map/ppermute | solution.py:24
  25.9 2.7 %collective-permute-start.14 = (bf16[96,768]{1,0:T(8,128)(2,1)S(1)}, bf16[96,768]{1,0:T(8,128)(2,1)S(1)}, u32[]{:S(2)}, u32[]{:S(2)}) collective-permute-start(bf16[96,768]{1,0:T(8,128)(2,1)S(1)} %collective-permute-done.12.xa), channel_id=1, source_target_pairs={{0,1},{1,0},{2,3},{3,2},{4,5},{5,4},{6,7},{7,6},{8,9},{9,8},{10,11... | collective-permute-start | bytes 442376 | tf_op jit(solution)/shard_map/ppermute | solution.py:24
  26.5 9.4 %collective-permute-start.19 = (bf16[192,768]{1,0:T(8,128)(2,1)S(1)}, bf16[192,768]{1,0:T(8,128)(2,1)S(1)}, u32[]{:S(2)}, u32[]{:S(2)}) collective-permute-start(bf16[192,768]{1,0:T(8,128)(2,1)S(1)} %collective-permute-done.18.xa), channel_id=1, source_target_pairs={{0,4},{4,0},{8,12},{12,8},{16,20},{20,16},{24,28},{28,24},{1,5},{5... | collective-permute-start | bytes 884744 | tf_op jit(solution)/shard_map/ppermute | solution.py:24
  29.6 9.1 %collective-permute-start.16 = (bf16[192,768]{1,0:T(8,128)(2,1)S(1)}, bf16[192,768]{1,0:T(8,128)(2,1)S(1)}, u32[]{:S(2)}, u32[]{:S(2)}) collective-permute-start(bf16[192,768]{1,0:T(8,128)(2,1)S(1)} %get-tuple-element.211.rows.n0), channel_id=1, source_target_pairs={{0,2},{1,3},{2,0},{3,1},{4,6},{5,7},{6,4},{7,5},{8,10},{9,11},{10,... | collective-permute-start | bytes 884744 | tf_op jit(solution)/shard_map/ppermute | solution.py:24
  31.1 8.1 %collective-permute-start.20 = (bf16[192,768]{1,0:T(8,128)(2,1)S(1)}, bf16[192,768]{1,0:T(8,128)(2,1)S(1)}, u32[]{:S(2)}, u32[]{:S(2)}) collective-permute-start(bf16[192,768]{1,0:T(8,128)(2,1)S(1)} %collective-permute-done.18.xa), channel_id=1, source_target_pairs={{0,1},{1,0},{2,3},{3,2},{4,5},{5,4},{6,7},{7,6},{8,9},{9,8},{10,11... | collective-permute-start | bytes 884744 | tf_op jit(solution)/shard_map/ppermute | solution.py:24
  38.7 6.6 %collective-permute-start.17 = (bf16[192,768]{1,0:T(8,128)(2,1)S(1)}, bf16[192,768]{1,0:T(8,128)(2,1)S(1)}, u32[]{:S(2)}, u32[]{:S(2)}) collective-permute-start(bf16[192,768]{1,0:T(8,128)(2,1)S(1)} %get-tuple-element.211.rows.n0), channel_id=1, source_target_pairs={{0,1},{1,0},{2,3},{3,2},{4,5},{5,4},{6,7},{7,6},{8,9},{9,8},{10,11... | collective-permute-start | bytes 884744 | tf_op jit(solution)/shard_map/ppermute | solution.py:24
  41.9 7.5 %collective-permute-start.22 = (bf16[192,768]{1,0:T(8,128)(2,1)S(1)}, bf16[192,768]{1,0:T(8,128)(2,1)S(1)}, u32[]{:S(2)}, u32[]{:S(2)}) collective-permute-start(bf16[192,768]{1,0:T(8,128)(2,1)S(1)} %collective-permute-done.16.rows.n_x.n1), channel_id=1, source_target_pairs={{0,1},{1,0},{2,3},{3,2},{4,5},{5,4},{6,7},{7,6},{8,9},{9,8},{10,11... | collective-permute-start | bytes 884744 | tf_op jit(solution)/shard_map/ppermute | solution.py:24
  42.2 3.2 %collective-permute-start.24 = (bf16[192,512]{1,0:T(8,128)(2,1)S(1)}, bf16[192,512]{1,0:T(8,128)(2,1)S(1)}, u32[]{:S(2)}, u32[]{:S(2)}) collective-permute-start(bf16[192,512]{1,0:T(8,128)(2,1)S(1)} %copy-done.6), channel_id=1, source_target_pairs={{0,1},{1,0},{2,3},{3,2},{4,5},{5,4},{6,7},{7,6},{8,9},{9,8},{10,11... | collective-permute-start | bytes 589832 | tf_op jit(solution)/shard_map/ppermute | solution.py:24
  42.5 7.0 %collective-permute-start.23 = (bf16[128,768]{1,0:T(8,128)(2,1)S(1)}, bf16[128,768]{1,0:T(8,128)(2,1)S(1)}, u32[]{:S(2)}, u32[]{:S(2)}) collective-permute-start(bf16[128,768]{1,0:T(8,128)(2,1)S(1)} %get-tuple-element.209), channel_id=1, source_target_pairs={{0,2},{1,3},{2,0},{3,1},{4,6},{5,7},{6,4},{7,5},{8,10},{9,11},{10,... | collective-permute-start | bytes 589832 | tf_op jit(solution)/shard_map/ppermute | solution.py:24
  50.2 7.5 %collective-permute-start.25 = (bf16[256,768]{1,0:T(8,128)(2,1)S(1)}, bf16[256,768]{1,0:T(8,128)(2,1)S(1)}, u32[]{:S(2)}, u32[]{:S(2)}) collective-permute-start(bf16[256,768]{1,0:T(8,128)(2,1)S(1)} %get-tuple-element.221), channel_id=1, source_target_pairs={{0,1},{1,0},{2,3},{3,2},{4,5},{5,4},{6,7},{7,6},{8,9},{9,8},{10,11... | collective-permute-start | bytes 1179656 | tf_op jit(solution)/shard_map/ppermute | solution.py:24
  50.2 3.3 %collective-permute-start.27 = (bf16[128,768]{1,0:T(8,128)(2,1)S(1)}, bf16[128,768]{1,0:T(8,128)(2,1)S(1)}, u32[]{:S(2)}, u32[]{:S(2)}) collective-permute-start(bf16[128,768]{1,0:T(8,128)(2,1)S(1)} %get-tuple-element.220.rows.f0), channel_id=1, source_target_pairs={{0,1},{1,0},{2,3},{3,2},{4,5},{5,4},{6,7},{7,6},{8,9},{9,8},{10,11... | collective-permute-start | bytes 589832 | tf_op jit(solution)/shard_map/ppermute | solution.py:24
  50.7 6.9 %collective-permute-start.26 = (bf16[128,768]{1,0:T(8,128)(2,1)S(1)}, bf16[128,768]{1,0:T(8,128)(2,1)S(1)}, u32[]{:S(2)}, u32[]{:S(2)}) collective-permute-start(bf16[128,768]{1,0:T(8,128)(2,1)S(1)} %get-tuple-element.220.rows.f0), channel_id=1, source_target_pairs={{0,2},{1,3},{2,0},{3,1},{4,6},{5,7},{6,4},{7,5},{8,10},{9,11},{10,... | collective-permute-start | bytes 589832 | tf_op jit(solution)/shard_map/ppermute | solution.py:24
  59.5 6.9 %collective-permute-start.30 = (bf16[128,768]{1,0:T(8,128)(2,1)S(1)}, bf16[128,768]{1,0:T(8,128)(2,1)S(1)}, u32[]{:S(2)}, u32[]{:S(2)}) collective-permute-start(bf16[128,768]{1,0:T(8,128)(2,1)S(1)} %get-tuple-element.232), channel_id=1, source_target_pairs={{0,2},{1,3},{2,0},{3,1},{4,6},{5,7},{6,4},{7,5},{8,10},{9,11},{10,... | collective-permute-start | bytes 589832 | tf_op jit(solution)/shard_map/ppermute | solution.py:24
  68.6 13.6 %collective-permute-start.37 = (bf16[384,768]{1,0:T(8,128)(2,1)S(1)}, bf16[384,768]{1,0:T(8,128)(2,1)S(1)}, u32[]{:S(2)}, u32[]{:S(2)}) collective-permute-start(bf16[384,768]{1,0:T(8,128)(2,1)S(1)} %get-tuple-element.268), channel_id=1, source_target_pairs={{0,1},{1,0},{2,3},{3,2},{4,5},{5,4},{6,7},{7,6},{8,9},{9,8},{10,11... | collective-permute-start | bytes 1769480 | tf_op jit(solution)/shard_map/ppermute | solution.py:24
  68.7 9.8 %collective-permute-start.32 = (bf16[192,768]{1,0:T(8,128)(2,1)S(1)}, bf16[192,768]{1,0:T(8,128)(2,1)S(1)}, u32[]{:S(2)}, u32[]{:S(2)}) collective-permute-start(bf16[192,768]{1,0:T(8,128)(2,1)S(1)} %get-tuple-element.246), channel_id=1, source_target_pairs={{0,4},{4,0},{8,12},{12,8},{16,20},{20,16},{24,28},{28,24},{1,5},{5... | collective-permute-start | bytes 884744 | tf_op jit(solution)/shard_map/ppermute | solution.py:746
  69.7 5.3 %collective-permute-start.33 = (bf16[480,128]{1,0:T(8,128)(2,1)S(1)}, bf16[480,128]{1,0:T(8,128)(2,1)S(1)}, u32[]{:S(2)}, u32[]{:S(2)}) collective-permute-start(bf16[480,128]{1,0:T(8,128)(2,1)S(1)} %get-tuple-element.251), channel_id=1, source_target_pairs={{0,2},{1,3},{2,0},{3,1},{4,6},{5,7},{6,4},{7,5},{8,10},{9,11},{10,... | collective-permute-start | bytes 368648 | tf_op jit(solution)/shard_map/ppermute | solution.py:24
  71.2 16.3 %collective-permute-start.35 = (bf16[192,768]{1,0:T(8,128)(2,1)S(1)}, bf16[192,768]{1,0:T(8,128)(2,1)S(1)}, u32[]{:S(2)}, u32[]{:S(2)}) collective-permute-start(bf16[192,768]{1,0:T(8,128)(2,1)S(1)} %get-tuple-element.256), channel_id=1, source_target_pairs={{0,4},{4,0},{8,12},{12,8},{16,20},{20,16},{24,28},{28,24},{1,5},{5... | collective-permute-start | bytes 884744 | tf_op jit(solution)/shard_map/ppermute | solution.py:746
  75.0 7.2 %collective-permute-start.34 = (bf16[480,128]{1,0:T(8,128)(2,1)S(1)}, bf16[480,128]{1,0:T(8,128)(2,1)S(1)}, u32[]{:S(2)}, u32[]{:S(2)}) collective-permute-start(bf16[480,128]{1,0:T(8,128)(2,1)S(1)} %collective-permute-done.33.u2), channel_id=1, source_target_pairs={{0,1},{1,0},{2,3},{3,2},{4,5},{5,4},{6,7},{7,6},{8,9},{9,8},{10,11... | collective-permute-start | bytes 368648 | tf_op jit(solution)/shard_map/ppermute | solution.py:24
  78.7 10.3 %collective-permute-start.36 = (bf16[192,768]{1,0:T(8,128)(2,1)S(1)}, bf16[192,768]{1,0:T(8,128)(2,1)S(1)}, u32[]{:S(2)}, u32[]{:S(2)}) collective-permute-start(bf16[192,768]{1,0:T(8,128)(2,1)S(1)} %get-tuple-element.247), channel_id=1, source_target_pairs={{0,8},{4,12},{24,16},{28,20},{1,9},{5,13},{25,17},{29,21},{2,10},{... | collective-permute-start | bytes 884744 | tf_op jit(solution)/shard_map/ppermute | solution.py:746
  82.3 7.7 %collective-permute-start.38 = (bf16[192,768]{1,0:T(8,128)(2,1)S(1)}, bf16[192,768]{1,0:T(8,128)(2,1)S(1)}, u32[]{:S(2)}, u32[]{:S(2)}) collective-permute-start(bf16[192,768]{1,0:T(8,128)(2,1)S(1)} %wo_low.1), channel_id=1, source_target_pairs={{0,2},{1,3},{2,0},{3,1},{4,6},{5,7},{6,4},{7,5},{8,10},{9,11},{10,... | collective-permute-start | bytes 884744 | tf_op jit(solution)/shard_map/ppermute | solution.py:24
  86.5 9.3 %collective-permute-start.39 = (bf16[192,768]{1,0:T(8,128)(2,1)S(1)}, bf16[192,768]{1,0:T(8,128)(2,1)S(1)}, u32[]{:S(2)}, u32[]{:S(2)}) collective-permute-start(bf16[192,768]{1,0:T(8,128)(2,1)S(1)} %get-tuple-element.280), channel_id=1, source_target_pairs={{0,4},{4,0},{8,12},{12,8},{16,20},{20,16},{24,28},{28,24},{1,5},{5... | collective-permute-start | bytes 884744 | tf_op jit(solution)/shard_map/ppermute | solution.py:746
  87.6 10.3 %collective-permute-start.40 = (bf16[192,768]{1,0:T(8,128)(2,1)S(1)}, bf16[192,768]{1,0:T(8,128)(2,1)S(1)}, u32[]{:S(2)}, u32[]{:S(2)}) collective-permute-start(bf16[192,768]{1,0:T(8,128)(2,1)S(1)} %get-tuple-element.260), channel_id=1, source_target_pairs={{0,8},{4,12},{24,16},{28,20},{1,9},{5,13},{25,17},{29,21},{2,10},{... | collective-permute-start | bytes 884744 | tf_op jit(solution)/shard_map/ppermute | solution.py:746
  89.0 10.7 %collective-permute-start.41 = (bf16[192,768]{1,0:T(8,128)(2,1)S(1)}, bf16[192,768]{1,0:T(8,128)(2,1)S(1)}, u32[]{:S(2)}, u32[]{:S(2)}) collective-permute-start(bf16[192,768]{1,0:T(8,128)(2,1)S(1)} %second_add.5.mine), channel_id=1, source_target_pairs={{8,16},{12,20},{16,8},{20,12},{9,17},{13,21},{17,9},{21,13},{10,18... | collective-permute-start | bytes 884744 | tf_op jit(solution)/shard_map/ppermute | solution.py:746
  91.1 10.6 %collective-permute-start.42 = (bf16[192,768]{1,0:T(8,128)(2,1)S(1)}, bf16[192,768]{1,0:T(8,128)(2,1)S(1)}, u32[]{:S(2)}, u32[]{:S(2)}) collective-permute-start(bf16[192,768]{1,0:T(8,128)(2,1)S(1)} %get-tuple-element.288), channel_id=1, source_target_pairs={{0,4},{4,0},{8,12},{12,8},{16,20},{20,16},{24,28},{28,24},{1,5},{5... | collective-permute-start | bytes 884744 | tf_op jit(solution)/shard_map/ppermute | solution.py:746
  95.9 9.9 %collective-permute-start.43 = (bf16[192,768]{1,0:T(8,128)(2,1)S(1)}, bf16[192,768]{1,0:T(8,128)(2,1)S(1)}, u32[]{:S(2)}, u32[]{:S(2)}) collective-permute-start(bf16[192,768]{1,0:T(8,128)(2,1)S(1)} %get-tuple-element.281), channel_id=1, source_target_pairs={{0,8},{4,12},{24,16},{28,20},{1,9},{5,13},{25,17},{29,21},{2,10},{... | collective-permute-start | bytes 884744 | tf_op jit(solution)/shard_map/ppermute | solution.py:746
  98.0 8.6 %collective-permute-start.44 = (bf16[192,768]{1,0:T(8,128)(2,1)S(1)}, bf16[192,768]{1,0:T(8,128)(2,1)S(1)}, u32[]{:S(2)}, u32[]{:S(2)}) collective-permute-start(bf16[192,768]{1,0:T(8,128)(2,1)S(1)} %second_add.6.mine), channel_id=1, source_target_pairs={{8,16},{12,20},{16,8},{20,12},{9,17},{13,21},{17,9},{21,13},{10,18... | collective-permute-start | bytes 884744 | tf_op jit(solution)/shard_map/ppermute | solution.py:746
  98.7 9.1 %collective-permute-start.45 = (bf16[192,768]{1,0:T(8,128)(2,1)S(1)}, bf16[192,768]{1,0:T(8,128)(2,1)S(1)}, u32[]{:S(2)}, u32[]{:S(2)}) collective-permute-start(bf16[192,768]{1,0:T(8,128)(2,1)S(1)} %get-tuple-element.271), channel_id=1, source_target_pairs={{0,4},{4,0},{8,12},{12,8},{16,20},{20,16},{24,28},{28,24},{1,5},{5... | collective-permute-start | bytes 884744 | tf_op jit(solution)/shard_map/ppermute | solution.py:746
  99.8 8.6 %collective-permute-start.46 = (bf16[192,768]{1,0:T(8,128)(2,1)S(1)}, bf16[192,768]{1,0:T(8,128)(2,1)S(1)}, u32[]{:S(2)}, u32[]{:S(2)}) collective-permute-start(bf16[192,768]{1,0:T(8,128)(2,1)S(1)} %third_add.3.mine), channel_id=1, source_target_pairs={{8,0},{12,4},{16,24},{20,28},{9,1},{13,5},{17,25},{21,29},{10,2},{... | collective-permute-start | bytes 884744 | tf_op jit(solution)/shard_map/ppermute | solution.py:746
  101.9 8.2 %collective-permute-start.47 = (bf16[192,768]{1,0:T(8,128)(2,1)S(1)}, bf16[192,768]{1,0:T(8,128)(2,1)S(1)}, u32[]{:S(2)}, u32[]{:S(2)}) collective-permute-start(bf16[192,768]{1,0:T(8,128)(2,1)S(1)} %get-tuple-element.289), channel_id=1, source_target_pairs={{0,8},{4,12},{24,16},{28,20},{1,9},{5,13},{25,17},{29,21},{2,10},{... | collective-permute-start | bytes 884744 | tf_op jit(solution)/shard_map/ppermute | solution.py:746
  105.9 4.9 %collective-permute-start.48 = (bf16[192,768]{1,0:T(8,128)(2,1)S(1)}, bf16[192,768]{1,0:T(8,128)(2,1)S(1)}, u32[]{:S(2)}, u32[]{:S(2)}) collective-permute-start(bf16[192,768]{1,0:T(8,128)(2,1)S(1)} %second_add.7.mine), channel_id=1, source_target_pairs={{8,16},{12,20},{16,8},{20,12},{9,17},{13,21},{17,9},{21,13},{10,18... | collective-permute-start | bytes 884744 | tf_op jit(solution)/shard_map/ppermute | solution.py:746
  106.6 12.0 %collective-permute-start.50 = (bf16[224,768]{1,0:T(8,128)(2,1)S(1)}, bf16[224,768]{1,0:T(8,128)(2,1)S(1)}, u32[]{:S(2)}, u32[]{:S(2)}) collective-permute-start(bf16[224,768]{1,0:T(8,128)(2,1)S(1)} %get-tuple-element.278), channel_id=1, source_target_pairs={{0,4},{4,0},{8,12},{12,8},{16,20},{20,16},{24,28},{28,24},{1,5},{5... | collective-permute-start | bytes 1032200 | tf_op jit(solution)/shard_map/ppermute | solution.py:746
  107.8 3.1 %collective-permute-start.49 = (bf16[96,768]{1,0:T(8,128)(2,1)S(1)}, bf16[96,768]{1,0:T(8,128)(2,1)S(1)}, u32[]{:S(2)}, u32[]{:S(2)}) collective-permute-start(bf16[96,768]{1,0:T(8,128)(2,1)S(1)} %get-tuple-element.297), channel_id=1, source_target_pairs={{0,1},{1,0},{2,3},{3,2},{4,5},{5,4},{6,7},{7,6},{8,9},{9,8},{10,11... | collective-permute-start | bytes 442376 | tf_op jit(solution)/shard_map/ppermute | solution.py:24
  110.1 11.3 %collective-permute-start.52 = (bf16[192,768]{1,0:T(8,128)(2,1)S(1)}, bf16[192,768]{1,0:T(8,128)(2,1)S(1)}, u32[]{:S(2)}, u32[]{:S(2)}) collective-permute-start(bf16[192,768]{1,0:T(8,128)(2,1)S(1)} %second_add.8.mine), channel_id=1, source_target_pairs={{8,16},{12,20},{16,8},{20,12},{9,17},{13,21},{17,9},{21,13},{10,18... | collective-permute-start | bytes 884744 | tf_op jit(solution)/shard_map/ppermute | solution.py:746
  110.9 9.1 %collective-permute-start.51 = (bf16[96,768]{1,0:T(8,128)(2,1)S(1)}, bf16[96,768]{1,0:T(8,128)(2,1)S(1)}, u32[]{:S(2)}, u32[]{:S(2)}) collective-permute-start(bf16[96,768]{1,0:T(8,128)(2,1)S(1)} %second_half.2), channel_id=1, source_target_pairs={{0,2},{1,3},{2,0},{3,1},{4,6},{5,7},{6,4},{7,5},{8,10},{9,11},{10,... | collective-permute-start | bytes 442376 | tf_op jit(solution)/shard_map/ppermute | solution.py:24
  112.5 13.5 %collective-permute-start.54 = (bf16[192,768]{1,0:T(8,128)(2,1)S(1)}, bf16[192,768]{1,0:T(8,128)(2,1)S(1)}, u32[]{:S(2)}, u32[]{:S(2)}) collective-permute-start(bf16[192,768]{1,0:T(8,128)(2,1)S(1)} %get-tuple-element.299), channel_id=1, source_target_pairs={{0,8},{4,12},{24,16},{28,20},{1,9},{5,13},{25,17},{29,21},{2,10},{... | collective-permute-start | bytes 884744 | tf_op jit(solution)/shard_map/ppermute | solution.py:746
  118.7 12.9 %collective-permute-start.56 = (bf16[224,768]{1,0:T(8,128)(2,1)S(1)}, bf16[224,768]{1,0:T(8,128)(2,1)S(1)}, u32[]{:S(2)}, u32[]{:S(2)}) collective-permute-start(bf16[224,768]{1,0:T(8,128)(2,1)S(1)} %get-tuple-element.306.mine), channel_id=1, source_target_pairs={{0,8},{4,12},{24,16},{28,20},{1,9},{5,13},{25,17},{29,21},{2,10},{... | collective-permute-start | bytes 1032200 | tf_op jit(solution)/shard_map/ppermute | solution.py:746
  120.1 10.4 %collective-permute-start.55 = (bf16[192,768]{1,0:T(8,128)(2,1)S(1)}, bf16[192,768]{1,0:T(8,128)(2,1)S(1)}, u32[]{:S(2)}, u32[]{:S(2)}) collective-permute-start(bf16[192,768]{1,0:T(8,128)(2,1)S(1)} %join_owners.2.mine), channel_id=1, source_target_pairs={{8,0},{12,4},{16,24},{20,28},{9,1},{13,5},{17,25},{21,29},{10,2},{... | collective-permute-start | bytes 884744 | tf_op jit(solution)/shard_map/ppermute | solution.py:746
  121.6 13.5 %collective-permute-start.58 = (bf16[192,768]{1,0:T(8,128)(2,1)S(1)}, bf16[192,768]{1,0:T(8,128)(2,1)S(1)}, u32[]{:S(2)}, u32[]{:S(2)}) collective-permute-start(bf16[192,768]{1,0:T(8,128)(2,1)S(1)} %third_add.4.mine), channel_id=1, source_target_pairs={{8,0},{12,4},{16,24},{20,28},{9,1},{13,5},{17,25},{21,29},{10,2},{... | collective-permute-start | bytes 884744 | tf_op jit(solution)/shard_map/ppermute | solution.py:746
  126.1 10.1 %collective-permute-start.59 = (bf16[192,768]{1,0:T(8,128)(2,1)S(1)}, bf16[192,768]{1,0:T(8,128)(2,1)S(1)}, u32[]{:S(2)}, u32[]{:S(2)}) collective-permute-start(bf16[192,768]{1,0:T(8,128)(2,1)S(1)} %second_add.9.mine), channel_id=1, source_target_pairs={{8,16},{12,20},{16,8},{20,12},{9,17},{13,21},{17,9},{21,13},{10,18... | collective-permute-start | bytes 884744 | tf_op jit(solution)/shard_map/ppermute | solution.py:746
  126.7 5.7 %collective-permute-start.57 = (bf16[96,768]{1,0:T(8,128)(2,1)S(1)}, bf16[96,768]{1,0:T(8,128)(2,1)S(1)}, u32[]{:S(2)}, u32[]{:S(2)}) collective-permute-start(bf16[96,768]{1,0:T(8,128)(2,1)S(1)} %second_half.3), channel_id=1, source_target_pairs={{0,2},{1,3},{2,0},{3,1},{4,6},{5,7},{6,4},{7,5},{8,10},{9,11},{10,... | collective-permute-start | bytes 442376 | tf_op jit(solution)/shard_map/ppermute | solution.py:24
  131.7 4.5 %collective-permute-start.60 = (bf16[224,768]{1,0:T(8,128)(2,1)S(1)}, bf16[224,768]{1,0:T(8,128)(2,1)S(1)}, u32[]{:S(2)}, u32[]{:S(2)}) collective-permute-start(bf16[224,768]{1,0:T(8,128)(2,1)S(1)} %second_add_pair.1.mine), channel_id=1, source_target_pairs={{8,16},{12,20},{16,8},{20,12},{9,17},{13,21},{17,9},{21,13},{10,18... | collective-permute-start | bytes 1032200 | tf_op jit(solution)/shard_map/ppermute | solution.py:746
  132.5 10.0 %collective-permute-start.61 = (bf16[192,768]{1,0:T(8,128)(2,1)S(1)}, bf16[192,768]{1,0:T(8,128)(2,1)S(1)}, u32[]{:S(2)}, u32[]{:S(2)}) collective-permute-start(bf16[192,768]{1,0:T(8,128)(2,1)S(1)} %join_owners.3.mine), channel_id=1, source_target_pairs={{8,0},{12,4},{16,24},{20,28},{9,1},{13,5},{17,25},{21,29},{10,2},{... | collective-permute-start | bytes 884744 | tf_op jit(solution)/shard_map/ppermute | solution.py:746
  133.8 10.1 %collective-permute-start.62 = (bf16[192,768]{1,0:T(8,128)(2,1)S(1)}, bf16[192,768]{1,0:T(8,128)(2,1)S(1)}, u32[]{:S(2)}, u32[]{:S(2)}) collective-permute-start(bf16[192,768]{1,0:T(8,128)(2,1)S(1)} %choose.5.mine0), channel_id=1, source_target_pairs={{0,4},{4,0},{8,12},{12,8},{16,20},{20,16},{24,28},{28,24},{1,5},{5... | collective-permute-start | bytes 884744 | tf_op jit(solution)/shard_map/ppermute | solution.py:746
  135.1 12.9 %collective-permute-start.63 = (bf16[192,768]{1,0:T(8,128)(2,1)S(1)}, bf16[192,768]{1,0:T(8,128)(2,1)S(1)}, u32[]{:S(2)}, u32[]{:S(2)}) collective-permute-start(bf16[192,768]{1,0:T(8,128)(2,1)S(1)} %choose.7.mine1), channel_id=1, source_target_pairs={{0,4},{4,0},{8,12},{12,8},{16,20},{20,16},{24,28},{28,24},{1,5},{5... | collective-permute-start | bytes 884744 | tf_op jit(solution)/shard_map/ppermute | solution.py:746
  136.1 22.7 %collective-permute-start.65 = (bf16[384,640]{1,0:T(8,128)(2,1)S(1)}, bf16[384,640]{1,0:T(8,128)(2,1)S(1)}, u32[]{:S(2)}, u32[]{:S(2)}) collective-permute-start(bf16[384,640]{1,0:T(8,128)(2,1)S(1)} %get-tuple-element.320), channel_id=1, source_target_pairs={{0,1},{1,0},{2,3},{3,2},{4,5},{5,4},{6,7},{7,6},{8,9},{9,8},{10,11... | collective-permute-start | bytes 1474568 | tf_op jit(solution)/shard_map/ppermute | solution.py:24
  136.3 25.7 %collective-permute-start.68 = (bf16[224,768]{1,0:T(8,128)(2,1)S(1)}, bf16[224,768]{1,0:T(8,128)(2,1)S(1)}, u32[]{:S(2)}, u32[]{:S(2)}) collective-permute-start(bf16[224,768]{1,0:T(8,128)(2,1)S(1)} %third_add_pair.1.mine), channel_id=1, source_target_pairs={{8,0},{12,4},{16,24},{20,28},{9,1},{13,5},{17,25},{21,29},{10,2},{... | collective-permute-start | bytes 1032200 | tf_op jit(solution)/shard_map/ppermute | solution.py:746
  142.5 16.3 %collective-permute-start.64 = (bf16[192,768]{1,0:T(8,128)(2,1)S(1)}, bf16[192,768]{1,0:T(8,128)(2,1)S(1)}, u32[]{:S(2)}, u32[]{:S(2)}) collective-permute-start(bf16[192,768]{1,0:T(8,128)(2,1)S(1)} %third_add.5.mine), channel_id=1, source_target_pairs={{8,0},{12,4},{16,24},{20,28},{9,1},{13,5},{17,25},{21,29},{10,2},{... | collective-permute-start | bytes 884744 | tf_op jit(solution)/shard_map/ppermute | solution.py:746
  143.8 16.6 %collective-permute-start.66 = (bf16[192,768]{1,0:T(8,128)(2,1)S(1)}, bf16[192,768]{1,0:T(8,128)(2,1)S(1)}, u32[]{:S(2)}, u32[]{:S(2)}) collective-permute-start(bf16[192,768]{1,0:T(8,128)(2,1)S(1)} %choose.6.mine0), channel_id=1, source_target_pairs={{0,4},{4,0},{8,12},{12,8},{16,20},{20,16},{24,28},{28,24},{1,5},{5... | collective-permute-start | bytes 884744 | tf_op jit(solution)/shard_map/ppermute | solution.py:746
  148.0 12.4 %collective-permute-start.67 = (bf16[192,768]{1,0:T(8,128)(2,1)S(1)}, bf16[192,768]{1,0:T(8,128)(2,1)S(1)}, u32[]{:S(2)}, u32[]{:S(2)}) collective-permute-start(bf16[192,768]{1,0:T(8,128)(2,1)S(1)} %choose.8.mine1), channel_id=1, source_target_pairs={{0,4},{4,0},{8,12},{12,8},{16,20},{20,16},{24,28},{28,24},{1,5},{5... | collective-permute-start | bytes 884744 | tf_op jit(solution)/shard_map/ppermute | solution.py:746
  158.9 6.8 %collective-permute-start.69 = (bf16[192,768]{1,0:T(8,128)(2,1)S(1)}, bf16[192,768]{1,0:T(8,128)(2,1)S(1)}, u32[]{:S(2)}, u32[]{:S(2)}) collective-permute-start(bf16[192,768]{1,0:T(8,128)(2,1)S(1)} %tokens_step.1), channel_id=1, source_target_pairs={{0,2},{1,3},{2,0},{3,1},{4,6},{5,7},{6,4},{7,5},{8,10},{9,11},{10,... | collective-permute-start | bytes 884744 | tf_op jit(solution)/shard_map/ppermute | solution.py:24
  159.3 9.5 %collective-permute-start.71 = (bf16[192,768]{1,0:T(8,128)(2,1)S(1)}, bf16[192,768]{1,0:T(8,128)(2,1)S(1)}, u32[]{:S(2)}, u32[]{:S(2)}) collective-permute-start(bf16[192,768]{1,0:T(8,128)(2,1)S(1)} %choose.9.vo_mine), channel_id=1, source_target_pairs={{0,4},{4,0},{8,12},{12,8},{16,20},{20,16},{24,28},{28,24},{1,5},{5... | collective-permute-start | bytes 884744 | tf_op jit(solution)/shard_map/ppermute | solution.py:746
  162.1 9.9 %collective-permute-start.70 = (bf16[192,768]{1,0:T(8,128)(2,1)S(1)}, bf16[192,768]{1,0:T(8,128)(2,1)S(1)}, u32[]{:S(2)}, u32[]{:S(2)}) collective-permute-start(bf16[192,768]{1,0:T(8,128)(2,1)S(1)} %get-tuple-element.342.qk_mine), channel_id=1, source_target_pairs={{0,4},{4,0},{8,12},{12,8},{16,20},{20,16},{24,28},{28,24},{1,5},{5... | collective-permute-start | bytes 884744 | tf_op jit(solution)/shard_map/ppermute | solution.py:746
  (25 other events, 202.6 us)
